TPU v7x, 32 devices: a whole 2x2x4 slice. The times are simulated.
32 devices in a mesh: section: 2 (over core), tm: 8 (over z, x), tile: 2 (over y).
Axes of the slice: x: 2, y: 2, z: 4, core: 2. Of those that a mesh axis runs over, the one named last changes fastest.
Arguments:
- features: bfloat16 [16, 16, 64, 256], P('tm', 'tile', None, 'section'), may hold values from -320 to 320
- norm_gain_in: float32 [256], replicated, may hold values from 0.1 to 1.9
- norm_shift_in: float32 [256], replicated, may hold values from -0.8 to 0.8
- conv_in_weight: bfloat16 [3, 3, 3, 256, 128], replicated, may hold values from -0.078125 to 0.078125
- conv_in_bias: float32 [128], replicated, may hold values from -1 to 1
- norm_gain_mid: float32 [128], replicated, may hold values from 0.1 to 1.9
- norm_shift_mid: float32 [128], replicated, may hold values from -0.8 to 0.8
- conv_mid_weight: bfloat16 [3, 3, 3, 128, 128], replicated, may hold values from -0.109375 to 0.109375
- conv_mid_bias: float32 [128], replicated, may hold values from -0.6 to 0.6
- skip_weight: bfloat16 [256, 128], replicated, may hold values from -0.09375 to 0.09375
- skip_bias: float32 [128], replicated, may hold values from -0.6 to 0.6
Outputs:
- block_out: bfloat16 [16, 16, 64, 128], P('tm', 'tile', 'section')
All inputs are finite; a program needn't handle non-finite values.
Results may differ from a plain program's by a relative error of at most 0.008.
Values may be sent and summed in bfloat16 or wider, within the bound.
No kernel may reach another device: no remote copies, remote signals or barrier semaphores. Data moves between devices by JAX's collectives and lax.ppermute only.
A program may use at most 64 MiB of HBM per device.

v0:
```python
import functools

import jax
import jax.numpy as jnp
from jax import lax
from jax.experimental import pallas as pl
from jax.experimental.pallas import tpu as pltpu
from jax.sharding import PartitionSpec as P

GROUPS = 32
AXES = ("section", "tm", "tile")
VMEM_LIMIT = 48 * 1024 * 1024
RIM = 16


def params():
    return pltpu.CompilerParams(vmem_limit_bytes=VMEM_LIMIT)


def cost(flops, moved):
    return pl.CostEstimate(flops=flops, bytes_accessed=moved, transcendentals=0)


def vmem_specs(count):
    return [pl.BlockSpec(memory_space=pltpu.VMEM)] * count


def silu(u):
    half = 0.5 * u
    return half + half * jnp.tanh(half)


def moments_of(cells):
    mean = jnp.sum(cells, axis=0, keepdims=True) * (1.0 / cells.shape[0])
    off = cells - mean
    return jnp.concatenate([mean, jnp.sum(off * off, axis=0, keepdims=True)], axis=0)


def group_matrix(channels, width):
    shape = (channels, channels)
    row = lax.broadcasted_iota(jnp.int32, shape, 0) // width
    col = lax.broadcasted_iota(jnp.int32, shape, 1) // width
    return jnp.where(row == col, 1.0, 0.0).astype(jnp.float32)


def group_sum(values, matrix):
    tall = jnp.broadcast_to(values, (8, values.shape[-1]))
    return jnp.dot(
        tall, matrix, preferred_element_type=jnp.float32, precision=lax.Precision.HIGHEST
    )[:1]


def scale_and_offset(moments, cells, width, gain, shift):
    devices, _, channels = moments.shape
    matrix = group_matrix(channels, width)
    means = moments[:, 0, :]
    mean = group_sum(jnp.sum(means, axis=0, keepdims=True), matrix) * (1.0 / (devices * width))
    off = means - mean
    total = jnp.sum(moments[:, 1, :] + float(cells) * (off * off), axis=0, keepdims=True)
    spread = group_sum(total, matrix) * (1.0 / (cells * devices * width))
    scale = lax.rsqrt(spread + 1e-6) * gain
    return mean, scale, shift


def apply_norm(values, norm):
    mean, scale, shift = norm
    return silu((values.astype(jnp.float32) - mean) * scale + shift).astype(jnp.bfloat16)


def first_kernel(pairs, x_ref, moments_ref, *edge_refs):
    x = x_ref[...]
    cells = x.astype(jnp.float32).reshape(-1, x.shape[-1])
    moments_ref[...] = jnp.broadcast_to(moments_of(cells)[None], moments_ref.shape)
    rows = x_ref.shape[1]
    if pairs:
        first = (rows - 2) * (1 - lax.axis_index("tile"))
        edge_refs[0][...] = x_ref[:, pl.ds(first, 2)]
    else:
        edge_refs[0][...] = x_ref[:, :2]
        edge_refs[1][...] = x_ref[:, -2:]


def scales_kernel(cells, moments_ref, gain_ref, shift_ref, norm_ref):
    sections, half = gain_ref.shape
    per_section = moments_ref.shape[0] // sections
    for k in range(sections):
        norm = scale_and_offset(
            moments_ref[k * per_section : (k + 1) * per_section],
            cells,
            sections * half // GROUPS,
            gain_ref[k : k + 1],
            shift_ref[k : k + 1],
        )
        norm_ref[k] = jnp.concatenate(norm, axis=0)


def conv_rows(act_ref, weight_ref, frames, rows, width):
    total = None
    for t, frame in enumerate(frames):
        for h in range(3) if frame is not None else ():
            cells = act_ref[frame, h : h + rows]
            cells = cells.reshape(rows * width, cells.shape[-1])
            taps = jnp.concatenate([weight_ref[t, h, w] for w in range(3)], axis=-1)
            part = jnp.dot(cells, taps, preferred_element_type=jnp.float32)
            total = part if total is None else total + part
    outputs = weight_ref.shape[-1]
    total = total.reshape(rows, width, 3 * outputs)
    before, middle, after = (total[..., k * outputs : (k + 1) * outputs] for k in range(3))
    before = jnp.concatenate([before[:, :1], before[:, :-1]], axis=1)
    after = jnp.concatenate([after[:, 1:], after[:, -1:]], axis=1)
    return middle + before + after


def middle_kernel(
    tiles,
    x_ref,
    prev_ref,
    up_ref,
    down_ref,
    up_prev_ref,
    down_prev_ref,
    other_x_ref,
    other_prev_ref,
    other_up_ref,
    other_down_ref,
    other_up_prev_ref,
    other_down_prev_ref,
    norm_ref,
    weight_ref,
    bias_ref,
    hidden_ref,
    out_moments_ref,
    act_ref,
):
    section, tm, tile = (lax.axis_index(axis) for axis in AXES)
    frames, rows, columns, half = x_ref.shape
    width = columns // 2 + RIM
    first = pl.multiple_of(section * (columns - width), RIM)
    cols = pl.ds(first, width)
    pieces = (
        (
            section,
            ((x_ref, up_ref, down_ref), (prev_ref, up_prev_ref, down_prev_ref)),
        ),
        (
            1 - section,
            (
                (other_x_ref, other_up_ref, other_down_ref),
                (other_prev_ref, other_up_prev_ref, other_down_prev_ref),
            ),
        ),
    )
    for which, (now, before) in pieces:
        norm = tuple(norm_ref[which, k : k + 1] for k in range(3))
        lanes = pl.ds(pl.multiple_of(which * half, half), half)
        for start, (body, up, down) in ((frames, now), (0, before)):
            for f in range(frames):
                act_ref[start + f, 2 : 2 + rows, :, lanes] = apply_norm(body[f, :, cols, :], norm)
                act_ref[start + f, 0:2, :, lanes] = apply_norm(up[f, :, cols, :], norm)
                act_ref[start + f, 2 + rows :, :, lanes] = apply_norm(down[f, :, cols, :], norm)

    @pl.when(tile == 0)
    def _():
        for f in range(2 * frames):
            act_ref[f, 1] = act_ref[f, 2]

    @pl.when(tile == tiles - 1)
    def _():
        for f in range(2 * frames):
            act_ref[f, rows + 2] = act_ref[f, rows + 1]

    @pl.when(tm == 0)
    def _():
        for f in range(frames):
            act_ref[f] = act_ref[frames]

    own = columns // 2
    for f in range(frames):
        hidden = conv_rows(act_ref, weight_ref, (f, f + 1, f + 2), rows + 2, width)
        hidden_ref[f] = (hidden + bias_ref[...]).astype(jnp.bfloat16)

    cells = hidden_ref[:, 1 : 1 + rows, pl.ds(first, own), :]
    cells = cells.astype(jnp.float32).reshape(-1, cells.shape[-1])
    out_moments_ref[...] = jnp.broadcast_to(moments_of(cells)[None], out_moments_ref.shape)


def sent_start(tiles, tile):
    return 1 - tile if tiles == 2 else 0


def pack_kernel(tiles, hidden_ref, sent_ref):
    section, tile = lax.axis_index("section"), lax.axis_index("tile")
    frames, padded, width, channels = hidden_ref.shape
    own = sent_ref.shape[2]
    first = pl.multiple_of(section * (width - own), RIM)
    sent_rows = sent_ref.shape[1] - 1
    top = sent_start(tiles, tile)
    for f in range(frames):
        sent_ref[f, :sent_rows] = hidden_ref[f, pl.ds(top, sent_rows), pl.ds(first, own), :]
        hidden = hidden_ref[f].astype(jnp.float32)
        rim = jnp.where(section == 0, hidden[:, own, :], hidden[:, width - own - 1, :])
        spare = jnp.zeros((own - padded, channels), jnp.float32)
        sent_ref[f, sent_rows] = jnp.concatenate([rim, spare], axis=0).astype(jnp.bfloat16)


def repeat_edges(act_ref, count, tiles, rows):
    tile = lax.axis_index("tile")

    @pl.when(tile == 0)
    def _():
        for f in range(count):
            act_ref[f, 0] = act_ref[f, 1]

    @pl.when(tile == tiles - 1)
    def _():
        for f in range(count):
            act_ref[f, rows + 1] = act_ref[f, rows]


def own_columns(values, own):
    section = lax.axis_index("section")
    width = values.shape[1]
    return jnp.where(section == 0, values[:, :own], values[:, width - own :])


def own_frames_kernel(
    tiles,
    hidden_ref,
    moments_ref,
    gain_ref,
    shift_ref,
    weight_ref,
    bias_ref,
    x_ref,
    other_x_ref,
    skip_ref,
    skip_bias_ref,
    part_ref,
    norm_ref,
    act_ref,
):
    section = lax.axis_index("section")
    frames, padded, width, outputs = hidden_ref.shape
    rows = padded - 2
    half = x_ref.shape[3]
    own = x_ref.shape[2] // 2
    norm = scale_and_offset(
        moments_ref[...],
        frames * rows * own,
        outputs // GROUPS,
        gain_ref[...],
        shift_ref[...],
    )
    norm_ref[...] = jnp.concatenate(norm, axis=0)
    for f in range(frames):
        act_ref[f] = apply_norm(hidden_ref[f], norm)
    repeat_edges(act_ref, frames, tiles, rows)
    mine = pl.ds(pl.multiple_of(section * own, own), own)
    skip_here = skip_ref[pl.ds(pl.multiple_of(section * half, half), half), :]
    skip_there = skip_ref[pl.ds(pl.multiple_of((1 - section) * half, half), half), :]
    for f in range(frames):
        taps = [k if k >= 0 else None for k in range(f - 2, f + 1)]
        residual = own_columns(conv_rows(act_ref, weight_ref, taps, rows, width), own)
        here = x_ref[f, :, mine, :].reshape(rows * own, half)
        there = other_x_ref[f, :, mine, :].reshape(rows * own, half)
        shortcut = jnp.dot(here, skip_here, preferred_element_type=jnp.float32)
        shortcut = shortcut + jnp.dot(there, skip_there, preferred_element_type=jnp.float32)
        part_ref[f] = (residual + bias_ref[...]) + (
            shortcut.reshape(rows, own, outputs) + skip_bias_ref[...]
        )


def last_kernel(
    tiles, hidden_ref, before_ref, norm_ref, weight_ref, part_ref, out_ref, act_ref
):
    section, tm, tile = (lax.axis_index(axis) for axis in AXES)
    frames, padded, width, outputs = hidden_ref.shape
    rows = padded - 2
    own = part_ref.shape[2]
    sent_rows = before_ref.shape[1] - 1
    top = sent_start(tiles, tile)
    first = pl.multiple_of(section * (width - own), RIM)
    beside = pl.multiple_of((1 - section) * own, RIM)
    norm = tuple(norm_ref[k : k + 1] for k in range(3))
    for f in range(frames):
        act_ref[f, pl.ds(top, sent_rows), pl.ds(first, own), :] = apply_norm(
            before_ref[f, :sent_rows], norm
        )
        rim = apply_norm(before_ref[f, sent_rows], norm).astype(jnp.float32)[:padded]
        rim = jnp.broadcast_to(rim[:, None, :], (padded, width - own, outputs))
        act_ref[f, :, pl.ds(beside, width - own), :] = rim.astype(jnp.bfloat16)

    @pl.when(tm == 0)
    def _():
        start = apply_norm(hidden_ref[0], norm)
        for f in range(frames):
            act_ref[f] = start

    repeat_edges(act_ref, frames, tiles, rows)
    for f in range(frames):
        taps = [k if k < frames else None for k in range(f, f + 3)]
        residual = own_columns(conv_rows(act_ref, weight_ref, taps, rows, width), own)
        out_ref[f] = (part_ref[f] + residual).astype(jnp.bfloat16)


def pairs_for(tm_count, tile_count, tm_step, tile_step):
    out = []
    for a in range(tm_count):
        for b in range(tile_count):
            c, d = a + tm_step, b + tile_step
            if 0 <= c < tm_count and 0 <= d < tile_count:
                out.append((a * tile_count + b, c * tile_count + d))
    return out


def to_everyone(moments):
    return lax.all_to_all(moments, AXES, 0, 0, tiled=True)


def shards(
    features,
    norm_gain_in,
    norm_shift_in,
    conv_in_weight,
    conv_in_bias,
    norm_gain_mid,
    norm_shift_mid,
    conv_mid_weight,
    conv_mid_bias,
    skip_weight,
    skip_bias,
):
    sections, tms, tiles = (lax.axis_size(axis) for axis in AXES)
    parties = sections * tms * tiles
    frames, rows, columns, half = features.shape
    own = columns // sections
    width = own + RIM
    middle = conv_in_weight.shape[-1]
    outputs = conv_mid_weight.shape[-1]
    grid_axes = ("tm", "tile")

    def shift(value, tm_step, tile_step):
        return lax.ppermute(value, grid_axes, pairs_for(tms, tiles, tm_step, tile_step))

    def swap(value):
        return lax.ppermute(value, "section", [(0, 1), (1, 0)])

    previous = shift(features, 1, 0)
    edge = jax.ShapeDtypeStruct((frames, 2, columns, half), features.dtype)
    edges = 1 if tiles == 2 else 2
    moments, *edge_rows = pl.pallas_call(
        functools.partial(first_kernel, tiles == 2),
        out_shape=(jax.ShapeDtypeStruct((parties, 2, half), jnp.float32),) + (edge,) * edges,
        in_specs=vmem_specs(1),
        out_specs=tuple(vmem_specs(1 + edges)),
        compiler_params=params(),
        cost_estimate=cost(1_000_000_000, 1_000_000),
        name="feature_moments",
    )(features)
    if tiles == 2:
        (facing,) = edge_rows
        crossing = [
            (a * 2 + b, (a + 1) * 2 + 1 - b) for a in range(tms - 1) for b in range(2)
        ]
        rims = [
            lax.ppermute(facing, "tile", [(0, 1), (1, 0)]),
            lax.ppermute(facing, grid_axes, crossing),
        ]
    else:
        top, bottom = edge_rows
        rims = [
            shift(bottom, 0, 1),
            shift(bottom, 1, 1),
            shift(top, 0, -1),
            shift(top, 1, -1),
        ]
    other = swap(features)
    moments = to_everyone(moments)
    norm_in = pl.pallas_call(
        functools.partial(scales_kernel, frames * rows * columns),
        out_shape=jax.ShapeDtypeStruct((sections, 3, half), jnp.float32),
        in_specs=vmem_specs(3),
        out_specs=pl.BlockSpec(memory_space=pltpu.VMEM),
        compiler_params=params(),
        cost_estimate=cost(1_000_000_000, 1_000_000),
        name="feature_scales",
    )(moments, norm_gain_in.reshape(sections, half), norm_shift_in.reshape(sections, half))
    previous, norm_in, *rims = lax.optimization_barrier((previous, norm_in, *rims))
    other_previous = swap(previous)
    other_rims = [swap(rim) for rim in rims]
    up, up_prev, down, down_prev = (rims * 2)[:4]
    other_up, other_up_prev, other_down, other_down_prev = (other_rims * 2)[:4]

    sent_rows = rows + (1 if tiles == 2 else 2)
    hidden, moments_mid = pl.pallas_call(
        functools.partial(middle_kernel, tiles),
        out_shape=(
            jax.ShapeDtypeStruct((frames, rows + 2, width, middle), jnp.bfloat16),
            jax.ShapeDtypeStruct((parties, 2, middle), jnp.float32),
        ),
        in_specs=vmem_specs(15),
        out_specs=tuple(vmem_specs(2)),
        scratch_shapes=[pltpu.VMEM((2 * frames, rows + 4, width, 2 * half), jnp.bfloat16)],
        compiler_params=params(),
        cost_estimate=cost(4_000_000_000, 1_000_000),
        name="norm_conv_in",
    )(
        features,
        previous,
        up,
        down,
        up_prev,
        down_prev,
        other,
        other_previous,
        other_up,
        other_down,
        other_up_prev,
        other_down_prev,
        norm_in,
        conv_in_weight,
        conv_in_bias.reshape(1, middle),
    )
    moments_mid = to_everyone(moments_mid)
    sent = pl.pallas_call(
        functools.partial(pack_kernel, tiles),
        out_shape=jax.ShapeDtypeStruct((frames, sent_rows + 1, own, middle), jnp.bfloat16),
        in_specs=vmem_specs(1),
        out_specs=pl.BlockSpec(memory_space=pltpu.VMEM),
        compiler_params=params(),
        cost_estimate=cost(1_000_000_000, 1_000_000),
        name="pack_hidden",
    )(hidden)
    before = shift(sent, 1, 0)
    part, norm_mid = pl.pallas_call(
        functools.partial(own_frames_kernel, tiles),
        out_shape=(
            jax.ShapeDtypeStruct((frames, rows, own, outputs), jnp.float32),
            jax.ShapeDtypeStruct((3, middle), jnp.float32),
        ),
        in_specs=vmem_specs(10),
        out_specs=tuple(vmem_specs(2)),
        scratch_shapes=[pltpu.VMEM((frames, rows + 2, width, middle), jnp.bfloat16)],
        compiler_params=params(),
        cost_estimate=cost(2_000_000_000, 1_000_000),
        name="conv_mid_own_frames",
    )(
        hidden,
        moments_mid,
        norm_gain_mid.reshape(1, middle),
        norm_shift_mid.reshape(1, middle),
        conv_mid_weight,
        conv_mid_bias.reshape(1, outputs),
        features,
        other,
        skip_weight,
        skip_bias.reshape(1, outputs),
    )
    return pl.pallas_call(
        functools.partial(last_kernel, tiles),
        out_shape=jax.ShapeDtypeStruct((frames, rows, own, outputs), jnp.bfloat16),
        in_specs=vmem_specs(5),
        out_specs=pl.BlockSpec(memory_space=pltpu.VMEM),
        scratch_shapes=[pltpu.VMEM((frames, rows + 2, width, middle), jnp.bfloat16)],
        compiler_params=params(),
        cost_estimate=cost(2_000_000_000, 1_000_000),
        name="conv_mid_previous_frames",
    )(hidden, before, norm_mid, conv_mid_weight, part)


def solution(mesh):
    in_specs = (P("tm", "tile", None, "section"),) + (P(),) * 10
    out_specs = P("tm", "tile", "section", None)
    return jax.shard_map(shards, mesh=mesh, in_specs=in_specs, out_specs=out_specs, check_vma=False)
```

profile of v0, /device:TPU:0, one launch (start us, length us, event | category | flops | bytes accessed | tf_op | source)
XLA Modules:
  0.0 41.4 jit_solution(13504036751188679529)
XLA Ops:
  0.0 4.8 %collective-permute-start = (bf16[2,8,64,128]{3,2,1,0:T(8,128)(2,1)}, bf16[2,8,64,128]{3,2,1,0:T(8,128)(2,1)S(1)}, u32[]{:S(2)}, u32[]{:S(2)}) collective-permute-start(bf16[2,8,64,128]{3,2,1,0:T(8,128)(2,1)} %x_ref.5), channel_id=1, source_target_pairs={{0,2},{1,3},{2,4},{3,5},{4,6},{5,7},{6,8},{7,9},{8,10},{9,11},{10,... | collective-permute-start | bytes 786440 | tf_op jit(solution)/shard_map/ppermute | solution.py:343
  4.9 0.0 copy-start.2
  4.9 0.9 %copy-done.2 = bf16[2,8,64,128]{3,2,1,0:T(8,128)(2,1)S(1)} copy-done((bf16[2,8,64,128]{3,2,1,0:T(8,128)(2,1)S(1)}, bf16[2,8,64,128]{3,2,1,0:T(8,128)(2,1)}, u32[]{:S(2)}) %copy-start.2) | copy-done | bytes 262168
  5.8 0.0 copy-start.3
  5.8 0.0 copy-start.5
  5.8 0.0 copy-start.6
  5.8 0.9 %feature_moments.1 = (f32[32,2,128]{2,1,0:T(2,128)}, bf16[2,2,64,128]{3,2,1,0:T(8,128)(2,1)S(1)}) custom-call(bf16[2,8,64,128]{3,2,1,0:T(8,128)(2,1)S(1)} %copy-done.2), custom_call_target="tpu_custom_call" | custom-call | flops 1000000000 | bytes 1000000 | tf_op jit(solution)/shard_map/feature_moments/pallas_call | solution.py:351
  6.7 4.9 %all-to-all-start = ((f32[32,2,128]{2,1,0:T(2,128)}), f32[32,2,128]{2,1,0:T(2,128)S(1)}, u32[]{:S(2)}, u32[]{:S(2)}) async-start(f32[32,2,128]{2,1,0:T(2,128)} %get-tuple-element.15), calls=%async_computation | async-start | bytes 65536 | tf_op jit(solution)/shard_map/all_to_all | solution.py:317
  11.6 4.6 %collective-permute-start.2 = (bf16[2,2,64,128]{3,2,1,0:T(8,128)(2,1)S(1)}, bf16[2,2,64,128]{3,2,1,0:T(8,128)(2,1)S(1)}, u32[]{:S(2)}, u32[]{:S(2)}) collective-permute-start(bf16[2,2,64,128]{3,2,1,0:T(8,128)(2,1)S(1)} %get-tuple-element.16), channel_id=1, source_target_pairs={{0,3},{1,2},{2,5},{3,4},{4,7},{5,6},{6,9},{7,8},{8,11},{9,10},{10,... | collective-permute-start | bytes 196616 | tf_op jit(solution)/shard_map/ppermute | solution.py:367
  16.2 0.6 %collective-permute-start.1 = (bf16[2,2,64,128]{3,2,1,0:T(8,128)(2,1)S(1)}, bf16[2,2,64,128]{3,2,1,0:T(8,128)(2,1)S(1)}, u32[]{:S(2)}, u32[]{:S(2)}) collective-permute-start(bf16[2,2,64,128]{3,2,1,0:T(8,128)(2,1)S(1)} %get-tuple-element.16), channel_id=1, source_target_pairs={{0,1},{1,0},{2,3},{3,2},{4,5},{5,4},{6,7},{7,6},{8,9},{9,8},{10,11... | collective-permute-start | bytes 196616 | tf_op jit(solution)/shard_map/ppermute | solution.py:366
  16.9 0.0 copy-done.3
  16.9 0.0 collective-permute-start.3
  16.9 2.0 %all-to-all-done.moments_ref = f32[32,2,128]{2,1,0:T(2,128)S(1)} async-done(((f32[32,2,128]{2,1,0:T(2,128)}), f32[32,2,128]{2,1,0:T(2,128)S(1)}, u32[]{:S(2)}, u32[]{:S(2)}) %all-to-all-start) | async-done | bytes 32800 | tf_op jit(solution)/shard_map/all_to_all | solution.py:317
  18.9 0.0 copy-done.5
  18.9 0.0 copy-done.6
  18.9 0.0 copy-start
  18.9 0.5 %feature_scales.1.norm_ref = f32[2,3,128]{2,1,0:T(4,128)S(1)} custom-call(f32[32,2,128]{2,1,0:T(2,128)S(1)} %all-to-all-done.moments_ref, f32[2,128]{1,0:T(2,128)S(1)} %bitcast.7, f32[2,128]{1,0:T(2,128)S(1)} %bitcast.8), custom_call_target="tpu_custom_call" | custom-call | flops 1000000000 | bytes 1000000 | tf_op jit(solution)/shard_map/feature_scales/pallas_call | solution.py:379
  19.5 0.0 collective-permute-done.2.up_prev_ref.down_prev_ref
  19.5 1.1 %collective-permute-done.1.up_ref.down_ref = bf16[2,2,64,128]{3,2,1,0:T(8,128)(2,1)S(1)} collective-permute-done((bf16[2,2,64,128]{3,2,1,0:T(8,128)(2,1)S(1)}, bf16[2,2,64,128]{3,2,1,0:T(8,128)(2,1)S(1)}, u32[]{:S(2)}, u32[]{:S(2)}) %collective-permute-start.1) | collective-permute-done | bytes 65568 | tf_op jit(solution)/shard_map/ppermute | solution.py:366
  20.6 0.0 collective-permute-done.prev_ref
  20.6 0.0 collective-permute-start.4
  20.6 0.5 %collective-permute-start.5 = (bf16[2,2,64,128]{3,2,1,0:T(8,128)(2,1)S(1)}, bf16[2,2,64,128]{3,2,1,0:T(8,128)(2,1)S(1)}, u32[]{:S(2)}, u32[]{:S(2)}) collective-permute-start(bf16[2,2,64,128]{3,2,1,0:T(8,128)(2,1)S(1)} %collective-permute-done.1.up_ref.down_ref), channel_id=1, source_target_pairs={{0,16},{16,0},{1,17},{17,1},{2,18},{18,2},{3,19},{19,3},{4,20},{20... | collective-permute-start | bytes 196616 | tf_op jit(solution)/shard_map/ppermute | solution.py:346
  21.1 0.0 collective-permute-start.6
  21.1 0.0 collective-permute-done.3.other_x_ref
  21.1 1.1 %collective-permute-done.5.other_up_ref.other_down_ref = bf16[2,2,64,128]{3,2,1,0:T(8,128)(2,1)S(1)} collective-permute-done((bf16[2,2,64,128]{3,2,1,0:T(8,128)(2,1)S(1)}, bf16[2,2,64,128]{3,2,1,0:T(8,128)(2,1)S(1)}, u32[]{:S(2)}, u32[]{:S(2)}) %collective-permute-start.5) | collective-permute-done | bytes 65568 | tf_op jit(solution)/shard_map/ppermute | solution.py:346
  22.2 0.1 collective-permute-done.6.other_up_prev_ref.other_down_prev_ref
  22.3 0.0 collective-permute-done.4.other_prev_ref
  22.3 0.0 copy-done
  22.3 0.0 copy-done.7
  22.3 3.9 %norm_conv_in.1 = (bf16[2,10,48,128]{3,2,1,0:T(8,128)(2,1)S(1)}, f32[32,2,128]{2,1,0:T(2,128)}) custom-call(bf16[2,8,64,128]{3,2,1,0:T(8,128)(2,1)S(1)} %copy-done.3, bf16[2,8,64,128]{3,2,1,0:T(8,128)(2,1)S(1)} %collective-permute-done.prev_ref, bf16[2,2,64,128]{3,2,1,0:T(8,128)(2,1)S(1)} %collective-permute-done.1.up_ref.down_ref, ...), custom_call_target="tpu_custom_call" | custom-call | flops 4000000000 | bytes 1000000 | tf_op jit(solution)/shard_map/norm_conv_in/pallas_call | solution.py:395
  26.3 4.7 %all-to-all-start.1 = ((f32[32,2,128]{2,1,0:T(2,128)}), f32[32,2,128]{2,1,0:T(2,128)S(1)}, u32[]{:S(2)}, u32[]{:S(2)}) async-start(f32[32,2,128]{2,1,0:T(2,128)} %get-tuple-element.22), calls=%async_computation.1 | async-start | bytes 65536 | tf_op jit(solution)/shard_map/all_to_all | solution.py:317
  30.9 0.0 copy-start.1
  31.0 0.0 copy-start.4
  31.0 0.0 copy-start.8
  31.0 0.0 copy-start.9
  31.0 0.0 copy-start.10
  31.0 0.0 copy-start.11
  31.1 3.8 %collective-permute-start.7 = (bf16[2,10,32,128]{3,2,1,0:T(8,128)(2,1)S(1)}, bf16[2,10,32,128]{3,2,1,0:T(8,128)(2,1)S(1)}, u32[]{:S(2)}, u32[]{:S(2)}) collective-permute-start(bf16[2,10,32,128]{3,2,1,0:T(8,128)(2,1)S(1)} %pack_hidden.1), channel_id=1, source_target_pairs={{0,2},{1,3},{2,4},{3,5},{4,6},{5,7},{6,8},{7,9},{8,10},{9,11},{10,... | collective-permute-start | bytes 491528 | tf_op jit(solution)/shard_map/ppermute | solution.py:343
  34.9 3.3 %all-to-all-done.1.moments_ref = f32[32,2,128]{2,1,0:T(2,128)S(1)} async-done(((f32[32,2,128]{2,1,0:T(2,128)}), f32[32,2,128]{2,1,0:T(2,128)S(1)}, u32[]{:S(2)}, u32[]{:S(2)}) %all-to-all-start.1) | async-done | bytes 32800 | tf_op jit(solution)/shard_map/all_to_all | solution.py:317
  38.2 0.0 copy-done.1
  38.2 0.0 copy-done.4
  38.2 0.0 copy-done.8
  38.2 0.0 copy-done.9
  38.2 0.0 copy-done.10
  38.2 0.0 copy-done.11
  38.2 1.5 %conv_mid_own_frames.1 = (f32[2,8,32,128]{3,2,1,0:T(8,128)S(1)}, f32[3,128]{1,0:T(4,128)S(1)}) custom-call(bf16[2,10,48,128]{3,2,1,0:T(8,128)(2,1)S(1)} %get-tuple-element.21.hidden_ref, f32[32,2,128]{2,1,0:T(2,128)S(1)} %all-to-all-done.1.moments_ref, f32[1,128]{1,0:T(1,128)S(1)} %bitcast.10, f32[1,128]{1,0:T(1,128)S(1)} %bitcast.11, ...), custom_call_target="tpu_custom_call" | custom-call | flops 2000000000 | bytes 1000000 | tf_op jit(solution)/shard_map/conv_mid_own_frames/pallas_call | solution.py:435
  39.7 0.0 collective-permute-done.7.before_ref
  39.7 1.7 %conv_mid_previous_frames.1 = bf16[2,8,32,128]{3,2,1,0:T(8,128)(2,1)} custom-call(bf16[2,10,48,128]{3,2,1,0:T(8,128)(2,1)S(1)} %get-tuple-element.21.hidden_ref, bf16[2,10,32,128]{3,2,1,0:T(8,128)(2,1)S(1)} %collective-permute-done.7.before_ref, f32[3,128]{1,0:T(4,128)S(1)} %get-tuple-element.23.norm_ref, bf16[3,3,3,128,128]{4,3,2,1,0:T(8,128)(2,1)S(1)} %copy-done.1, ...), custom_call_target="tpu_custom_call" | custom-call | flops 2000000000 | bytes 1000000 | tf_op jit(solution)/shard_map/conv_mid_previous_frames/pallas_call | solution.py:459
  (2 shorter events, 0.0 us)
Async XLA Ops:
  0.0 20.6 %collective-permute-start = (bf16[2,8,64,128]{3,2,1,0:T(8,128)(2,1)}, bf16[2,8,64,128]{3,2,1,0:T(8,128)(2,1)S(1)}, u32[]{:S(2)}, u32[]{:S(2)}) collective-permute-start(bf16[2,8,64,128]{3,2,1,0:T(8,128)(2,1)} %x_ref.5), channel_id=1, source_target_pairs={{0,2},{1,3},{2,4},{3,5},{4,6},{5,7},{6,8},{7,9},{8,10},{9,11},{10,... | collective-permute-start | bytes 786440 | tf_op jit(solution)/shard_map/ppermute | solution.py:343
  4.9 1.0 %copy-start.2 = (bf16[2,8,64,128]{3,2,1,0:T(8,128)(2,1)S(1)}, bf16[2,8,64,128]{3,2,1,0:T(8,128)(2,1)}, u32[]{:S(2)}) copy-start(bf16[2,8,64,128]{3,2,1,0:T(8,128)(2,1)} %x_ref.5) | copy-start | bytes 786436
  5.8 11.1 %copy-start.3 = (bf16[2,8,64,128]{3,2,1,0:T(8,128)(2,1)S(1)}, bf16[2,8,64,128]{3,2,1,0:T(8,128)(2,1)}, u32[]{:S(2)}) copy-start(bf16[2,8,64,128]{3,2,1,0:T(8,128)(2,1)} %x_ref.5) | copy-start | bytes 786436
  5.8 13.1 %copy-start.5 = (f32[256]{0:T(256)S(1)}, f32[256]{0:T(256)}, u32[]{:S(2)}) copy-start(f32[256]{0:T(256)} %param.12) | copy-start | bytes 3076
  5.8 13.1 %copy-start.6 = (f32[256]{0:T(256)S(1)}, f32[256]{0:T(256)}, u32[]{:S(2)}) copy-start(f32[256]{0:T(256)} %param.13) | copy-start | bytes 3076
  6.7 12.2 %all-to-all-start = ((f32[32,2,128]{2,1,0:T(2,128)}), f32[32,2,128]{2,1,0:T(2,128)S(1)}, u32[]{:S(2)}, u32[]{:S(2)}) async-start(f32[32,2,128]{2,1,0:T(2,128)} %get-tuple-element.15), calls=%async_computation | async-start | bytes 65536 | tf_op jit(solution)/shard_map/all_to_all | solution.py:317
  11.6 7.8 %collective-permute-start.2 = (bf16[2,2,64,128]{3,2,1,0:T(8,128)(2,1)S(1)}, bf16[2,2,64,128]{3,2,1,0:T(8,128)(2,1)S(1)}, u32[]{:S(2)}, u32[]{:S(2)}) collective-permute-start(bf16[2,2,64,128]{3,2,1,0:T(8,128)(2,1)S(1)} %get-tuple-element.16), channel_id=1, source_target_pairs={{0,3},{1,2},{2,5},{3,4},{4,7},{5,6},{6,9},{7,8},{8,11},{9,10},{10,... | collective-permute-start | bytes 196616 | tf_op jit(solution)/shard_map/ppermute | solution.py:367
  16.2 4.3 %collective-permute-start.1 = (bf16[2,2,64,128]{3,2,1,0:T(8,128)(2,1)S(1)}, bf16[2,2,64,128]{3,2,1,0:T(8,128)(2,1)S(1)}, u32[]{:S(2)}, u32[]{:S(2)}) collective-permute-start(bf16[2,2,64,128]{3,2,1,0:T(8,128)(2,1)S(1)} %get-tuple-element.16), channel_id=1, source_target_pairs={{0,1},{1,0},{2,3},{3,2},{4,5},{5,4},{6,7},{7,6},{8,9},{9,8},{10,11... | collective-permute-start | bytes 196616 | tf_op jit(solution)/shard_map/ppermute | solution.py:366
  16.9 4.2 %collective-permute-start.3 = (bf16[2,8,64,128]{3,2,1,0:T(8,128)(2,1)S(1)}, bf16[2,8,64,128]{3,2,1,0:T(8,128)(2,1)S(1)}, u32[]{:S(2)}, u32[]{:S(2)}) collective-permute-start(bf16[2,8,64,128]{3,2,1,0:T(8,128)(2,1)S(1)} %copy-done.3), channel_id=1, source_target_pairs={{0,16},{16,0},{1,17},{17,1},{2,18},{18,2},{3,19},{19,3},{4,20},{20... | collective-permute-start | bytes 786440 | tf_op jit(solution)/shard_map/ppermute | solution.py:346
  18.9 3.4 %copy-start = (bf16[3,3,3,256,128]{4,3,2,1,0:T(8,128)(2,1)S(1)}, bf16[3,3,3,256,128]{4,3,2,1,0:T(8,128)(2,1)}, u32[]{:S(2)}) copy-start(bf16[3,3,3,256,128]{4,3,2,1,0:T(8,128)(2,1)} %weight_ref.3) | copy-start | bytes 5308420
  18.9 3.4 %copy-start.7 = (f32[128]{0:T(128)S(1)}, f32[128]{0:T(128)}, u32[]{:S(2)}) copy-start(f32[128]{0:T(128)} %param.15) | copy-start | bytes 1540
  20.6 1.8 %collective-permute-start.4 = (bf16[2,8,64,128]{3,2,1,0:T(8,128)(2,1)S(1)}, bf16[2,8,64,128]{3,2,1,0:T(8,128)(2,1)S(1)}, u32[]{:S(2)}, u32[]{:S(2)}) collective-permute-start(bf16[2,8,64,128]{3,2,1,0:T(8,128)(2,1)S(1)} %collective-permute-done.prev_ref), channel_id=1, source_target_pairs={{0,16},{16,0},{1,17},{17,1},{2,18},{18,2},{3,19},{19,3},{4,20},{20... | collective-permute-start | bytes 786440 | tf_op jit(solution)/shard_map/ppermute | solution.py:346
  20.6 1.6 %collective-permute-start.5 = (bf16[2,2,64,128]{3,2,1,0:T(8,128)(2,1)S(1)}, bf16[2,2,64,128]{3,2,1,0:T(8,128)(2,1)S(1)}, u32[]{:S(2)}, u32[]{:S(2)}) collective-permute-start(bf16[2,2,64,128]{3,2,1,0:T(8,128)(2,1)S(1)} %collective-permute-done.1.up_ref.down_ref), channel_id=1, source_target_pairs={{0,16},{16,0},{1,17},{17,1},{2,18},{18,2},{3,19},{19,3},{4,20},{20... | collective-permute-start | bytes 196616 | tf_op jit(solution)/shard_map/ppermute | solution.py:346
  21.1 1.3 %collective-permute-start.6 = (bf16[2,2,64,128]{3,2,1,0:T(8,128)(2,1)S(1)}, bf16[2,2,64,128]{3,2,1,0:T(8,128)(2,1)S(1)}, u32[]{:S(2)}, u32[]{:S(2)}) collective-permute-start(bf16[2,2,64,128]{3,2,1,0:T(8,128)(2,1)S(1)} %collective-permute-done.2.up_prev_ref.down_prev_ref), channel_id=1, source_target_pairs={{0,16},{16,0},{1,17},{17,1},{2,18},{18,2},{3,19},{19,3},{4,20},{20... | collective-permute-start | bytes 196616 | tf_op jit(solution)/shard_map/ppermute | solution.py:346
  26.3 11.9 %all-to-all-start.1 = ((f32[32,2,128]{2,1,0:T(2,128)}), f32[32,2,128]{2,1,0:T(2,128)S(1)}, u32[]{:S(2)}, u32[]{:S(2)}) async-start(f32[32,2,128]{2,1,0:T(2,128)} %get-tuple-element.22), calls=%async_computation.1 | async-start | bytes 65536 | tf_op jit(solution)/shard_map/all_to_all | solution.py:317
  30.9 7.2 %copy-start.1 = (bf16[3,3,3,128,128]{4,3,2,1,0:T(8,128)(2,1)S(1)}, bf16[3,3,3,128,128]{4,3,2,1,0:T(8,128)(2,1)}, u32[]{:S(2)}) copy-start(bf16[3,3,3,128,128]{4,3,2,1,0:T(8,128)(2,1)} %weight_ref.5) | copy-start | bytes 2654212
  31.0 7.2 %copy-start.4 = (bf16[256,128]{1,0:T(8,128)(2,1)S(1)}, bf16[256,128]{1,0:T(8,128)(2,1)}, u32[]{:S(2)}) copy-start(bf16[256,128]{1,0:T(8,128)(2,1)} %skip_ref.1) | copy-start | bytes 196612
  31.0 7.2 %copy-start.8 = (f32[128]{0:T(128)S(1)}, f32[128]{0:T(128)}, u32[]{:S(2)}) copy-start(f32[128]{0:T(128)} %param.16) | copy-start | bytes 1540
  31.0 7.2 %copy-start.9 = (f32[128]{0:T(128)S(1)}, f32[128]{0:T(128)}, u32[]{:S(2)}) copy-start(f32[128]{0:T(128)} %param.17) | copy-start | bytes 1540
  31.0 7.2 %copy-start.10 = (f32[128]{0:T(128)S(1)}, f32[128]{0:T(128)}, u32[]{:S(2)}) copy-start(f32[128]{0:T(128)} %param.19) | copy-start | bytes 1540
  31.0 7.2 %copy-start.11 = (f32[128]{0:T(128)S(1)}, f32[128]{0:T(128)}, u32[]{:S(2)}) copy-start(f32[128]{0:T(128)} %param.21) | copy-start | bytes 1540
  31.1 8.7 %collective-permute-start.7 = (bf16[2,10,32,128]{3,2,1,0:T(8,128)(2,1)S(1)}, bf16[2,10,32,128]{3,2,1,0:T(8,128)(2,1)S(1)}, u32[]{:S(2)}, u32[]{:S(2)}) collective-permute-start(bf16[2,10,32,128]{3,2,1,0:T(8,128)(2,1)S(1)} %pack_hidden.1), channel_id=1, source_target_pairs={{0,2},{1,3},{2,4},{3,5},{4,6},{5,7},{6,8},{7,9},{8,10},{9,11},{10,... | collective-permute-start | bytes 491528 | tf_op jit(solution)/shard_map/ppermute | solution.py:343
where the time goes:
time: 41.7 us; the launch traced here: 41.4 us
  starting transfers between devices  24 us (58%)
  Pallas kernels  8.61 us (21%)
  waiting for transfers between devices  7.69 us (18%)
  local copies, waits for them, and re-layouts  1 us (2%)
    all_to_all x2, starting transfers between devices, to_everyone(): return lax.all_to_all(moments, AXES, 0, 0, tiled=True)  9.58 us
    ppermute x2, starting transfers between devices, shift(): lax.ppermute(value, grid_axes, pairs_for(tms, tiles, tm_step, tile_step))  8.66 us
    all_to_all x2, waiting for transfers between devices, to_everyone(): return lax.all_to_all(moments, AXES, 0, 0, tiled=True)  5.33 us
    ppermute x1, starting transfers between devices, shards(): lax.ppermute(facing, grid_axes, crossing)  4.58 us
    pallas_call x1, Pallas kernels, shards(): pl.pallas_call(functools.partial(middle_kernel, tiles), out_shape=(jax.Sh...  3.93 us
    pallas_call x1, Pallas kernels, shards(): pl.pallas_call(functools.partial(last_kernel, tiles), out_shape=jax.Shape...  1.68 us
    pallas_call x1, Pallas kernels, shards(): pl.pallas_call(functools.partial(own_frames_kernel, tiles), out_shape=(ja...  1.54 us
    ppermute x4, waiting for transfers between devices, swap(): return lax.ppermute(value, 'section', [(0, 1), (1, 0)])  1.25 us
  transfers between devices with their start and end apart: 10, of which 5 were waited for; matrix products, arithmetic and copies ran while one was open for 0% of the time, Pallas kernels for 7%

commit v1 on v0

--- a/solution.py
+++ b/solution.py
@@ -67,17 +67,21 @@
     return silu((values.astype(jnp.float32) - mean) * scale + shift).astype(jnp.bfloat16)
 
 
-def first_kernel(pairs, x_ref, moments_ref, *edge_refs):
+def first_kernel(x_ref, moments_ref):
     x = x_ref[...]
     cells = x.astype(jnp.float32).reshape(-1, x.shape[-1])
     moments_ref[...] = jnp.broadcast_to(moments_of(cells)[None], moments_ref.shape)
-    rows = x_ref.shape[1]
+
+
+def rows_kernel(pairs, x_ref, prev_ref, *edge_refs):
+    frames, rows = x_ref.shape[:2]
     if pairs:
-        first = (rows - 2) * (1 - lax.axis_index("tile"))
-        edge_refs[0][...] = x_ref[:, pl.ds(first, 2)]
+        starts = [(rows - 2) * (1 - lax.axis_index("tile"))]
     else:
-        edge_refs[0][...] = x_ref[:, :2]
-        edge_refs[1][...] = x_ref[:, -2:]
+        starts = [0, rows - 2]
+    for start, edge_ref in zip(starts, edge_refs):
+        edge_ref[:frames] = prev_ref[:, pl.ds(start, 2)]
+        edge_ref[frames:] = x_ref[:, pl.ds(start, 2)]
 
 
 def scales_kernel(cells, moments_ref, gain_ref, shift_ref, norm_ref):
@@ -117,14 +121,10 @@
     prev_ref,
     up_ref,
     down_ref,
-    up_prev_ref,
-    down_prev_ref,
     other_x_ref,
     other_prev_ref,
     other_up_ref,
     other_down_ref,
-    other_up_prev_ref,
-    other_down_prev_ref,
     norm_ref,
     weight_ref,
     bias_ref,
@@ -138,26 +138,17 @@
     first = pl.multiple_of(section * (columns - width), RIM)
     cols = pl.ds(first, width)
     pieces = (
-        (
-            section,
-            ((x_ref, up_ref, down_ref), (prev_ref, up_prev_ref, down_prev_ref)),
-        ),
-        (
-            1 - section,
-            (
-                (other_x_ref, other_up_ref, other_down_ref),
-                (other_prev_ref, other_up_prev_ref, other_down_prev_ref),
-            ),
-        ),
+        (section, prev_ref, x_ref, up_ref, down_ref),
+        (1 - section, other_prev_ref, other_x_ref, other_up_ref, other_down_ref),
     )
-    for which, (now, before) in pieces:
+    for which, before, now, up, down in pieces:
         norm = tuple(norm_ref[which, k : k + 1] for k in range(3))
         lanes = pl.ds(pl.multiple_of(which * half, half), half)
-        for start, (body, up, down) in ((frames, now), (0, before)):
-            for f in range(frames):
-                act_ref[start + f, 2 : 2 + rows, :, lanes] = apply_norm(body[f, :, cols, :], norm)
-                act_ref[start + f, 0:2, :, lanes] = apply_norm(up[f, :, cols, :], norm)
-                act_ref[start + f, 2 + rows :, :, lanes] = apply_norm(down[f, :, cols, :], norm)
+        for f in range(2 * frames):
+            body = before[f, :, cols, :] if f < frames else now[f - frames, :, cols, :]
+            act_ref[f, 2 : 2 + rows, :, lanes] = apply_norm(body, norm)
+            act_ref[f, 0:2, :, lanes] = apply_norm(up[f, :, cols, :], norm)
+            act_ref[f, 2 + rows :, :, lanes] = apply_norm(down[f, :, cols, :], norm)
 
     @pl.when(tile == 0)
     def _():
@@ -346,36 +337,32 @@
         return lax.ppermute(value, "section", [(0, 1), (1, 0)])
 
     previous = shift(features, 1, 0)
-    edge = jax.ShapeDtypeStruct((frames, 2, columns, half), features.dtype)
-    edges = 1 if tiles == 2 else 2
-    moments, *edge_rows = pl.pallas_call(
-        functools.partial(first_kernel, tiles == 2),
-        out_shape=(jax.ShapeDtypeStruct((parties, 2, half), jnp.float32),) + (edge,) * edges,
+    moments = pl.pallas_call(
+        first_kernel,
+        out_shape=jax.ShapeDtypeStruct((parties, 2, half), jnp.float32),
         in_specs=vmem_specs(1),
-        out_specs=tuple(vmem_specs(1 + edges)),
+        out_specs=pl.BlockSpec(memory_space=pltpu.VMEM),
         compiler_params=params(),
         cost_estimate=cost(1_000_000_000, 1_000_000),
         name="feature_moments",
     )(features)
+    moments = to_everyone(moments)
+    other = swap(features)
+    edges = 1 if tiles == 2 else 2
+    edge_rows = pl.pallas_call(
+        functools.partial(rows_kernel, tiles == 2),
+        out_shape=(jax.ShapeDtypeStruct((2 * frames, 2, columns, half), features.dtype),) * edges,
+        in_specs=vmem_specs(2),
+        out_specs=tuple(vmem_specs(edges)),
+        compiler_params=params(),
+        cost_estimate=cost(500_000_000, 1_000_000),
+        name="facing_rows",
+    )(features, previous)
     if tiles == 2:
-        (facing,) = edge_rows
-        crossing = [
-            (a * 2 + b, (a + 1) * 2 + 1 - b) for a in range(tms - 1) for b in range(2)
-        ]
-        rims = [
-            lax.ppermute(facing, "tile", [(0, 1), (1, 0)]),
-            lax.ppermute(facing, grid_axes, crossing),
-        ]
+        rims = [lax.ppermute(edge_rows[0], "tile", [(0, 1), (1, 0)])]
     else:
-        top, bottom = edge_rows
-        rims = [
-            shift(bottom, 0, 1),
-            shift(bottom, 1, 1),
-            shift(top, 0, -1),
-            shift(top, 1, -1),
-        ]
-    other = swap(features)
-    moments = to_everyone(moments)
+        rims = [shift(edge_rows[1], 0, 1), shift(edge_rows[0], 0, -1)]
+    other_previous = swap(previous)
     norm_in = pl.pallas_call(
         functools.partial(scales_kernel, frames * rows * columns),
         out_shape=jax.ShapeDtypeStruct((sections, 3, half), jnp.float32),
@@ -385,11 +372,10 @@
         cost_estimate=cost(1_000_000_000, 1_000_000),
         name="feature_scales",
     )(moments, norm_gain_in.reshape(sections, half), norm_shift_in.reshape(sections, half))
-    previous, norm_in, *rims = lax.optimization_barrier((previous, norm_in, *rims))
-    other_previous = swap(previous)
+    norm_in, *rims = lax.optimization_barrier((norm_in, *rims))
     other_rims = [swap(rim) for rim in rims]
-    up, up_prev, down, down_prev = (rims * 2)[:4]
-    other_up, other_up_prev, other_down, other_down_prev = (other_rims * 2)[:4]
+    up, down = (rims * 2)[:2]
+    other_up, other_down = (other_rims * 2)[:2]
 
     sent_rows = rows + (1 if tiles == 2 else 2)
     hidden, moments_mid = pl.pallas_call(
@@ -398,7 +384,7 @@
             jax.ShapeDtypeStruct((frames, rows + 2, width, middle), jnp.bfloat16),
             jax.ShapeDtypeStruct((parties, 2, middle), jnp.float32),
         ),
-        in_specs=vmem_specs(15),
+        in_specs=vmem_specs(11),
         out_specs=tuple(vmem_specs(2)),
         scratch_shapes=[pltpu.VMEM((2 * frames, rows + 4, width, 2 * half), jnp.bfloat16)],
         compiler_params=params(),
@@ -409,14 +395,10 @@
         previous,
         up,
         down,
-        up_prev,
-        down_prev,
         other,
         other_previous,
         other_up,
         other_down,
-        other_up_prev,
-        other_down_prev,
         norm_in,
         conv_in_weight,
         conv_in_bias.reshape(1, middle),

time: 41.7 us -> 39.1 us (0.938)
  starting transfers between devices: 24 us -> 19.6 us
  waiting for transfers between devices: 7.69 us -> 9.43 us
    ppermute x2 -> x1, starting transfers between devices: 5.2 us -> 1.83 us  [shards(): rims = [lax.ppermute(edge_rows[0], 'tile', [(0, 1), (1, 0)])]]
    all_to_all x2, waiting for transfers between devices: 5.33 us -> 8.09 us  [to_everyone(): return lax.all_to_all(moments, AXES, 0, 0, tiled=True)]
    ppermute x2 -> x1, waiting for transfers between devices: 1.1 us -> 0.01 us  [shards(): rims = [lax.ppermute(edge_rows[0], 'tile', [(0, 1), (1, 0)])]]
    all_to_all x2, starting transfers between devices: 9.58 us -> 8.59 us  [to_everyone(): return lax.all_to_all(moments, AXES, 0, 0, tiled=True)]
    ppermute x4 -> x3, waiting for transfers between devices: 1.25 us -> 1.33 us  [swap(): return lax.ppermute(value, 'section', [(0, 1), (1, 0)])]
    pallas_call x1 -> x2, Pallas kernels: 0.91 us -> 0.93 us  [the longest x1 0.91 us: shards(): pl.pallas_call(first_kernel, out_shape=jax.ShapeDtypeStruct((parties, 2,...]
  transfers between devices with their start and end apart: 10 -> 8, of which waited for: 5 -> 3; matrix products, arithmetic and copies ran while one was open for 0% -> 0% of each run, Pallas kernels for 7% -> 8%
where the time goes in v1:
time: 39.1 us; the launch traced here: 38.9 us
  starting transfers between devices  19.6 us (50%)
  waiting for transfers between devices  9.43 us (24%)
  Pallas kernels  8.62 us (22%)
  local copies, waits for them, and re-layouts  1 us (3%)
    ppermute x2, starting transfers between devices, shift(): lax.ppermute(value, grid_axes, pairs_for(tms, tiles, tm_step, tile_step))  8.66 us
    all_to_all x2, starting transfers between devices, to_everyone(): return lax.all_to_all(moments, AXES, 0, 0, tiled=True)  8.59 us
    all_to_all x2, waiting for transfers between devices, to_everyone(): return lax.all_to_all(moments, AXES, 0, 0, tiled=True)  8.09 us
    pallas_call x1, Pallas kernels, shards(): pl.pallas_call(functools.partial(middle_kernel, tiles), out_shape=(jax.Sh...  3.92 us
    ppermute x1, starting transfers between devices, shards(): rims = [lax.ppermute(edge_rows[0], 'tile', [(0, 1), (1, 0)])]  1.83 us
    pallas_call x1, Pallas kernels, shards(): pl.pallas_call(functools.partial(last_kernel, tiles), out_shape=jax.Shape...  1.68 us
    pallas_call x1, Pallas kernels, shards(): pl.pallas_call(functools.partial(own_frames_kernel, tiles), out_shape=(ja...  1.53 us
    ppermute x3, waiting for transfers between devices, swap(): return lax.ppermute(value, 'section', [(0, 1), (1, 0)])  1.33 us
  transfers between devices with their start and end apart: 8, of which 3 were waited for; matrix products, arithmetic and copies ran while one was open for 0% of the time, Pallas kernels for 8%

profile of v1, /device:TPU:0, one launch (start us, length us, event | category | flops | bytes accessed | tf_op | source)
XLA Modules:
  0.0 38.9 jit_solution(4900551804328416204)
XLA Ops:
  0.0 4.8 %collective-permute-start = (bf16[2,8,64,128]{3,2,1,0:T(8,128)(2,1)}, bf16[2,8,64,128]{3,2,1,0:T(8,128)(2,1)S(1)}, u32[]{:S(2)}, u32[]{:S(2)}) collective-permute-start(bf16[2,8,64,128]{3,2,1,0:T(8,128)(2,1)} %x_ref.7), channel_id=1, source_target_pairs={{0,2},{1,3},{2,4},{3,5},{4,6},{5,7},{6,8},{7,9},{8,10},{9,11},{10,... | collective-permute-start | bytes 786440 | tf_op jit(solution)/shard_map/ppermute | solution.py:334
  4.9 0.0 copy-start.2
  4.9 0.9 %copy-done.2 = bf16[2,8,64,128]{3,2,1,0:T(8,128)(2,1)S(1)} copy-done((bf16[2,8,64,128]{3,2,1,0:T(8,128)(2,1)S(1)}, bf16[2,8,64,128]{3,2,1,0:T(8,128)(2,1)}, u32[]{:S(2)}) %copy-start.2) | copy-done | bytes 262168
  5.8 0.0 copy-start.3
  5.8 0.9 %feature_moments.1 = f32[32,2,128]{2,1,0:T(2,128)} custom-call(bf16[2,8,64,128]{3,2,1,0:T(8,128)(2,1)S(1)} %copy-done.2), custom_call_target="tpu_custom_call" | custom-call | flops 1000000000 | bytes 1000000 | tf_op jit(solution)/shard_map/feature_moments/pallas_call | solution.py:340
  6.7 0.0 copy-start.5
  6.7 0.0 copy-start.6
  6.7 4.9 %all-to-all-start = ((f32[32,2,128]{2,1,0:T(2,128)}), f32[32,2,128]{2,1,0:T(2,128)S(1)}, u32[]{:S(2)}, u32[]{:S(2)}) async-start(f32[32,2,128]{2,1,0:T(2,128)} %feature_moments.1), calls=%async_computation | async-start | bytes 65536 | tf_op jit(solution)/shard_map/all_to_all | solution.py:308
  11.6 0.0 collective-permute-done.prev_ref
  11.7 0.0 copy-done.3
  11.7 1.8 %collective-permute-start.1 = (bf16[4,2,64,128]{3,2,1,0:T(8,128)(2,1)S(1)}, bf16[4,2,64,128]{3,2,1,0:T(8,128)(2,1)S(1)}, u32[]{:S(2)}, u32[]{:S(2)}) collective-permute-start(bf16[4,2,64,128]{3,2,1,0:T(8,128)(2,1)S(1)} %facing_rows.1), channel_id=1, source_target_pairs={{0,1},{1,0},{2,3},{3,2},{4,5},{5,4},{6,7},{7,6},{8,9},{9,8},{10,11... | collective-permute-start | bytes 393224 | tf_op jit(solution)/shard_map/ppermute | solution.py:362
  13.5 0.0 collective-permute-start.2
  13.5 0.5 %collective-permute-start.3 = (bf16[2,8,64,128]{3,2,1,0:T(8,128)(2,1)S(1)}, bf16[2,8,64,128]{3,2,1,0:T(8,128)(2,1)S(1)}, u32[]{:S(2)}, u32[]{:S(2)}) collective-permute-start(bf16[2,8,64,128]{3,2,1,0:T(8,128)(2,1)S(1)} %collective-permute-done.prev_ref), channel_id=1, source_target_pairs={{0,16},{16,0},{1,17},{17,1},{2,18},{18,2},{3,19},{19,3},{4,20},{20... | collective-permute-start | bytes 786440 | tf_op jit(solution)/shard_map/ppermute | solution.py:337
  14.0 4.8 %all-to-all-done.moments_ref = f32[32,2,128]{2,1,0:T(2,128)S(1)} async-done(((f32[32,2,128]{2,1,0:T(2,128)}), f32[32,2,128]{2,1,0:T(2,128)S(1)}, u32[]{:S(2)}, u32[]{:S(2)}) %all-to-all-start) | async-done | bytes 32800 | tf_op jit(solution)/shard_map/all_to_all | solution.py:308
  18.9 0.0 copy-done.5
  18.9 0.0 copy-done.6
  18.9 0.0 copy-start
  18.9 0.0 copy-start.7
  18.9 0.5 %feature_scales.1.norm_ref = f32[2,3,128]{2,1,0:T(4,128)S(1)} custom-call(f32[32,2,128]{2,1,0:T(2,128)S(1)} %all-to-all-done.moments_ref, f32[2,128]{1,0:T(2,128)S(1)} %bitcast.7, f32[2,128]{1,0:T(2,128)S(1)} %bitcast.8), custom_call_target="tpu_custom_call" | custom-call | flops 1000000000 | bytes 1000000 | tf_op jit(solution)/shard_map/feature_scales/pallas_call | solution.py:366
  19.4 0.0 collective-permute-done.1.up_ref.down_ref
  19.4 0.0 collective-permute-start.4
  19.5 0.0 collective-permute-done.2.other_x_ref
  19.5 1.3 %collective-permute-done.4.other_up_ref.other_down_ref = bf16[4,2,64,128]{3,2,1,0:T(8,128)(2,1)S(1)} collective-permute-done((bf16[4,2,64,128]{3,2,1,0:T(8,128)(2,1)S(1)}, bf16[4,2,64,128]{3,2,1,0:T(8,128)(2,1)S(1)}, u32[]{:S(2)}, u32[]{:S(2)}) %collective-permute-start.4) | collective-permute-done | bytes 131104 | tf_op jit(solution)/shard_map/ppermute | solution.py:337
  20.8 0.0 collective-permute-done.3.other_prev_ref
  20.8 0.0 copy-done
  20.8 0.0 copy-done.7
  20.8 3.9 %norm_conv_in.1 = (bf16[2,10,48,128]{3,2,1,0:T(8,128)(2,1)S(1)}, f32[32,2,128]{2,1,0:T(2,128)}) custom-call(bf16[2,8,64,128]{3,2,1,0:T(8,128)(2,1)S(1)} %copy-done.3, bf16[2,8,64,128]{3,2,1,0:T(8,128)(2,1)S(1)} %collective-permute-done.prev_ref, bf16[4,2,64,128]{3,2,1,0:T(8,128)(2,1)S(1)} %collective-permute-done.1.up_ref.down_ref, ...), custom_call_target="tpu_custom_call" | custom-call | flops 4000000000 | bytes 1000000 | tf_op jit(solution)/shard_map/norm_conv_in/pallas_call | solution.py:381
  24.7 3.7 %all-to-all-start.1 = ((f32[32,2,128]{2,1,0:T(2,128)}), f32[32,2,128]{2,1,0:T(2,128)S(1)}, u32[]{:S(2)}, u32[]{:S(2)}) async-start(f32[32,2,128]{2,1,0:T(2,128)} %get-tuple-element.14), calls=%async_computation.1 | async-start | bytes 65536 | tf_op jit(solution)/shard_map/all_to_all | solution.py:308
  28.4 0.0 copy-start.1
  28.4 0.0 copy-start.4
  28.4 0.0 copy-start.8
  28.4 0.0 copy-start.9
  28.5 0.0 copy-start.10
  28.5 0.0 copy-start.11
  28.5 3.8 %collective-permute-start.5 = (bf16[2,10,32,128]{3,2,1,0:T(8,128)(2,1)S(1)}, bf16[2,10,32,128]{3,2,1,0:T(8,128)(2,1)S(1)}, u32[]{:S(2)}, u32[]{:S(2)}) collective-permute-start(bf16[2,10,32,128]{3,2,1,0:T(8,128)(2,1)S(1)} %pack_hidden.1), channel_id=1, source_target_pairs={{0,2},{1,3},{2,4},{3,5},{4,6},{5,7},{6,8},{7,9},{8,10},{9,11},{10,... | collective-permute-start | bytes 491528 | tf_op jit(solution)/shard_map/ppermute | solution.py:334
  32.3 3.3 %all-to-all-done.1.moments_ref = f32[32,2,128]{2,1,0:T(2,128)S(1)} async-done(((f32[32,2,128]{2,1,0:T(2,128)}), f32[32,2,128]{2,1,0:T(2,128)S(1)}, u32[]{:S(2)}, u32[]{:S(2)}) %all-to-all-start.1) | async-done | bytes 32800 | tf_op jit(solution)/shard_map/all_to_all | solution.py:308
  35.6 0.0 copy-done.1
  35.6 0.0 copy-done.4
  35.6 0.0 copy-done.8
  35.6 0.0 copy-done.9
  35.6 0.0 copy-done.10
  35.6 0.0 copy-done.11
  35.7 1.5 %conv_mid_own_frames.1 = (f32[2,8,32,128]{3,2,1,0:T(8,128)S(1)}, f32[3,128]{1,0:T(4,128)S(1)}) custom-call(bf16[2,10,48,128]{3,2,1,0:T(8,128)(2,1)S(1)} %get-tuple-element.13.hidden_ref, f32[32,2,128]{2,1,0:T(2,128)S(1)} %all-to-all-done.1.moments_ref, f32[1,128]{1,0:T(1,128)S(1)} %bitcast.10, f32[1,128]{1,0:T(1,128)S(1)} %bitcast.11, ...), custom_call_target="tpu_custom_call" | custom-call | flops 2000000000 | bytes 1000000 | tf_op jit(solution)/shard_map/conv_mid_own_frames/pallas_call | solution.py:417
  37.2 0.0 collective-permute-done.5.before_ref
  37.2 1.7 %conv_mid_previous_frames.1 = bf16[2,8,32,128]{3,2,1,0:T(8,128)(2,1)} custom-call(bf16[2,10,48,128]{3,2,1,0:T(8,128)(2,1)S(1)} %get-tuple-element.13.hidden_ref, bf16[2,10,32,128]{3,2,1,0:T(8,128)(2,1)S(1)} %collective-permute-done.5.before_ref, f32[3,128]{1,0:T(4,128)S(1)} %get-tuple-element.15.norm_ref, bf16[3,3,3,128,128]{4,3,2,1,0:T(8,128)(2,1)S(1)} %copy-done.1, ...), custom_call_target="tpu_custom_call" | custom-call | flops 2000000000 | bytes 1000000 | tf_op jit(solution)/shard_map/conv_mid_previous_frames/pallas_call | solution.py:441
  (2 shorter events, 0.0 us)
Async XLA Ops:
  0.0 11.7 %collective-permute-start = (bf16[2,8,64,128]{3,2,1,0:T(8,128)(2,1)}, bf16[2,8,64,128]{3,2,1,0:T(8,128)(2,1)S(1)}, u32[]{:S(2)}, u32[]{:S(2)}) collective-permute-start(bf16[2,8,64,128]{3,2,1,0:T(8,128)(2,1)} %x_ref.7), channel_id=1, source_target_pairs={{0,2},{1,3},{2,4},{3,5},{4,6},{5,7},{6,8},{7,9},{8,10},{9,11},{10,... | collective-permute-start | bytes 786440 | tf_op jit(solution)/shard_map/ppermute | solution.py:334
  4.9 1.0 %copy-start.2 = (bf16[2,8,64,128]{3,2,1,0:T(8,128)(2,1)S(1)}, bf16[2,8,64,128]{3,2,1,0:T(8,128)(2,1)}, u32[]{:S(2)}) copy-start(bf16[2,8,64,128]{3,2,1,0:T(8,128)(2,1)} %x_ref.7) | copy-start | bytes 786436
  5.8 5.9 %copy-start.3 = (bf16[2,8,64,128]{3,2,1,0:T(8,128)(2,1)S(1)}, bf16[2,8,64,128]{3,2,1,0:T(8,128)(2,1)}, u32[]{:S(2)}) copy-start(bf16[2,8,64,128]{3,2,1,0:T(8,128)(2,1)} %x_ref.7) | copy-start | bytes 786436
  6.7 12.1 %copy-start.5 = (f32[256]{0:T(256)S(1)}, f32[256]{0:T(256)}, u32[]{:S(2)}) copy-start(f32[256]{0:T(256)} %param.12) | copy-start | bytes 3076
  6.7 12.1 %copy-start.6 = (f32[256]{0:T(256)S(1)}, f32[256]{0:T(256)}, u32[]{:S(2)}) copy-start(f32[256]{0:T(256)} %param.13) | copy-start | bytes 3076
  6.7 12.1 %all-to-all-start = ((f32[32,2,128]{2,1,0:T(2,128)}), f32[32,2,128]{2,1,0:T(2,128)S(1)}, u32[]{:S(2)}, u32[]{:S(2)}) async-start(f32[32,2,128]{2,1,0:T(2,128)} %feature_moments.1), calls=%async_computation | async-start | bytes 65536 | tf_op jit(solution)/shard_map/all_to_all | solution.py:308
  11.7 7.7 %collective-permute-start.1 = (bf16[4,2,64,128]{3,2,1,0:T(8,128)(2,1)S(1)}, bf16[4,2,64,128]{3,2,1,0:T(8,128)(2,1)S(1)}, u32[]{:S(2)}, u32[]{:S(2)}) collective-permute-start(bf16[4,2,64,128]{3,2,1,0:T(8,128)(2,1)S(1)} %facing_rows.1), channel_id=1, source_target_pairs={{0,1},{1,0},{2,3},{3,2},{4,5},{5,4},{6,7},{7,6},{8,9},{9,8},{10,11... | collective-permute-start | bytes 393224 | tf_op jit(solution)/shard_map/ppermute | solution.py:362
  13.5 5.9 %collective-permute-start.2 = (bf16[2,8,64,128]{3,2,1,0:T(8,128)(2,1)S(1)}, bf16[2,8,64,128]{3,2,1,0:T(8,128)(2,1)S(1)}, u32[]{:S(2)}, u32[]{:S(2)}) collective-permute-start(bf16[2,8,64,128]{3,2,1,0:T(8,128)(2,1)S(1)} %copy-done.3), channel_id=1, source_target_pairs={{0,16},{16,0},{1,17},{17,1},{2,18},{18,2},{3,19},{19,3},{4,20},{20... | collective-permute-start | bytes 786440 | tf_op jit(solution)/shard_map/ppermute | solution.py:337
  13.5 7.3 %collective-permute-start.3 = (bf16[2,8,64,128]{3,2,1,0:T(8,128)(2,1)S(1)}, bf16[2,8,64,128]{3,2,1,0:T(8,128)(2,1)S(1)}, u32[]{:S(2)}, u32[]{:S(2)}) collective-permute-start(bf16[2,8,64,128]{3,2,1,0:T(8,128)(2,1)S(1)} %collective-permute-done.prev_ref), channel_id=1, source_target_pairs={{0,16},{16,0},{1,17},{17,1},{2,18},{18,2},{3,19},{19,3},{4,20},{20... | collective-permute-start | bytes 786440 | tf_op jit(solution)/shard_map/ppermute | solution.py:337
  18.9 1.9 %copy-start = (bf16[3,3,3,256,128]{4,3,2,1,0:T(8,128)(2,1)S(1)}, bf16[3,3,3,256,128]{4,3,2,1,0:T(8,128)(2,1)}, u32[]{:S(2)}) copy-start(bf16[3,3,3,256,128]{4,3,2,1,0:T(8,128)(2,1)} %weight_ref.3) | copy-start | bytes 5308420
  18.9 1.9 %copy-start.7 = (f32[128]{0:T(128)S(1)}, f32[128]{0:T(128)}, u32[]{:S(2)}) copy-start(f32[128]{0:T(128)} %param.15) | copy-start | bytes 1540
  19.4 1.4 %collective-permute-start.4 = (bf16[4,2,64,128]{3,2,1,0:T(8,128)(2,1)S(1)}, bf16[4,2,64,128]{3,2,1,0:T(8,128)(2,1)S(1)}, u32[]{:S(2)}, u32[]{:S(2)}) collective-permute-start(bf16[4,2,64,128]{3,2,1,0:T(8,128)(2,1)S(1)} %collective-permute-done.1.up_ref.down_ref), channel_id=1, source_target_pairs={{0,16},{16,0},{1,17},{17,1},{2,18},{18,2},{3,19},{19,3},{4,20},{20... | collective-permute-start | bytes 393224 | tf_op jit(solution)/shard_map/ppermute | solution.py:337
  24.7 10.9 %all-to-all-start.1 = ((f32[32,2,128]{2,1,0:T(2,128)}), f32[32,2,128]{2,1,0:T(2,128)S(1)}, u32[]{:S(2)}, u32[]{:S(2)}) async-start(f32[32,2,128]{2,1,0:T(2,128)} %get-tuple-element.14), calls=%async_computation.1 | async-start | bytes 65536 | tf_op jit(solution)/shard_map/all_to_all | solution.py:308
  28.4 7.2 %copy-start.1 = (bf16[3,3,3,128,128]{4,3,2,1,0:T(8,128)(2,1)S(1)}, bf16[3,3,3,128,128]{4,3,2,1,0:T(8,128)(2,1)}, u32[]{:S(2)}) copy-start(bf16[3,3,3,128,128]{4,3,2,1,0:T(8,128)(2,1)} %weight_ref.5) | copy-start | bytes 2654212
  28.4 7.2 %copy-start.4 = (bf16[256,128]{1,0:T(8,128)(2,1)S(1)}, bf16[256,128]{1,0:T(8,128)(2,1)}, u32[]{:S(2)}) copy-start(bf16[256,128]{1,0:T(8,128)(2,1)} %skip_ref.1) | copy-start | bytes 196612
  28.4 7.2 %copy-start.8 = (f32[128]{0:T(128)S(1)}, f32[128]{0:T(128)}, u32[]{:S(2)}) copy-start(f32[128]{0:T(128)} %param.16) | copy-start | bytes 1540
  28.4 7.2 %copy-start.9 = (f32[128]{0:T(128)S(1)}, f32[128]{0:T(128)}, u32[]{:S(2)}) copy-start(f32[128]{0:T(128)} %param.17) | copy-start | bytes 1540
  28.5 7.2 %copy-start.10 = (f32[128]{0:T(128)S(1)}, f32[128]{0:T(128)}, u32[]{:S(2)}) copy-start(f32[128]{0:T(128)} %param.19) | copy-start | bytes 1540
  28.5 7.2 %copy-start.11 = (f32[128]{0:T(128)S(1)}, f32[128]{0:T(128)}, u32[]{:S(2)}) copy-start(f32[128]{0:T(128)} %param.21) | copy-start | bytes 1540
  28.5 8.7 %collective-permute-start.5 = (bf16[2,10,32,128]{3,2,1,0:T(8,128)(2,1)S(1)}, bf16[2,10,32,128]{3,2,1,0:T(8,128)(2,1)S(1)}, u32[]{:S(2)}, u32[]{:S(2)}) collective-permute-start(bf16[2,10,32,128]{3,2,1,0:T(8,128)(2,1)S(1)} %pack_hidden.1), channel_id=1, source_target_pairs={{0,2},{1,3},{2,4},{3,5},{4,6},{5,7},{6,8},{7,9},{8,10},{9,11},{10,... | collective-permute-start | bytes 491528 | tf_op jit(solution)/shard_map/ppermute | solution.py:334

commit v2 on v1

--- a/solution.py
+++ b/solution.py
@@ -10,11 +10,12 @@
 GROUPS = 32
 AXES = ("section", "tm", "tile")
 VMEM_LIMIT = 48 * 1024 * 1024
+FULL_LIMIT = 63 * 1024 * 1024
 RIM = 16
 
 
-def params():
-    return pltpu.CompilerParams(vmem_limit_bytes=VMEM_LIMIT)
+def params(limit=VMEM_LIMIT):
+    return pltpu.CompilerParams(vmem_limit_bytes=limit)
 
 
 def cost(flops, moved):
@@ -40,14 +41,18 @@
     shape = (channels, channels)
     row = lax.broadcasted_iota(jnp.int32, shape, 0) // width
     col = lax.broadcasted_iota(jnp.int32, shape, 1) // width
-    return jnp.where(row == col, 1.0, 0.0).astype(jnp.float32)
+    return jnp.where(row == col, 1.0, 0.0).astype(jnp.bfloat16)
 
 
 def group_sum(values, matrix):
-    tall = jnp.broadcast_to(values, (8, values.shape[-1]))
-    return jnp.dot(
-        tall, matrix, preferred_element_type=jnp.float32, precision=lax.Precision.HIGHEST
-    )[:1]
+    parts = []
+    for _ in range(3):
+        part = values.astype(jnp.bfloat16).astype(jnp.float32)
+        parts.append(jnp.broadcast_to(part, (8, part.shape[-1])))
+        values = values - part
+    stacked = jnp.concatenate(parts + [jnp.zeros_like(parts[0])], axis=0).astype(jnp.bfloat16)
+    summed = jnp.dot(stacked, matrix, preferred_element_type=jnp.float32)
+    return summed[0:1] + summed[8:9] + summed[16:17]
 
 
 def scale_and_offset(moments, cells, width, gain, shift):
@@ -67,7 +72,10 @@
     return silu((values.astype(jnp.float32) - mean) * scale + shift).astype(jnp.bfloat16)
 
 
-def first_kernel(x_ref, moments_ref):
+def first_kernel(x_hbm, moments_ref, x_ref, sem):
+    copy = pltpu.make_async_copy(x_hbm, x_ref, sem)
+    copy.start()
+    copy.wait()
     x = x_ref[...]
     cells = x.astype(jnp.float32).reshape(-1, x.shape[-1])
     moments_ref[...] = jnp.broadcast_to(moments_of(cells)[None], moments_ref.shape)
@@ -98,16 +106,12 @@
         norm_ref[k] = jnp.concatenate(norm, axis=0)
 
 
-def conv_rows(act_ref, weight_ref, frames, rows, width):
-    total = None
-    for t, frame in enumerate(frames):
-        for h in range(3) if frame is not None else ():
-            cells = act_ref[frame, h : h + rows]
-            cells = cells.reshape(rows * width, cells.shape[-1])
-            taps = jnp.concatenate([weight_ref[t, h, w] for w in range(3)], axis=-1)
-            part = jnp.dot(cells, taps, preferred_element_type=jnp.float32)
-            total = part if total is None else total + part
-    outputs = weight_ref.shape[-1]
+def column_taps(weight_ref, t, h):
+    return jnp.concatenate([weight_ref[t, h, w] for w in range(3)], axis=-1)
+
+
+def shift_and_add(total, rows, width):
+    outputs = total.shape[-1] // 3
     total = total.reshape(rows, width, 3 * outputs)
     before, middle, after = (total[..., k * outputs : (k + 1) * outputs] for k in range(3))
     before = jnp.concatenate([before[:, :1], before[:, :-1]], axis=1)
@@ -115,40 +119,68 @@
     return middle + before + after
 
 
-def middle_kernel(
-    tiles,
-    x_ref,
-    prev_ref,
-    up_ref,
-    down_ref,
-    other_x_ref,
-    other_prev_ref,
-    other_up_ref,
-    other_down_ref,
-    norm_ref,
-    weight_ref,
-    bias_ref,
-    hidden_ref,
-    out_moments_ref,
-    act_ref,
-):
+def conv_in_rows(act_ref, weight_ref, frames, top, rows, width):
+    totals = [None] * frames
+    for a in range(act_ref.shape[0]):
+        reached = [f for f in range(frames) if 0 <= a - f <= 2]
+        for h in range(3):
+            cells = act_ref[a, pl.ds(top + h, rows)]
+            cells = cells.reshape(rows * width, cells.shape[-1])
+            taps = [column_taps(weight_ref, a - f, h) for f in reached]
+            sums = jnp.dot(
+                cells, jnp.concatenate(taps, axis=-1), preferred_element_type=jnp.float32
+            )
+            n = sums.shape[-1] // len(reached)
+            for k, f in enumerate(reached):
+                part = sums[:, k * n : (k + 1) * n]
+                totals[f] = part if totals[f] is None else totals[f] + part
+    return [shift_and_add(total, rows, width) for total in totals]
+
+
+def conv_mid_rows(act_ref, weight_ref, taken, rows, width):
+    cells, taps = [], []
+    for t, frame in taken:
+        for h in range(3):
+            block = act_ref[frame, h : h + rows]
+            cells.append(block.reshape(rows * width, block.shape[-1]))
+            taps.append(column_taps(weight_ref, t, h))
+    total = jnp.dot(
+        jnp.concatenate(cells, axis=-1),
+        jnp.concatenate(taps, axis=0),
+        preferred_element_type=jnp.float32,
+    )
+    return shift_and_add(total, rows, width)
+
+
+def first_row(tiles, tile):
+    return 1 - tile if tiles == 2 else 0
+
+
+def middle_kernel(tiles, sides, *refs):
+    x_ref, prev_ref, other_x_ref, other_prev_ref = refs[:4]
+    rim_refs, other_rim_refs = refs[4 : 4 + sides], refs[4 + sides : 4 + 2 * sides]
+    norm_ref, weight_ref, bias_ref, hidden_ref, out_moments_ref, act_ref = refs[4 + 2 * sides :]
     section, tm, tile = (lax.axis_index(axis) for axis in AXES)
     frames, rows, columns, half = x_ref.shape
-    width = columns // 2 + RIM
+    kept = hidden_ref.shape[1]
+    own = columns // 2
+    width = own + RIM
     first = pl.multiple_of(section * (columns - width), RIM)
     cols = pl.ds(first, width)
+    top = first_row(tiles, tile)
+    rim_rows = (0, rows + 2) if sides == 2 else ((rows + 2) * (1 - tile),)
     pieces = (
-        (section, prev_ref, x_ref, up_ref, down_ref),
-        (1 - section, other_prev_ref, other_x_ref, other_up_ref, other_down_ref),
+        (section, prev_ref, x_ref, rim_refs),
+        (1 - section, other_prev_ref, other_x_ref, other_rim_refs),
     )
-    for which, before, now, up, down in pieces:
+    for which, before, now, rims in pieces:
         norm = tuple(norm_ref[which, k : k + 1] for k in range(3))
         lanes = pl.ds(pl.multiple_of(which * half, half), half)
         for f in range(2 * frames):
             body = before[f, :, cols, :] if f < frames else now[f - frames, :, cols, :]
             act_ref[f, 2 : 2 + rows, :, lanes] = apply_norm(body, norm)
-            act_ref[f, 0:2, :, lanes] = apply_norm(up[f, :, cols, :], norm)
-            act_ref[f, 2 + rows :, :, lanes] = apply_norm(down[f, :, cols, :], norm)
+            for row, rim in zip(rim_rows, rims):
+                act_ref[f, pl.ds(row, 2), :, lanes] = apply_norm(rim[f, :, cols, :], norm)
 
     @pl.when(tile == 0)
     def _():
@@ -165,33 +197,25 @@
         for f in range(frames):
             act_ref[f] = act_ref[frames]
 
-    own = columns // 2
-    for f in range(frames):
-        hidden = conv_rows(act_ref, weight_ref, (f, f + 1, f + 2), rows + 2, width)
+    for f, hidden in enumerate(conv_in_rows(act_ref, weight_ref, frames, top, kept, width)):
         hidden_ref[f] = (hidden + bias_ref[...]).astype(jnp.bfloat16)
 
-    cells = hidden_ref[:, 1 : 1 + rows, pl.ds(first, own), :]
+    cells = hidden_ref[:, pl.ds(1 - top, rows), pl.ds(first, own), :]
     cells = cells.astype(jnp.float32).reshape(-1, cells.shape[-1])
     out_moments_ref[...] = jnp.broadcast_to(moments_of(cells)[None], out_moments_ref.shape)
 
 
-def sent_start(tiles, tile):
-    return 1 - tile if tiles == 2 else 0
-
-
-def pack_kernel(tiles, hidden_ref, sent_ref):
-    section, tile = lax.axis_index("section"), lax.axis_index("tile")
-    frames, padded, width, channels = hidden_ref.shape
+def pack_kernel(hidden_ref, sent_ref):
+    section = lax.axis_index("section")
+    frames, kept, width, channels = hidden_ref.shape
     own = sent_ref.shape[2]
     first = pl.multiple_of(section * (width - own), RIM)
-    sent_rows = sent_ref.shape[1] - 1
-    top = sent_start(tiles, tile)
     for f in range(frames):
-        sent_ref[f, :sent_rows] = hidden_ref[f, pl.ds(top, sent_rows), pl.ds(first, own), :]
+        sent_ref[f, :kept] = hidden_ref[f, :, pl.ds(first, own), :]
         hidden = hidden_ref[f].astype(jnp.float32)
         rim = jnp.where(section == 0, hidden[:, own, :], hidden[:, width - own - 1, :])
-        spare = jnp.zeros((own - padded, channels), jnp.float32)
-        sent_ref[f, sent_rows] = jnp.concatenate([rim, spare], axis=0).astype(jnp.bfloat16)
+        spare = jnp.zeros((own - kept, channels), jnp.float32)
+        sent_ref[f, kept] = jnp.concatenate([rim, spare], axis=0).astype(jnp.bfloat16)
 
 
 def repeat_edges(act_ref, count, tiles, rows):
@@ -230,11 +254,11 @@
     norm_ref,
     act_ref,
 ):
-    section = lax.axis_index("section")
-    frames, padded, width, outputs = hidden_ref.shape
-    rows = padded - 2
-    half = x_ref.shape[3]
+    section, tile = lax.axis_index("section"), lax.axis_index("tile")
+    frames, kept, width, outputs = hidden_ref.shape
+    rows, half = x_ref.shape[1], x_ref.shape[3]
     own = x_ref.shape[2] // 2
+    top = first_row(tiles, tile)
     norm = scale_and_offset(
         moments_ref[...],
         frames * rows * own,
@@ -244,14 +268,14 @@
     )
     norm_ref[...] = jnp.concatenate(norm, axis=0)
     for f in range(frames):
-        act_ref[f] = apply_norm(hidden_ref[f], norm)
+        act_ref[f, pl.ds(top, kept)] = apply_norm(hidden_ref[f], norm)
     repeat_edges(act_ref, frames, tiles, rows)
     mine = pl.ds(pl.multiple_of(section * own, own), own)
     skip_here = skip_ref[pl.ds(pl.multiple_of(section * half, half), half), :]
     skip_there = skip_ref[pl.ds(pl.multiple_of((1 - section) * half, half), half), :]
     for f in range(frames):
-        taps = [k if k >= 0 else None for k in range(f - 2, f + 1)]
-        residual = own_columns(conv_rows(act_ref, weight_ref, taps, rows, width), own)
+        taken = [(k - f + 2, k) for k in range(f - 2, f + 1) if k >= 0]
+        residual = own_columns(conv_mid_rows(act_ref, weight_ref, taken, rows, width), own)
         here = x_ref[f, :, mine, :].reshape(rows * own, half)
         there = other_x_ref[f, :, mine, :].reshape(rows * own, half)
         shortcut = jnp.dot(here, skip_here, preferred_element_type=jnp.float32)
@@ -265,32 +289,28 @@
     tiles, hidden_ref, before_ref, norm_ref, weight_ref, part_ref, out_ref, act_ref
 ):
     section, tm, tile = (lax.axis_index(axis) for axis in AXES)
-    frames, padded, width, outputs = hidden_ref.shape
-    rows = padded - 2
-    own = part_ref.shape[2]
-    sent_rows = before_ref.shape[1] - 1
-    top = sent_start(tiles, tile)
+    frames, kept, width, outputs = hidden_ref.shape
+    rows, own = part_ref.shape[1:3]
+    top = first_row(tiles, tile)
     first = pl.multiple_of(section * (width - own), RIM)
     beside = pl.multiple_of((1 - section) * own, RIM)
     norm = tuple(norm_ref[k : k + 1] for k in range(3))
     for f in range(frames):
-        act_ref[f, pl.ds(top, sent_rows), pl.ds(first, own), :] = apply_norm(
-            before_ref[f, :sent_rows], norm
-        )
-        rim = apply_norm(before_ref[f, sent_rows], norm).astype(jnp.float32)[:padded]
-        rim = jnp.broadcast_to(rim[:, None, :], (padded, width - own, outputs))
-        act_ref[f, :, pl.ds(beside, width - own), :] = rim.astype(jnp.bfloat16)
+        act_ref[f, pl.ds(top, kept), pl.ds(first, own), :] = apply_norm(before_ref[f, :kept], norm)
+        rim = apply_norm(before_ref[f, kept], norm).astype(jnp.float32)[:kept]
+        rim = jnp.broadcast_to(rim[:, None, :], (kept, width - own, outputs))
+        act_ref[f, pl.ds(top, kept), pl.ds(beside, width - own), :] = rim.astype(jnp.bfloat16)
 
     @pl.when(tm == 0)
     def _():
         start = apply_norm(hidden_ref[0], norm)
         for f in range(frames):
-            act_ref[f] = start
+            act_ref[f, pl.ds(top, kept)] = start
 
     repeat_edges(act_ref, frames, tiles, rows)
     for f in range(frames):
-        taps = [k if k < frames else None for k in range(f, f + 3)]
-        residual = own_columns(conv_rows(act_ref, weight_ref, taps, rows, width), own)
+        taken = [(k - f, k) for k in range(f, f + 3) if k < frames]
+        residual = own_columns(conv_mid_rows(act_ref, weight_ref, taken, rows, width), own)
         out_ref[f] = (part_ref[f] + residual).astype(jnp.bfloat16)
 
 
@@ -340,9 +360,13 @@
     moments = pl.pallas_call(
         first_kernel,
         out_shape=jax.ShapeDtypeStruct((parties, 2, half), jnp.float32),
-        in_specs=vmem_specs(1),
+        in_specs=[pl.BlockSpec(memory_space=pl.ANY)],
         out_specs=pl.BlockSpec(memory_space=pltpu.VMEM),
-        compiler_params=params(),
+        scratch_shapes=[
+            pltpu.VMEM(features.shape, features.dtype),
+            pltpu.SemaphoreType.DMA,
+        ],
+        compiler_params=params(FULL_LIMIT),
         cost_estimate=cost(1_000_000_000, 1_000_000),
         name="feature_moments",
     )(features)
@@ -374,17 +398,15 @@
     )(moments, norm_gain_in.reshape(sections, half), norm_shift_in.reshape(sections, half))
     norm_in, *rims = lax.optimization_barrier((norm_in, *rims))
     other_rims = [swap(rim) for rim in rims]
-    up, down = (rims * 2)[:2]
-    other_up, other_down = (other_rims * 2)[:2]
-
-    sent_rows = rows + (1 if tiles == 2 else 2)
+
+    kept = rows + edges
     hidden, moments_mid = pl.pallas_call(
-        functools.partial(middle_kernel, tiles),
+        functools.partial(middle_kernel, tiles, edges),
         out_shape=(
-            jax.ShapeDtypeStruct((frames, rows + 2, width, middle), jnp.bfloat16),
+            jax.ShapeDtypeStruct((frames, kept, width, middle), jnp.bfloat16),
             jax.ShapeDtypeStruct((parties, 2, middle), jnp.float32),
         ),
-        in_specs=vmem_specs(11),
+        in_specs=vmem_specs(7 + 2 * edges),
         out_specs=tuple(vmem_specs(2)),
         scratch_shapes=[pltpu.VMEM((2 * frames, rows + 4, width, 2 * half), jnp.bfloat16)],
         compiler_params=params(),
@@ -393,20 +415,18 @@
     )(
         features,
         previous,
-        up,
-        down,
         other,
         other_previous,
-        other_up,
-        other_down,
+        *rims,
+        *other_rims,
         norm_in,
         conv_in_weight,
         conv_in_bias.reshape(1, middle),
     )
     moments_mid = to_everyone(moments_mid)
     sent = pl.pallas_call(
-        functools.partial(pack_kernel, tiles),
-        out_shape=jax.ShapeDtypeStruct((frames, sent_rows + 1, own, middle), jnp.bfloat16),
+        pack_kernel,
+        out_shape=jax.ShapeDtypeStruct((frames, kept + 1, own, middle), jnp.bfloat16),
         in_specs=vmem_specs(1),
         out_specs=pl.BlockSpec(memory_space=pltpu.VMEM),
         compiler_params=params(),

time: 39.1 us -> 38.2 us (0.977)
  local copies, waits for them, and re-layouts: 1 us -> 0.06 us
  starting transfers between devices: 19.6 us -> 20 us
    pallas_call x1, Pallas kernels: 0.91 us -> 1.87 us  [shards(): pl.pallas_call(first_kernel, out_shape=jax.ShapeDtypeStruct((parties, 2,...]
    unnamed x24 -> x22, local copies, waits for them, and re-layouts: 1 us -> 0.06 us
    pallas_call x2, Pallas kernels: 3.95 us -> 3.44 us  [the longest x1 3.41 us: shards(): pl.pallas_call(functools.partial(middle_kernel, tiles, edges), out_shape=...]
  transfers between devices with their start and end apart: 8 -> 8, of which waited for: 3 -> 3; matrix products, arithmetic and copies ran while one was open for 0% -> 0% of each run, Pallas kernels for 8% -> 9%
where the time goes in v2:
time: 38.2 us; the launch traced here: 38 us
  starting transfers between devices  20 us (52%)
  waiting for transfers between devices  9.43 us (25%)
  Pallas kernels  8.31 us (22%)
    ppermute x2, starting transfers between devices, shift(): lax.ppermute(value, grid_axes, pairs_for(tms, tiles, tm_step, tile_step))  8.79 us
    all_to_all x2, starting transfers between devices, to_everyone(): return lax.all_to_all(moments, AXES, 0, 0, tiled=True)  8.75 us
    all_to_all x2, waiting for transfers between devices, to_everyone(): return lax.all_to_all(moments, AXES, 0, 0, tiled=True)  8.09 us
    pallas_call x1, Pallas kernels, shards(): pl.pallas_call(functools.partial(middle_kernel, tiles, edges), out_shape=...  3.41 us
    pallas_call x1, Pallas kernels, shards(): pl.pallas_call(first_kernel, out_shape=jax.ShapeDtypeStruct((parties, 2,...  1.87 us
    ppermute x1, starting transfers between devices, shards(): rims = [lax.ppermute(edge_rows[0], 'tile', [(0, 1), (1, 0)])]  1.83 us
    pallas_call x1, Pallas kernels, shards(): pl.pallas_call(functools.partial(last_kernel, tiles), out_shape=jax.Shape...  1.51 us
    ppermute x3, waiting for transfers between devices, swap(): return lax.ppermute(value, 'section', [(0, 1), (1, 0)])  1.33 us
  transfers between devices with their start and end apart: 8, of which 3 were waited for; matrix products, arithmetic and copies ran while one was open for 0% of the time, Pallas kernels for 9%

profile of v2, /device:TPU:0, one launch (start us, length us, event | category | flops | bytes accessed | tf_op | source)
XLA Modules:
  0.0 38.0 jit_solution(13623410759360853579)
XLA Ops:
  0.0 0.0 copy-start.2
  0.0 5.0 %collective-permute-start = (bf16[2,8,64,128]{3,2,1,0:T(8,128)(2,1)}, bf16[2,8,64,128]{3,2,1,0:T(8,128)(2,1)S(1)}, u32[]{:S(2)}, u32[]{:S(2)}) collective-permute-start(bf16[2,8,64,128]{3,2,1,0:T(8,128)(2,1)} %x_ref.3), channel_id=1, source_target_pairs={{0,2},{1,3},{2,4},{3,5},{4,6},{5,7},{6,8},{7,9},{8,10},{9,11},{10,... | collective-permute-start | bytes 786440 | tf_op jit(solution)/shard_map/ppermute | solution.py:354
  5.0 1.9 %feature_moments.1 = f32[32,2,128]{2,1,0:T(2,128)} custom-call(bf16[2,8,64,128]{3,2,1,0:T(8,128)(2,1)} %x_ref.3), custom_call_target="tpu_custom_call" | custom-call | flops 1000000000 | bytes 1000000 | tf_op jit(solution)/shard_map/feature_moments/pallas_call | solution.py:360
  6.9 0.0 copy-start.4
  6.9 0.0 copy-start.5
  6.9 4.9 %all-to-all-start = ((f32[32,2,128]{2,1,0:T(2,128)}), f32[32,2,128]{2,1,0:T(2,128)S(1)}, u32[]{:S(2)}, u32[]{:S(2)}) async-start(f32[32,2,128]{2,1,0:T(2,128)} %feature_moments.1), calls=%async_computation | async-start | bytes 65536 | tf_op jit(solution)/shard_map/all_to_all | solution.py:328
  11.8 0.0 collective-permute-done.prev_ref.refs_1_
  11.8 0.0 copy-done.2
  11.9 1.8 %collective-permute-start.3 = (bf16[4,2,64,128]{3,2,1,0:T(8,128)(2,1)S(1)}, bf16[4,2,64,128]{3,2,1,0:T(8,128)(2,1)S(1)}, u32[]{:S(2)}, u32[]{:S(2)}) collective-permute-start(bf16[4,2,64,128]{3,2,1,0:T(8,128)(2,1)S(1)} %facing_rows.1), channel_id=1, source_target_pairs={{0,1},{1,0},{2,3},{3,2},{4,5},{5,4},{6,7},{7,6},{8,9},{9,8},{10,11... | collective-permute-start | bytes 393224 | tf_op jit(solution)/shard_map/ppermute | solution.py:386
  13.7 0.0 collective-permute-start.1
  13.7 0.5 %collective-permute-start.2 = (bf16[2,8,64,128]{3,2,1,0:T(8,128)(2,1)S(1)}, bf16[2,8,64,128]{3,2,1,0:T(8,128)(2,1)S(1)}, u32[]{:S(2)}, u32[]{:S(2)}) collective-permute-start(bf16[2,8,64,128]{3,2,1,0:T(8,128)(2,1)S(1)} %collective-permute-done.prev_ref.refs_1_), channel_id=1, source_target_pairs={{0,16},{16,0},{1,17},{17,1},{2,18},{18,2},{3,19},{19,3},{4,20},{20... | collective-permute-start | bytes 786440 | tf_op jit(solution)/shard_map/ppermute | solution.py:357
  14.2 4.8 %all-to-all-done.moments_ref = f32[32,2,128]{2,1,0:T(2,128)S(1)} async-done(((f32[32,2,128]{2,1,0:T(2,128)}), f32[32,2,128]{2,1,0:T(2,128)S(1)}, u32[]{:S(2)}, u32[]{:S(2)}) %all-to-all-start) | async-done | bytes 32800 | tf_op jit(solution)/shard_map/all_to_all | solution.py:328
  19.0 0.0 copy-done.4
  19.0 0.0 copy-done.5
  19.0 0.0 copy-start
  19.0 0.0 copy-start.6
  19.0 0.3 feature_scales.1.refs_6_
  19.4 0.0 collective-permute-done.3.refs_4_
  19.4 0.1 collective-permute-start.4
  19.4 0.0 collective-permute-done.1.refs_2_.other_x_ref
  19.5 1.3 %collective-permute-done.4.refs_5_ = bf16[4,2,64,128]{3,2,1,0:T(8,128)(2,1)S(1)} collective-permute-done((bf16[4,2,64,128]{3,2,1,0:T(8,128)(2,1)S(1)}, bf16[4,2,64,128]{3,2,1,0:T(8,128)(2,1)S(1)}, u32[]{:S(2)}, u32[]{:S(2)}) %collective-permute-start.4) | collective-permute-done | bytes 131104 | tf_op jit(solution)/shard_map/ppermute | solution.py:357
  20.8 0.0 collective-permute-done.2.refs_3_
  20.8 0.0 copy-done
  20.8 0.0 copy-done.6
  20.8 3.4 %norm_conv_in.1 = (bf16[2,9,48,128]{3,2,1,0:T(8,128)(2,1)S(1)}, f32[32,2,128]{2,1,0:T(2,128)}) custom-call(bf16[2,8,64,128]{3,2,1,0:T(8,128)(2,1)S(1)} %copy-done.2, bf16[2,8,64,128]{3,2,1,0:T(8,128)(2,1)S(1)} %collective-permute-done.prev_ref.refs_1_, bf16[2,8,64,128]{3,2,1,0:T(8,128)(2,1)S(1)} %collective-permute-done.1.refs_2_.other_x_ref, ...), custom_call_target="tpu_custom_call" | custom-call | flops 4000000000 | bytes 1000000 | tf_op jit(solution)/shard_map/norm_conv_in/pallas_call | solution.py:403
  24.2 3.8 %all-to-all-start.1 = ((f32[32,2,128]{2,1,0:T(2,128)}), f32[32,2,128]{2,1,0:T(2,128)S(1)}, u32[]{:S(2)}, u32[]{:S(2)}) async-start(f32[32,2,128]{2,1,0:T(2,128)} %get-tuple-element.14), calls=%async_computation.1 | async-start | bytes 65536 | tf_op jit(solution)/shard_map/all_to_all | solution.py:328
  28.0 0.0 copy-start.1
  28.0 0.0 copy-start.3
  28.1 0.0 copy-start.7
  28.1 0.0 copy-start.8
  28.1 0.0 copy-start.9
  28.1 0.0 copy-start.10
  28.1 3.8 %collective-permute-start.5 = (bf16[2,10,32,128]{3,2,1,0:T(8,128)(2,1)S(1)}, bf16[2,10,32,128]{3,2,1,0:T(8,128)(2,1)S(1)}, u32[]{:S(2)}, u32[]{:S(2)}) collective-permute-start(bf16[2,10,32,128]{3,2,1,0:T(8,128)(2,1)S(1)} %pack_hidden.1), channel_id=1, source_target_pairs={{0,2},{1,3},{2,4},{3,5},{4,6},{5,7},{6,8},{7,9},{8,10},{9,11},{10,... | collective-permute-start | bytes 491528 | tf_op jit(solution)/shard_map/ppermute | solution.py:354
  32.0 3.3 %all-to-all-done.1.moments_ref = f32[32,2,128]{2,1,0:T(2,128)S(1)} async-done(((f32[32,2,128]{2,1,0:T(2,128)}), f32[32,2,128]{2,1,0:T(2,128)S(1)}, u32[]{:S(2)}, u32[]{:S(2)}) %all-to-all-start.1) | async-done | bytes 32800 | tf_op jit(solution)/shard_map/all_to_all | solution.py:328
  35.2 0.0 copy-done.1
  35.2 0.0 copy-done.3
  35.2 0.0 copy-done.7
  35.3 0.0 copy-done.8
  35.3 0.0 copy-done.9
  35.3 0.0 copy-done.10
  35.3 1.2 %conv_mid_own_frames.1 = (f32[2,8,32,128]{3,2,1,0:T(8,128)S(1)}, f32[3,128]{1,0:T(4,128)S(1)}) custom-call(bf16[2,9,48,128]{3,2,1,0:T(8,128)(2,1)S(1)} %get-tuple-element.13.hidden_ref, f32[32,2,128]{2,1,0:T(2,128)S(1)} %all-to-all-done.1.moments_ref, f32[1,128]{1,0:T(1,128)S(1)} %bitcast.10, f32[1,128]{1,0:T(1,128)S(1)} %bitcast.11, ...), custom_call_target="tpu_custom_call" | custom-call | flops 2000000000 | bytes 1000000 | tf_op jit(solution)/shard_map/conv_mid_own_frames/pallas_call | solution.py:437
  36.5 0.0 collective-permute-done.5.before_ref
  36.5 1.5 %conv_mid_previous_frames.1 = bf16[2,8,32,128]{3,2,1,0:T(8,128)(2,1)} custom-call(bf16[2,9,48,128]{3,2,1,0:T(8,128)(2,1)S(1)} %get-tuple-element.13.hidden_ref, bf16[2,10,32,128]{3,2,1,0:T(8,128)(2,1)S(1)} %collective-permute-done.5.before_ref, f32[3,128]{1,0:T(4,128)S(1)} %get-tuple-element.15.norm_ref, bf16[3,3,3,128,128]{4,3,2,1,0:T(8,128)(2,1)S(1)} %copy-done.1, ...), custom_call_target="tpu_custom_call" | custom-call | flops 2000000000 | bytes 1000000 | tf_op jit(solution)/shard_map/conv_mid_previous_frames/pallas_call | solution.py:461
  (2 shorter events, 0.0 us)
Async XLA Ops:
  0.0 11.8 %copy-start.2 = (bf16[2,8,64,128]{3,2,1,0:T(8,128)(2,1)S(1)}, bf16[2,8,64,128]{3,2,1,0:T(8,128)(2,1)}, u32[]{:S(2)}) copy-start(bf16[2,8,64,128]{3,2,1,0:T(8,128)(2,1)} %x_ref.3) | copy-start | bytes 786436
  0.0 11.8 %collective-permute-start = (bf16[2,8,64,128]{3,2,1,0:T(8,128)(2,1)}, bf16[2,8,64,128]{3,2,1,0:T(8,128)(2,1)S(1)}, u32[]{:S(2)}, u32[]{:S(2)}) collective-permute-start(bf16[2,8,64,128]{3,2,1,0:T(8,128)(2,1)} %x_ref.3), channel_id=1, source_target_pairs={{0,2},{1,3},{2,4},{3,5},{4,6},{5,7},{6,8},{7,9},{8,10},{9,11},{10,... | collective-permute-start | bytes 786440 | tf_op jit(solution)/shard_map/ppermute | solution.py:354
  6.9 12.2 %copy-start.4 = (f32[256]{0:T(256)S(1)}, f32[256]{0:T(256)}, u32[]{:S(2)}) copy-start(f32[256]{0:T(256)} %param.12) | copy-start | bytes 3076
  6.9 12.2 %copy-start.5 = (f32[256]{0:T(256)S(1)}, f32[256]{0:T(256)}, u32[]{:S(2)}) copy-start(f32[256]{0:T(256)} %param.13) | copy-start | bytes 3076
  6.9 12.1 %all-to-all-start = ((f32[32,2,128]{2,1,0:T(2,128)}), f32[32,2,128]{2,1,0:T(2,128)S(1)}, u32[]{:S(2)}, u32[]{:S(2)}) async-start(f32[32,2,128]{2,1,0:T(2,128)} %feature_moments.1), calls=%async_computation | async-start | bytes 65536 | tf_op jit(solution)/shard_map/all_to_all | solution.py:328
  11.9 7.5 %collective-permute-start.3 = (bf16[4,2,64,128]{3,2,1,0:T(8,128)(2,1)S(1)}, bf16[4,2,64,128]{3,2,1,0:T(8,128)(2,1)S(1)}, u32[]{:S(2)}, u32[]{:S(2)}) collective-permute-start(bf16[4,2,64,128]{3,2,1,0:T(8,128)(2,1)S(1)} %facing_rows.1), channel_id=1, source_target_pairs={{0,1},{1,0},{2,3},{3,2},{4,5},{5,4},{6,7},{7,6},{8,9},{9,8},{10,11... | collective-permute-start | bytes 393224 | tf_op jit(solution)/shard_map/ppermute | solution.py:386
  13.7 5.7 %collective-permute-start.1 = (bf16[2,8,64,128]{3,2,1,0:T(8,128)(2,1)S(1)}, bf16[2,8,64,128]{3,2,1,0:T(8,128)(2,1)S(1)}, u32[]{:S(2)}, u32[]{:S(2)}) collective-permute-start(bf16[2,8,64,128]{3,2,1,0:T(8,128)(2,1)S(1)} %copy-done.2), channel_id=1, source_target_pairs={{0,16},{16,0},{1,17},{17,1},{2,18},{18,2},{3,19},{19,3},{4,20},{20... | collective-permute-start | bytes 786440 | tf_op jit(solution)/shard_map/ppermute | solution.py:357
  13.7 7.1 %collective-permute-start.2 = (bf16[2,8,64,128]{3,2,1,0:T(8,128)(2,1)S(1)}, bf16[2,8,64,128]{3,2,1,0:T(8,128)(2,1)S(1)}, u32[]{:S(2)}, u32[]{:S(2)}) collective-permute-start(bf16[2,8,64,128]{3,2,1,0:T(8,128)(2,1)S(1)} %collective-permute-done.prev_ref.refs_1_), channel_id=1, source_target_pairs={{0,16},{16,0},{1,17},{17,1},{2,18},{18,2},{3,19},{19,3},{4,20},{20... | collective-permute-start | bytes 786440 | tf_op jit(solution)/shard_map/ppermute | solution.py:357
  19.0 1.7 %copy-start = (bf16[3,3,3,256,128]{4,3,2,1,0:T(8,128)(2,1)S(1)}, bf16[3,3,3,256,128]{4,3,2,1,0:T(8,128)(2,1)}, u32[]{:S(2)}) copy-start(bf16[3,3,3,256,128]{4,3,2,1,0:T(8,128)(2,1)} %refs_7_.1) | copy-start | bytes 5308420
  19.0 1.7 %copy-start.6 = (f32[128]{0:T(128)S(1)}, f32[128]{0:T(128)}, u32[]{:S(2)}) copy-start(f32[128]{0:T(128)} %param.15) | copy-start | bytes 1540
  19.4 1.4 %collective-permute-start.4 = (bf16[4,2,64,128]{3,2,1,0:T(8,128)(2,1)S(1)}, bf16[4,2,64,128]{3,2,1,0:T(8,128)(2,1)S(1)}, u32[]{:S(2)}, u32[]{:S(2)}) collective-permute-start(bf16[4,2,64,128]{3,2,1,0:T(8,128)(2,1)S(1)} %collective-permute-done.3.refs_4_), channel_id=1, source_target_pairs={{0,16},{16,0},{1,17},{17,1},{2,18},{18,2},{3,19},{19,3},{4,20},{20... | collective-permute-start | bytes 393224 | tf_op jit(solution)/shard_map/ppermute | solution.py:357
  24.2 11.0 %all-to-all-start.1 = ((f32[32,2,128]{2,1,0:T(2,128)}), f32[32,2,128]{2,1,0:T(2,128)S(1)}, u32[]{:S(2)}, u32[]{:S(2)}) async-start(f32[32,2,128]{2,1,0:T(2,128)} %get-tuple-element.14), calls=%async_computation.1 | async-start | bytes 65536 | tf_op jit(solution)/shard_map/all_to_all | solution.py:328
  28.0 7.2 %copy-start.1 = (bf16[3,3,3,128,128]{4,3,2,1,0:T(8,128)(2,1)S(1)}, bf16[3,3,3,128,128]{4,3,2,1,0:T(8,128)(2,1)}, u32[]{:S(2)}) copy-start(bf16[3,3,3,128,128]{4,3,2,1,0:T(8,128)(2,1)} %weight_ref.3) | copy-start | bytes 2654212
  28.0 7.2 %copy-start.3 = (bf16[256,128]{1,0:T(8,128)(2,1)S(1)}, bf16[256,128]{1,0:T(8,128)(2,1)}, u32[]{:S(2)}) copy-start(bf16[256,128]{1,0:T(8,128)(2,1)} %skip_ref.1) | copy-start | bytes 196612
  28.1 7.2 %copy-start.7 = (f32[128]{0:T(128)S(1)}, f32[128]{0:T(128)}, u32[]{:S(2)}) copy-start(f32[128]{0:T(128)} %param.16) | copy-start | bytes 1540
  28.1 7.2 %copy-start.8 = (f32[128]{0:T(128)S(1)}, f32[128]{0:T(128)}, u32[]{:S(2)}) copy-start(f32[128]{0:T(128)} %param.17) | copy-start | bytes 1540
  28.1 7.2 %copy-start.9 = (f32[128]{0:T(128)S(1)}, f32[128]{0:T(128)}, u32[]{:S(2)}) copy-start(f32[128]{0:T(128)} %param.19) | copy-start | bytes 1540
  28.1 7.2 %copy-start.10 = (f32[128]{0:T(128)S(1)}, f32[128]{0:T(128)}, u32[]{:S(2)}) copy-start(f32[128]{0:T(128)} %param.21) | copy-start | bytes 1540
  28.1 8.3 %collective-permute-start.5 = (bf16[2,10,32,128]{3,2,1,0:T(8,128)(2,1)S(1)}, bf16[2,10,32,128]{3,2,1,0:T(8,128)(2,1)S(1)}, u32[]{:S(2)}, u32[]{:S(2)}) collective-permute-start(bf16[2,10,32,128]{3,2,1,0:T(8,128)(2,1)S(1)} %pack_hidden.1), channel_id=1, source_target_pairs={{0,2},{1,3},{2,4},{3,5},{4,6},{5,7},{6,8},{7,9},{8,10},{9,11},{10,... | collective-permute-start | bytes 491528 | tf_op jit(solution)/shard_map/ppermute | solution.py:354

commit v3 on v2

--- a/solution.py
+++ b/solution.py
@@ -156,29 +156,38 @@
     return 1 - tile if tiles == 2 else 0
 
 
+def body_kernel(x_ref, prev_ref, other_x_ref, other_prev_ref, norm_ref, body_ref):
+    section = lax.axis_index("section")
+    frames, _, columns, half = x_ref.shape
+    width = body_ref.shape[2]
+    cols = pl.ds(pl.multiple_of(section * (columns - width), RIM), width)
+    pieces = ((section, prev_ref, x_ref), (1 - section, other_prev_ref, other_x_ref))
+    for which, before, now in pieces:
+        norm = tuple(norm_ref[which, k : k + 1] for k in range(3))
+        lanes = pl.ds(pl.multiple_of(which * half, half), half)
+        for f in range(2 * frames):
+            rows = before[f, :, cols, :] if f < frames else now[f - frames, :, cols, :]
+            body_ref[f, :, :, lanes] = apply_norm(rows, norm)
+
+
 def middle_kernel(tiles, sides, *refs):
-    x_ref, prev_ref, other_x_ref, other_prev_ref = refs[:4]
-    rim_refs, other_rim_refs = refs[4 : 4 + sides], refs[4 + sides : 4 + 2 * sides]
-    norm_ref, weight_ref, bias_ref, hidden_ref, out_moments_ref, act_ref = refs[4 + 2 * sides :]
+    body_ref = refs[0]
+    rim_refs, other_rim_refs = refs[1 : 1 + sides], refs[1 + sides : 1 + 2 * sides]
+    norm_ref, weight_ref, bias_ref, hidden_ref, out_moments_ref, act_ref = refs[1 + 2 * sides :]
     section, tm, tile = (lax.axis_index(axis) for axis in AXES)
-    frames, rows, columns, half = x_ref.shape
+    columns, half = rim_refs[0].shape[2:]
+    frames, rows, width = body_ref.shape[0] // 2, body_ref.shape[1], body_ref.shape[2]
     kept = hidden_ref.shape[1]
     own = columns // 2
-    width = own + RIM
     first = pl.multiple_of(section * (columns - width), RIM)
     cols = pl.ds(first, width)
     top = first_row(tiles, tile)
     rim_rows = (0, rows + 2) if sides == 2 else ((rows + 2) * (1 - tile),)
-    pieces = (
-        (section, prev_ref, x_ref, rim_refs),
-        (1 - section, other_prev_ref, other_x_ref, other_rim_refs),
-    )
-    for which, before, now, rims in pieces:
+    act_ref[:, 2 : 2 + rows] = body_ref[...]
+    for which, rims in ((section, rim_refs), (1 - section, other_rim_refs)):
         norm = tuple(norm_ref[which, k : k + 1] for k in range(3))
         lanes = pl.ds(pl.multiple_of(which * half, half), half)
         for f in range(2 * frames):
-            body = before[f, :, cols, :] if f < frames else now[f - frames, :, cols, :]
-            act_ref[f, 2 : 2 + rows, :, lanes] = apply_norm(body, norm)
             for row, rim in zip(rim_rows, rims):
                 act_ref[f, pl.ds(row, 2), :, lanes] = apply_norm(rim[f, :, cols, :], norm)
 
@@ -238,6 +247,21 @@
     return jnp.where(section == 0, values[:, :own], values[:, width - own :])
 
 
+def shortcut_kernel(x_ref, other_x_ref, skip_ref, skip_bias_ref, bias_ref, part_ref):
+    section = lax.axis_index("section")
+    frames, rows, columns, half = x_ref.shape
+    own = columns // 2
+    mine = pl.ds(pl.multiple_of(section * own, own), own)
+    skip_here = skip_ref[pl.ds(pl.multiple_of(section * half, half), half), :]
+    skip_there = skip_ref[pl.ds(pl.multiple_of((1 - section) * half, half), half), :]
+    for f in range(frames):
+        here = x_ref[f, :, mine, :].reshape(rows * own, half)
+        there = other_x_ref[f, :, mine, :].reshape(rows * own, half)
+        shortcut = jnp.dot(here, skip_here, preferred_element_type=jnp.float32)
+        shortcut = shortcut + jnp.dot(there, skip_there, preferred_element_type=jnp.float32)
+        part_ref[f] = (shortcut + (skip_bias_ref[...] + bias_ref[...])).reshape(rows, own, -1)
+
+
 def own_frames_kernel(
     tiles,
     hidden_ref,
@@ -245,20 +269,14 @@
     gain_ref,
     shift_ref,
     weight_ref,
-    bias_ref,
-    x_ref,
-    other_x_ref,
-    skip_ref,
-    skip_bias_ref,
+    shortcut_ref,
     part_ref,
     norm_ref,
     act_ref,
 ):
-    section, tile = lax.axis_index("section"), lax.axis_index("tile")
     frames, kept, width, outputs = hidden_ref.shape
-    rows, half = x_ref.shape[1], x_ref.shape[3]
-    own = x_ref.shape[2] // 2
-    top = first_row(tiles, tile)
+    rows, own = part_ref.shape[1:3]
+    top = first_row(tiles, lax.axis_index("tile"))
     norm = scale_and_offset(
         moments_ref[...],
         frames * rows * own,
@@ -270,23 +288,14 @@
     for f in range(frames):
         act_ref[f, pl.ds(top, kept)] = apply_norm(hidden_ref[f], norm)
     repeat_edges(act_ref, frames, tiles, rows)
-    mine = pl.ds(pl.multiple_of(section * own, own), own)
-    skip_here = skip_ref[pl.ds(pl.multiple_of(section * half, half), half), :]
-    skip_there = skip_ref[pl.ds(pl.multiple_of((1 - section) * half, half), half), :]
     for f in range(frames):
         taken = [(k - f + 2, k) for k in range(f - 2, f + 1) if k >= 0]
         residual = own_columns(conv_mid_rows(act_ref, weight_ref, taken, rows, width), own)
-        here = x_ref[f, :, mine, :].reshape(rows * own, half)
-        there = other_x_ref[f, :, mine, :].reshape(rows * own, half)
-        shortcut = jnp.dot(here, skip_here, preferred_element_type=jnp.float32)
-        shortcut = shortcut + jnp.dot(there, skip_there, preferred_element_type=jnp.float32)
-        part_ref[f] = (residual + bias_ref[...]) + (
-            shortcut.reshape(rows, own, outputs) + skip_bias_ref[...]
-        )
+        part_ref[f] = shortcut_ref[f] + residual
 
 
 def last_kernel(
-    tiles, hidden_ref, before_ref, norm_ref, weight_ref, part_ref, out_ref, act_ref
+    tiles, hidden_ref, before_ref, norm_ref, weight_ref, part_ref, out_hbm, act_ref, out_ref, sems
 ):
     section, tm, tile = (lax.axis_index(axis) for axis in AXES)
     frames, kept, width, outputs = hidden_ref.shape
@@ -308,10 +317,15 @@
             act_ref[f, pl.ds(top, kept)] = start
 
     repeat_edges(act_ref, frames, tiles, rows)
+    copies = []
     for f in range(frames):
         taken = [(k - f, k) for k in range(f, f + 3) if k < frames]
         residual = own_columns(conv_mid_rows(act_ref, weight_ref, taken, rows, width), own)
         out_ref[f] = (part_ref[f] + residual).astype(jnp.bfloat16)
+        copies.append(pltpu.make_async_copy(out_ref.at[f], out_hbm.at[f], sems.at[f]))
+        copies[-1].start()
+    for copy in copies:
+        copy.wait()
 
 
 def pairs_for(tm_count, tile_count, tm_step, tile_step):
@@ -357,7 +371,7 @@
         return lax.ppermute(value, "section", [(0, 1), (1, 0)])
 
     previous = shift(features, 1, 0)
-    moments = pl.pallas_call(
+    sums = pl.pallas_call(
         first_kernel,
         out_shape=jax.ShapeDtypeStruct((parties, 2, half), jnp.float32),
         in_specs=[pl.BlockSpec(memory_space=pl.ANY)],
@@ -370,7 +384,8 @@
         cost_estimate=cost(1_000_000_000, 1_000_000),
         name="feature_moments",
     )(features)
-    moments = to_everyone(moments)
+    moments = to_everyone(sums)
+    previous, _ = lax.optimization_barrier((previous, sums))
     other = swap(features)
     edges = 1 if tiles == 2 else 2
     edge_rows = pl.pallas_call(
@@ -400,23 +415,29 @@
     other_rims = [swap(rim) for rim in rims]
 
     kept = rows + edges
+    body = pl.pallas_call(
+        body_kernel,
+        out_shape=jax.ShapeDtypeStruct((2 * frames, rows, width, 2 * half), jnp.bfloat16),
+        in_specs=vmem_specs(5),
+        out_specs=pl.BlockSpec(memory_space=pltpu.VMEM),
+        compiler_params=params(),
+        cost_estimate=cost(1_000_000_000, 1_000_000),
+        name="norm_body",
+    )(features, previous, other, other_previous, norm_in)
     hidden, moments_mid = pl.pallas_call(
         functools.partial(middle_kernel, tiles, edges),
         out_shape=(
             jax.ShapeDtypeStruct((frames, kept, width, middle), jnp.bfloat16),
             jax.ShapeDtypeStruct((parties, 2, middle), jnp.float32),
         ),
-        in_specs=vmem_specs(7 + 2 * edges),
+        in_specs=vmem_specs(4 + 2 * edges),
         out_specs=tuple(vmem_specs(2)),
         scratch_shapes=[pltpu.VMEM((2 * frames, rows + 4, width, 2 * half), jnp.bfloat16)],
         compiler_params=params(),
         cost_estimate=cost(4_000_000_000, 1_000_000),
-        name="norm_conv_in",
+        name="conv_in",
     )(
-        features,
-        previous,
-        other,
-        other_previous,
+        body,
         *rims,
         *other_rims,
         norm_in,
@@ -434,13 +455,29 @@
         name="pack_hidden",
     )(hidden)
     before = shift(sent, 1, 0)
+    shown, _ = lax.optimization_barrier((other, sent))
+    shortcut = pl.pallas_call(
+        shortcut_kernel,
+        out_shape=jax.ShapeDtypeStruct((frames, rows, own, outputs), jnp.float32),
+        in_specs=vmem_specs(5),
+        out_specs=pl.BlockSpec(memory_space=pltpu.VMEM),
+        compiler_params=params(),
+        cost_estimate=cost(300_000_000, 1_000_000),
+        name="shortcut",
+    )(
+        features,
+        shown,
+        skip_weight,
+        skip_bias.reshape(1, outputs),
+        conv_mid_bias.reshape(1, outputs),
+    )
     part, norm_mid = pl.pallas_call(
         functools.partial(own_frames_kernel, tiles),
         out_shape=(
             jax.ShapeDtypeStruct((frames, rows, own, outputs), jnp.float32),
             jax.ShapeDtypeStruct((3, middle), jnp.float32),
         ),
-        in_specs=vmem_specs(10),
+        in_specs=vmem_specs(6),
         out_specs=tuple(vmem_specs(2)),
         scratch_shapes=[pltpu.VMEM((frames, rows + 2, width, middle), jnp.bfloat16)],
         compiler_params=params(),
@@ -452,18 +489,18 @@
         norm_gain_mid.reshape(1, middle),
         norm_shift_mid.reshape(1, middle),
         conv_mid_weight,
-        conv_mid_bias.reshape(1, outputs),
-        features,
-        other,
-        skip_weight,
-        skip_bias.reshape(1, outputs),
+        shortcut,
     )
     return pl.pallas_call(
         functools.partial(last_kernel, tiles),
         out_shape=jax.ShapeDtypeStruct((frames, rows, own, outputs), jnp.bfloat16),
         in_specs=vmem_specs(5),
-        out_specs=pl.BlockSpec(memory_space=pltpu.VMEM),
-        scratch_shapes=[pltpu.VMEM((frames, rows + 2, width, middle), jnp.bfloat16)],
+        out_specs=pl.BlockSpec(memory_space=pl.ANY),
+        scratch_shapes=[
+            pltpu.VMEM((frames, rows + 2, width, middle), jnp.bfloat16),
+            pltpu.VMEM((frames, rows, own, outputs), jnp.bfloat16),
+            pltpu.SemaphoreType.DMA((frames,)),
+        ],
         compiler_params=params(),
         cost_estimate=cost(2_000_000_000, 1_000_000),
         name="conv_mid_previous_frames",

time: 38.2 us -> 43.6 us (1.14)
  waiting for transfers between devices: 9.43 us -> 13.1 us
  starting transfers between devices: 20 us -> 21.4 us
    ppermute x2, waiting for transfers between devices: 0.01 us -> 3.87 us  [shift(): lax.ppermute(value, grid_axes, pairs_for(tms, tiles, tm_step, tile_step))]
    all_to_all x2, starting transfers between devices: 8.75 us -> 10.6 us  [to_everyone(): return lax.all_to_all(moments, AXES, 0, 0, tiled=True)]
    pallas_call x0 -> x2, Pallas kernels: none -> 0.7 us  [the longest x1 0.48 us: shards(): pl.pallas_call(body_kernel, out_shape=jax.ShapeDtypeStruct((2 * frames, r...]
    ppermute x3, waiting for transfers between devices: 1.33 us -> 0.83 us  [swap(): return lax.ppermute(value, 'section', [(0, 1), (1, 0)])]
    ppermute x3, starting transfers between devices: 0.58 us -> 0.14 us  [swap(): return lax.ppermute(value, 'section', [(0, 1), (1, 0)])]
  transfers between devices with their start and end apart: 8 -> 8, of which waited for: 3 -> 4; matrix products, arithmetic and copies ran while one was open for 0% -> 0% of each run, Pallas kernels for 9% -> 9%
where the time goes in v3:
time: 43.6 us; the launch traced here: 43.3 us
  starting transfers between devices  21.4 us (49%)
  waiting for transfers between devices  13.1 us (30%)
  Pallas kernels  8.5 us (19%)
    all_to_all x2, starting transfers between devices, to_everyone(): return lax.all_to_all(moments, AXES, 0, 0, tiled=True)  10.6 us
    ppermute x2, starting transfers between devices, shift(): lax.ppermute(value, grid_axes, pairs_for(tms, tiles, tm_step, tile_step))  8.79 us
    all_to_all x2, waiting for transfers between devices, to_everyone(): return lax.all_to_all(moments, AXES, 0, 0, tiled=True)  8.35 us
    ppermute x2, waiting for transfers between devices, shift(): lax.ppermute(value, grid_axes, pairs_for(tms, tiles, tm_step, tile_step))  3.87 us
    pallas_call x1, Pallas kernels, shards(): pl.pallas_call(functools.partial(middle_kernel, tiles, edges), out_shape=...  2.97 us
    pallas_call x1, Pallas kernels, shards(): pl.pallas_call(first_kernel, out_shape=jax.ShapeDtypeStruct((parties, 2,...  1.87 us
    ppermute x1, starting transfers between devices, shards(): rims = [lax.ppermute(edge_rows[0], 'tile', [(0, 1), (1, 0)])]  1.83 us
    pallas_call x1, Pallas kernels, shards(): pl.pallas_call(functools.partial(last_kernel, tiles), out_shape=jax.Shape...  1.51 us
  transfers between devices with their start and end apart: 8, of which 4 were waited for; matrix products, arithmetic and copies ran while one was open for 0% of the time, Pallas kernels for 9%

profile of v3, /device:TPU:0, one launch (start us, length us, event | category | flops | bytes accessed | tf_op | source)
XLA Modules:
  0.0 43.3 jit_solution(16180105525358631932)
XLA Ops:
  0.0 0.0 copy-start.2
  0.0 5.0 %collective-permute-start = (bf16[2,8,64,128]{3,2,1,0:T(8,128)(2,1)}, bf16[2,8,64,128]{3,2,1,0:T(8,128)(2,1)S(1)}, u32[]{:S(2)}, u32[]{:S(2)}) collective-permute-start(bf16[2,8,64,128]{3,2,1,0:T(8,128)(2,1)} %x_ref.5), channel_id=1, source_target_pairs={{0,2},{1,3},{2,4},{3,5},{4,6},{5,7},{6,8},{7,9},{8,10},{9,11},{10,... | collective-permute-start | bytes 786440 | tf_op jit(solution)/shard_map/ppermute | solution.py:368
  5.0 0.1 collective-permute-start.1
  5.1 1.9 %feature_moments.1 = f32[32,2,128]{2,1,0:T(2,128)} custom-call(bf16[2,8,64,128]{3,2,1,0:T(8,128)(2,1)} %x_ref.5), custom_call_target="tpu_custom_call" | custom-call | flops 1000000000 | bytes 1000000 | tf_op jit(solution)/shard_map/feature_moments/pallas_call | solution.py:374
  6.9 0.0 copy-start.4
  7.0 0.0 copy-start.5
  7.0 3.9 %collective-permute-done.prev_ref = bf16[2,8,64,128]{3,2,1,0:T(8,128)(2,1)S(1)} collective-permute-done((bf16[2,8,64,128]{3,2,1,0:T(8,128)(2,1)}, bf16[2,8,64,128]{3,2,1,0:T(8,128)(2,1)S(1)}, u32[]{:S(2)}, u32[]{:S(2)}) %collective-permute-start) | collective-permute-done | bytes 262176 | tf_op jit(solution)/shard_map/ppermute | solution.py:368
  10.8 0.0 collective-permute-start.2
  10.8 6.8 %all-to-all-start = ((f32[32,2,128]{2,1,0:T(2,128)}), f32[32,2,128]{2,1,0:T(2,128)S(1)}, u32[]{:S(2)}, u32[]{:S(2)}) async-start(f32[32,2,128]{2,1,0:T(2,128)} %feature_moments.1), calls=%async_computation | async-start | bytes 65536 | tf_op jit(solution)/shard_map/all_to_all | solution.py:342
  17.7 0.0 copy-done.2
  17.7 1.8 %collective-permute-start.3 = (bf16[4,2,64,128]{3,2,1,0:T(8,128)(2,1)S(1)}, bf16[4,2,64,128]{3,2,1,0:T(8,128)(2,1)S(1)}, u32[]{:S(2)}, u32[]{:S(2)}) collective-permute-start(bf16[4,2,64,128]{3,2,1,0:T(8,128)(2,1)S(1)} %facing_rows.1), channel_id=1, source_target_pairs={{0,1},{1,0},{2,3},{3,2},{4,5},{5,4},{6,7},{7,6},{8,9},{9,8},{10,11... | collective-permute-start | bytes 393224 | tf_op jit(solution)/shard_map/ppermute | solution.py:401
  19.6 5.3 %all-to-all-done.moments_ref = f32[32,2,128]{2,1,0:T(2,128)S(1)} async-done(((f32[32,2,128]{2,1,0:T(2,128)}), f32[32,2,128]{2,1,0:T(2,128)S(1)}, u32[]{:S(2)}, u32[]{:S(2)}) %all-to-all-start) | async-done | bytes 32800 | tf_op jit(solution)/shard_map/all_to_all | solution.py:342
  24.9 0.0 copy-done.4
  24.9 0.0 copy-done.5
  24.9 0.3 feature_scales.1.norm_ref.refs_3_
  25.2 0.0 copy-start
  25.2 0.0 copy-start.6
  25.2 0.0 collective-permute-done.3.refs_1_
  25.2 0.1 collective-permute-start.4
  25.3 0.0 collective-permute-done.1.other_x_ref
  25.3 0.0 collective-permute-done.2.other_prev_ref
  25.3 0.5 %norm_body.1.refs_0_ = bf16[4,8,48,256]{3,2,1,0:T(8,128)(2,1)S(1)} custom-call(bf16[2,8,64,128]{3,2,1,0:T(8,128)(2,1)S(1)} %copy-done.2, bf16[2,8,64,128]{3,2,1,0:T(8,128)(2,1)S(1)} %collective-permute-done.prev_ref, bf16[2,8,64,128]{3,2,1,0:T(8,128)(2,1)S(1)} %collective-permute-done.1.other_x_ref, ...), custom_call_target="tpu_custom_call" | custom-call | flops 1000000000 | bytes 1000000 | tf_op jit(solution)/shard_map/norm_body/pallas_call | solution.py:418
  25.8 0.8 %collective-permute-done.4.refs_2_ = bf16[4,2,64,128]{3,2,1,0:T(8,128)(2,1)S(1)} collective-permute-done((bf16[4,2,64,128]{3,2,1,0:T(8,128)(2,1)S(1)}, bf16[4,2,64,128]{3,2,1,0:T(8,128)(2,1)S(1)}, u32[]{:S(2)}, u32[]{:S(2)}) %collective-permute-start.4) | collective-permute-done | bytes 131104 | tf_op jit(solution)/shard_map/ppermute | solution.py:371
  26.7 0.0 copy-done
  26.7 0.0 copy-done.6
  26.7 3.0 %conv_in.1 = (bf16[2,9,48,128]{3,2,1,0:T(8,128)(2,1)S(1)}, f32[32,2,128]{2,1,0:T(2,128)}) custom-call(bf16[4,8,48,256]{3,2,1,0:T(8,128)(2,1)S(1)} %norm_body.1.refs_0_, bf16[4,2,64,128]{3,2,1,0:T(8,128)(2,1)S(1)} %collective-permute-done.3.refs_1_, bf16[4,2,64,128]{3,2,1,0:T(8,128)(2,1)S(1)} %collective-permute-done.4.refs_2_, ...), custom_call_target="tpu_custom_call" | custom-call | flops 4000000000 | bytes 1000000 | tf_op jit(solution)/shard_map/conv_in/pallas_call | solution.py:427
  29.7 3.8 %all-to-all-start.1 = ((f32[32,2,128]{2,1,0:T(2,128)}), f32[32,2,128]{2,1,0:T(2,128)S(1)}, u32[]{:S(2)}, u32[]{:S(2)}) async-start(f32[32,2,128]{2,1,0:T(2,128)} %get-tuple-element.17), calls=%async_computation.1 | async-start | bytes 65536 | tf_op jit(solution)/shard_map/all_to_all | solution.py:342
  33.4 0.0 copy-start.3
  33.4 0.0 copy-start.7
  33.5 0.0 copy-start.8
  33.5 0.0 copy-start.1
  33.5 0.0 copy-start.9
  33.5 0.0 copy-start.10
  33.5 3.8 %collective-permute-start.5 = (bf16[2,10,32,128]{3,2,1,0:T(8,128)(2,1)S(1)}, bf16[2,10,32,128]{3,2,1,0:T(8,128)(2,1)S(1)}, u32[]{:S(2)}, u32[]{:S(2)}) collective-permute-start(bf16[2,10,32,128]{3,2,1,0:T(8,128)(2,1)S(1)} %pack_hidden.1), channel_id=1, source_target_pairs={{0,2},{1,3},{2,4},{3,5},{4,6},{5,7},{6,8},{7,9},{8,10},{9,11},{10,... | collective-permute-start | bytes 491528 | tf_op jit(solution)/shard_map/ppermute | solution.py:368
  37.4 0.0 copy-done.3
  37.4 0.0 copy-done.7
  37.4 0.0 copy-done.8
  37.4 0.2 shortcut.1.shortcut_ref
  37.6 3.0 %all-to-all-done.1.moments_ref = f32[32,2,128]{2,1,0:T(2,128)S(1)} async-done(((f32[32,2,128]{2,1,0:T(2,128)}), f32[32,2,128]{2,1,0:T(2,128)S(1)}, u32[]{:S(2)}, u32[]{:S(2)}) %all-to-all-start.1) | async-done | bytes 32800 | tf_op jit(solution)/shard_map/all_to_all | solution.py:342
  40.6 0.0 copy-done.1
  40.6 0.0 copy-done.9
  40.6 0.0 copy-done.10
  40.7 1.1 %conv_mid_own_frames.1 = (f32[2,8,32,128]{3,2,1,0:T(8,128)S(1)}, f32[3,128]{1,0:T(4,128)S(1)}) custom-call(bf16[2,9,48,128]{3,2,1,0:T(8,128)(2,1)S(1)} %get-tuple-element.16.hidden_ref, f32[32,2,128]{2,1,0:T(2,128)S(1)} %all-to-all-done.1.moments_ref, f32[1,128]{1,0:T(1,128)S(1)} %bitcast.12, f32[1,128]{1,0:T(1,128)S(1)} %bitcast.13, ...), custom_call_target="tpu_custom_call" | custom-call | flops 2000000000 | bytes 1000000 | tf_op jit(solution)/shard_map/conv_mid_own_frames/pallas_call | solution.py:474
  41.8 0.0 collective-permute-done.5.before_ref
  41.8 1.5 %conv_mid_previous_frames.1 = bf16[2,8,32,128]{3,2,1,0:T(8,128)(2,1)} custom-call(bf16[2,9,48,128]{3,2,1,0:T(8,128)(2,1)S(1)} %get-tuple-element.16.hidden_ref, bf16[2,10,32,128]{3,2,1,0:T(8,128)(2,1)S(1)} %collective-permute-done.5.before_ref, f32[3,128]{1,0:T(4,128)S(1)} %get-tuple-element.19.norm_ref, bf16[3,3,3,128,128]{4,3,2,1,0:T(8,128)(2,1)S(1)} %copy-done.1, ...), custom_call_target="tpu_custom_call" | custom-call | flops 2000000000 | bytes 1000000 | tf_op jit(solution)/shard_map/conv_mid_previous_frames/pallas_call | solution.py:494
  (2 shorter events, 0.0 us)
Async XLA Ops:
  0.0 17.7 %copy-start.2 = (bf16[2,8,64,128]{3,2,1,0:T(8,128)(2,1)S(1)}, bf16[2,8,64,128]{3,2,1,0:T(8,128)(2,1)}, u32[]{:S(2)}) copy-start(bf16[2,8,64,128]{3,2,1,0:T(8,128)(2,1)} %x_ref.5) | copy-start | bytes 786436
  0.0 10.8 %collective-permute-start = (bf16[2,8,64,128]{3,2,1,0:T(8,128)(2,1)}, bf16[2,8,64,128]{3,2,1,0:T(8,128)(2,1)S(1)}, u32[]{:S(2)}, u32[]{:S(2)}) collective-permute-start(bf16[2,8,64,128]{3,2,1,0:T(8,128)(2,1)} %x_ref.5), channel_id=1, source_target_pairs={{0,2},{1,3},{2,4},{3,5},{4,6},{5,7},{6,8},{7,9},{8,10},{9,11},{10,... | collective-permute-start | bytes 786440 | tf_op jit(solution)/shard_map/ppermute | solution.py:368
  5.0 20.3 %collective-permute-start.1 = (bf16[2,8,64,128]{3,2,1,0:T(8,128)(2,1)}, bf16[2,8,64,128]{3,2,1,0:T(8,128)(2,1)S(1)}, u32[]{:S(2)}, u32[]{:S(2)}) collective-permute-start(bf16[2,8,64,128]{3,2,1,0:T(8,128)(2,1)} %x_ref.5), channel_id=1, source_target_pairs={{0,16},{16,0},{1,17},{17,1},{2,18},{18,2},{3,19},{19,3},{4,20},{20... | collective-permute-start | bytes 786440 | tf_op jit(solution)/shard_map/ppermute | solution.py:371
  6.9 18.0 %copy-start.4 = (f32[256]{0:T(256)S(1)}, f32[256]{0:T(256)}, u32[]{:S(2)}) copy-start(f32[256]{0:T(256)} %param.12) | copy-start | bytes 3076
  7.0 18.0 %copy-start.5 = (f32[256]{0:T(256)S(1)}, f32[256]{0:T(256)}, u32[]{:S(2)}) copy-start(f32[256]{0:T(256)} %param.13) | copy-start | bytes 3076
  10.8 14.5 %collective-permute-start.2 = (bf16[2,8,64,128]{3,2,1,0:T(8,128)(2,1)S(1)}, bf16[2,8,64,128]{3,2,1,0:T(8,128)(2,1)S(1)}, u32[]{:S(2)}, u32[]{:S(2)}) collective-permute-start(bf16[2,8,64,128]{3,2,1,0:T(8,128)(2,1)S(1)} %collective-permute-done.prev_ref), channel_id=1, source_target_pairs={{0,16},{16,0},{1,17},{17,1},{2,18},{18,2},{3,19},{19,3},{4,20},{20... | collective-permute-start | bytes 786440 | tf_op jit(solution)/shard_map/ppermute | solution.py:371
  10.8 14.1 %all-to-all-start = ((f32[32,2,128]{2,1,0:T(2,128)}), f32[32,2,128]{2,1,0:T(2,128)S(1)}, u32[]{:S(2)}, u32[]{:S(2)}) async-start(f32[32,2,128]{2,1,0:T(2,128)} %feature_moments.1), calls=%async_computation | async-start | bytes 65536 | tf_op jit(solution)/shard_map/all_to_all | solution.py:342
  17.7 7.5 %collective-permute-start.3 = (bf16[4,2,64,128]{3,2,1,0:T(8,128)(2,1)S(1)}, bf16[4,2,64,128]{3,2,1,0:T(8,128)(2,1)S(1)}, u32[]{:S(2)}, u32[]{:S(2)}) collective-permute-start(bf16[4,2,64,128]{3,2,1,0:T(8,128)(2,1)S(1)} %facing_rows.1), channel_id=1, source_target_pairs={{0,1},{1,0},{2,3},{3,2},{4,5},{5,4},{6,7},{7,6},{8,9},{9,8},{10,11... | collective-permute-start | bytes 393224 | tf_op jit(solution)/shard_map/ppermute | solution.py:401
  25.2 1.5 %copy-start = (bf16[3,3,3,256,128]{4,3,2,1,0:T(8,128)(2,1)S(1)}, bf16[3,3,3,256,128]{4,3,2,1,0:T(8,128)(2,1)}, u32[]{:S(2)}) copy-start(bf16[3,3,3,256,128]{4,3,2,1,0:T(8,128)(2,1)} %refs_4_.1) | copy-start | bytes 5308420
  25.2 1.5 %copy-start.6 = (f32[128]{0:T(128)S(1)}, f32[128]{0:T(128)}, u32[]{:S(2)}) copy-start(f32[128]{0:T(128)} %param.15) | copy-start | bytes 1540
  25.2 1.4 %collective-permute-start.4 = (bf16[4,2,64,128]{3,2,1,0:T(8,128)(2,1)S(1)}, bf16[4,2,64,128]{3,2,1,0:T(8,128)(2,1)S(1)}, u32[]{:S(2)}, u32[]{:S(2)}) collective-permute-start(bf16[4,2,64,128]{3,2,1,0:T(8,128)(2,1)S(1)} %collective-permute-done.3.refs_1_), channel_id=1, source_target_pairs={{0,16},{16,0},{1,17},{17,1},{2,18},{18,2},{3,19},{19,3},{4,20},{20... | collective-permute-start | bytes 393224 | tf_op jit(solution)/shard_map/ppermute | solution.py:371
  29.7 11.0 %all-to-all-start.1 = ((f32[32,2,128]{2,1,0:T(2,128)}), f32[32,2,128]{2,1,0:T(2,128)S(1)}, u32[]{:S(2)}, u32[]{:S(2)}) async-start(f32[32,2,128]{2,1,0:T(2,128)} %get-tuple-element.17), calls=%async_computation.1 | async-start | bytes 65536 | tf_op jit(solution)/shard_map/all_to_all | solution.py:342
  33.4 3.9 %copy-start.3 = (bf16[256,128]{1,0:T(8,128)(2,1)S(1)}, bf16[256,128]{1,0:T(8,128)(2,1)}, u32[]{:S(2)}) copy-start(bf16[256,128]{1,0:T(8,128)(2,1)} %skip_ref.1) | copy-start | bytes 196612
  33.4 3.9 %copy-start.7 = (f32[128]{0:T(128)S(1)}, f32[128]{0:T(128)}, u32[]{:S(2)}) copy-start(f32[128]{0:T(128)} %param.21) | copy-start | bytes 1540
  33.5 3.9 %copy-start.8 = (f32[128]{0:T(128)S(1)}, f32[128]{0:T(128)}, u32[]{:S(2)}) copy-start(f32[128]{0:T(128)} %param.19) | copy-start | bytes 1540
  33.5 7.2 %copy-start.1 = (bf16[3,3,3,128,128]{4,3,2,1,0:T(8,128)(2,1)S(1)}, bf16[3,3,3,128,128]{4,3,2,1,0:T(8,128)(2,1)}, u32[]{:S(2)}) copy-start(bf16[3,3,3,128,128]{4,3,2,1,0:T(8,128)(2,1)} %weight_ref.3) | copy-start | bytes 2654212
  33.5 7.2 %copy-start.9 = (f32[128]{0:T(128)S(1)}, f32[128]{0:T(128)}, u32[]{:S(2)}) copy-start(f32[128]{0:T(128)} %param.16) | copy-start | bytes 1540
  33.5 7.2 %copy-start.10 = (f32[128]{0:T(128)S(1)}, f32[128]{0:T(128)}, u32[]{:S(2)}) copy-start(f32[128]{0:T(128)} %param.17) | copy-start | bytes 1540
  33.5 8.2 %collective-permute-start.5 = (bf16[2,10,32,128]{3,2,1,0:T(8,128)(2,1)S(1)}, bf16[2,10,32,128]{3,2,1,0:T(8,128)(2,1)S(1)}, u32[]{:S(2)}, u32[]{:S(2)}) collective-permute-start(bf16[2,10,32,128]{3,2,1,0:T(8,128)(2,1)S(1)} %pack_hidden.1), channel_id=1, source_target_pairs={{0,2},{1,3},{2,4},{3,5},{4,6},{5,7},{6,8},{7,9},{8,10},{9,11},{10,... | collective-permute-start | bytes 491528 | tf_op jit(solution)/shard_map/ppermute | solution.py:368

commit v4 on v3

--- a/solution.py
+++ b/solution.py
@@ -156,24 +156,26 @@
     return 1 - tile if tiles == 2 else 0
 
 
-def body_kernel(x_ref, prev_ref, other_x_ref, other_prev_ref, norm_ref, body_ref):
+def body_kernel(x_ref, prev_ref, other_x_ref, norm_ref, body_ref):
     section = lax.axis_index("section")
     frames, _, columns, half = x_ref.shape
     width = body_ref.shape[2]
     cols = pl.ds(pl.multiple_of(section * (columns - width), RIM), width)
-    pieces = ((section, prev_ref, x_ref), (1 - section, other_prev_ref, other_x_ref))
-    for which, before, now in pieces:
+    for which, first, ref in (
+        (section, 0, prev_ref),
+        (section, frames, x_ref),
+        (1 - section, frames, other_x_ref),
+    ):
         norm = tuple(norm_ref[which, k : k + 1] for k in range(3))
         lanes = pl.ds(pl.multiple_of(which * half, half), half)
-        for f in range(2 * frames):
-            rows = before[f, :, cols, :] if f < frames else now[f - frames, :, cols, :]
-            body_ref[f, :, :, lanes] = apply_norm(rows, norm)
+        for f in range(frames):
+            body_ref[first + f, :, :, lanes] = apply_norm(ref[f, :, cols, :], norm)
 
 
 def middle_kernel(tiles, sides, *refs):
-    body_ref = refs[0]
-    rim_refs, other_rim_refs = refs[1 : 1 + sides], refs[1 + sides : 1 + 2 * sides]
-    norm_ref, weight_ref, bias_ref, hidden_ref, out_moments_ref, act_ref = refs[1 + 2 * sides :]
+    body_ref, other_prev_ref = refs[:2]
+    rim_refs, other_rim_refs = refs[2 : 2 + sides], refs[2 + sides : 2 + 2 * sides]
+    norm_ref, weight_ref, bias_ref, hidden_ref, out_moments_ref, act_ref = refs[2 + 2 * sides :]
     section, tm, tile = (lax.axis_index(axis) for axis in AXES)
     columns, half = rim_refs[0].shape[2:]
     frames, rows, width = body_ref.shape[0] // 2, body_ref.shape[1], body_ref.shape[2]
@@ -190,6 +192,8 @@
         for f in range(2 * frames):
             for row, rim in zip(rim_rows, rims):
                 act_ref[f, pl.ds(row, 2), :, lanes] = apply_norm(rim[f, :, cols, :], norm)
+    for f in range(frames):
+        act_ref[f, 2 : 2 + rows, :, lanes] = apply_norm(other_prev_ref[f, :, cols, :], norm)
 
     @pl.when(tile == 0)
     def _():
@@ -408,7 +412,7 @@
         in_specs=vmem_specs(3),
         out_specs=pl.BlockSpec(memory_space=pltpu.VMEM),
         compiler_params=params(),
-        cost_estimate=cost(1_000_000_000, 1_000_000),
+        cost_estimate=cost(2_000_000_000, 1_000_000),
         name="feature_scales",
     )(moments, norm_gain_in.reshape(sections, half), norm_shift_in.reshape(sections, half))
     norm_in, *rims = lax.optimization_barrier((norm_in, *rims))
@@ -418,19 +422,19 @@
     body = pl.pallas_call(
         body_kernel,
         out_shape=jax.ShapeDtypeStruct((2 * frames, rows, width, 2 * half), jnp.bfloat16),
-        in_specs=vmem_specs(5),
+        in_specs=vmem_specs(4),
         out_specs=pl.BlockSpec(memory_space=pltpu.VMEM),
         compiler_params=params(),
         cost_estimate=cost(1_000_000_000, 1_000_000),
         name="norm_body",
-    )(features, previous, other, other_previous, norm_in)
+    )(features, previous, other, norm_in)
     hidden, moments_mid = pl.pallas_call(
         functools.partial(middle_kernel, tiles, edges),
         out_shape=(
             jax.ShapeDtypeStruct((frames, kept, width, middle), jnp.bfloat16),
             jax.ShapeDtypeStruct((parties, 2, middle), jnp.float32),
         ),
-        in_specs=vmem_specs(4 + 2 * edges),
+        in_specs=vmem_specs(5 + 2 * edges),
         out_specs=tuple(vmem_specs(2)),
         scratch_shapes=[pltpu.VMEM((2 * frames, rows + 4, width, 2 * half), jnp.bfloat16)],
         compiler_params=params(),
@@ -438,6 +442,7 @@
         name="conv_in",
     )(
         body,
+        other_previous,
         *rims,
         *other_rims,
         norm_in,

time: 43.6 us -> 38.4 us (0.88)
  waiting for transfers between devices: 13.1 us -> 8.75 us
  starting transfers between devices: 21.4 us -> 20.5 us
    ppermute x2, waiting for transfers between devices: 3.87 us -> 0.01 us  [shift(): lax.ppermute(value, grid_axes, pairs_for(tms, tiles, tm_step, tile_step))]
    all_to_all x2, starting transfers between devices: 10.6 us -> 9.24 us  [to_everyone(): return lax.all_to_all(moments, AXES, 0, 0, tiled=True)]
    all_to_all x2, waiting for transfers between devices: 8.35 us -> 7.79 us  [to_everyone(): return lax.all_to_all(moments, AXES, 0, 0, tiled=True)]
    ppermute x3, starting transfers between devices: 0.14 us -> 0.65 us  [swap(): return lax.ppermute(value, 'section', [(0, 1), (1, 0)])]
  transfers between devices with their start and end apart: 8 -> 8, of which waited for: 4 -> 3; matrix products, arithmetic and copies ran while one was open for 0% -> 0% of each run, Pallas kernels for 9% -> 10%
where the time goes in v4:
time: 38.4 us; the launch traced here: 38.1 us
  starting transfers between devices  20.5 us (53%)
  waiting for transfers between devices  8.75 us (23%)
  Pallas kernels  8.48 us (22%)
    all_to_all x2, starting transfers between devices, to_everyone(): return lax.all_to_all(moments, AXES, 0, 0, tiled=True)  9.24 us
    ppermute x2, starting transfers between devices, shift(): lax.ppermute(value, grid_axes, pairs_for(tms, tiles, tm_step, tile_step))  8.79 us
    all_to_all x2, waiting for transfers between devices, to_everyone(): return lax.all_to_all(moments, AXES, 0, 0, tiled=True)  7.79 us
    pallas_call x1, Pallas kernels, shards(): pl.pallas_call(functools.partial(middle_kernel, tiles, edges), out_shape=...  3.09 us
    pallas_call x1, Pallas kernels, shards(): pl.pallas_call(first_kernel, out_shape=jax.ShapeDtypeStruct((parties, 2,...  1.87 us
    ppermute x1, starting transfers between devices, shards(): rims = [lax.ppermute(edge_rows[0], 'tile', [(0, 1), (1, 0)])]  1.83 us
    pallas_call x1, Pallas kernels, shards(): pl.pallas_call(functools.partial(last_kernel, tiles), out_shape=jax.Shape...  1.51 us
    pallas_call x1, Pallas kernels, shards(): pl.pallas_call(functools.partial(own_frames_kernel, tiles), out_shape=(ja...  1.1 us
  transfers between devices with their start and end apart: 8, of which 3 were waited for; matrix products, arithmetic and copies ran while one was open for 0% of the time, Pallas kernels for 10%

profile of v4, /device:TPU:0, one launch (start us, length us, event | category | flops | bytes accessed | tf_op | source)
XLA Modules:
  0.0 38.1 jit_solution(1877190202670822003)
XLA Ops:
  0.0 0.0 copy-start.2
  0.0 5.0 %collective-permute-start = (bf16[2,8,64,128]{3,2,1,0:T(8,128)(2,1)}, bf16[2,8,64,128]{3,2,1,0:T(8,128)(2,1)S(1)}, u32[]{:S(2)}, u32[]{:S(2)}) collective-permute-start(bf16[2,8,64,128]{3,2,1,0:T(8,128)(2,1)} %x_ref.5), channel_id=1, source_target_pairs={{0,2},{1,3},{2,4},{3,5},{4,6},{5,7},{6,8},{7,9},{8,10},{9,11},{10,... | collective-permute-start | bytes 786440 | tf_op jit(solution)/shard_map/ppermute | solution.py:372
  5.0 1.9 %feature_moments.1 = f32[32,2,128]{2,1,0:T(2,128)} custom-call(bf16[2,8,64,128]{3,2,1,0:T(8,128)(2,1)} %x_ref.5), custom_call_target="tpu_custom_call" | custom-call | flops 1000000000 | bytes 1000000 | tf_op jit(solution)/shard_map/feature_moments/pallas_call | solution.py:378
  6.9 0.0 copy-start.4
  6.9 0.0 copy-start.5
  6.9 4.9 %all-to-all-start = ((f32[32,2,128]{2,1,0:T(2,128)}), f32[32,2,128]{2,1,0:T(2,128)S(1)}, u32[]{:S(2)}, u32[]{:S(2)}) async-start(f32[32,2,128]{2,1,0:T(2,128)} %feature_moments.1), calls=%async_computation | async-start | bytes 65536 | tf_op jit(solution)/shard_map/all_to_all | solution.py:346
  11.8 0.0 copy-done.2
  11.8 0.3 collective-permute-start.1
  12.1 0.0 collective-permute-done.prev_ref
  12.2 0.3 collective-permute-start.3
  12.4 1.8 %collective-permute-start.2 = (bf16[4,2,64,128]{3,2,1,0:T(8,128)(2,1)S(1)}, bf16[4,2,64,128]{3,2,1,0:T(8,128)(2,1)S(1)}, u32[]{:S(2)}, u32[]{:S(2)}) collective-permute-start(bf16[4,2,64,128]{3,2,1,0:T(8,128)(2,1)S(1)} %facing_rows.1), channel_id=1, source_target_pairs={{0,1},{1,0},{2,3},{3,2},{4,5},{5,4},{6,7},{7,6},{8,9},{9,8},{10,11... | collective-permute-start | bytes 393224 | tf_op jit(solution)/shard_map/ppermute | solution.py:405
  14.3 4.8 %all-to-all-done.moments_ref = f32[32,2,128]{2,1,0:T(2,128)S(1)} async-done(((f32[32,2,128]{2,1,0:T(2,128)}), f32[32,2,128]{2,1,0:T(2,128)S(1)}, u32[]{:S(2)}, u32[]{:S(2)}) %all-to-all-start) | async-done | bytes 32800 | tf_op jit(solution)/shard_map/all_to_all | solution.py:346
  19.0 0.0 copy-done.4
  19.0 0.0 copy-done.5
  19.0 0.3 feature_scales.1.norm_ref.refs_4_
  19.3 0.0 copy-start
  19.4 0.0 copy-start.6
  19.4 0.0 collective-permute-done.2.refs_2_
  19.4 0.1 collective-permute-start.4
  19.5 0.0 collective-permute-done.1.other_x_ref
  19.5 0.4 norm_body.1.refs_0_
  19.8 0.0 collective-permute-done.3.refs_1_
  19.8 0.9 %collective-permute-done.4.refs_3_ = bf16[4,2,64,128]{3,2,1,0:T(8,128)(2,1)S(1)} collective-permute-done((bf16[4,2,64,128]{3,2,1,0:T(8,128)(2,1)S(1)}, bf16[4,2,64,128]{3,2,1,0:T(8,128)(2,1)S(1)}, u32[]{:S(2)}, u32[]{:S(2)}) %collective-permute-start.4) | collective-permute-done | bytes 131104 | tf_op jit(solution)/shard_map/ppermute | solution.py:375
  20.8 0.0 copy-done
  20.8 0.0 copy-done.6
  20.8 3.1 %conv_in.1 = (bf16[2,9,48,128]{3,2,1,0:T(8,128)(2,1)S(1)}, f32[32,2,128]{2,1,0:T(2,128)}) custom-call(bf16[4,8,48,256]{3,2,1,0:T(8,128)(2,1)S(1)} %norm_body.1.refs_0_, bf16[2,8,64,128]{3,2,1,0:T(8,128)(2,1)S(1)} %collective-permute-done.3.refs_1_, bf16[4,2,64,128]{3,2,1,0:T(8,128)(2,1)S(1)} %collective-permute-done.2.refs_2_, ...), custom_call_target="tpu_custom_call" | custom-call | flops 4000000000 | bytes 1000000 | tf_op jit(solution)/shard_map/conv_in/pallas_call | solution.py:431
  23.9 4.3 %all-to-all-start.1 = ((f32[32,2,128]{2,1,0:T(2,128)}), f32[32,2,128]{2,1,0:T(2,128)S(1)}, u32[]{:S(2)}, u32[]{:S(2)}) async-start(f32[32,2,128]{2,1,0:T(2,128)} %get-tuple-element.17), calls=%async_computation.1 | async-start | bytes 65536 | tf_op jit(solution)/shard_map/all_to_all | solution.py:346
  28.2 0.0 copy-start.3
  28.3 0.0 copy-start.7
  28.3 0.0 copy-start.8
  28.3 0.0 copy-start.1
  28.3 0.0 copy-start.9
  28.3 0.0 copy-start.10
  28.3 3.8 %collective-permute-start.5 = (bf16[2,10,32,128]{3,2,1,0:T(8,128)(2,1)S(1)}, bf16[2,10,32,128]{3,2,1,0:T(8,128)(2,1)S(1)}, u32[]{:S(2)}, u32[]{:S(2)}) collective-permute-start(bf16[2,10,32,128]{3,2,1,0:T(8,128)(2,1)S(1)} %pack_hidden.1), channel_id=1, source_target_pairs={{0,2},{1,3},{2,4},{3,5},{4,6},{5,7},{6,8},{7,9},{8,10},{9,11},{10,... | collective-permute-start | bytes 491528 | tf_op jit(solution)/shard_map/ppermute | solution.py:372
  32.2 0.0 copy-done.3
  32.2 0.0 copy-done.7
  32.2 0.0 copy-done.8
  32.2 0.2 shortcut.1.shortcut_ref
  32.4 3.0 %all-to-all-done.1.moments_ref = f32[32,2,128]{2,1,0:T(2,128)S(1)} async-done(((f32[32,2,128]{2,1,0:T(2,128)}), f32[32,2,128]{2,1,0:T(2,128)S(1)}, u32[]{:S(2)}, u32[]{:S(2)}) %all-to-all-start.1) | async-done | bytes 32800 | tf_op jit(solution)/shard_map/all_to_all | solution.py:346
  35.5 0.0 copy-done.1
  35.5 0.0 copy-done.9
  35.5 0.0 copy-done.10
  35.5 1.1 %conv_mid_own_frames.1 = (f32[2,8,32,128]{3,2,1,0:T(8,128)S(1)}, f32[3,128]{1,0:T(4,128)S(1)}) custom-call(bf16[2,9,48,128]{3,2,1,0:T(8,128)(2,1)S(1)} %get-tuple-element.16.hidden_ref, f32[32,2,128]{2,1,0:T(2,128)S(1)} %all-to-all-done.1.moments_ref, f32[1,128]{1,0:T(1,128)S(1)} %bitcast.12, f32[1,128]{1,0:T(1,128)S(1)} %bitcast.13, ...), custom_call_target="tpu_custom_call" | custom-call | flops 2000000000 | bytes 1000000 | tf_op jit(solution)/shard_map/conv_mid_own_frames/pallas_call | solution.py:479
  36.6 0.0 collective-permute-done.5.before_ref
  36.6 1.5 %conv_mid_previous_frames.1 = bf16[2,8,32,128]{3,2,1,0:T(8,128)(2,1)} custom-call(bf16[2,9,48,128]{3,2,1,0:T(8,128)(2,1)S(1)} %get-tuple-element.16.hidden_ref, bf16[2,10,32,128]{3,2,1,0:T(8,128)(2,1)S(1)} %collective-permute-done.5.before_ref, f32[3,128]{1,0:T(4,128)S(1)} %get-tuple-element.19.norm_ref, bf16[3,3,3,128,128]{4,3,2,1,0:T(8,128)(2,1)S(1)} %copy-done.1, ...), custom_call_target="tpu_custom_call" | custom-call | flops 2000000000 | bytes 1000000 | tf_op jit(solution)/shard_map/conv_mid_previous_frames/pallas_call | solution.py:499
  (2 shorter events, 0.0 us)
Async XLA Ops:
  0.0 11.8 %copy-start.2 = (bf16[2,8,64,128]{3,2,1,0:T(8,128)(2,1)S(1)}, bf16[2,8,64,128]{3,2,1,0:T(8,128)(2,1)}, u32[]{:S(2)}) copy-start(bf16[2,8,64,128]{3,2,1,0:T(8,128)(2,1)} %x_ref.5) | copy-start | bytes 786436
  0.0 12.1 %collective-permute-start = (bf16[2,8,64,128]{3,2,1,0:T(8,128)(2,1)}, bf16[2,8,64,128]{3,2,1,0:T(8,128)(2,1)S(1)}, u32[]{:S(2)}, u32[]{:S(2)}) collective-permute-start(bf16[2,8,64,128]{3,2,1,0:T(8,128)(2,1)} %x_ref.5), channel_id=1, source_target_pairs={{0,2},{1,3},{2,4},{3,5},{4,6},{5,7},{6,8},{7,9},{8,10},{9,11},{10,... | collective-permute-start | bytes 786440 | tf_op jit(solution)/shard_map/ppermute | solution.py:372
  6.9 12.2 %copy-start.4 = (f32[256]{0:T(256)S(1)}, f32[256]{0:T(256)}, u32[]{:S(2)}) copy-start(f32[256]{0:T(256)} %param.12) | copy-start | bytes 3076
  6.9 12.2 %copy-start.5 = (f32[256]{0:T(256)S(1)}, f32[256]{0:T(256)}, u32[]{:S(2)}) copy-start(f32[256]{0:T(256)} %param.13) | copy-start | bytes 3076
  6.9 12.1 %all-to-all-start = ((f32[32,2,128]{2,1,0:T(2,128)}), f32[32,2,128]{2,1,0:T(2,128)S(1)}, u32[]{:S(2)}, u32[]{:S(2)}) async-start(f32[32,2,128]{2,1,0:T(2,128)} %feature_moments.1), calls=%async_computation | async-start | bytes 65536 | tf_op jit(solution)/shard_map/all_to_all | solution.py:346
  11.8 7.6 %collective-permute-start.1 = (bf16[2,8,64,128]{3,2,1,0:T(8,128)(2,1)S(1)}, bf16[2,8,64,128]{3,2,1,0:T(8,128)(2,1)S(1)}, u32[]{:S(2)}, u32[]{:S(2)}) collective-permute-start(bf16[2,8,64,128]{3,2,1,0:T(8,128)(2,1)S(1)} %copy-done.2), channel_id=1, source_target_pairs={{0,16},{16,0},{1,17},{17,1},{2,18},{18,2},{3,19},{19,3},{4,20},{20... | collective-permute-start | bytes 786440 | tf_op jit(solution)/shard_map/ppermute | solution.py:375
  12.2 7.7 %collective-permute-start.3 = (bf16[2,8,64,128]{3,2,1,0:T(8,128)(2,1)S(1)}, bf16[2,8,64,128]{3,2,1,0:T(8,128)(2,1)S(1)}, u32[]{:S(2)}, u32[]{:S(2)}) collective-permute-start(bf16[2,8,64,128]{3,2,1,0:T(8,128)(2,1)S(1)} %collective-permute-done.prev_ref), channel_id=1, source_target_pairs={{0,16},{16,0},{1,17},{17,1},{2,18},{18,2},{3,19},{19,3},{4,20},{20... | collective-permute-start | bytes 786440 | tf_op jit(solution)/shard_map/ppermute | solution.py:375
  12.4 6.9 %collective-permute-start.2 = (bf16[4,2,64,128]{3,2,1,0:T(8,128)(2,1)S(1)}, bf16[4,2,64,128]{3,2,1,0:T(8,128)(2,1)S(1)}, u32[]{:S(2)}, u32[]{:S(2)}) collective-permute-start(bf16[4,2,64,128]{3,2,1,0:T(8,128)(2,1)S(1)} %facing_rows.1), channel_id=1, source_target_pairs={{0,1},{1,0},{2,3},{3,2},{4,5},{5,4},{6,7},{7,6},{8,9},{9,8},{10,11... | collective-permute-start | bytes 393224 | tf_op jit(solution)/shard_map/ppermute | solution.py:405
  19.3 1.5 %copy-start = (bf16[3,3,3,256,128]{4,3,2,1,0:T(8,128)(2,1)S(1)}, bf16[3,3,3,256,128]{4,3,2,1,0:T(8,128)(2,1)}, u32[]{:S(2)}) copy-start(bf16[3,3,3,256,128]{4,3,2,1,0:T(8,128)(2,1)} %refs_5_.1) | copy-start | bytes 5308420
  19.4 1.5 %copy-start.6 = (f32[128]{0:T(128)S(1)}, f32[128]{0:T(128)}, u32[]{:S(2)}) copy-start(f32[128]{0:T(128)} %param.15) | copy-start | bytes 1540
  19.4 1.4 %collective-permute-start.4 = (bf16[4,2,64,128]{3,2,1,0:T(8,128)(2,1)S(1)}, bf16[4,2,64,128]{3,2,1,0:T(8,128)(2,1)S(1)}, u32[]{:S(2)}, u32[]{:S(2)}) collective-permute-start(bf16[4,2,64,128]{3,2,1,0:T(8,128)(2,1)S(1)} %collective-permute-done.2.refs_2_), channel_id=1, source_target_pairs={{0,16},{16,0},{1,17},{17,1},{2,18},{18,2},{3,19},{19,3},{4,20},{20... | collective-permute-start | bytes 393224 | tf_op jit(solution)/shard_map/ppermute | solution.py:375
  23.9 11.5 %all-to-all-start.1 = ((f32[32,2,128]{2,1,0:T(2,128)}), f32[32,2,128]{2,1,0:T(2,128)S(1)}, u32[]{:S(2)}, u32[]{:S(2)}) async-start(f32[32,2,128]{2,1,0:T(2,128)} %get-tuple-element.17), calls=%async_computation.1 | async-start | bytes 65536 | tf_op jit(solution)/shard_map/all_to_all | solution.py:346
  28.2 3.9 %copy-start.3 = (bf16[256,128]{1,0:T(8,128)(2,1)S(1)}, bf16[256,128]{1,0:T(8,128)(2,1)}, u32[]{:S(2)}) copy-start(bf16[256,128]{1,0:T(8,128)(2,1)} %skip_ref.1) | copy-start | bytes 196612
  28.3 3.9 %copy-start.7 = (f32[128]{0:T(128)S(1)}, f32[128]{0:T(128)}, u32[]{:S(2)}) copy-start(f32[128]{0:T(128)} %param.21) | copy-start | bytes 1540
  28.3 3.9 %copy-start.8 = (f32[128]{0:T(128)S(1)}, f32[128]{0:T(128)}, u32[]{:S(2)}) copy-start(f32[128]{0:T(128)} %param.19) | copy-start | bytes 1540
  28.3 7.2 %copy-start.1 = (bf16[3,3,3,128,128]{4,3,2,1,0:T(8,128)(2,1)S(1)}, bf16[3,3,3,128,128]{4,3,2,1,0:T(8,128)(2,1)}, u32[]{:S(2)}) copy-start(bf16[3,3,3,128,128]{4,3,2,1,0:T(8,128)(2,1)} %weight_ref.3) | copy-start | bytes 2654212
  28.3 7.2 %copy-start.9 = (f32[128]{0:T(128)S(1)}, f32[128]{0:T(128)}, u32[]{:S(2)}) copy-start(f32[128]{0:T(128)} %param.16) | copy-start | bytes 1540
  28.3 7.2 %copy-start.10 = (f32[128]{0:T(128)S(1)}, f32[128]{0:T(128)}, u32[]{:S(2)}) copy-start(f32[128]{0:T(128)} %param.17) | copy-start | bytes 1540
  28.3 8.2 %collective-permute-start.5 = (bf16[2,10,32,128]{3,2,1,0:T(8,128)(2,1)S(1)}, bf16[2,10,32,128]{3,2,1,0:T(8,128)(2,1)S(1)}, u32[]{:S(2)}, u32[]{:S(2)}) collective-permute-start(bf16[2,10,32,128]{3,2,1,0:T(8,128)(2,1)S(1)} %pack_hidden.1), channel_id=1, source_target_pairs={{0,2},{1,3},{2,4},{3,5},{4,6},{5,7},{6,8},{7,9},{8,10},{9,11},{10,... | collective-permute-start | bytes 491528 | tf_op jit(solution)/shard_map/ppermute | solution.py:372

commit v5 on v4

--- a/solution.py
+++ b/solution.py
@@ -81,8 +81,13 @@
     moments_ref[...] = jnp.broadcast_to(moments_of(cells)[None], moments_ref.shape)
 
 
-def rows_kernel(pairs, x_ref, prev_ref, *edge_refs):
-    frames, rows = x_ref.shape[:2]
+def rows_kernel(pairs, x_ref, prev_ref, for_x_ref, for_prev_ref, *edge_refs):
+    frames, rows, columns = x_ref.shape[:3]
+    width = for_x_ref.shape[2]
+    start = (1 - lax.axis_index("section")) * (columns - width)
+    theirs = pl.ds(pl.multiple_of(start, RIM), width)
+    for_x_ref[...] = x_ref[:, :, theirs, :]
+    for_prev_ref[...] = prev_ref[:, :, theirs, :]
     if pairs:
         starts = [(rows - 2) * (1 - lax.axis_index("tile"))]
     else:
@@ -160,11 +165,11 @@
     section = lax.axis_index("section")
     frames, _, columns, half = x_ref.shape
     width = body_ref.shape[2]
-    cols = pl.ds(pl.multiple_of(section * (columns - width), RIM), width)
-    for which, first, ref in (
-        (section, 0, prev_ref),
-        (section, frames, x_ref),
-        (1 - section, frames, other_x_ref),
+    mine = pl.ds(pl.multiple_of(section * (columns - width), RIM), width)
+    for which, first, ref, cols in (
+        (section, 0, prev_ref, mine),
+        (section, frames, x_ref, mine),
+        (1 - section, frames, other_x_ref, slice(None)),
     ):
         norm = tuple(norm_ref[which, k : k + 1] for k in range(3))
         lanes = pl.ds(pl.multiple_of(which * half, half), half)
@@ -193,7 +198,7 @@
             for row, rim in zip(rim_rows, rims):
                 act_ref[f, pl.ds(row, 2), :, lanes] = apply_norm(rim[f, :, cols, :], norm)
     for f in range(frames):
-        act_ref[f, 2 : 2 + rows, :, lanes] = apply_norm(other_prev_ref[f, :, cols, :], norm)
+        act_ref[f, 2 : 2 + rows, :, lanes] = apply_norm(other_prev_ref[f], norm)
 
     @pl.when(tile == 0)
     def _():
@@ -256,11 +261,12 @@
     frames, rows, columns, half = x_ref.shape
     own = columns // 2
     mine = pl.ds(pl.multiple_of(section * own, own), own)
+    within = pl.ds(pl.multiple_of(section * (other_x_ref.shape[2] - own), RIM), own)
     skip_here = skip_ref[pl.ds(pl.multiple_of(section * half, half), half), :]
     skip_there = skip_ref[pl.ds(pl.multiple_of((1 - section) * half, half), half), :]
     for f in range(frames):
         here = x_ref[f, :, mine, :].reshape(rows * own, half)
-        there = other_x_ref[f, :, mine, :].reshape(rows * own, half)
+        there = other_x_ref[f, :, within, :].reshape(rows * own, half)
         shortcut = jnp.dot(here, skip_here, preferred_element_type=jnp.float32)
         shortcut = shortcut + jnp.dot(there, skip_there, preferred_element_type=jnp.float32)
         part_ref[f] = (shortcut + (skip_bias_ref[...] + bias_ref[...])).reshape(rows, own, -1)
@@ -390,13 +396,14 @@
     )(features)
     moments = to_everyone(sums)
     previous, _ = lax.optimization_barrier((previous, sums))
-    other = swap(features)
     edges = 1 if tiles == 2 else 2
-    edge_rows = pl.pallas_call(
+    edge = jax.ShapeDtypeStruct((2 * frames, 2, columns, half), features.dtype)
+    cut = jax.ShapeDtypeStruct((frames, rows, width, half), features.dtype)
+    for_x, for_previous, *edge_rows = pl.pallas_call(
         functools.partial(rows_kernel, tiles == 2),
-        out_shape=(jax.ShapeDtypeStruct((2 * frames, 2, columns, half), features.dtype),) * edges,
+        out_shape=(cut, cut) + (edge,) * edges,
         in_specs=vmem_specs(2),
-        out_specs=tuple(vmem_specs(edges)),
+        out_specs=tuple(vmem_specs(2 + edges)),
         compiler_params=params(),
         cost_estimate=cost(500_000_000, 1_000_000),
         name="facing_rows",
@@ -405,7 +412,8 @@
         rims = [lax.ppermute(edge_rows[0], "tile", [(0, 1), (1, 0)])]
     else:
         rims = [shift(edge_rows[1], 0, 1), shift(edge_rows[0], 0, -1)]
-    other_previous = swap(previous)
+    other = swap(for_x)
+    other_previous = swap(for_previous)
     norm_in = pl.pallas_call(
         functools.partial(scales_kernel, frames * rows * columns),
         out_shape=jax.ShapeDtypeStruct((sections, 3, half), jnp.float32),

time: 38.4 us -> 37.8 us (0.984)
  starting transfers between devices: 20.5 us -> 19.9 us
    all_to_all x2, starting transfers between devices: 9.24 us -> 8.72 us  [to_everyone(): return lax.all_to_all(moments, AXES, 0, 0, tiled=True)]
where the time goes in v5:
time: 37.8 us; the launch traced here: 37.6 us
  starting transfers between devices  19.9 us (53%)
  waiting for transfers between devices  8.76 us (23%)
  Pallas kernels  8.51 us (23%)
    ppermute x2, starting transfers between devices, shift(): lax.ppermute(value, grid_axes, pairs_for(tms, tiles, tm_step, tile_step))  8.79 us
    all_to_all x2, starting transfers between devices, to_everyone(): return lax.all_to_all(moments, AXES, 0, 0, tiled=True)  8.72 us
    all_to_all x2, waiting for transfers between devices, to_everyone(): return lax.all_to_all(moments, AXES, 0, 0, tiled=True)  7.81 us
    pallas_call x1, Pallas kernels, shards(): pl.pallas_call(functools.partial(middle_kernel, tiles, edges), out_shape=...  3.08 us
    pallas_call x1, Pallas kernels, shards(): pl.pallas_call(first_kernel, out_shape=jax.ShapeDtypeStruct((parties, 2,...  1.87 us
    ppermute x1, starting transfers between devices, shards(): rims = [lax.ppermute(edge_rows[0], 'tile', [(0, 1), (1, 0)])]  1.83 us
    pallas_call x1, Pallas kernels, shards(): pl.pallas_call(functools.partial(last_kernel, tiles), out_shape=jax.Shape...  1.5 us
    pallas_call x1, Pallas kernels, shards(): pl.pallas_call(functools.partial(own_frames_kernel, tiles), out_shape=(ja...  1.1 us
  transfers between devices with their start and end apart: 8, of which 3 were waited for; matrix products, arithmetic and copies ran while one was open for 0% of the time, Pallas kernels for 10%

profile of v5, /device:TPU:0, one launch (start us, length us, event | category | flops | bytes accessed | tf_op | source)
XLA Modules:
  0.0 37.6 jit_solution(1865387869629872281)
XLA Ops:
  0.0 0.0 copy-start.2
  0.0 5.0 %collective-permute-start = (bf16[2,8,64,128]{3,2,1,0:T(8,128)(2,1)}, bf16[2,8,64,128]{3,2,1,0:T(8,128)(2,1)S(1)}, u32[]{:S(2)}, u32[]{:S(2)}) collective-permute-start(bf16[2,8,64,128]{3,2,1,0:T(8,128)(2,1)} %x_ref.5), channel_id=1, source_target_pairs={{0,2},{1,3},{2,4},{3,5},{4,6},{5,7},{6,8},{7,9},{8,10},{9,11},{10,... | collective-permute-start | bytes 786440 | tf_op jit(solution)/shard_map/ppermute | solution.py:378
  5.0 1.9 %feature_moments.1 = f32[32,2,128]{2,1,0:T(2,128)} custom-call(bf16[2,8,64,128]{3,2,1,0:T(8,128)(2,1)} %x_ref.5), custom_call_target="tpu_custom_call" | custom-call | flops 1000000000 | bytes 1000000 | tf_op jit(solution)/shard_map/feature_moments/pallas_call | solution.py:384
  6.9 0.0 copy-start.4
  6.9 0.0 copy-start.5
  6.9 4.9 %all-to-all-start = ((f32[32,2,128]{2,1,0:T(2,128)}), f32[32,2,128]{2,1,0:T(2,128)S(1)}, u32[]{:S(2)}, u32[]{:S(2)}) async-start(f32[32,2,128]{2,1,0:T(2,128)} %feature_moments.1), calls=%async_computation | async-start | bytes 65536 | tf_op jit(solution)/shard_map/all_to_all | solution.py:352
  11.8 0.0 collective-permute-done.prev_ref
  11.8 0.0 copy-done.2
  11.9 1.8 %collective-permute-start.2 = (bf16[4,2,64,128]{3,2,1,0:T(8,128)(2,1)S(1)}, bf16[4,2,64,128]{3,2,1,0:T(8,128)(2,1)S(1)}, u32[]{:S(2)}, u32[]{:S(2)}) collective-permute-start(bf16[4,2,64,128]{3,2,1,0:T(8,128)(2,1)S(1)} %get-tuple-element.18), channel_id=1, source_target_pairs={{0,1},{1,0},{2,3},{3,2},{4,5},{5,4},{6,7},{7,6},{8,9},{9,8},{10,11... | collective-permute-start | bytes 393224 | tf_op jit(solution)/shard_map/ppermute | solution.py:412
  13.7 0.0 collective-permute-start.1
  13.7 0.5 %collective-permute-start.3 = (bf16[2,8,48,128]{3,2,1,0:T(8,128)(2,1)S(1)}, bf16[2,8,48,128]{3,2,1,0:T(8,128)(2,1)S(1)}, u32[]{:S(2)}, u32[]{:S(2)}) collective-permute-start(bf16[2,8,48,128]{3,2,1,0:T(8,128)(2,1)S(1)} %get-tuple-element.20), channel_id=1, source_target_pairs={{0,16},{16,0},{1,17},{17,1},{2,18},{18,2},{3,19},{19,3},{4,20},{20... | collective-permute-start | bytes 589832 | tf_op jit(solution)/shard_map/ppermute | solution.py:381
  14.2 4.8 %all-to-all-done.moments_ref = f32[32,2,128]{2,1,0:T(2,128)S(1)} async-done(((f32[32,2,128]{2,1,0:T(2,128)}), f32[32,2,128]{2,1,0:T(2,128)S(1)}, u32[]{:S(2)}, u32[]{:S(2)}) %all-to-all-start) | async-done | bytes 32800 | tf_op jit(solution)/shard_map/all_to_all | solution.py:352
  19.0 0.0 copy-done.4
  19.0 0.0 copy-done.5
  19.0 0.3 feature_scales.1.norm_ref.refs_4_
  19.3 0.0 copy-start
  19.4 0.0 copy-start.6
  19.4 0.0 collective-permute-done.2.refs_2_
  19.4 0.1 collective-permute-start.4
  19.5 0.0 collective-permute-done.1.other_x_ref
  19.5 0.4 norm_body.1.refs_0_
  19.8 0.0 collective-permute-done.3.refs_1_
  19.8 0.9 %collective-permute-done.4.refs_3_ = bf16[4,2,64,128]{3,2,1,0:T(8,128)(2,1)S(1)} collective-permute-done((bf16[4,2,64,128]{3,2,1,0:T(8,128)(2,1)S(1)}, bf16[4,2,64,128]{3,2,1,0:T(8,128)(2,1)S(1)}, u32[]{:S(2)}, u32[]{:S(2)}) %collective-permute-start.4) | collective-permute-done | bytes 131104 | tf_op jit(solution)/shard_map/ppermute | solution.py:381
  20.8 0.0 copy-done
  20.8 0.0 copy-done.6
  20.8 3.1 %conv_in.1 = (bf16[2,9,48,128]{3,2,1,0:T(8,128)(2,1)S(1)}, f32[32,2,128]{2,1,0:T(2,128)}) custom-call(bf16[4,8,48,256]{3,2,1,0:T(8,128)(2,1)S(1)} %norm_body.1.refs_0_, bf16[2,8,48,128]{3,2,1,0:T(8,128)(2,1)S(1)} %collective-permute-done.3.refs_1_, bf16[4,2,64,128]{3,2,1,0:T(8,128)(2,1)S(1)} %collective-permute-done.2.refs_2_, ...), custom_call_target="tpu_custom_call" | custom-call | flops 4000000000 | bytes 1000000 | tf_op jit(solution)/shard_map/conv_in/pallas_call | solution.py:439
  23.9 3.8 %all-to-all-start.1 = ((f32[32,2,128]{2,1,0:T(2,128)}), f32[32,2,128]{2,1,0:T(2,128)S(1)}, u32[]{:S(2)}, u32[]{:S(2)}) async-start(f32[32,2,128]{2,1,0:T(2,128)} %get-tuple-element.23), calls=%async_computation.1 | async-start | bytes 65536 | tf_op jit(solution)/shard_map/all_to_all | solution.py:352
  27.7 0.0 copy-start.3
  27.7 0.0 copy-start.7
  27.7 0.0 copy-start.8
  27.7 0.0 copy-start.1
  27.8 0.0 copy-start.9
  27.8 0.0 copy-start.10
  27.8 3.8 %collective-permute-start.5 = (bf16[2,10,32,128]{3,2,1,0:T(8,128)(2,1)S(1)}, bf16[2,10,32,128]{3,2,1,0:T(8,128)(2,1)S(1)}, u32[]{:S(2)}, u32[]{:S(2)}) collective-permute-start(bf16[2,10,32,128]{3,2,1,0:T(8,128)(2,1)S(1)} %pack_hidden.1), channel_id=1, source_target_pairs={{0,2},{1,3},{2,4},{3,5},{4,6},{5,7},{6,8},{7,9},{8,10},{9,11},{10,... | collective-permute-start | bytes 491528 | tf_op jit(solution)/shard_map/ppermute | solution.py:378
  31.6 0.0 copy-done.3
  31.6 0.0 copy-done.7
  31.7 0.0 copy-done.8
  31.7 0.2 shortcut.1.shortcut_ref
  31.9 3.0 %all-to-all-done.1.moments_ref = f32[32,2,128]{2,1,0:T(2,128)S(1)} async-done(((f32[32,2,128]{2,1,0:T(2,128)}), f32[32,2,128]{2,1,0:T(2,128)S(1)}, u32[]{:S(2)}, u32[]{:S(2)}) %all-to-all-start.1) | async-done | bytes 32800 | tf_op jit(solution)/shard_map/all_to_all | solution.py:352
  34.9 0.0 copy-done.1
  34.9 0.0 copy-done.9
  34.9 0.0 copy-done.10
  34.9 1.1 %conv_mid_own_frames.1 = (f32[2,8,32,128]{3,2,1,0:T(8,128)S(1)}, f32[3,128]{1,0:T(4,128)S(1)}) custom-call(bf16[2,9,48,128]{3,2,1,0:T(8,128)(2,1)S(1)} %get-tuple-element.22.hidden_ref, f32[32,2,128]{2,1,0:T(2,128)S(1)} %all-to-all-done.1.moments_ref, f32[1,128]{1,0:T(1,128)S(1)} %bitcast.12, f32[1,128]{1,0:T(1,128)S(1)} %bitcast.13, ...), custom_call_target="tpu_custom_call" | custom-call | flops 2000000000 | bytes 1000000 | tf_op jit(solution)/shard_map/conv_mid_own_frames/pallas_call | solution.py:487
  36.0 0.0 collective-permute-done.5.before_ref
  36.0 1.5 %conv_mid_previous_frames.1 = bf16[2,8,32,128]{3,2,1,0:T(8,128)(2,1)} custom-call(bf16[2,9,48,128]{3,2,1,0:T(8,128)(2,1)S(1)} %get-tuple-element.22.hidden_ref, bf16[2,10,32,128]{3,2,1,0:T(8,128)(2,1)S(1)} %collective-permute-done.5.before_ref, f32[3,128]{1,0:T(4,128)S(1)} %get-tuple-element.25.norm_ref, bf16[3,3,3,128,128]{4,3,2,1,0:T(8,128)(2,1)S(1)} %copy-done.1, ...), custom_call_target="tpu_custom_call" | custom-call | flops 2000000000 | bytes 1000000 | tf_op jit(solution)/shard_map/conv_mid_previous_frames/pallas_call | solution.py:507
  (2 shorter events, 0.1 us)
Async XLA Ops:
  0.0 11.8 %copy-start.2 = (bf16[2,8,64,128]{3,2,1,0:T(8,128)(2,1)S(1)}, bf16[2,8,64,128]{3,2,1,0:T(8,128)(2,1)}, u32[]{:S(2)}) copy-start(bf16[2,8,64,128]{3,2,1,0:T(8,128)(2,1)} %x_ref.5) | copy-start | bytes 786436
  0.0 11.8 %collective-permute-start = (bf16[2,8,64,128]{3,2,1,0:T(8,128)(2,1)}, bf16[2,8,64,128]{3,2,1,0:T(8,128)(2,1)S(1)}, u32[]{:S(2)}, u32[]{:S(2)}) collective-permute-start(bf16[2,8,64,128]{3,2,1,0:T(8,128)(2,1)} %x_ref.5), channel_id=1, source_target_pairs={{0,2},{1,3},{2,4},{3,5},{4,6},{5,7},{6,8},{7,9},{8,10},{9,11},{10,... | collective-permute-start | bytes 786440 | tf_op jit(solution)/shard_map/ppermute | solution.py:378
  6.9 12.2 %copy-start.4 = (f32[256]{0:T(256)S(1)}, f32[256]{0:T(256)}, u32[]{:S(2)}) copy-start(f32[256]{0:T(256)} %param.12) | copy-start | bytes 3076
  6.9 12.2 %copy-start.5 = (f32[256]{0:T(256)S(1)}, f32[256]{0:T(256)}, u32[]{:S(2)}) copy-start(f32[256]{0:T(256)} %param.13) | copy-start | bytes 3076
  6.9 12.1 %all-to-all-start = ((f32[32,2,128]{2,1,0:T(2,128)}), f32[32,2,128]{2,1,0:T(2,128)S(1)}, u32[]{:S(2)}, u32[]{:S(2)}) async-start(f32[32,2,128]{2,1,0:T(2,128)} %feature_moments.1), calls=%async_computation | async-start | bytes 65536 | tf_op jit(solution)/shard_map/all_to_all | solution.py:352
  11.9 7.5 %collective-permute-start.2 = (bf16[4,2,64,128]{3,2,1,0:T(8,128)(2,1)S(1)}, bf16[4,2,64,128]{3,2,1,0:T(8,128)(2,1)S(1)}, u32[]{:S(2)}, u32[]{:S(2)}) collective-permute-start(bf16[4,2,64,128]{3,2,1,0:T(8,128)(2,1)S(1)} %get-tuple-element.18), channel_id=1, source_target_pairs={{0,1},{1,0},{2,3},{3,2},{4,5},{5,4},{6,7},{7,6},{8,9},{9,8},{10,11... | collective-permute-start | bytes 393224 | tf_op jit(solution)/shard_map/ppermute | solution.py:412
  13.7 5.7 %collective-permute-start.1 = (bf16[2,8,48,128]{3,2,1,0:T(8,128)(2,1)S(1)}, bf16[2,8,48,128]{3,2,1,0:T(8,128)(2,1)S(1)}, u32[]{:S(2)}, u32[]{:S(2)}) collective-permute-start(bf16[2,8,48,128]{3,2,1,0:T(8,128)(2,1)S(1)} %get-tuple-element.17), channel_id=1, source_target_pairs={{0,16},{16,0},{1,17},{17,1},{2,18},{18,2},{3,19},{19,3},{4,20},{20... | collective-permute-start | bytes 589832 | tf_op jit(solution)/shard_map/ppermute | solution.py:381
  13.7 6.1 %collective-permute-start.3 = (bf16[2,8,48,128]{3,2,1,0:T(8,128)(2,1)S(1)}, bf16[2,8,48,128]{3,2,1,0:T(8,128)(2,1)S(1)}, u32[]{:S(2)}, u32[]{:S(2)}) collective-permute-start(bf16[2,8,48,128]{3,2,1,0:T(8,128)(2,1)S(1)} %get-tuple-element.20), channel_id=1, source_target_pairs={{0,16},{16,0},{1,17},{17,1},{2,18},{18,2},{3,19},{19,3},{4,20},{20... | collective-permute-start | bytes 589832 | tf_op jit(solution)/shard_map/ppermute | solution.py:381
  19.3 1.5 %copy-start = (bf16[3,3,3,256,128]{4,3,2,1,0:T(8,128)(2,1)S(1)}, bf16[3,3,3,256,128]{4,3,2,1,0:T(8,128)(2,1)}, u32[]{:S(2)}) copy-start(bf16[3,3,3,256,128]{4,3,2,1,0:T(8,128)(2,1)} %refs_5_.1) | copy-start | bytes 5308420
  19.4 1.5 %copy-start.6 = (f32[128]{0:T(128)S(1)}, f32[128]{0:T(128)}, u32[]{:S(2)}) copy-start(f32[128]{0:T(128)} %param.15) | copy-start | bytes 1540
  19.4 1.4 %collective-permute-start.4 = (bf16[4,2,64,128]{3,2,1,0:T(8,128)(2,1)S(1)}, bf16[4,2,64,128]{3,2,1,0:T(8,128)(2,1)S(1)}, u32[]{:S(2)}, u32[]{:S(2)}) collective-permute-start(bf16[4,2,64,128]{3,2,1,0:T(8,128)(2,1)S(1)} %collective-permute-done.2.refs_2_), channel_id=1, source_target_pairs={{0,16},{16,0},{1,17},{17,1},{2,18},{18,2},{3,19},{19,3},{4,20},{20... | collective-permute-start | bytes 393224 | tf_op jit(solution)/shard_map/ppermute | solution.py:381
  23.9 11.0 %all-to-all-start.1 = ((f32[32,2,128]{2,1,0:T(2,128)}), f32[32,2,128]{2,1,0:T(2,128)S(1)}, u32[]{:S(2)}, u32[]{:S(2)}) async-start(f32[32,2,128]{2,1,0:T(2,128)} %get-tuple-element.23), calls=%async_computation.1 | async-start | bytes 65536 | tf_op jit(solution)/shard_map/all_to_all | solution.py:352
  27.7 3.9 %copy-start.3 = (bf16[256,128]{1,0:T(8,128)(2,1)S(1)}, bf16[256,128]{1,0:T(8,128)(2,1)}, u32[]{:S(2)}) copy-start(bf16[256,128]{1,0:T(8,128)(2,1)} %skip_ref.1) | copy-start | bytes 196612
  27.7 3.9 %copy-start.7 = (f32[128]{0:T(128)S(1)}, f32[128]{0:T(128)}, u32[]{:S(2)}) copy-start(f32[128]{0:T(128)} %param.21) | copy-start | bytes 1540
  27.7 3.9 %copy-start.8 = (f32[128]{0:T(128)S(1)}, f32[128]{0:T(128)}, u32[]{:S(2)}) copy-start(f32[128]{0:T(128)} %param.19) | copy-start | bytes 1540
  27.7 7.2 %copy-start.1 = (bf16[3,3,3,128,128]{4,3,2,1,0:T(8,128)(2,1)S(1)}, bf16[3,3,3,128,128]{4,3,2,1,0:T(8,128)(2,1)}, u32[]{:S(2)}) copy-start(bf16[3,3,3,128,128]{4,3,2,1,0:T(8,128)(2,1)} %weight_ref.3) | copy-start | bytes 2654212
  27.8 7.2 %copy-start.9 = (f32[128]{0:T(128)S(1)}, f32[128]{0:T(128)}, u32[]{:S(2)}) copy-start(f32[128]{0:T(128)} %param.16) | copy-start | bytes 1540
  27.8 7.2 %copy-start.10 = (f32[128]{0:T(128)S(1)}, f32[128]{0:T(128)}, u32[]{:S(2)}) copy-start(f32[128]{0:T(128)} %param.17) | copy-start | bytes 1540
  27.8 8.2 %collective-permute-start.5 = (bf16[2,10,32,128]{3,2,1,0:T(8,128)(2,1)S(1)}, bf16[2,10,32,128]{3,2,1,0:T(8,128)(2,1)S(1)}, u32[]{:S(2)}, u32[]{:S(2)}) collective-permute-start(bf16[2,10,32,128]{3,2,1,0:T(8,128)(2,1)S(1)} %pack_hidden.1), channel_id=1, source_target_pairs={{0,2},{1,3},{2,4},{3,5},{4,6},{5,7},{6,8},{7,9},{8,10},{9,11},{10,... | collective-permute-start | bytes 491528 | tf_op jit(solution)/shard_map/ppermute | solution.py:378

commit v6 on v5

--- a/solution.py
+++ b/solution.py
@@ -81,20 +81,24 @@
     moments_ref[...] = jnp.broadcast_to(moments_of(cells)[None], moments_ref.shape)
 
 
+def facing(pairs, block_ref, edge_refs):
+    rows = block_ref.shape[1]
+    starts = [(rows - 2) * (1 - lax.axis_index("tile"))] if pairs else [0, rows - 2]
+    for start, edge_ref in zip(starts, edge_refs):
+        edge_ref[...] = block_ref[:, pl.ds(start, 2)]
+
+
+def own_rows_kernel(pairs, x_ref, order_ref, *edge_refs):
+    facing(pairs, x_ref, edge_refs)
+
+
 def rows_kernel(pairs, x_ref, prev_ref, for_x_ref, for_prev_ref, *edge_refs):
-    frames, rows, columns = x_ref.shape[:3]
-    width = for_x_ref.shape[2]
+    columns, width = x_ref.shape[2], for_x_ref.shape[2]
     start = (1 - lax.axis_index("section")) * (columns - width)
     theirs = pl.ds(pl.multiple_of(start, RIM), width)
     for_x_ref[...] = x_ref[:, :, theirs, :]
     for_prev_ref[...] = prev_ref[:, :, theirs, :]
-    if pairs:
-        starts = [(rows - 2) * (1 - lax.axis_index("tile"))]
-    else:
-        starts = [0, rows - 2]
-    for start, edge_ref in zip(starts, edge_refs):
-        edge_ref[:frames] = prev_ref[:, pl.ds(start, 2)]
-        edge_ref[frames:] = x_ref[:, pl.ds(start, 2)]
+    facing(pairs, prev_ref, edge_refs)
 
 
 def scales_kernel(cells, moments_ref, gain_ref, shift_ref, norm_ref):
@@ -179,8 +183,8 @@
 
 def middle_kernel(tiles, sides, *refs):
     body_ref, other_prev_ref = refs[:2]
-    rim_refs, other_rim_refs = refs[2 : 2 + sides], refs[2 + sides : 2 + 2 * sides]
-    norm_ref, weight_ref, bias_ref, hidden_ref, out_moments_ref, act_ref = refs[2 + 2 * sides :]
+    rim_refs, other_rim_refs = refs[2 : 2 + 2 * sides], refs[2 + 2 * sides : 2 + 4 * sides]
+    norm_ref, weight_ref, bias_ref, hidden_ref, out_moments_ref, act_ref = refs[2 + 4 * sides :]
     section, tm, tile = (lax.axis_index(axis) for axis in AXES)
     columns, half = rim_refs[0].shape[2:]
     frames, rows, width = body_ref.shape[0] // 2, body_ref.shape[1], body_ref.shape[2]
@@ -194,9 +198,10 @@
     for which, rims in ((section, rim_refs), (1 - section, other_rim_refs)):
         norm = tuple(norm_ref[which, k : k + 1] for k in range(3))
         lanes = pl.ds(pl.multiple_of(which * half, half), half)
-        for f in range(2 * frames):
-            for row, rim in zip(rim_rows, rims):
-                act_ref[f, pl.ds(row, 2), :, lanes] = apply_norm(rim[f, :, cols, :], norm)
+        for k, rim in enumerate(rims):
+            start, row = k // sides * frames, rim_rows[k % sides]
+            for f in range(frames):
+                act_ref[start + f, pl.ds(row, 2), :, lanes] = apply_norm(rim[f, :, cols, :], norm)
     for f in range(frames):
         act_ref[f, 2 : 2 + rows, :, lanes] = apply_norm(other_prev_ref[f], norm)
 
@@ -397,9 +402,18 @@
     moments = to_everyone(sums)
     previous, _ = lax.optimization_barrier((previous, sums))
     edges = 1 if tiles == 2 else 2
-    edge = jax.ShapeDtypeStruct((2 * frames, 2, columns, half), features.dtype)
+    edge = jax.ShapeDtypeStruct((frames, 2, columns, half), features.dtype)
     cut = jax.ShapeDtypeStruct((frames, rows, width, half), features.dtype)
-    for_x, for_previous, *edge_rows = pl.pallas_call(
+    own_edges = pl.pallas_call(
+        functools.partial(own_rows_kernel, tiles == 2),
+        out_shape=(edge,) * edges,
+        in_specs=[*vmem_specs(1), pl.BlockSpec(memory_space=pl.ANY)],
+        out_specs=tuple(vmem_specs(edges)),
+        compiler_params=params(),
+        cost_estimate=cost(0, 1_000),
+        name="own_facing_rows",
+    )(features, sums)
+    for_x, for_previous, *previous_edges = pl.pallas_call(
         functools.partial(rows_kernel, tiles == 2),
         out_shape=(cut, cut) + (edge,) * edges,
         in_specs=vmem_specs(2),
@@ -408,10 +422,14 @@
         cost_estimate=cost(500_000_000, 1_000_000),
         name="facing_rows",
     )(features, previous)
-    if tiles == 2:
-        rims = [lax.ppermute(edge_rows[0], "tile", [(0, 1), (1, 0)])]
-    else:
-        rims = [shift(edge_rows[1], 0, 1), shift(edge_rows[0], 0, -1)]
+
+    def from_neighbours(edge_rows):
+        if tiles == 2:
+            return [lax.ppermute(edge_rows[0], "tile", [(0, 1), (1, 0)])]
+        return [shift(edge_rows[1], 0, 1), shift(edge_rows[0], 0, -1)]
+
+    own_rims = from_neighbours(own_edges)
+    rims = from_neighbours(previous_edges) + own_rims
     other = swap(for_x)
     other_previous = swap(for_previous)
     norm_in = pl.pallas_call(
@@ -442,7 +460,7 @@
             jax.ShapeDtypeStruct((frames, kept, width, middle), jnp.bfloat16),
             jax.ShapeDtypeStruct((parties, 2, middle), jnp.float32),
         ),
-        in_specs=vmem_specs(5 + 2 * edges),
+        in_specs=vmem_specs(5 + 4 * edges),
         out_specs=tuple(vmem_specs(2)),
         scratch_shapes=[pltpu.VMEM((2 * frames, rows + 4, width, 2 * half), jnp.bfloat16)],
         compiler_params=params(),

time: 37.8 us -> 38.4 us (1.016)
  starting transfers between devices: 19.9 us -> 21 us
  waiting for transfers between devices: 8.76 us -> 8.29 us
    all_to_all x2, starting transfers between devices: 8.72 us -> 9.2 us  [to_everyone(): return lax.all_to_all(moments, AXES, 0, 0, tiled=True)]
    ppermute x3 -> x4, waiting for transfers between devices: 0.95 us -> 0.55 us  [swap(): return lax.ppermute(value, 'section', [(0, 1), (1, 0)])]
    ppermute x3 -> x4, starting transfers between devices: 0.58 us -> 0.89 us  [swap(): return lax.ppermute(value, 'section', [(0, 1), (1, 0)])]
    ppermute x1 -> x2, starting transfers between devices: 1.83 us -> 2.09 us  [from_neighbours(): return [lax.ppermute(edge_rows[0], 'tile', [(0, 1), (1, 0)])]]
  transfers between devices with their start and end apart: 8 -> 10, of which waited for: 3 -> 4; matrix products, arithmetic and copies ran while one was open for 0% -> 0% of each run, Pallas kernels for 10% -> 10%
where the time goes in v6:
time: 38.4 us; the launch traced here: 38.1 us
  starting transfers between devices  21 us (55%)
  Pallas kernels  8.49 us (22%)
  waiting for transfers between devices  8.29 us (22%)
    all_to_all x2, starting transfers between devices, to_everyone(): return lax.all_to_all(moments, AXES, 0, 0, tiled=True)  9.2 us
    ppermute x2, starting transfers between devices, shift(): lax.ppermute(value, grid_axes, pairs_for(tms, tiles, tm_step, tile_step))  8.79 us
    all_to_all x2, waiting for transfers between devices, to_everyone(): return lax.all_to_all(moments, AXES, 0, 0, tiled=True)  7.73 us
    pallas_call x1, Pallas kernels, shards(): pl.pallas_call(functools.partial(middle_kernel, tiles, edges), out_shape=...  3.08 us
    ppermute x2, starting transfers between devices, from_neighbours(): return [lax.ppermute(edge_rows[0], 'tile', [(0, 1), (1, 0)])]  2.09 us
    pallas_call x1, Pallas kernels, shards(): pl.pallas_call(first_kernel, out_shape=jax.ShapeDtypeStruct((parties, 2,...  1.87 us
    pallas_call x1, Pallas kernels, shards(): pl.pallas_call(functools.partial(last_kernel, tiles), out_shape=jax.Shape...  1.5 us
    pallas_call x1, Pallas kernels, shards(): pl.pallas_call(functools.partial(own_frames_kernel, tiles), out_shape=(ja...  1.09 us
  transfers between devices with their start and end apart: 10, of which 4 were waited for; matrix products, arithmetic and copies ran while one was open for 0% of the time, Pallas kernels for 10%

profile of v6, /device:TPU:0, one launch (start us, length us, event | category | flops | bytes accessed | tf_op | source)
XLA Modules:
  0.0 38.1 jit_solution(8233260691422907652)
XLA Ops:
  0.0 5.0 %collective-permute-start = (bf16[2,8,64,128]{3,2,1,0:T(8,128)(2,1)}, bf16[2,8,64,128]{3,2,1,0:T(8,128)(2,1)S(1)}, u32[]{:S(2)}, u32[]{:S(2)}) collective-permute-start(bf16[2,8,64,128]{3,2,1,0:T(8,128)(2,1)} %x_ref.7), channel_id=1, source_target_pairs={{0,2},{1,3},{2,4},{3,5},{4,6},{5,7},{6,8},{7,9},{8,10},{9,11},{10,... | collective-permute-start | bytes 786440 | tf_op jit(solution)/shard_map/ppermute | solution.py:383
  5.0 1.9 %feature_moments.1.order_ref = f32[32,2,128]{2,1,0:T(2,128)} custom-call(bf16[2,8,64,128]{3,2,1,0:T(8,128)(2,1)} %x_ref.7), custom_call_target="tpu_custom_call" | custom-call | flops 1000000000 | bytes 1000000 | tf_op jit(solution)/shard_map/feature_moments/pallas_call | solution.py:389
  6.9 0.0 copy-start.1
  6.9 0.0 copy-start.5
  6.9 0.0 copy-start.6
  6.9 4.9 %all-to-all-start = ((f32[32,2,128]{2,1,0:T(2,128)}), f32[32,2,128]{2,1,0:T(2,128)S(1)}, u32[]{:S(2)}, u32[]{:S(2)}) async-start(f32[32,2,128]{2,1,0:T(2,128)} %feature_moments.1.order_ref), calls=%async_computation | async-start | bytes 65536 | tf_op jit(solution)/shard_map/all_to_all | solution.py:357
  11.8 0.0 collective-permute-done.prev_ref
  11.8 0.0 copy-done
  11.9 0.3 collective-permute-start.1
  12.2 0.0 copy-done.1
  12.2 1.7 %collective-permute-start.3 = (bf16[2,2,64,128]{3,2,1,0:T(8,128)(2,1)S(1)}, bf16[2,2,64,128]{3,2,1,0:T(8,128)(2,1)S(1)}, u32[]{:S(2)}, u32[]{:S(2)}) collective-permute-start(bf16[2,2,64,128]{3,2,1,0:T(8,128)(2,1)S(1)} %own_facing_rows.1), channel_id=1, source_target_pairs={{0,1},{1,0},{2,3},{3,2},{4,5},{5,4},{6,7},{7,6},{8,9},{9,8},{10,11... | collective-permute-start | bytes 196616 | tf_op jit(solution)/shard_map/ppermute | solution.py:428
  14.0 0.3 collective-permute-start.2
  14.3 0.0 collective-permute-start.4
  14.3 4.7 %all-to-all-done.moments_ref = f32[32,2,128]{2,1,0:T(2,128)S(1)} async-done(((f32[32,2,128]{2,1,0:T(2,128)}), f32[32,2,128]{2,1,0:T(2,128)S(1)}, u32[]{:S(2)}, u32[]{:S(2)}) %all-to-all-start) | async-done | bytes 32800 | tf_op jit(solution)/shard_map/all_to_all | solution.py:357
  19.0 0.0 copy-done.5
  19.0 0.0 copy-done.6
  19.0 0.3 feature_scales.1.norm_ref.refs_6_
  19.4 0.0 copy-start.2
  19.4 0.0 copy-start.7
  19.4 0.0 collective-permute-done.3.refs_3_
  19.4 0.0 collective-permute-done.2.refs_2_
  19.4 0.1 collective-permute-start.5
  19.5 0.5 %collective-permute-start.6 = (bf16[2,2,64,128]{3,2,1,0:T(8,128)(2,1)S(1)}, bf16[2,2,64,128]{3,2,1,0:T(8,128)(2,1)S(1)}, u32[]{:S(2)}, u32[]{:S(2)}) collective-permute-start(bf16[2,2,64,128]{3,2,1,0:T(8,128)(2,1)S(1)} %collective-permute-done.3.refs_3_), channel_id=1, source_target_pairs={{0,16},{16,0},{1,17},{17,1},{2,18},{18,2},{3,19},{19,3},{4,20},{20... | collective-permute-start | bytes 196616 | tf_op jit(solution)/shard_map/ppermute | solution.py:386
  20.0 0.0 collective-permute-done.1.other_x_ref
  20.0 0.4 norm_body.1.refs_0_
  20.3 0.4 %collective-permute-done.5.refs_4_ = bf16[2,2,64,128]{3,2,1,0:T(8,128)(2,1)S(1)} collective-permute-done((bf16[2,2,64,128]{3,2,1,0:T(8,128)(2,1)S(1)}, bf16[2,2,64,128]{3,2,1,0:T(8,128)(2,1)S(1)}, u32[]{:S(2)}, u32[]{:S(2)}) %collective-permute-start.5) | collective-permute-done | bytes 65568 | tf_op jit(solution)/shard_map/ppermute | solution.py:386
  20.7 0.2 collective-permute-done.6.refs_5_
  20.9 0.0 collective-permute-done.4.refs_1_
  20.9 0.0 copy-done.2
  20.9 0.0 copy-done.7
  20.9 3.1 %conv_in.1 = (bf16[2,9,48,128]{3,2,1,0:T(8,128)(2,1)S(1)}, f32[32,2,128]{2,1,0:T(2,128)}) custom-call(bf16[4,8,48,256]{3,2,1,0:T(8,128)(2,1)S(1)} %norm_body.1.refs_0_, bf16[2,8,48,128]{3,2,1,0:T(8,128)(2,1)S(1)} %collective-permute-done.4.refs_1_, bf16[2,2,64,128]{3,2,1,0:T(8,128)(2,1)S(1)} %collective-permute-done.2.refs_2_, ...), custom_call_target="tpu_custom_call" | custom-call | flops 4000000000 | bytes 1000000 | tf_op jit(solution)/shard_map/conv_in/pallas_call | solution.py:457
  24.0 4.3 %all-to-all-start.1 = ((f32[32,2,128]{2,1,0:T(2,128)}), f32[32,2,128]{2,1,0:T(2,128)S(1)}, u32[]{:S(2)}, u32[]{:S(2)}) async-start(f32[32,2,128]{2,1,0:T(2,128)} %get-tuple-element.25), calls=%async_computation.1 | async-start | bytes 65536 | tf_op jit(solution)/shard_map/all_to_all | solution.py:357
  28.2 0.0 copy-start.4
  28.3 0.0 copy-start.8
  28.3 0.0 copy-start.9
  28.3 0.0 copy-start.3
  28.3 0.0 copy-start.10
  28.3 0.0 copy-start.11
  28.3 3.8 %collective-permute-start.7 = (bf16[2,10,32,128]{3,2,1,0:T(8,128)(2,1)S(1)}, bf16[2,10,32,128]{3,2,1,0:T(8,128)(2,1)S(1)}, u32[]{:S(2)}, u32[]{:S(2)}) collective-permute-start(bf16[2,10,32,128]{3,2,1,0:T(8,128)(2,1)S(1)} %pack_hidden.1), channel_id=1, source_target_pairs={{0,2},{1,3},{2,4},{3,5},{4,6},{5,7},{6,8},{7,9},{8,10},{9,11},{10,... | collective-permute-start | bytes 491528 | tf_op jit(solution)/shard_map/ppermute | solution.py:383
  32.2 0.0 copy-done.4
  32.2 0.0 copy-done.8
  32.2 0.0 copy-done.9
  32.2 0.2 shortcut.1.shortcut_ref
  32.4 3.0 %all-to-all-done.1.moments_ref = f32[32,2,128]{2,1,0:T(2,128)S(1)} async-done(((f32[32,2,128]{2,1,0:T(2,128)}), f32[32,2,128]{2,1,0:T(2,128)S(1)}, u32[]{:S(2)}, u32[]{:S(2)}) %all-to-all-start.1) | async-done | bytes 32800 | tf_op jit(solution)/shard_map/all_to_all | solution.py:357
  35.5 0.0 copy-done.10
  35.5 1.1 %conv_mid_own_frames.1 = (f32[2,8,32,128]{3,2,1,0:T(8,128)S(1)}, f32[3,128]{1,0:T(4,128)S(1)}) custom-call(bf16[2,9,48,128]{3,2,1,0:T(8,128)(2,1)S(1)} %get-tuple-element.24.hidden_ref, f32[32,2,128]{2,1,0:T(2,128)S(1)} %all-to-all-done.1.moments_ref, f32[1,128]{1,0:T(1,128)S(1)} %bitcast.12, f32[1,128]{1,0:T(1,128)S(1)} %bitcast.13, ...), custom_call_target="tpu_custom_call" | custom-call | flops 2000000000 | bytes 1000000 | tf_op jit(solution)/shard_map/conv_mid_own_frames/pallas_call | solution.py:505
  36.6 0.0 collective-permute-done.7.before_ref
  36.6 1.5 %conv_mid_previous_frames.1 = bf16[2,8,32,128]{3,2,1,0:T(8,128)(2,1)} custom-call(bf16[2,9,48,128]{3,2,1,0:T(8,128)(2,1)S(1)} %get-tuple-element.24.hidden_ref, bf16[2,10,32,128]{3,2,1,0:T(8,128)(2,1)S(1)} %collective-permute-done.7.before_ref, f32[3,128]{1,0:T(4,128)S(1)} %get-tuple-element.27.norm_ref, bf16[3,3,3,128,128]{4,3,2,1,0:T(8,128)(2,1)S(1)} %copy-done.3, ...), custom_call_target="tpu_custom_call" | custom-call | flops 2000000000 | bytes 1000000 | tf_op jit(solution)/shard_map/conv_mid_previous_frames/pallas_call | solution.py:525
  (6 shorter events, 0.1 us)
Async XLA Ops:
  0.0 11.8 %copy-start = (bf16[2,8,64,128]{3,2,1,0:T(8,128)(2,1)S(1)}, bf16[2,8,64,128]{3,2,1,0:T(8,128)(2,1)}, u32[]{:S(2)}) copy-start(bf16[2,8,64,128]{3,2,1,0:T(8,128)(2,1)} %x_ref.7) | copy-start | bytes 786436
  0.0 11.8 %collective-permute-start = (bf16[2,8,64,128]{3,2,1,0:T(8,128)(2,1)}, bf16[2,8,64,128]{3,2,1,0:T(8,128)(2,1)S(1)}, u32[]{:S(2)}, u32[]{:S(2)}) collective-permute-start(bf16[2,8,64,128]{3,2,1,0:T(8,128)(2,1)} %x_ref.7), channel_id=1, source_target_pairs={{0,2},{1,3},{2,4},{3,5},{4,6},{5,7},{6,8},{7,9},{8,10},{9,11},{10,... | collective-permute-start | bytes 786440 | tf_op jit(solution)/shard_map/ppermute | solution.py:383
  6.9 5.4 %copy-start.1 = (f32[32,2,128]{2,1,0:T(2,128)S(1)}, f32[32,2,128]{2,1,0:T(2,128)}, u32[]{:S(2)}) copy-start(f32[32,2,128]{2,1,0:T(2,128)} %feature_moments.1.order_ref) | copy-start | bytes 98308
  6.9 12.2 %copy-start.5 = (f32[256]{0:T(256)S(1)}, f32[256]{0:T(256)}, u32[]{:S(2)}) copy-start(f32[256]{0:T(256)} %param.12) | copy-start | bytes 3076
  6.9 12.2 %copy-start.6 = (f32[256]{0:T(256)S(1)}, f32[256]{0:T(256)}, u32[]{:S(2)}) copy-start(f32[256]{0:T(256)} %param.13) | copy-start | bytes 3076
  6.9 12.1 %all-to-all-start = ((f32[32,2,128]{2,1,0:T(2,128)}), f32[32,2,128]{2,1,0:T(2,128)S(1)}, u32[]{:S(2)}, u32[]{:S(2)}) async-start(f32[32,2,128]{2,1,0:T(2,128)} %feature_moments.1.order_ref), calls=%async_computation | async-start | bytes 65536 | tf_op jit(solution)/shard_map/all_to_all | solution.py:357
  11.9 8.1 %collective-permute-start.1 = (bf16[2,8,48,128]{3,2,1,0:T(8,128)(2,1)S(1)}, bf16[2,8,48,128]{3,2,1,0:T(8,128)(2,1)S(1)}, u32[]{:S(2)}, u32[]{:S(2)}) collective-permute-start(bf16[2,8,48,128]{3,2,1,0:T(8,128)(2,1)S(1)} %get-tuple-element.18), channel_id=1, source_target_pairs={{0,16},{16,0},{1,17},{17,1},{2,18},{18,2},{3,19},{19,3},{4,20},{20... | collective-permute-start | bytes 589832 | tf_op jit(solution)/shard_map/ppermute | solution.py:386
  12.2 7.2 %collective-permute-start.3 = (bf16[2,2,64,128]{3,2,1,0:T(8,128)(2,1)S(1)}, bf16[2,2,64,128]{3,2,1,0:T(8,128)(2,1)S(1)}, u32[]{:S(2)}, u32[]{:S(2)}) collective-permute-start(bf16[2,2,64,128]{3,2,1,0:T(8,128)(2,1)S(1)} %own_facing_rows.1), channel_id=1, source_target_pairs={{0,1},{1,0},{2,3},{3,2},{4,5},{5,4},{6,7},{7,6},{8,9},{9,8},{10,11... | collective-permute-start | bytes 196616 | tf_op jit(solution)/shard_map/ppermute | solution.py:428
  14.0 5.4 %collective-permute-start.2 = (bf16[2,2,64,128]{3,2,1,0:T(8,128)(2,1)S(1)}, bf16[2,2,64,128]{3,2,1,0:T(8,128)(2,1)S(1)}, u32[]{:S(2)}, u32[]{:S(2)}) collective-permute-start(bf16[2,2,64,128]{3,2,1,0:T(8,128)(2,1)S(1)} %get-tuple-element.19), channel_id=1, source_target_pairs={{0,1},{1,0},{2,3},{3,2},{4,5},{5,4},{6,7},{7,6},{8,9},{9,8},{10,11... | collective-permute-start | bytes 196616 | tf_op jit(solution)/shard_map/ppermute | solution.py:428
  14.3 6.6 %collective-permute-start.4 = (bf16[2,8,48,128]{3,2,1,0:T(8,128)(2,1)S(1)}, bf16[2,8,48,128]{3,2,1,0:T(8,128)(2,1)S(1)}, u32[]{:S(2)}, u32[]{:S(2)}) collective-permute-start(bf16[2,8,48,128]{3,2,1,0:T(8,128)(2,1)S(1)} %get-tuple-element.21), channel_id=1, source_target_pairs={{0,16},{16,0},{1,17},{17,1},{2,18},{18,2},{3,19},{19,3},{4,20},{20... | collective-permute-start | bytes 589832 | tf_op jit(solution)/shard_map/ppermute | solution.py:386
  19.4 1.5 %copy-start.2 = (bf16[3,3,3,256,128]{4,3,2,1,0:T(8,128)(2,1)S(1)}, bf16[3,3,3,256,128]{4,3,2,1,0:T(8,128)(2,1)}, u32[]{:S(2)}) copy-start(bf16[3,3,3,256,128]{4,3,2,1,0:T(8,128)(2,1)} %refs_7_.1) | copy-start | bytes 5308420
  19.4 1.5 %copy-start.7 = (f32[128]{0:T(128)S(1)}, f32[128]{0:T(128)}, u32[]{:S(2)}) copy-start(f32[128]{0:T(128)} %param.15) | copy-start | bytes 1540
  19.4 1.3 %collective-permute-start.5 = (bf16[2,2,64,128]{3,2,1,0:T(8,128)(2,1)S(1)}, bf16[2,2,64,128]{3,2,1,0:T(8,128)(2,1)S(1)}, u32[]{:S(2)}, u32[]{:S(2)}) collective-permute-start(bf16[2,2,64,128]{3,2,1,0:T(8,128)(2,1)S(1)} %collective-permute-done.2.refs_2_), channel_id=1, source_target_pairs={{0,16},{16,0},{1,17},{17,1},{2,18},{18,2},{3,19},{19,3},{4,20},{20... | collective-permute-start | bytes 196616 | tf_op jit(solution)/shard_map/ppermute | solution.py:386
  19.5 1.4 %collective-permute-start.6 = (bf16[2,2,64,128]{3,2,1,0:T(8,128)(2,1)S(1)}, bf16[2,2,64,128]{3,2,1,0:T(8,128)(2,1)S(1)}, u32[]{:S(2)}, u32[]{:S(2)}) collective-permute-start(bf16[2,2,64,128]{3,2,1,0:T(8,128)(2,1)S(1)} %collective-permute-done.3.refs_3_), channel_id=1, source_target_pairs={{0,16},{16,0},{1,17},{17,1},{2,18},{18,2},{3,19},{19,3},{4,20},{20... | collective-permute-start | bytes 196616 | tf_op jit(solution)/shard_map/ppermute | solution.py:386
  24.0 11.5 %all-to-all-start.1 = ((f32[32,2,128]{2,1,0:T(2,128)}), f32[32,2,128]{2,1,0:T(2,128)S(1)}, u32[]{:S(2)}, u32[]{:S(2)}) async-start(f32[32,2,128]{2,1,0:T(2,128)} %get-tuple-element.25), calls=%async_computation.1 | async-start | bytes 65536 | tf_op jit(solution)/shard_map/all_to_all | solution.py:357
  28.2 3.9 %copy-start.4 = (bf16[256,128]{1,0:T(8,128)(2,1)S(1)}, bf16[256,128]{1,0:T(8,128)(2,1)}, u32[]{:S(2)}) copy-start(bf16[256,128]{1,0:T(8,128)(2,1)} %skip_ref.1) | copy-start | bytes 196612
  28.3 3.9 %copy-start.8 = (f32[128]{0:T(128)S(1)}, f32[128]{0:T(128)}, u32[]{:S(2)}) copy-start(f32[128]{0:T(128)} %param.21) | copy-start | bytes 1540
  28.3 3.9 %copy-start.9 = (f32[128]{0:T(128)S(1)}, f32[128]{0:T(128)}, u32[]{:S(2)}) copy-start(f32[128]{0:T(128)} %param.19) | copy-start | bytes 1540
  28.3 7.2 %copy-start.3 = (bf16[3,3,3,128,128]{4,3,2,1,0:T(8,128)(2,1)S(1)}, bf16[3,3,3,128,128]{4,3,2,1,0:T(8,128)(2,1)}, u32[]{:S(2)}) copy-start(bf16[3,3,3,128,128]{4,3,2,1,0:T(8,128)(2,1)} %weight_ref.3) | copy-start | bytes 2654212
  28.3 7.2 %copy-start.10 = (f32[128]{0:T(128)S(1)}, f32[128]{0:T(128)}, u32[]{:S(2)}) copy-start(f32[128]{0:T(128)} %param.16) | copy-start | bytes 1540
  28.3 7.2 %copy-start.11 = (f32[128]{0:T(128)S(1)}, f32[128]{0:T(128)}, u32[]{:S(2)}) copy-start(f32[128]{0:T(128)} %param.17) | copy-start | bytes 1540
  28.3 8.2 %collective-permute-start.7 = (bf16[2,10,32,128]{3,2,1,0:T(8,128)(2,1)S(1)}, bf16[2,10,32,128]{3,2,1,0:T(8,128)(2,1)S(1)}, u32[]{:S(2)}, u32[]{:S(2)}) collective-permute-start(bf16[2,10,32,128]{3,2,1,0:T(8,128)(2,1)S(1)} %pack_hidden.1), channel_id=1, source_target_pairs={{0,2},{1,3},{2,4},{3,5},{4,6},{5,7},{6,8},{7,9},{8,10},{9,11},{10,... | collective-permute-start | bytes 491528 | tf_op jit(solution)/shard_map/ppermute | solution.py:383

commit v7 on v5

--- a/solution.py
+++ b/solution.py
@@ -72,13 +72,29 @@
     return silu((values.astype(jnp.float32) - mean) * scale + shift).astype(jnp.bfloat16)
 
 
-def first_kernel(x_hbm, moments_ref, x_ref, sem):
-    copy = pltpu.make_async_copy(x_hbm, x_ref, sem)
-    copy.start()
-    copy.wait()
-    x = x_ref[...]
-    cells = x.astype(jnp.float32).reshape(-1, x.shape[-1])
-    moments_ref[...] = jnp.broadcast_to(moments_of(cells)[None], moments_ref.shape)
+def first_kernel(x_hbm, moments_ref, x_ref, sems):
+    frames, rows = x_ref.shape[:2]
+    pieces = [(f, slice(k, k + rows // 2)) for f in range(frames) for k in (0, rows // 2)]
+    copies = [
+        pltpu.make_async_copy(x_hbm.at[f, part], x_ref.at[f, part], sems.at[k])
+        for k, (f, part) in enumerate(pieces)
+    ]
+    for copy in copies:
+        copy.start()
+    means, spreads = [], []
+    for copy, (f, part) in zip(copies, pieces):
+        copy.wait()
+        cells = x_ref[f, part].astype(jnp.float32).reshape(-1, x_ref.shape[-1])
+        mean = jnp.sum(cells, axis=0, keepdims=True) * (1.0 / cells.shape[0])
+        off = cells - mean
+        means.append(mean)
+        spreads.append(jnp.sum(off * off, axis=0, keepdims=True))
+    mean = sum(means) * (1.0 / len(pieces))
+    spread = sum(spreads)
+    for part in means:
+        spread = spread + float(cells.shape[0]) * ((part - mean) * (part - mean))
+    own = jnp.concatenate([mean, spread], axis=0)
+    moments_ref[...] = jnp.broadcast_to(own[None], moments_ref.shape)
 
 
 def rows_kernel(pairs, x_ref, prev_ref, for_x_ref, for_prev_ref, *edge_refs):
@@ -388,7 +404,7 @@
         out_specs=pl.BlockSpec(memory_space=pltpu.VMEM),
         scratch_shapes=[
             pltpu.VMEM(features.shape, features.dtype),
-            pltpu.SemaphoreType.DMA,
+            pltpu.SemaphoreType.DMA((2 * frames,)),
         ],
         compiler_params=params(FULL_LIMIT),
         cost_estimate=cost(1_000_000_000, 1_000_000),

time: 37.8 us -> 37.8 us (level)
  no operation moved by 1% of the time
where the time goes in v7:
time: 37.8 us; the launch traced here: 37.5 us
  starting transfers between devices  19.9 us (53%)
  waiting for transfers between devices  8.76 us (23%)
  Pallas kernels  8.51 us (23%)
    ppermute x2, starting transfers between devices, shift(): lax.ppermute(value, grid_axes, pairs_for(tms, tiles, tm_step, tile_step))  8.79 us
    all_to_all x2, starting transfers between devices, to_everyone(): return lax.all_to_all(moments, AXES, 0, 0, tiled=True)  8.69 us
    all_to_all x2, waiting for transfers between devices, to_everyone(): return lax.all_to_all(moments, AXES, 0, 0, tiled=True)  7.81 us
    pallas_call x1, Pallas kernels, shards(): pl.pallas_call(functools.partial(middle_kernel, tiles, edges), out_shape=...  3.07 us
    pallas_call x1, Pallas kernels, shards(): pl.pallas_call(first_kernel, out_shape=jax.ShapeDtypeStruct((parties, 2,...  1.87 us
    ppermute x1, starting transfers between devices, shards(): rims = [lax.ppermute(edge_rows[0], 'tile', [(0, 1), (1, 0)])]  1.83 us
    pallas_call x1, Pallas kernels, shards(): pl.pallas_call(functools.partial(last_kernel, tiles), out_shape=jax.Shape...  1.51 us
    pallas_call x1, Pallas kernels, shards(): pl.pallas_call(functools.partial(own_frames_kernel, tiles), out_shape=(ja...  1.1 us
  transfers between devices with their start and end apart: 8, of which 3 were waited for; matrix products, arithmetic and copies ran while one was open for 0% of the time, Pallas kernels for 10%

profile of v7, /device:TPU:0, one launch (start us, length us, event | category | flops | bytes accessed | tf_op | source)
XLA Modules:
  0.0 37.5 jit_solution(16670795906129737489)
XLA Ops:
  0.0 0.0 copy-start.2
  0.0 5.0 %collective-permute-start = (bf16[2,8,64,128]{3,2,1,0:T(8,128)(2,1)}, bf16[2,8,64,128]{3,2,1,0:T(8,128)(2,1)S(1)}, u32[]{:S(2)}, u32[]{:S(2)}) collective-permute-start(bf16[2,8,64,128]{3,2,1,0:T(8,128)(2,1)} %x_ref.5), channel_id=1, source_target_pairs={{0,2},{1,3},{2,4},{3,5},{4,6},{5,7},{6,8},{7,9},{8,10},{9,11},{10,... | collective-permute-start | bytes 786440 | tf_op jit(solution)/shard_map/ppermute | solution.py:394
  5.0 1.9 %feature_moments.1 = f32[32,2,128]{2,1,0:T(2,128)} custom-call(bf16[2,8,64,128]{3,2,1,0:T(8,128)(2,1)} %x_ref.5), custom_call_target="tpu_custom_call" | custom-call | flops 1000000000 | bytes 1000000 | tf_op jit(solution)/shard_map/feature_moments/pallas_call | solution.py:400
  6.9 0.0 copy-start.4
  6.9 0.0 copy-start.5
  6.9 4.9 %all-to-all-start = ((f32[32,2,128]{2,1,0:T(2,128)}), f32[32,2,128]{2,1,0:T(2,128)S(1)}, u32[]{:S(2)}, u32[]{:S(2)}) async-start(f32[32,2,128]{2,1,0:T(2,128)} %feature_moments.1), calls=%async_computation | async-start | bytes 65536 | tf_op jit(solution)/shard_map/all_to_all | solution.py:368
  11.8 0.0 collective-permute-done.prev_ref
  11.8 0.0 copy-done.2
  11.9 1.8 %collective-permute-start.2 = (bf16[4,2,64,128]{3,2,1,0:T(8,128)(2,1)S(1)}, bf16[4,2,64,128]{3,2,1,0:T(8,128)(2,1)S(1)}, u32[]{:S(2)}, u32[]{:S(2)}) collective-permute-start(bf16[4,2,64,128]{3,2,1,0:T(8,128)(2,1)S(1)} %get-tuple-element.18), channel_id=1, source_target_pairs={{0,1},{1,0},{2,3},{3,2},{4,5},{5,4},{6,7},{7,6},{8,9},{9,8},{10,11... | collective-permute-start | bytes 393224 | tf_op jit(solution)/shard_map/ppermute | solution.py:428
  13.7 0.0 collective-permute-start.1
  13.7 0.5 %collective-permute-start.3 = (bf16[2,8,48,128]{3,2,1,0:T(8,128)(2,1)S(1)}, bf16[2,8,48,128]{3,2,1,0:T(8,128)(2,1)S(1)}, u32[]{:S(2)}, u32[]{:S(2)}) collective-permute-start(bf16[2,8,48,128]{3,2,1,0:T(8,128)(2,1)S(1)} %get-tuple-element.20), channel_id=1, source_target_pairs={{0,16},{16,0},{1,17},{17,1},{2,18},{18,2},{3,19},{19,3},{4,20},{20... | collective-permute-start | bytes 589832 | tf_op jit(solution)/shard_map/ppermute | solution.py:397
  14.2 4.8 %all-to-all-done.moments_ref = f32[32,2,128]{2,1,0:T(2,128)S(1)} async-done(((f32[32,2,128]{2,1,0:T(2,128)}), f32[32,2,128]{2,1,0:T(2,128)S(1)}, u32[]{:S(2)}, u32[]{:S(2)}) %all-to-all-start) | async-done | bytes 32800 | tf_op jit(solution)/shard_map/all_to_all | solution.py:368
  19.0 0.0 copy-done.4
  19.0 0.0 copy-done.5
  19.0 0.3 feature_scales.1.norm_ref.refs_4_
  19.3 0.0 copy-start
  19.3 0.0 copy-start.6
  19.3 0.0 collective-permute-done.2.refs_2_
  19.3 0.1 collective-permute-start.4
  19.4 0.0 collective-permute-done.1.other_x_ref
  19.4 0.4 norm_body.1.refs_0_
  19.8 0.0 collective-permute-done.3.refs_1_
  19.8 0.9 %collective-permute-done.4.refs_3_ = bf16[4,2,64,128]{3,2,1,0:T(8,128)(2,1)S(1)} collective-permute-done((bf16[4,2,64,128]{3,2,1,0:T(8,128)(2,1)S(1)}, bf16[4,2,64,128]{3,2,1,0:T(8,128)(2,1)S(1)}, u32[]{:S(2)}, u32[]{:S(2)}) %collective-permute-start.4) | collective-permute-done | bytes 131104 | tf_op jit(solution)/shard_map/ppermute | solution.py:397
  20.8 0.0 copy-done
  20.8 0.0 copy-done.6
  20.8 3.1 %conv_in.1 = (bf16[2,9,48,128]{3,2,1,0:T(8,128)(2,1)S(1)}, f32[32,2,128]{2,1,0:T(2,128)}) custom-call(bf16[4,8,48,256]{3,2,1,0:T(8,128)(2,1)S(1)} %norm_body.1.refs_0_, bf16[2,8,48,128]{3,2,1,0:T(8,128)(2,1)S(1)} %collective-permute-done.3.refs_1_, bf16[4,2,64,128]{3,2,1,0:T(8,128)(2,1)S(1)} %collective-permute-done.2.refs_2_, ...), custom_call_target="tpu_custom_call" | custom-call | flops 4000000000 | bytes 1000000 | tf_op jit(solution)/shard_map/conv_in/pallas_call | solution.py:455
  23.9 3.8 %all-to-all-start.1 = ((f32[32,2,128]{2,1,0:T(2,128)}), f32[32,2,128]{2,1,0:T(2,128)S(1)}, u32[]{:S(2)}, u32[]{:S(2)}) async-start(f32[32,2,128]{2,1,0:T(2,128)} %get-tuple-element.23), calls=%async_computation.1 | async-start | bytes 65536 | tf_op jit(solution)/shard_map/all_to_all | solution.py:368
  27.7 0.0 copy-start.3
  27.7 0.0 copy-start.7
  27.7 0.0 copy-start.8
  27.7 0.0 copy-start.1
  27.7 0.0 copy-start.9
  27.7 0.0 copy-start.10
  27.8 3.8 %collective-permute-start.5 = (bf16[2,10,32,128]{3,2,1,0:T(8,128)(2,1)S(1)}, bf16[2,10,32,128]{3,2,1,0:T(8,128)(2,1)S(1)}, u32[]{:S(2)}, u32[]{:S(2)}) collective-permute-start(bf16[2,10,32,128]{3,2,1,0:T(8,128)(2,1)S(1)} %pack_hidden.1), channel_id=1, source_target_pairs={{0,2},{1,3},{2,4},{3,5},{4,6},{5,7},{6,8},{7,9},{8,10},{9,11},{10,... | collective-permute-start | bytes 491528 | tf_op jit(solution)/shard_map/ppermute | solution.py:394
  31.6 0.0 copy-done.3
  31.6 0.0 copy-done.7
  31.6 0.0 copy-done.8
  31.6 0.2 shortcut.1.shortcut_ref
  31.9 3.0 %all-to-all-done.1.moments_ref = f32[32,2,128]{2,1,0:T(2,128)S(1)} async-done(((f32[32,2,128]{2,1,0:T(2,128)}), f32[32,2,128]{2,1,0:T(2,128)S(1)}, u32[]{:S(2)}, u32[]{:S(2)}) %all-to-all-start.1) | async-done | bytes 32800 | tf_op jit(solution)/shard_map/all_to_all | solution.py:368
  34.9 0.0 copy-done.1
  34.9 0.0 copy-done.9
  34.9 0.0 copy-done.10
  34.9 1.1 %conv_mid_own_frames.1 = (f32[2,8,32,128]{3,2,1,0:T(8,128)S(1)}, f32[3,128]{1,0:T(4,128)S(1)}) custom-call(bf16[2,9,48,128]{3,2,1,0:T(8,128)(2,1)S(1)} %get-tuple-element.22.hidden_ref, f32[32,2,128]{2,1,0:T(2,128)S(1)} %all-to-all-done.1.moments_ref, f32[1,128]{1,0:T(1,128)S(1)} %bitcast.12, f32[1,128]{1,0:T(1,128)S(1)} %bitcast.13, ...), custom_call_target="tpu_custom_call" | custom-call | flops 2000000000 | bytes 1000000 | tf_op jit(solution)/shard_map/conv_mid_own_frames/pallas_call | solution.py:503
  36.0 0.0 collective-permute-done.5.before_ref
  36.0 1.5 %conv_mid_previous_frames.1 = bf16[2,8,32,128]{3,2,1,0:T(8,128)(2,1)} custom-call(bf16[2,9,48,128]{3,2,1,0:T(8,128)(2,1)S(1)} %get-tuple-element.22.hidden_ref, bf16[2,10,32,128]{3,2,1,0:T(8,128)(2,1)S(1)} %collective-permute-done.5.before_ref, f32[3,128]{1,0:T(4,128)S(1)} %get-tuple-element.25.norm_ref, bf16[3,3,3,128,128]{4,3,2,1,0:T(8,128)(2,1)S(1)} %copy-done.1, ...), custom_call_target="tpu_custom_call" | custom-call | flops 2000000000 | bytes 1000000 | tf_op jit(solution)/shard_map/conv_mid_previous_frames/pallas_call | solution.py:523
  (2 shorter events, 0.1 us)
Async XLA Ops:
  0.0 11.8 %copy-start.2 = (bf16[2,8,64,128]{3,2,1,0:T(8,128)(2,1)S(1)}, bf16[2,8,64,128]{3,2,1,0:T(8,128)(2,1)}, u32[]{:S(2)}) copy-start(bf16[2,8,64,128]{3,2,1,0:T(8,128)(2,1)} %x_ref.5) | copy-start | bytes 786436
  0.0 11.8 %collective-permute-start = (bf16[2,8,64,128]{3,2,1,0:T(8,128)(2,1)}, bf16[2,8,64,128]{3,2,1,0:T(8,128)(2,1)S(1)}, u32[]{:S(2)}, u32[]{:S(2)}) collective-permute-start(bf16[2,8,64,128]{3,2,1,0:T(8,128)(2,1)} %x_ref.5), channel_id=1, source_target_pairs={{0,2},{1,3},{2,4},{3,5},{4,6},{5,7},{6,8},{7,9},{8,10},{9,11},{10,... | collective-permute-start | bytes 786440 | tf_op jit(solution)/shard_map/ppermute | solution.py:394
  6.9 12.1 %copy-start.4 = (f32[256]{0:T(256)S(1)}, f32[256]{0:T(256)}, u32[]{:S(2)}) copy-start(f32[256]{0:T(256)} %param.12) | copy-start | bytes 3076
  6.9 12.1 %copy-start.5 = (f32[256]{0:T(256)S(1)}, f32[256]{0:T(256)}, u32[]{:S(2)}) copy-start(f32[256]{0:T(256)} %param.13) | copy-start | bytes 3076
  6.9 12.1 %all-to-all-start = ((f32[32,2,128]{2,1,0:T(2,128)}), f32[32,2,128]{2,1,0:T(2,128)S(1)}, u32[]{:S(2)}, u32[]{:S(2)}) async-start(f32[32,2,128]{2,1,0:T(2,128)} %feature_moments.1), calls=%async_computation | async-start | bytes 65536 | tf_op jit(solution)/shard_map/all_to_all | solution.py:368
  11.9 7.5 %collective-permute-start.2 = (bf16[4,2,64,128]{3,2,1,0:T(8,128)(2,1)S(1)}, bf16[4,2,64,128]{3,2,1,0:T(8,128)(2,1)S(1)}, u32[]{:S(2)}, u32[]{:S(2)}) collective-permute-start(bf16[4,2,64,128]{3,2,1,0:T(8,128)(2,1)S(1)} %get-tuple-element.18), channel_id=1, source_target_pairs={{0,1},{1,0},{2,3},{3,2},{4,5},{5,4},{6,7},{7,6},{8,9},{9,8},{10,11... | collective-permute-start | bytes 393224 | tf_op jit(solution)/shard_map/ppermute | solution.py:428
  13.7 5.7 %collective-permute-start.1 = (bf16[2,8,48,128]{3,2,1,0:T(8,128)(2,1)S(1)}, bf16[2,8,48,128]{3,2,1,0:T(8,128)(2,1)S(1)}, u32[]{:S(2)}, u32[]{:S(2)}) collective-permute-start(bf16[2,8,48,128]{3,2,1,0:T(8,128)(2,1)S(1)} %get-tuple-element.17), channel_id=1, source_target_pairs={{0,16},{16,0},{1,17},{17,1},{2,18},{18,2},{3,19},{19,3},{4,20},{20... | collective-permute-start | bytes 589832 | tf_op jit(solution)/shard_map/ppermute | solution.py:397
  13.7 6.1 %collective-permute-start.3 = (bf16[2,8,48,128]{3,2,1,0:T(8,128)(2,1)S(1)}, bf16[2,8,48,128]{3,2,1,0:T(8,128)(2,1)S(1)}, u32[]{:S(2)}, u32[]{:S(2)}) collective-permute-start(bf16[2,8,48,128]{3,2,1,0:T(8,128)(2,1)S(1)} %get-tuple-element.20), channel_id=1, source_target_pairs={{0,16},{16,0},{1,17},{17,1},{2,18},{18,2},{3,19},{19,3},{4,20},{20... | collective-permute-start | bytes 589832 | tf_op jit(solution)/shard_map/ppermute | solution.py:397
  19.3 1.5 %copy-start = (bf16[3,3,3,256,128]{4,3,2,1,0:T(8,128)(2,1)S(1)}, bf16[3,3,3,256,128]{4,3,2,1,0:T(8,128)(2,1)}, u32[]{:S(2)}) copy-start(bf16[3,3,3,256,128]{4,3,2,1,0:T(8,128)(2,1)} %refs_5_.1) | copy-start | bytes 5308420
  19.3 1.5 %copy-start.6 = (f32[128]{0:T(128)S(1)}, f32[128]{0:T(128)}, u32[]{:S(2)}) copy-start(f32[128]{0:T(128)} %param.15) | copy-start | bytes 1540
  19.3 1.4 %collective-permute-start.4 = (bf16[4,2,64,128]{3,2,1,0:T(8,128)(2,1)S(1)}, bf16[4,2,64,128]{3,2,1,0:T(8,128)(2,1)S(1)}, u32[]{:S(2)}, u32[]{:S(2)}) collective-permute-start(bf16[4,2,64,128]{3,2,1,0:T(8,128)(2,1)S(1)} %collective-permute-done.2.refs_2_), channel_id=1, source_target_pairs={{0,16},{16,0},{1,17},{17,1},{2,18},{18,2},{3,19},{19,3},{4,20},{20... | collective-permute-start | bytes 393224 | tf_op jit(solution)/shard_map/ppermute | solution.py:397
  23.9 11.0 %all-to-all-start.1 = ((f32[32,2,128]{2,1,0:T(2,128)}), f32[32,2,128]{2,1,0:T(2,128)S(1)}, u32[]{:S(2)}, u32[]{:S(2)}) async-start(f32[32,2,128]{2,1,0:T(2,128)} %get-tuple-element.23), calls=%async_computation.1 | async-start | bytes 65536 | tf_op jit(solution)/shard_map/all_to_all | solution.py:368
  27.7 3.9 %copy-start.3 = (bf16[256,128]{1,0:T(8,128)(2,1)S(1)}, bf16[256,128]{1,0:T(8,128)(2,1)}, u32[]{:S(2)}) copy-start(bf16[256,128]{1,0:T(8,128)(2,1)} %skip_ref.1) | copy-start | bytes 196612
  27.7 3.9 %copy-start.7 = (f32[128]{0:T(128)S(1)}, f32[128]{0:T(128)}, u32[]{:S(2)}) copy-start(f32[128]{0:T(128)} %param.21) | copy-start | bytes 1540
  27.7 3.9 %copy-start.8 = (f32[128]{0:T(128)S(1)}, f32[128]{0:T(128)}, u32[]{:S(2)}) copy-start(f32[128]{0:T(128)} %param.19) | copy-start | bytes 1540
  27.7 7.2 %copy-start.1 = (bf16[3,3,3,128,128]{4,3,2,1,0:T(8,128)(2,1)S(1)}, bf16[3,3,3,128,128]{4,3,2,1,0:T(8,128)(2,1)}, u32[]{:S(2)}) copy-start(bf16[3,3,3,128,128]{4,3,2,1,0:T(8,128)(2,1)} %weight_ref.3) | copy-start | bytes 2654212
  27.7 7.2 %copy-start.9 = (f32[128]{0:T(128)S(1)}, f32[128]{0:T(128)}, u32[]{:S(2)}) copy-start(f32[128]{0:T(128)} %param.16) | copy-start | bytes 1540
  27.7 7.2 %copy-start.10 = (f32[128]{0:T(128)S(1)}, f32[128]{0:T(128)}, u32[]{:S(2)}) copy-start(f32[128]{0:T(128)} %param.17) | copy-start | bytes 1540
  27.8 8.2 %collective-permute-start.5 = (bf16[2,10,32,128]{3,2,1,0:T(8,128)(2,1)S(1)}, bf16[2,10,32,128]{3,2,1,0:T(8,128)(2,1)S(1)}, u32[]{:S(2)}, u32[]{:S(2)}) collective-permute-start(bf16[2,10,32,128]{3,2,1,0:T(8,128)(2,1)S(1)} %pack_hidden.1), channel_id=1, source_target_pairs={{0,2},{1,3},{2,4},{3,5},{4,6},{5,7},{6,8},{7,9},{8,10},{9,11},{10,... | collective-permute-start | bytes 491528 | tf_op jit(solution)/shard_map/ppermute | solution.py:394

commit v8 on v5

--- a/solution.py
+++ b/solution.py
@@ -10,7 +10,6 @@
 GROUPS = 32
 AXES = ("section", "tm", "tile")
 VMEM_LIMIT = 48 * 1024 * 1024
-FULL_LIMIT = 63 * 1024 * 1024
 RIM = 16
 
 
@@ -55,9 +54,8 @@
     return summed[0:1] + summed[8:9] + summed[16:17]
 
 
-def scale_and_offset(moments, cells, width, gain, shift):
-    devices, _, channels = moments.shape
-    matrix = group_matrix(channels, width)
+def scale_and_offset(moments, cells, width, gain, shift, matrix):
+    devices = moments.shape[0]
     means = moments[:, 0, :]
     mean = group_sum(jnp.sum(means, axis=0, keepdims=True), matrix) * (1.0 / (devices * width))
     off = means - mean
@@ -72,10 +70,11 @@
     return silu((values.astype(jnp.float32) - mean) * scale + shift).astype(jnp.bfloat16)
 
 
-def first_kernel(x_hbm, moments_ref, x_ref, sem):
-    copy = pltpu.make_async_copy(x_hbm, x_ref, sem)
-    copy.start()
-    copy.wait()
+def matrix_kernel(width, matrix_ref):
+    matrix_ref[...] = group_matrix(matrix_ref.shape[0], width)
+
+
+def first_kernel(x_ref, order_ref, moments_ref):
     x = x_ref[...]
     cells = x.astype(jnp.float32).reshape(-1, x.shape[-1])
     moments_ref[...] = jnp.broadcast_to(moments_of(cells)[None], moments_ref.shape)
@@ -97,7 +96,7 @@
         edge_ref[frames:] = x_ref[:, pl.ds(start, 2)]
 
 
-def scales_kernel(cells, moments_ref, gain_ref, shift_ref, norm_ref):
+def scales_kernel(cells, moments_ref, gain_ref, shift_ref, matrix_ref, norm_ref):
     sections, half = gain_ref.shape
     per_section = moments_ref.shape[0] // sections
     for k in range(sections):
@@ -107,6 +106,7 @@
             sections * half // GROUPS,
             gain_ref[k : k + 1],
             shift_ref[k : k + 1],
+            matrix_ref[...],
         )
         norm_ref[k] = jnp.concatenate(norm, axis=0)
 
@@ -293,6 +293,7 @@
         outputs // GROUPS,
         gain_ref[...],
         shift_ref[...],
+        group_matrix(outputs, outputs // GROUPS),
     )
     norm_ref[...] = jnp.concatenate(norm, axis=0)
     for f in range(frames):
@@ -381,19 +382,23 @@
         return lax.ppermute(value, "section", [(0, 1), (1, 0)])
 
     previous = shift(features, 1, 0)
+    matrix = pl.pallas_call(
+        functools.partial(matrix_kernel, half * sections // GROUPS),
+        out_shape=jax.ShapeDtypeStruct((half, half), jnp.bfloat16),
+        out_specs=pl.BlockSpec(memory_space=pltpu.VMEM),
+        compiler_params=params(),
+        cost_estimate=cost(1_000_000_000, 1_000_000),
+        name="group_matrix",
+    )()
     sums = pl.pallas_call(
         first_kernel,
         out_shape=jax.ShapeDtypeStruct((parties, 2, half), jnp.float32),
-        in_specs=[pl.BlockSpec(memory_space=pl.ANY)],
+        in_specs=[*vmem_specs(1), pl.BlockSpec(memory_space=pl.ANY)],
         out_specs=pl.BlockSpec(memory_space=pltpu.VMEM),
-        scratch_shapes=[
-            pltpu.VMEM(features.shape, features.dtype),
-            pltpu.SemaphoreType.DMA,
-        ],
-        compiler_params=params(FULL_LIMIT),
+        compiler_params=params(),
         cost_estimate=cost(1_000_000_000, 1_000_000),
         name="feature_moments",
-    )(features)
+    )(features, matrix)
     moments = to_everyone(sums)
     previous, _ = lax.optimization_barrier((previous, sums))
     edges = 1 if tiles == 2 else 2
@@ -417,12 +422,12 @@
     norm_in = pl.pallas_call(
         functools.partial(scales_kernel, frames * rows * columns),
         out_shape=jax.ShapeDtypeStruct((sections, 3, half), jnp.float32),
-        in_specs=vmem_specs(3),
+        in_specs=vmem_specs(4),
         out_specs=pl.BlockSpec(memory_space=pltpu.VMEM),
         compiler_params=params(),
         cost_estimate=cost(2_000_000_000, 1_000_000),
         name="feature_scales",
-    )(moments, norm_gain_in.reshape(sections, half), norm_shift_in.reshape(sections, half))
+    )(moments, norm_gain_in.reshape(sections, half), norm_shift_in.reshape(sections, half), matrix)
     norm_in, *rims = lax.optimization_barrier((norm_in, *rims))
     other_rims = [swap(rim) for rim in rims]
 

time: 37.8 us -> 37.1 us (0.981)
  Pallas kernels: 8.51 us -> 7.55 us
    pallas_call x1, Pallas kernels: 1.87 us -> 0.91 us  [shards(): pl.pallas_call(first_kernel, out_shape=jax.ShapeDtypeStruct((parties, 2,...]
  transfers between devices with their start and end apart: 8 -> 8, of which waited for: 3 -> 3; matrix products, arithmetic and copies ran while one was open for 0% -> 0% of each run, Pallas kernels for 10% -> 8%
where the time goes in v8:
time: 37.1 us; the launch traced here: 36.8 us
  starting transfers between devices  20.2 us (54%)
  waiting for transfers between devices  8.77 us (24%)
  Pallas kernels  7.55 us (20%)
    all_to_all x2, starting transfers between devices, to_everyone(): return lax.all_to_all(moments, AXES, 0, 0, tiled=True)  8.98 us
    ppermute x2, starting transfers between devices, shift(): lax.ppermute(value, grid_axes, pairs_for(tms, tiles, tm_step, tile_step))  8.79 us
    all_to_all x2, waiting for transfers between devices, to_everyone(): return lax.all_to_all(moments, AXES, 0, 0, tiled=True)  7.81 us
    pallas_call x1, Pallas kernels, shards(): pl.pallas_call(functools.partial(middle_kernel, tiles, edges), out_shape=...  3.07 us
    ppermute x1, starting transfers between devices, shards(): rims = [lax.ppermute(edge_rows[0], 'tile', [(0, 1), (1, 0)])]  1.83 us
    pallas_call x1, Pallas kernels, shards(): pl.pallas_call(functools.partial(last_kernel, tiles), out_shape=jax.Shape...  1.5 us
    pallas_call x1, Pallas kernels, shards(): pl.pallas_call(functools.partial(own_frames_kernel, tiles), out_shape=(ja...  1.09 us
    ppermute x3, waiting for transfers between devices, swap(): return lax.ppermute(value, 'section', [(0, 1), (1, 0)])  0.95 us
  transfers between devices with their start and end apart: 8, of which 3 were waited for; matrix products, arithmetic and copies ran while one was open for 0% of the time, Pallas kernels for 8%

profile of v8, /device:TPU:0, one launch (start us, length us, event | category | flops | bytes accessed | tf_op | source)
XLA Modules:
  0.0 36.8 jit_solution(10622152430841808892)
XLA Ops:
  0.0 0.0 copy-start.2
  0.0 5.0 %collective-permute-start = (bf16[2,8,64,128]{3,2,1,0:T(8,128)(2,1)}, bf16[2,8,64,128]{3,2,1,0:T(8,128)(2,1)S(1)}, u32[]{:S(2)}, u32[]{:S(2)}) collective-permute-start(bf16[2,8,64,128]{3,2,1,0:T(8,128)(2,1)} %x_ref.7), channel_id=1, source_target_pairs={{0,2},{1,3},{2,4},{3,5},{4,6},{5,7},{6,8},{7,9},{8,10},{9,11},{10,... | collective-permute-start | bytes 786440 | tf_op jit(solution)/shard_map/ppermute | solution.py:379
  5.0 0.0 copy-done.2
  5.0 0.9 %feature_moments.1 = f32[32,2,128]{2,1,0:T(2,128)} custom-call(bf16[2,8,64,128]{3,2,1,0:T(8,128)(2,1)S(1)} %copy-done.2, bf16[128,128]{1,0:T(8,128)(2,1)S(1)} %group_matrix.1.order_ref.matrix_ref), custom_call_target="tpu_custom_call" | custom-call | flops 1000000000 | bytes 1000000 | tf_op jit(solution)/shard_map/feature_moments/pallas_call | solution.py:393
  5.9 0.0 copy-start.4
  5.9 0.0 copy-start.5
  5.9 4.9 %all-to-all-start = ((f32[32,2,128]{2,1,0:T(2,128)}), f32[32,2,128]{2,1,0:T(2,128)S(1)}, u32[]{:S(2)}, u32[]{:S(2)}) async-start(f32[32,2,128]{2,1,0:T(2,128)} %feature_moments.1), calls=%async_computation | async-start | bytes 65536 | tf_op jit(solution)/shard_map/all_to_all | solution.py:353
  10.9 0.0 collective-permute-done.prev_ref
  10.9 1.8 %collective-permute-start.2 = (bf16[4,2,64,128]{3,2,1,0:T(8,128)(2,1)S(1)}, bf16[4,2,64,128]{3,2,1,0:T(8,128)(2,1)S(1)}, u32[]{:S(2)}, u32[]{:S(2)}) collective-permute-start(bf16[4,2,64,128]{3,2,1,0:T(8,128)(2,1)S(1)} %get-tuple-element.18), channel_id=1, source_target_pairs={{0,1},{1,0},{2,3},{3,2},{4,5},{5,4},{6,7},{7,6},{8,9},{9,8},{10,11... | collective-permute-start | bytes 393224 | tf_op jit(solution)/shard_map/ppermute | solution.py:417
  12.8 0.0 collective-permute-start.1
  12.8 0.5 %collective-permute-start.3 = (bf16[2,8,48,128]{3,2,1,0:T(8,128)(2,1)S(1)}, bf16[2,8,48,128]{3,2,1,0:T(8,128)(2,1)S(1)}, u32[]{:S(2)}, u32[]{:S(2)}) collective-permute-start(bf16[2,8,48,128]{3,2,1,0:T(8,128)(2,1)S(1)} %get-tuple-element.20), channel_id=1, source_target_pairs={{0,16},{16,0},{1,17},{17,1},{2,18},{18,2},{3,19},{19,3},{4,20},{20... | collective-permute-start | bytes 589832 | tf_op jit(solution)/shard_map/ppermute | solution.py:382
  13.3 4.8 %all-to-all-done.moments_ref = f32[32,2,128]{2,1,0:T(2,128)S(1)} async-done(((f32[32,2,128]{2,1,0:T(2,128)}), f32[32,2,128]{2,1,0:T(2,128)S(1)}, u32[]{:S(2)}, u32[]{:S(2)}) %all-to-all-start) | async-done | bytes 32800 | tf_op jit(solution)/shard_map/all_to_all | solution.py:353
  18.1 0.0 copy-done.4
  18.1 0.0 copy-done.5
  18.1 0.3 feature_scales.1.norm_ref.refs_4_
  18.4 0.0 copy-start
  18.4 0.0 copy-start.6
  18.4 0.0 collective-permute-done.2.refs_2_
  18.4 0.1 collective-permute-start.4
  18.5 0.0 collective-permute-done.1.other_x_ref
  18.5 0.4 norm_body.1.refs_0_
  18.9 0.0 collective-permute-done.3.refs_1_
  18.9 0.9 %collective-permute-done.4.refs_3_ = bf16[4,2,64,128]{3,2,1,0:T(8,128)(2,1)S(1)} collective-permute-done((bf16[4,2,64,128]{3,2,1,0:T(8,128)(2,1)S(1)}, bf16[4,2,64,128]{3,2,1,0:T(8,128)(2,1)S(1)}, u32[]{:S(2)}, u32[]{:S(2)}) %collective-permute-start.4) | collective-permute-done | bytes 131104 | tf_op jit(solution)/shard_map/ppermute | solution.py:382
  19.8 0.0 copy-done
  19.9 0.0 copy-done.6
  19.9 3.1 %conv_in.1 = (bf16[2,9,48,128]{3,2,1,0:T(8,128)(2,1)S(1)}, f32[32,2,128]{2,1,0:T(2,128)}) custom-call(bf16[4,8,48,256]{3,2,1,0:T(8,128)(2,1)S(1)} %norm_body.1.refs_0_, bf16[2,8,48,128]{3,2,1,0:T(8,128)(2,1)S(1)} %collective-permute-done.3.refs_1_, bf16[4,2,64,128]{3,2,1,0:T(8,128)(2,1)S(1)} %collective-permute-done.2.refs_2_, ...), custom_call_target="tpu_custom_call" | custom-call | flops 4000000000 | bytes 1000000 | tf_op jit(solution)/shard_map/conv_in/pallas_call | solution.py:444
  22.9 4.1 %all-to-all-start.1 = ((f32[32,2,128]{2,1,0:T(2,128)}), f32[32,2,128]{2,1,0:T(2,128)S(1)}, u32[]{:S(2)}, u32[]{:S(2)}) async-start(f32[32,2,128]{2,1,0:T(2,128)} %get-tuple-element.23), calls=%async_computation.1 | async-start | bytes 65536 | tf_op jit(solution)/shard_map/all_to_all | solution.py:353
  27.0 0.0 copy-start.3
  27.0 0.0 copy-start.7
  27.0 0.0 copy-start.8
  27.0 0.0 copy-start.1
  27.1 0.0 copy-start.9
  27.1 0.0 copy-start.10
  27.1 3.8 %collective-permute-start.5 = (bf16[2,10,32,128]{3,2,1,0:T(8,128)(2,1)S(1)}, bf16[2,10,32,128]{3,2,1,0:T(8,128)(2,1)S(1)}, u32[]{:S(2)}, u32[]{:S(2)}) collective-permute-start(bf16[2,10,32,128]{3,2,1,0:T(8,128)(2,1)S(1)} %pack_hidden.1), channel_id=1, source_target_pairs={{0,2},{1,3},{2,4},{3,5},{4,6},{5,7},{6,8},{7,9},{8,10},{9,11},{10,... | collective-permute-start | bytes 491528 | tf_op jit(solution)/shard_map/ppermute | solution.py:379
  30.9 0.0 copy-done.3
  30.9 0.0 copy-done.7
  31.0 0.0 copy-done.8
  31.0 0.2 shortcut.1.shortcut_ref
  31.2 3.0 %all-to-all-done.1.moments_ref = f32[32,2,128]{2,1,0:T(2,128)S(1)} async-done(((f32[32,2,128]{2,1,0:T(2,128)}), f32[32,2,128]{2,1,0:T(2,128)S(1)}, u32[]{:S(2)}, u32[]{:S(2)}) %all-to-all-start.1) | async-done | bytes 32800 | tf_op jit(solution)/shard_map/all_to_all | solution.py:353
  34.2 0.0 copy-done.1
  34.2 0.0 copy-done.9
  34.2 0.0 copy-done.10
  34.2 1.1 %conv_mid_own_frames.1 = (f32[2,8,32,128]{3,2,1,0:T(8,128)S(1)}, f32[3,128]{1,0:T(4,128)S(1)}) custom-call(bf16[2,9,48,128]{3,2,1,0:T(8,128)(2,1)S(1)} %get-tuple-element.22.hidden_ref, f32[32,2,128]{2,1,0:T(2,128)S(1)} %all-to-all-done.1.moments_ref, f32[1,128]{1,0:T(1,128)S(1)} %bitcast.12, f32[1,128]{1,0:T(1,128)S(1)} %bitcast.13, ...), custom_call_target="tpu_custom_call" | custom-call | flops 2000000000 | bytes 1000000 | tf_op jit(solution)/shard_map/conv_mid_own_frames/pallas_call | solution.py:492
  35.3 0.0 collective-permute-done.5.before_ref
  35.3 1.5 %conv_mid_previous_frames.1 = bf16[2,8,32,128]{3,2,1,0:T(8,128)(2,1)} custom-call(bf16[2,9,48,128]{3,2,1,0:T(8,128)(2,1)S(1)} %get-tuple-element.22.hidden_ref, bf16[2,10,32,128]{3,2,1,0:T(8,128)(2,1)S(1)} %collective-permute-done.5.before_ref, f32[3,128]{1,0:T(4,128)S(1)} %get-tuple-element.25.norm_ref, bf16[3,3,3,128,128]{4,3,2,1,0:T(8,128)(2,1)S(1)} %copy-done.1, ...), custom_call_target="tpu_custom_call" | custom-call | flops 2000000000 | bytes 1000000 | tf_op jit(solution)/shard_map/conv_mid_previous_frames/pallas_call | solution.py:512
  (3 shorter events, 0.1 us)
Async XLA Ops:
  0.0 5.0 %copy-start.2 = (bf16[2,8,64,128]{3,2,1,0:T(8,128)(2,1)S(1)}, bf16[2,8,64,128]{3,2,1,0:T(8,128)(2,1)}, u32[]{:S(2)}) copy-start(bf16[2,8,64,128]{3,2,1,0:T(8,128)(2,1)} %x_ref.7) | copy-start | bytes 786436
  0.0 10.9 %collective-permute-start = (bf16[2,8,64,128]{3,2,1,0:T(8,128)(2,1)}, bf16[2,8,64,128]{3,2,1,0:T(8,128)(2,1)S(1)}, u32[]{:S(2)}, u32[]{:S(2)}) collective-permute-start(bf16[2,8,64,128]{3,2,1,0:T(8,128)(2,1)} %x_ref.7), channel_id=1, source_target_pairs={{0,2},{1,3},{2,4},{3,5},{4,6},{5,7},{6,8},{7,9},{8,10},{9,11},{10,... | collective-permute-start | bytes 786440 | tf_op jit(solution)/shard_map/ppermute | solution.py:379
  5.9 12.1 %copy-start.4 = (f32[256]{0:T(256)S(1)}, f32[256]{0:T(256)}, u32[]{:S(2)}) copy-start(f32[256]{0:T(256)} %param.12) | copy-start | bytes 3076
  5.9 12.1 %copy-start.5 = (f32[256]{0:T(256)S(1)}, f32[256]{0:T(256)}, u32[]{:S(2)}) copy-start(f32[256]{0:T(256)} %param.13) | copy-start | bytes 3076
  5.9 12.1 %all-to-all-start = ((f32[32,2,128]{2,1,0:T(2,128)}), f32[32,2,128]{2,1,0:T(2,128)S(1)}, u32[]{:S(2)}, u32[]{:S(2)}) async-start(f32[32,2,128]{2,1,0:T(2,128)} %feature_moments.1), calls=%async_computation | async-start | bytes 65536 | tf_op jit(solution)/shard_map/all_to_all | solution.py:353
  10.9 7.5 %collective-permute-start.2 = (bf16[4,2,64,128]{3,2,1,0:T(8,128)(2,1)S(1)}, bf16[4,2,64,128]{3,2,1,0:T(8,128)(2,1)S(1)}, u32[]{:S(2)}, u32[]{:S(2)}) collective-permute-start(bf16[4,2,64,128]{3,2,1,0:T(8,128)(2,1)S(1)} %get-tuple-element.18), channel_id=1, source_target_pairs={{0,1},{1,0},{2,3},{3,2},{4,5},{5,4},{6,7},{7,6},{8,9},{9,8},{10,11... | collective-permute-start | bytes 393224 | tf_op jit(solution)/shard_map/ppermute | solution.py:417
  12.8 5.7 %collective-permute-start.1 = (bf16[2,8,48,128]{3,2,1,0:T(8,128)(2,1)S(1)}, bf16[2,8,48,128]{3,2,1,0:T(8,128)(2,1)S(1)}, u32[]{:S(2)}, u32[]{:S(2)}) collective-permute-start(bf16[2,8,48,128]{3,2,1,0:T(8,128)(2,1)S(1)} %get-tuple-element.17), channel_id=1, source_target_pairs={{0,16},{16,0},{1,17},{17,1},{2,18},{18,2},{3,19},{19,3},{4,20},{20... | collective-permute-start | bytes 589832 | tf_op jit(solution)/shard_map/ppermute | solution.py:382
  12.8 6.1 %collective-permute-start.3 = (bf16[2,8,48,128]{3,2,1,0:T(8,128)(2,1)S(1)}, bf16[2,8,48,128]{3,2,1,0:T(8,128)(2,1)S(1)}, u32[]{:S(2)}, u32[]{:S(2)}) collective-permute-start(bf16[2,8,48,128]{3,2,1,0:T(8,128)(2,1)S(1)} %get-tuple-element.20), channel_id=1, source_target_pairs={{0,16},{16,0},{1,17},{17,1},{2,18},{18,2},{3,19},{19,3},{4,20},{20... | collective-permute-start | bytes 589832 | tf_op jit(solution)/shard_map/ppermute | solution.py:382
  18.4 1.5 %copy-start = (bf16[3,3,3,256,128]{4,3,2,1,0:T(8,128)(2,1)S(1)}, bf16[3,3,3,256,128]{4,3,2,1,0:T(8,128)(2,1)}, u32[]{:S(2)}) copy-start(bf16[3,3,3,256,128]{4,3,2,1,0:T(8,128)(2,1)} %refs_5_.1) | copy-start | bytes 5308420
  18.4 1.5 %copy-start.6 = (f32[128]{0:T(128)S(1)}, f32[128]{0:T(128)}, u32[]{:S(2)}) copy-start(f32[128]{0:T(128)} %param.15) | copy-start | bytes 1540
  18.4 1.4 %collective-permute-start.4 = (bf16[4,2,64,128]{3,2,1,0:T(8,128)(2,1)S(1)}, bf16[4,2,64,128]{3,2,1,0:T(8,128)(2,1)S(1)}, u32[]{:S(2)}, u32[]{:S(2)}) collective-permute-start(bf16[4,2,64,128]{3,2,1,0:T(8,128)(2,1)S(1)} %collective-permute-done.2.refs_2_), channel_id=1, source_target_pairs={{0,16},{16,0},{1,17},{17,1},{2,18},{18,2},{3,19},{19,3},{4,20},{20... | collective-permute-start | bytes 393224 | tf_op jit(solution)/shard_map/ppermute | solution.py:382
  22.9 11.3 %all-to-all-start.1 = ((f32[32,2,128]{2,1,0:T(2,128)}), f32[32,2,128]{2,1,0:T(2,128)S(1)}, u32[]{:S(2)}, u32[]{:S(2)}) async-start(f32[32,2,128]{2,1,0:T(2,128)} %get-tuple-element.23), calls=%async_computation.1 | async-start | bytes 65536 | tf_op jit(solution)/shard_map/all_to_all | solution.py:353
  27.0 3.9 %copy-start.3 = (bf16[256,128]{1,0:T(8,128)(2,1)S(1)}, bf16[256,128]{1,0:T(8,128)(2,1)}, u32[]{:S(2)}) copy-start(bf16[256,128]{1,0:T(8,128)(2,1)} %skip_ref.1) | copy-start | bytes 196612
  27.0 3.9 %copy-start.7 = (f32[128]{0:T(128)S(1)}, f32[128]{0:T(128)}, u32[]{:S(2)}) copy-start(f32[128]{0:T(128)} %param.21) | copy-start | bytes 1540
  27.0 3.9 %copy-start.8 = (f32[128]{0:T(128)S(1)}, f32[128]{0:T(128)}, u32[]{:S(2)}) copy-start(f32[128]{0:T(128)} %param.19) | copy-start | bytes 1540
  27.0 7.2 %copy-start.1 = (bf16[3,3,3,128,128]{4,3,2,1,0:T(8,128)(2,1)S(1)}, bf16[3,3,3,128,128]{4,3,2,1,0:T(8,128)(2,1)}, u32[]{:S(2)}) copy-start(bf16[3,3,3,128,128]{4,3,2,1,0:T(8,128)(2,1)} %weight_ref.3) | copy-start | bytes 2654212
  27.1 7.2 %copy-start.9 = (f32[128]{0:T(128)S(1)}, f32[128]{0:T(128)}, u32[]{:S(2)}) copy-start(f32[128]{0:T(128)} %param.16) | copy-start | bytes 1540
  27.1 7.2 %copy-start.10 = (f32[128]{0:T(128)S(1)}, f32[128]{0:T(128)}, u32[]{:S(2)}) copy-start(f32[128]{0:T(128)} %param.17) | copy-start | bytes 1540
  27.1 8.2 %collective-permute-start.5 = (bf16[2,10,32,128]{3,2,1,0:T(8,128)(2,1)S(1)}, bf16[2,10,32,128]{3,2,1,0:T(8,128)(2,1)S(1)}, u32[]{:S(2)}, u32[]{:S(2)}) collective-permute-start(bf16[2,10,32,128]{3,2,1,0:T(8,128)(2,1)S(1)} %pack_hidden.1), channel_id=1, source_target_pairs={{0,2},{1,3},{2,4},{3,5},{4,6},{5,7},{6,8},{7,9},{8,10},{9,11},{10,... | collective-permute-start | bytes 491528 | tf_op jit(solution)/shard_map/ppermute | solution.py:379

commit v9 on v8

--- a/solution.py
+++ b/solution.py
@@ -80,20 +80,26 @@
     moments_ref[...] = jnp.broadcast_to(moments_of(cells)[None], moments_ref.shape)
 
 
+def facing_rows(pairs, block_ref, frame, edge_refs):
+    rows = block_ref.shape[1]
+    starts = [(rows - 1) * (1 - lax.axis_index("tile"))] if pairs else [0, rows - 1]
+    for start, edge_ref in zip(starts, edge_refs):
+        edge_ref[frame : frame + block_ref.shape[0]] = block_ref[:, pl.ds(start, 1)]
+
+
+def rim_places(sides, rows):
+    return (0, rows + 1) if sides == 2 else ((rows + 1) * (1 - lax.axis_index("tile")),)
+
+
 def rows_kernel(pairs, x_ref, prev_ref, for_x_ref, for_prev_ref, *edge_refs):
-    frames, rows, columns = x_ref.shape[:3]
+    frames, _, columns = x_ref.shape[:3]
     width = for_x_ref.shape[2]
     start = (1 - lax.axis_index("section")) * (columns - width)
     theirs = pl.ds(pl.multiple_of(start, RIM), width)
     for_x_ref[...] = x_ref[:, :, theirs, :]
     for_prev_ref[...] = prev_ref[:, :, theirs, :]
-    if pairs:
-        starts = [(rows - 2) * (1 - lax.axis_index("tile"))]
-    else:
-        starts = [0, rows - 2]
-    for start, edge_ref in zip(starts, edge_refs):
-        edge_ref[:frames] = prev_ref[:, pl.ds(start, 2)]
-        edge_ref[frames:] = x_ref[:, pl.ds(start, 2)]
+    facing_rows(pairs, prev_ref, 0, edge_refs)
+    facing_rows(pairs, x_ref, frames, edge_refs)
 
 
 def scales_kernel(cells, moments_ref, gain_ref, shift_ref, matrix_ref, norm_ref):
@@ -124,12 +130,12 @@
     return middle + before + after
 
 
-def conv_in_rows(act_ref, weight_ref, frames, top, rows, width):
+def conv_in_rows(act_ref, weight_ref, frames, rows, width):
     totals = [None] * frames
     for a in range(act_ref.shape[0]):
         reached = [f for f in range(frames) if 0 <= a - f <= 2]
         for h in range(3):
-            cells = act_ref[a, pl.ds(top + h, rows)]
+            cells = act_ref[a, h : h + rows]
             cells = cells.reshape(rows * width, cells.shape[-1])
             taps = [column_taps(weight_ref, a - f, h) for f in reached]
             sums = jnp.dot(
@@ -155,10 +161,6 @@
         preferred_element_type=jnp.float32,
     )
     return shift_and_add(total, rows, width)
-
-
-def first_row(tiles, tile):
-    return 1 - tile if tiles == 2 else 0
 
 
 def body_kernel(x_ref, prev_ref, other_x_ref, norm_ref, body_ref):
@@ -181,59 +183,49 @@
     body_ref, other_prev_ref = refs[:2]
     rim_refs, other_rim_refs = refs[2 : 2 + sides], refs[2 + sides : 2 + 2 * sides]
     norm_ref, weight_ref, bias_ref, hidden_ref, out_moments_ref, act_ref = refs[2 + 2 * sides :]
-    section, tm, tile = (lax.axis_index(axis) for axis in AXES)
+    section, tm = lax.axis_index("section"), lax.axis_index("tm")
     columns, half = rim_refs[0].shape[2:]
     frames, rows, width = body_ref.shape[0] // 2, body_ref.shape[1], body_ref.shape[2]
-    kept = hidden_ref.shape[1]
     own = columns // 2
     first = pl.multiple_of(section * (columns - width), RIM)
     cols = pl.ds(first, width)
-    top = first_row(tiles, tile)
-    rim_rows = (0, rows + 2) if sides == 2 else ((rows + 2) * (1 - tile),)
-    act_ref[:, 2 : 2 + rows] = body_ref[...]
+    places = rim_places(sides, rows)
+    act_ref[:, 1 : 1 + rows] = body_ref[...]
     for which, rims in ((section, rim_refs), (1 - section, other_rim_refs)):
         norm = tuple(norm_ref[which, k : k + 1] for k in range(3))
         lanes = pl.ds(pl.multiple_of(which * half, half), half)
         for f in range(2 * frames):
-            for row, rim in zip(rim_rows, rims):
-                act_ref[f, pl.ds(row, 2), :, lanes] = apply_norm(rim[f, :, cols, :], norm)
-    for f in range(frames):
-        act_ref[f, 2 : 2 + rows, :, lanes] = apply_norm(other_prev_ref[f], norm)
-
-    @pl.when(tile == 0)
-    def _():
-        for f in range(2 * frames):
-            act_ref[f, 1] = act_ref[f, 2]
-
-    @pl.when(tile == tiles - 1)
-    def _():
-        for f in range(2 * frames):
-            act_ref[f, rows + 2] = act_ref[f, rows + 1]
+            for row, rim in zip(places, rims):
+                act_ref[f, pl.ds(row, 1), :, lanes] = apply_norm(rim[f, :, cols, :], norm)
+    for f in range(frames):
+        act_ref[f, 1 : 1 + rows, :, lanes] = apply_norm(other_prev_ref[f], norm)
+    repeat_edges(act_ref, 2 * frames, tiles, rows)
 
     @pl.when(tm == 0)
     def _():
         for f in range(frames):
             act_ref[f] = act_ref[frames]
 
-    for f, hidden in enumerate(conv_in_rows(act_ref, weight_ref, frames, top, kept, width)):
+    for f, hidden in enumerate(conv_in_rows(act_ref, weight_ref, frames, rows, width)):
         hidden_ref[f] = (hidden + bias_ref[...]).astype(jnp.bfloat16)
 
-    cells = hidden_ref[:, pl.ds(1 - top, rows), pl.ds(first, own), :]
+    cells = hidden_ref[:, :, pl.ds(first, own), :]
     cells = cells.astype(jnp.float32).reshape(-1, cells.shape[-1])
     out_moments_ref[...] = jnp.broadcast_to(moments_of(cells)[None], out_moments_ref.shape)
 
 
-def pack_kernel(hidden_ref, sent_ref):
+def pack_kernel(pairs, hidden_ref, sent_ref, *edge_refs):
     section = lax.axis_index("section")
-    frames, kept, width, channels = hidden_ref.shape
+    frames, rows, width, channels = hidden_ref.shape
     own = sent_ref.shape[2]
     first = pl.multiple_of(section * (width - own), RIM)
     for f in range(frames):
-        sent_ref[f, :kept] = hidden_ref[f, :, pl.ds(first, own), :]
+        sent_ref[f, :rows] = hidden_ref[f, :, pl.ds(first, own), :]
         hidden = hidden_ref[f].astype(jnp.float32)
         rim = jnp.where(section == 0, hidden[:, own, :], hidden[:, width - own - 1, :])
-        spare = jnp.zeros((own - kept, channels), jnp.float32)
-        sent_ref[f, kept] = jnp.concatenate([rim, spare], axis=0).astype(jnp.bfloat16)
+        spare = jnp.zeros((own - rows, channels), jnp.float32)
+        sent_ref[f, rows] = jnp.concatenate([rim, spare], axis=0).astype(jnp.bfloat16)
+    facing_rows(pairs, hidden_ref, 0, edge_refs)
 
 
 def repeat_edges(act_ref, count, tiles, rows):
@@ -272,21 +264,12 @@
         part_ref[f] = (shortcut + (skip_bias_ref[...] + bias_ref[...])).reshape(rows, own, -1)
 
 
-def own_frames_kernel(
-    tiles,
-    hidden_ref,
-    moments_ref,
-    gain_ref,
-    shift_ref,
-    weight_ref,
-    shortcut_ref,
-    part_ref,
-    norm_ref,
-    act_ref,
-):
-    frames, kept, width, outputs = hidden_ref.shape
-    rows, own = part_ref.shape[1:3]
-    top = first_row(tiles, lax.axis_index("tile"))
+def own_frames_kernel(tiles, sides, *refs):
+    rims, refs = refs[:sides], refs[sides:]
+    hidden_ref, moments_ref, gain_ref, shift_ref, weight_ref, shortcut_ref = refs[:6]
+    part_ref, norm_ref, act_ref = refs[6:]
+    frames, rows, width, outputs = hidden_ref.shape
+    own = part_ref.shape[2]
     norm = scale_and_offset(
         moments_ref[...],
         frames * rows * own,
@@ -297,7 +280,9 @@
     )
     norm_ref[...] = jnp.concatenate(norm, axis=0)
     for f in range(frames):
-        act_ref[f, pl.ds(top, kept)] = apply_norm(hidden_ref[f], norm)
+        act_ref[f, 1 : 1 + rows] = apply_norm(hidden_ref[f], norm)
+        for row, rim in zip(rim_places(sides, rows), rims):
+            act_ref[f, pl.ds(row, 1)] = apply_norm(rim[f], norm)
     repeat_edges(act_ref, frames, tiles, rows)
     for f in range(frames):
         taken = [(k - f + 2, k) for k in range(f - 2, f + 1) if k >= 0]
@@ -305,27 +290,32 @@
         part_ref[f] = shortcut_ref[f] + residual
 
 
-def last_kernel(
-    tiles, hidden_ref, before_ref, norm_ref, weight_ref, part_ref, out_hbm, act_ref, out_ref, sems
-):
-    section, tm, tile = (lax.axis_index(axis) for axis in AXES)
-    frames, kept, width, outputs = hidden_ref.shape
-    rows, own = part_ref.shape[1:3]
-    top = first_row(tiles, tile)
+def last_kernel(tiles, sides, *refs):
+    own_rims, rims, refs = refs[:sides], refs[sides : 2 * sides], refs[2 * sides :]
+    hidden_ref, before_ref, norm_ref, weight_ref, part_ref, out_hbm, act_ref, out_ref, sems = refs
+    section, tm = lax.axis_index("section"), lax.axis_index("tm")
+    frames, rows, width, outputs = hidden_ref.shape
+    own = part_ref.shape[2]
     first = pl.multiple_of(section * (width - own), RIM)
     beside = pl.multiple_of((1 - section) * own, RIM)
     norm = tuple(norm_ref[k : k + 1] for k in range(3))
-    for f in range(frames):
-        act_ref[f, pl.ds(top, kept), pl.ds(first, own), :] = apply_norm(before_ref[f, :kept], norm)
-        rim = apply_norm(before_ref[f, kept], norm).astype(jnp.float32)[:kept]
-        rim = jnp.broadcast_to(rim[:, None, :], (kept, width - own, outputs))
-        act_ref[f, pl.ds(top, kept), pl.ds(beside, width - own), :] = rim.astype(jnp.bfloat16)
+    places = rim_places(sides, rows)
+    for f in range(frames):
+        act_ref[f, 1 : 1 + rows, pl.ds(first, own), :] = apply_norm(before_ref[f, :rows], norm)
+        column = apply_norm(before_ref[f, rows], norm).astype(jnp.float32)[:rows]
+        column = jnp.broadcast_to(column[:, None, :], (rows, width - own, outputs))
+        act_ref[f, 1 : 1 + rows, pl.ds(beside, width - own), :] = column.astype(jnp.bfloat16)
+        for row, rim in zip(places, rims):
+            act_ref[f, pl.ds(row, 1)] = apply_norm(rim[f], norm)
 
     @pl.when(tm == 0)
     def _():
         start = apply_norm(hidden_ref[0], norm)
+        start_rims = [apply_norm(rim[0], norm) for rim in own_rims]
         for f in range(frames):
-            act_ref[f, pl.ds(top, kept)] = start
+            act_ref[f, 1 : 1 + rows] = start
+            for row, rim in zip(places, start_rims):
+                act_ref[f, pl.ds(row, 1)] = rim
 
     repeat_edges(act_ref, frames, tiles, rows)
     copies = []
@@ -402,7 +392,7 @@
     moments = to_everyone(sums)
     previous, _ = lax.optimization_barrier((previous, sums))
     edges = 1 if tiles == 2 else 2
-    edge = jax.ShapeDtypeStruct((2 * frames, 2, columns, half), features.dtype)
+    edge = jax.ShapeDtypeStruct((2 * frames, 1, columns, half), features.dtype)
     cut = jax.ShapeDtypeStruct((frames, rows, width, half), features.dtype)
     for_x, for_previous, *edge_rows = pl.pallas_call(
         functools.partial(rows_kernel, tiles == 2),
@@ -413,10 +403,13 @@
         cost_estimate=cost(500_000_000, 1_000_000),
         name="facing_rows",
     )(features, previous)
-    if tiles == 2:
-        rims = [lax.ppermute(edge_rows[0], "tile", [(0, 1), (1, 0)])]
-    else:
-        rims = [shift(edge_rows[1], 0, 1), shift(edge_rows[0], 0, -1)]
+
+    def from_neighbours(facing):
+        if tiles == 2:
+            return [lax.ppermute(facing[0], "tile", [(0, 1), (1, 0)])]
+        return [shift(facing[1], 0, 1), shift(facing[0], 0, -1)]
+
+    rims = from_neighbours(edge_rows)
     other = swap(for_x)
     other_previous = swap(for_previous)
     norm_in = pl.pallas_call(
@@ -425,13 +418,12 @@
         in_specs=vmem_specs(4),
         out_specs=pl.BlockSpec(memory_space=pltpu.VMEM),
         compiler_params=params(),
-        cost_estimate=cost(2_000_000_000, 1_000_000),
+        cost_estimate=cost(3_000_000_000, 1_000_000),
         name="feature_scales",
     )(moments, norm_gain_in.reshape(sections, half), norm_shift_in.reshape(sections, half), matrix)
     norm_in, *rims = lax.optimization_barrier((norm_in, *rims))
     other_rims = [swap(rim) for rim in rims]
 
-    kept = rows + edges
     body = pl.pallas_call(
         body_kernel,
         out_shape=jax.ShapeDtypeStruct((2 * frames, rows, width, 2 * half), jnp.bfloat16),
@@ -444,12 +436,12 @@
     hidden, moments_mid = pl.pallas_call(
         functools.partial(middle_kernel, tiles, edges),
         out_shape=(
-            jax.ShapeDtypeStruct((frames, kept, width, middle), jnp.bfloat16),
+            jax.ShapeDtypeStruct((frames, rows, width, middle), jnp.bfloat16),
             jax.ShapeDtypeStruct((parties, 2, middle), jnp.float32),
         ),
         in_specs=vmem_specs(5 + 2 * edges),
         out_specs=tuple(vmem_specs(2)),
-        scratch_shapes=[pltpu.VMEM((2 * frames, rows + 4, width, 2 * half), jnp.bfloat16)],
+        scratch_shapes=[pltpu.VMEM((2 * frames, rows + 2, width, 2 * half), jnp.bfloat16)],
         compiler_params=params(),
         cost_estimate=cost(4_000_000_000, 1_000_000),
         name="conv_in",
@@ -463,16 +455,20 @@
         conv_in_bias.reshape(1, middle),
     )
     moments_mid = to_everyone(moments_mid)
-    sent = pl.pallas_call(
-        pack_kernel,
-        out_shape=jax.ShapeDtypeStruct((frames, kept + 1, own, middle), jnp.bfloat16),
+    row = jax.ShapeDtypeStruct((frames, 1, width, middle), jnp.bfloat16)
+    sent, *facing = pl.pallas_call(
+        functools.partial(pack_kernel, tiles == 2),
+        out_shape=(jax.ShapeDtypeStruct((frames, rows + 1, own, middle), jnp.bfloat16),)
+        + (row,) * edges,
         in_specs=vmem_specs(1),
-        out_specs=pl.BlockSpec(memory_space=pltpu.VMEM),
+        out_specs=tuple(vmem_specs(1 + edges)),
         compiler_params=params(),
         cost_estimate=cost(1_000_000_000, 1_000_000),
         name="pack_hidden",
     )(hidden)
     before = shift(sent, 1, 0)
+    hidden_rims = from_neighbours(facing)
+    before_rims = [shift(rim, 1, 0) for rim in hidden_rims]
     shown, _ = lax.optimization_barrier((other, sent))
     shortcut = pl.pallas_call(
         shortcut_kernel,
@@ -490,18 +486,19 @@
         conv_mid_bias.reshape(1, outputs),
     )
     part, norm_mid = pl.pallas_call(
-        functools.partial(own_frames_kernel, tiles),
+        functools.partial(own_frames_kernel, tiles, edges),
         out_shape=(
             jax.ShapeDtypeStruct((frames, rows, own, outputs), jnp.float32),
             jax.ShapeDtypeStruct((3, middle), jnp.float32),
         ),
-        in_specs=vmem_specs(6),
+        in_specs=vmem_specs(6 + edges),
         out_specs=tuple(vmem_specs(2)),
         scratch_shapes=[pltpu.VMEM((frames, rows + 2, width, middle), jnp.bfloat16)],
         compiler_params=params(),
         cost_estimate=cost(2_000_000_000, 1_000_000),
         name="conv_mid_own_frames",
     )(
+        *hidden_rims,
         hidden,
         moments_mid,
         norm_gain_mid.reshape(1, middle),
@@ -510,9 +507,9 @@
         shortcut,
     )
     return pl.pallas_call(
-        functools.partial(last_kernel, tiles),
+        functools.partial(last_kernel, tiles, edges),
         out_shape=jax.ShapeDtypeStruct((frames, rows, own, outputs), jnp.bfloat16),
-        in_specs=vmem_specs(5),
+        in_specs=vmem_specs(5 + 2 * edges),
         out_specs=pl.BlockSpec(memory_space=pl.ANY),
         scratch_shapes=[
             pltpu.VMEM((frames, rows + 2, width, middle), jnp.bfloat16),
@@ -522,7 +519,7 @@
         compiler_params=params(),
         cost_estimate=cost(2_000_000_000, 1_000_000),
         name="conv_mid_previous_frames",
-    )(hidden, before, norm_mid, conv_mid_weight, part)
+    )(*hidden_rims, *before_rims, hidden, before, norm_mid, conv_mid_weight, part)
 
 
 def solution(mesh):

time: 37.1 us -> 40.5 us (1.092)
  starting transfers between devices: 20.2 us -> 24.3 us
  waiting for transfers between devices: 8.77 us -> 8.17 us
    ppermute x2 -> x3, starting transfers between devices: 8.79 us -> 12.1 us  [shift(): lax.ppermute(value, grid_axes, pairs_for(tms, tiles, tm_step, tile_step))]
    all_to_all x2, waiting for transfers between devices: 7.81 us -> 4.8 us  [to_everyone(): return lax.all_to_all(moments, AXES, 0, 0, tiled=True)]
    ppermute x1 -> x2, waiting for transfers between devices: 0.01 us -> 2.13 us  [from_neighbours(): return [lax.ppermute(facing[0], 'tile', [(0, 1), (1, 0)])]]
    ppermute x1 -> x2, starting transfers between devices: 1.83 us -> 3.36 us  [from_neighbours(): return [lax.ppermute(facing[0], 'tile', [(0, 1), (1, 0)])]]
    all_to_all x2, starting transfers between devices: 8.98 us -> 8.23 us  [to_everyone(): return lax.all_to_all(moments, AXES, 0, 0, tiled=True)]
  transfers between devices with their start and end apart: 8 -> 10, of which waited for: 3 -> 4; matrix products, arithmetic and copies ran while one was open for 0% -> 0% of each run, Pallas kernels for 8% -> 7%
where the time goes in v9:
time: 40.5 us; the launch traced here: 40.1 us
  starting transfers between devices  24.3 us (60%)
  waiting for transfers between devices  8.17 us (20%)
  Pallas kernels  7.21 us (18%)
    ppermute x3, starting transfers between devices, shift(): lax.ppermute(value, grid_axes, pairs_for(tms, tiles, tm_step, tile_step))  12.1 us
    all_to_all x2, starting transfers between devices, to_everyone(): return lax.all_to_all(moments, AXES, 0, 0, tiled=True)  8.23 us
    all_to_all x2, waiting for transfers between devices, to_everyone(): return lax.all_to_all(moments, AXES, 0, 0, tiled=True)  4.8 us
    ppermute x2, starting transfers between devices, from_neighbours(): return [lax.ppermute(facing[0], 'tile', [(0, 1), (1, 0)])]  3.36 us
    pallas_call x1, Pallas kernels, shards(): pl.pallas_call(functools.partial(middle_kernel, tiles, edges), out_shape=...  2.74 us
    ppermute x2, waiting for transfers between devices, from_neighbours(): return [lax.ppermute(facing[0], 'tile', [(0, 1), (1, 0)])]  2.13 us
    pallas_call x1, Pallas kernels, shards(): pl.pallas_call(functools.partial(last_kernel, tiles, edges), out_shape=ja...  1.5 us
    pallas_call x1, Pallas kernels, shards(): pl.pallas_call(functools.partial(own_frames_kernel, tiles, edges), out_sh...  1.09 us
  transfers between devices with their start and end apart: 10, of which 4 were waited for; matrix products, arithmetic and copies ran while one was open for 0% of the time, Pallas kernels for 7%

profile of v9, /device:TPU:0, one launch (start us, length us, event | category | flops | bytes accessed | tf_op | source)
XLA Modules:
  0.0 40.1 jit_solution(4447454169498952371)
XLA Ops:
  0.0 0.0 copy-start.2
  0.0 5.0 %collective-permute-start = (bf16[2,8,64,128]{3,2,1,0:T(8,128)(2,1)}, bf16[2,8,64,128]{3,2,1,0:T(8,128)(2,1)S(1)}, u32[]{:S(2)}, u32[]{:S(2)}) collective-permute-start(bf16[2,8,64,128]{3,2,1,0:T(8,128)(2,1)} %x_ref.7), channel_id=1, source_target_pairs={{0,2},{1,3},{2,4},{3,5},{4,6},{5,7},{6,8},{7,9},{8,10},{9,11},{10,... | collective-permute-start | bytes 786440 | tf_op jit(solution)/shard_map/ppermute | solution.py:369
  5.0 0.0 copy-done.2
  5.0 0.9 %feature_moments.1 = f32[32,2,128]{2,1,0:T(2,128)} custom-call(bf16[2,8,64,128]{3,2,1,0:T(8,128)(2,1)S(1)} %copy-done.2, bf16[128,128]{1,0:T(8,128)(2,1)S(1)} %group_matrix.1.order_ref.matrix_ref), custom_call_target="tpu_custom_call" | custom-call | flops 1000000000 | bytes 1000000 | tf_op jit(solution)/shard_map/feature_moments/pallas_call | solution.py:383
  5.9 0.0 copy-start.4
  5.9 4.9 %all-to-all-start = ((f32[32,2,128]{2,1,0:T(2,128)}), f32[32,2,128]{2,1,0:T(2,128)S(1)}, u32[]{:S(2)}, u32[]{:S(2)}) async-start(f32[32,2,128]{2,1,0:T(2,128)} %feature_moments.1), calls=%async_computation | async-start | bytes 65536 | tf_op jit(solution)/shard_map/all_to_all | solution.py:343
  10.9 0.0 collective-permute-done.prev_ref
  10.9 1.8 %collective-permute-start.2 = (bf16[4,1,64,128]{3,2,1,0:T(8,128)(2,1)S(1)}, bf16[4,1,64,128]{3,2,1,0:T(8,128)(2,1)S(1)}, u32[]{:S(2)}, u32[]{:S(2)}) collective-permute-start(bf16[4,1,64,128]{3,2,1,0:T(8,128)(2,1)S(1)} %get-tuple-element.20), channel_id=1, source_target_pairs={{0,1},{1,0},{2,3},{3,2},{4,5},{5,4},{6,7},{7,6},{8,9},{9,8},{10,11... | collective-permute-start | bytes 196616 | tf_op jit(solution)/shard_map/ppermute | solution.py:409
  12.7 0.0 collective-permute-start.1
  12.8 0.5 %collective-permute-start.3 = (bf16[2,8,48,128]{3,2,1,0:T(8,128)(2,1)S(1)}, bf16[2,8,48,128]{3,2,1,0:T(8,128)(2,1)S(1)}, u32[]{:S(2)}, u32[]{:S(2)}) collective-permute-start(bf16[2,8,48,128]{3,2,1,0:T(8,128)(2,1)S(1)} %get-tuple-element.22), channel_id=1, source_target_pairs={{0,16},{16,0},{1,17},{17,1},{2,18},{18,2},{3,19},{19,3},{4,20},{20... | collective-permute-start | bytes 589832 | tf_op jit(solution)/shard_map/ppermute | solution.py:372
  13.3 4.8 %all-to-all-done.moments_ref = f32[32,2,128]{2,1,0:T(2,128)S(1)} async-done(((f32[32,2,128]{2,1,0:T(2,128)}), f32[32,2,128]{2,1,0:T(2,128)S(1)}, u32[]{:S(2)}, u32[]{:S(2)}) %all-to-all-start) | async-done | bytes 32800 | tf_op jit(solution)/shard_map/all_to_all | solution.py:343
  18.1 0.0 copy-done.4
  18.1 0.0 copy-done.5
  18.1 0.3 feature_scales.1.norm_ref.refs_4_
  18.4 0.0 copy-start
  18.4 0.0 copy-start.6
  18.4 0.0 collective-permute-done.2.refs_2_
  18.4 0.1 collective-permute-start.4
  18.5 0.0 collective-permute-done.1.other_x_ref
  18.5 0.4 norm_body.1.refs_0_
  18.9 0.9 %collective-permute-done.4.refs_3_ = bf16[4,1,64,128]{3,2,1,0:T(8,128)(2,1)S(1)} collective-permute-done((bf16[4,1,64,128]{3,2,1,0:T(8,128)(2,1)S(1)}, bf16[4,1,64,128]{3,2,1,0:T(8,128)(2,1)S(1)}, u32[]{:S(2)}, u32[]{:S(2)}) %collective-permute-start.4) | collective-permute-done | bytes 65568 | tf_op jit(solution)/shard_map/ppermute | solution.py:372
  19.7 0.0 collective-permute-done.3.refs_1_
  19.7 0.1 copy-done
  19.9 0.0 copy-done.6
  19.9 2.7 %conv_in.1 = (bf16[2,8,48,128]{3,2,1,0:T(8,128)(2,1)S(1)}, f32[32,2,128]{2,1,0:T(2,128)}) custom-call(bf16[4,8,48,256]{3,2,1,0:T(8,128)(2,1)S(1)} %norm_body.1.refs_0_, bf16[2,8,48,128]{3,2,1,0:T(8,128)(2,1)S(1)} %collective-permute-done.3.refs_1_, bf16[4,1,64,128]{3,2,1,0:T(8,128)(2,1)S(1)} %collective-permute-done.2.refs_2_, ...), custom_call_target="tpu_custom_call" | custom-call | flops 4000000000 | bytes 1000000 | tf_op jit(solution)/shard_map/conv_in/pallas_call | solution.py:436
  22.6 3.3 %all-to-all-start.1 = ((f32[32,2,128]{2,1,0:T(2,128)}), f32[32,2,128]{2,1,0:T(2,128)S(1)}, u32[]{:S(2)}, u32[]{:S(2)}) async-start(f32[32,2,128]{2,1,0:T(2,128)} %get-tuple-element.27), calls=%async_computation.1 | async-start | bytes 65536 | tf_op jit(solution)/shard_map/all_to_all | solution.py:343
  25.9 0.0 copy-start.3
  25.9 0.0 copy-start.7
  25.9 0.0 copy-start.8
  26.0 0.0 copy-start.1
  26.0 0.0 copy-start.9
  26.0 0.0 copy-start.10
  26.0 3.8 %collective-permute-start.7 = (bf16[2,9,32,128]{3,2,1,0:T(8,128)(2,1)S(1)}, bf16[2,9,32,128]{3,2,1,0:T(8,128)(2,1)S(1)}, u32[]{:S(2)}, u32[]{:S(2)}) collective-permute-start(bf16[2,9,32,128]{3,2,1,0:T(8,128)(2,1)S(1)} %get-tuple-element.26), channel_id=1, source_target_pairs={{0,2},{1,3},{2,4},{3,5},{4,6},{5,7},{6,8},{7,9},{8,10},{9,11},{10,... | collective-permute-start | bytes 442376 | tf_op jit(solution)/shard_map/ppermute | solution.py:369
  29.9 1.5 %collective-permute-start.5 = (bf16[2,1,48,128]{3,2,1,0:T(8,128)(2,1)S(1)}, bf16[2,1,48,128]{3,2,1,0:T(8,128)(2,1)S(1)}, u32[]{:S(2)}, u32[]{:S(2)}) collective-permute-start(bf16[2,1,48,128]{3,2,1,0:T(8,128)(2,1)S(1)} %get-tuple-element.25), channel_id=1, source_target_pairs={{0,1},{1,0},{2,3},{3,2},{4,5},{5,4},{6,7},{7,6},{8,9},{9,8},{10,11... | collective-permute-start | bytes 73736 | tf_op jit(solution)/shard_map/ppermute | solution.py:409
  31.4 0.0 copy-done.3
  31.4 0.0 copy-done.7
  31.4 0.0 copy-done.8
  31.4 0.2 shortcut.1.refs_6_
  31.6 2.1 %collective-permute-done.5.refs_0_ = bf16[2,1,48,128]{3,2,1,0:T(8,128)(2,1)S(1)} collective-permute-done((bf16[2,1,48,128]{3,2,1,0:T(8,128)(2,1)S(1)}, bf16[2,1,48,128]{3,2,1,0:T(8,128)(2,1)S(1)}, u32[]{:S(2)}, u32[]{:S(2)}) %collective-permute-start.5) | collective-permute-done | bytes 24608 | tf_op jit(solution)/shard_map/ppermute | solution.py:409
  33.7 3.4 %collective-permute-start.6 = (bf16[2,1,48,128]{3,2,1,0:T(8,128)(2,1)S(1)}, bf16[2,1,48,128]{3,2,1,0:T(8,128)(2,1)S(1)}, u32[]{:S(2)}, u32[]{:S(2)}) collective-permute-start(bf16[2,1,48,128]{3,2,1,0:T(8,128)(2,1)S(1)} %collective-permute-done.5.refs_0_), channel_id=1, source_target_pairs={{0,2},{1,3},{2,4},{3,5},{4,6},{5,7},{6,8},{7,9},{8,10},{9,11},{10,... | collective-permute-start | bytes 73736 | tf_op jit(solution)/shard_map/ppermute | solution.py:369
  37.1 0.0 all-to-all-done.1.refs_2_
  37.1 0.0 copy-done.1
  37.1 0.0 copy-done.9
  37.1 0.0 copy-done.10
  37.1 1.1 %conv_mid_own_frames.1 = (f32[2,8,32,128]{3,2,1,0:T(8,128)S(1)}, f32[3,128]{1,0:T(4,128)S(1)}) custom-call(bf16[2,1,48,128]{3,2,1,0:T(8,128)(2,1)S(1)} %collective-permute-done.5.refs_0_, bf16[2,8,48,128]{3,2,1,0:T(8,128)(2,1)S(1)} %get-tuple-element.24.hidden_ref.refs_1_.refs_2_, f32[32,2,128]{2,1,0:T(2,128)S(1)} %all-to-all-done.1.refs_2_, ...), custom_call_target="tpu_custom_call" | custom-call | flops 2000000000 | bytes 1000000 | tf_op jit(solution)/shard_map/conv_mid_own_frames/pallas_call | solution.py:488
  38.2 0.4 collective-permute-done.6.refs_1_
  38.6 0.0 collective-permute-done.7.refs_3_
  38.6 1.5 %conv_mid_previous_frames.1 = bf16[2,8,32,128]{3,2,1,0:T(8,128)(2,1)} custom-call(bf16[2,1,48,128]{3,2,1,0:T(8,128)(2,1)S(1)} %collective-permute-done.5.refs_0_, bf16[2,1,48,128]{3,2,1,0:T(8,128)(2,1)S(1)} %collective-permute-done.6.refs_1_, bf16[2,8,48,128]{3,2,1,0:T(8,128)(2,1)S(1)} %get-tuple-element.24.hidden_ref.refs_1_.refs_2_, ...), custom_call_target="tpu_custom_call" | custom-call | flops 2000000000 | bytes 1000000 | tf_op jit(solution)/shard_map/conv_mid_previous_frames/pallas_call | solution.py:509
  (4 shorter events, 0.1 us)
Async XLA Ops:
  0.0 5.0 %copy-start.2 = (bf16[2,8,64,128]{3,2,1,0:T(8,128)(2,1)S(1)}, bf16[2,8,64,128]{3,2,1,0:T(8,128)(2,1)}, u32[]{:S(2)}) copy-start(bf16[2,8,64,128]{3,2,1,0:T(8,128)(2,1)} %x_ref.7) | copy-start | bytes 786436
  0.0 10.9 %collective-permute-start = (bf16[2,8,64,128]{3,2,1,0:T(8,128)(2,1)}, bf16[2,8,64,128]{3,2,1,0:T(8,128)(2,1)S(1)}, u32[]{:S(2)}, u32[]{:S(2)}) collective-permute-start(bf16[2,8,64,128]{3,2,1,0:T(8,128)(2,1)} %x_ref.7), channel_id=1, source_target_pairs={{0,2},{1,3},{2,4},{3,5},{4,6},{5,7},{6,8},{7,9},{8,10},{9,11},{10,... | collective-permute-start | bytes 786440 | tf_op jit(solution)/shard_map/ppermute | solution.py:369
  5.9 12.1 %copy-start.4 = (f32[256]{0:T(256)S(1)}, f32[256]{0:T(256)}, u32[]{:S(2)}) copy-start(f32[256]{0:T(256)} %param.12) | copy-start | bytes 3076
  5.9 12.1 %copy-start.5 = (f32[256]{0:T(256)S(1)}, f32[256]{0:T(256)}, u32[]{:S(2)}) copy-start(f32[256]{0:T(256)} %param.13) | copy-start | bytes 3076
  5.9 12.1 %all-to-all-start = ((f32[32,2,128]{2,1,0:T(2,128)}), f32[32,2,128]{2,1,0:T(2,128)S(1)}, u32[]{:S(2)}, u32[]{:S(2)}) async-start(f32[32,2,128]{2,1,0:T(2,128)} %feature_moments.1), calls=%async_computation | async-start | bytes 65536 | tf_op jit(solution)/shard_map/all_to_all | solution.py:343
  10.9 7.5 %collective-permute-start.2 = (bf16[4,1,64,128]{3,2,1,0:T(8,128)(2,1)S(1)}, bf16[4,1,64,128]{3,2,1,0:T(8,128)(2,1)S(1)}, u32[]{:S(2)}, u32[]{:S(2)}) collective-permute-start(bf16[4,1,64,128]{3,2,1,0:T(8,128)(2,1)S(1)} %get-tuple-element.20), channel_id=1, source_target_pairs={{0,1},{1,0},{2,3},{3,2},{4,5},{5,4},{6,7},{7,6},{8,9},{9,8},{10,11... | collective-permute-start | bytes 196616 | tf_op jit(solution)/shard_map/ppermute | solution.py:409
  12.7 5.7 %collective-permute-start.1 = (bf16[2,8,48,128]{3,2,1,0:T(8,128)(2,1)S(1)}, bf16[2,8,48,128]{3,2,1,0:T(8,128)(2,1)S(1)}, u32[]{:S(2)}, u32[]{:S(2)}) collective-permute-start(bf16[2,8,48,128]{3,2,1,0:T(8,128)(2,1)S(1)} %get-tuple-element.19), channel_id=1, source_target_pairs={{0,16},{16,0},{1,17},{17,1},{2,18},{18,2},{3,19},{19,3},{4,20},{20... | collective-permute-start | bytes 589832 | tf_op jit(solution)/shard_map/ppermute | solution.py:372
  12.8 7.0 %collective-permute-start.3 = (bf16[2,8,48,128]{3,2,1,0:T(8,128)(2,1)S(1)}, bf16[2,8,48,128]{3,2,1,0:T(8,128)(2,1)S(1)}, u32[]{:S(2)}, u32[]{:S(2)}) collective-permute-start(bf16[2,8,48,128]{3,2,1,0:T(8,128)(2,1)S(1)} %get-tuple-element.22), channel_id=1, source_target_pairs={{0,16},{16,0},{1,17},{17,1},{2,18},{18,2},{3,19},{19,3},{4,20},{20... | collective-permute-start | bytes 589832 | tf_op jit(solution)/shard_map/ppermute | solution.py:372
  18.4 1.5 %copy-start = (bf16[3,3,3,256,128]{4,3,2,1,0:T(8,128)(2,1)S(1)}, bf16[3,3,3,256,128]{4,3,2,1,0:T(8,128)(2,1)}, u32[]{:S(2)}) copy-start(bf16[3,3,3,256,128]{4,3,2,1,0:T(8,128)(2,1)} %refs_5_.3) | copy-start | bytes 5308420
  18.4 1.5 %copy-start.6 = (f32[128]{0:T(128)S(1)}, f32[128]{0:T(128)}, u32[]{:S(2)}) copy-start(f32[128]{0:T(128)} %param.15) | copy-start | bytes 1540
  18.4 1.3 %collective-permute-start.4 = (bf16[4,1,64,128]{3,2,1,0:T(8,128)(2,1)S(1)}, bf16[4,1,64,128]{3,2,1,0:T(8,128)(2,1)S(1)}, u32[]{:S(2)}, u32[]{:S(2)}) collective-permute-start(bf16[4,1,64,128]{3,2,1,0:T(8,128)(2,1)S(1)} %collective-permute-done.2.refs_2_), channel_id=1, source_target_pairs={{0,16},{16,0},{1,17},{17,1},{2,18},{18,2},{3,19},{19,3},{4,20},{20... | collective-permute-start | bytes 196616 | tf_op jit(solution)/shard_map/ppermute | solution.py:372
  22.6 14.5 %all-to-all-start.1 = ((f32[32,2,128]{2,1,0:T(2,128)}), f32[32,2,128]{2,1,0:T(2,128)S(1)}, u32[]{:S(2)}, u32[]{:S(2)}) async-start(f32[32,2,128]{2,1,0:T(2,128)} %get-tuple-element.27), calls=%async_computation.1 | async-start | bytes 65536 | tf_op jit(solution)/shard_map/all_to_all | solution.py:343
  25.9 5.5 %copy-start.3 = (bf16[256,128]{1,0:T(8,128)(2,1)S(1)}, bf16[256,128]{1,0:T(8,128)(2,1)}, u32[]{:S(2)}) copy-start(bf16[256,128]{1,0:T(8,128)(2,1)} %skip_ref.1) | copy-start | bytes 196612
  25.9 5.4 %copy-start.7 = (f32[128]{0:T(128)S(1)}, f32[128]{0:T(128)}, u32[]{:S(2)}) copy-start(f32[128]{0:T(128)} %param.21) | copy-start | bytes 1540
  25.9 5.4 %copy-start.8 = (f32[128]{0:T(128)S(1)}, f32[128]{0:T(128)}, u32[]{:S(2)}) copy-start(f32[128]{0:T(128)} %param.19) | copy-start | bytes 1540
  26.0 11.2 %copy-start.1 = (bf16[3,3,3,128,128]{4,3,2,1,0:T(8,128)(2,1)S(1)}, bf16[3,3,3,128,128]{4,3,2,1,0:T(8,128)(2,1)}, u32[]{:S(2)}) copy-start(bf16[3,3,3,128,128]{4,3,2,1,0:T(8,128)(2,1)} %refs_5_.5) | copy-start | bytes 2654212
  26.0 11.2 %copy-start.9 = (f32[128]{0:T(128)S(1)}, f32[128]{0:T(128)}, u32[]{:S(2)}) copy-start(f32[128]{0:T(128)} %param.16) | copy-start | bytes 1540
  26.0 11.2 %copy-start.10 = (f32[128]{0:T(128)S(1)}, f32[128]{0:T(128)}, u32[]{:S(2)}) copy-start(f32[128]{0:T(128)} %param.17) | copy-start | bytes 1540
  26.0 12.6 %collective-permute-start.7 = (bf16[2,9,32,128]{3,2,1,0:T(8,128)(2,1)S(1)}, bf16[2,9,32,128]{3,2,1,0:T(8,128)(2,1)S(1)}, u32[]{:S(2)}, u32[]{:S(2)}) collective-permute-start(bf16[2,9,32,128]{3,2,1,0:T(8,128)(2,1)S(1)} %get-tuple-element.26), channel_id=1, source_target_pairs={{0,2},{1,3},{2,4},{3,5},{4,6},{5,7},{6,8},{7,9},{8,10},{9,11},{10,... | collective-permute-start | bytes 442376 | tf_op jit(solution)/shard_map/ppermute | solution.py:369
  29.9 3.9 %collective-permute-start.5 = (bf16[2,1,48,128]{3,2,1,0:T(8,128)(2,1)S(1)}, bf16[2,1,48,128]{3,2,1,0:T(8,128)(2,1)S(1)}, u32[]{:S(2)}, u32[]{:S(2)}) collective-permute-start(bf16[2,1,48,128]{3,2,1,0:T(8,128)(2,1)S(1)} %get-tuple-element.25), channel_id=1, source_target_pairs={{0,1},{1,0},{2,3},{3,2},{4,5},{5,4},{6,7},{7,6},{8,9},{9,8},{10,11... | collective-permute-start | bytes 73736 | tf_op jit(solution)/shard_map/ppermute | solution.py:409
  33.7 4.9 %collective-permute-start.6 = (bf16[2,1,48,128]{3,2,1,0:T(8,128)(2,1)S(1)}, bf16[2,1,48,128]{3,2,1,0:T(8,128)(2,1)S(1)}, u32[]{:S(2)}, u32[]{:S(2)}) collective-permute-start(bf16[2,1,48,128]{3,2,1,0:T(8,128)(2,1)S(1)} %collective-permute-done.5.refs_0_), channel_id=1, source_target_pairs={{0,2},{1,3},{2,4},{3,5},{4,6},{5,7},{6,8},{7,9},{8,10},{9,11},{10,... | collective-permute-start | bytes 73736 | tf_op jit(solution)/shard_map/ppermute | solution.py:369

commit v10 on v8

--- a/solution.py
+++ b/solution.py
@@ -180,11 +180,11 @@
 def middle_kernel(tiles, sides, *refs):
     body_ref, other_prev_ref = refs[:2]
     rim_refs, other_rim_refs = refs[2 : 2 + sides], refs[2 + sides : 2 + 2 * sides]
-    norm_ref, weight_ref, bias_ref, hidden_ref, out_moments_ref, act_ref = refs[2 + 2 * sides :]
+    norm_ref, weight_ref, bias_ref, hidden_ref, out_moments_hbm = refs[2 + 2 * sides :][:5]
+    act_ref, out_moments_ref, sem = refs[-3:]
     section, tm, tile = (lax.axis_index(axis) for axis in AXES)
     columns, half = rim_refs[0].shape[2:]
     frames, rows, width = body_ref.shape[0] // 2, body_ref.shape[1], body_ref.shape[2]
-    kept = hidden_ref.shape[1]
     own = columns // 2
     first = pl.multiple_of(section * (columns - width), RIM)
     cols = pl.ds(first, width)
@@ -215,12 +215,23 @@
         for f in range(frames):
             act_ref[f] = act_ref[frames]
 
-    for f, hidden in enumerate(conv_in_rows(act_ref, weight_ref, frames, top, kept, width)):
-        hidden_ref[f] = (hidden + bias_ref[...]).astype(jnp.bfloat16)
-
+    def hidden_rows(start, count, at):
+        sums = conv_in_rows(act_ref, weight_ref, frames, start, count, width)
+        for f, hidden in enumerate(sums):
+            hidden_ref[f, pl.ds(at, count)] = (hidden + bias_ref[...]).astype(jnp.bfloat16)
+
+    hidden_rows(1, rows, 1 - top)
     cells = hidden_ref[:, pl.ds(1 - top, rows), pl.ds(first, own), :]
     cells = cells.astype(jnp.float32).reshape(-1, cells.shape[-1])
     out_moments_ref[...] = jnp.broadcast_to(moments_of(cells)[None], out_moments_ref.shape)
+    copy = pltpu.make_async_copy(out_moments_ref, out_moments_hbm, sem)
+    copy.start()
+    if sides == 2:
+        hidden_rows(0, 1, 0)
+        hidden_rows(rows + 1, 1, rows + 1)
+    else:
+        hidden_rows((rows + 1) * (1 - tile), 1, rows * (1 - tile))
+    copy.wait()
 
 
 def pack_kernel(hidden_ref, sent_ref):
@@ -315,11 +326,13 @@
     first = pl.multiple_of(section * (width - own), RIM)
     beside = pl.multiple_of((1 - section) * own, RIM)
     norm = tuple(norm_ref[k : k + 1] for k in range(3))
-    for f in range(frames):
-        act_ref[f, pl.ds(top, kept), pl.ds(first, own), :] = apply_norm(before_ref[f, :kept], norm)
-        rim = apply_norm(before_ref[f, kept], norm).astype(jnp.float32)[:kept]
-        rim = jnp.broadcast_to(rim[:, None, :], (kept, width - own, outputs))
-        act_ref[f, pl.ds(top, kept), pl.ds(beside, width - own), :] = rim.astype(jnp.bfloat16)
+    @pl.when(tm > 0)
+    def _():
+        for f in range(frames):
+            act_ref[f, pl.ds(top, kept), pl.ds(first, own), :] = apply_norm(before_ref[f, :kept], norm)
+            rim = apply_norm(before_ref[f, kept], norm).astype(jnp.float32)[:kept]
+            rim = jnp.broadcast_to(rim[:, None, :], (kept, width - own, outputs))
+            act_ref[f, pl.ds(top, kept), pl.ds(beside, width - own), :] = rim.astype(jnp.bfloat16)
 
     @pl.when(tm == 0)
     def _():
@@ -448,8 +461,12 @@
             jax.ShapeDtypeStruct((parties, 2, middle), jnp.float32),
         ),
         in_specs=vmem_specs(5 + 2 * edges),
-        out_specs=tuple(vmem_specs(2)),
-        scratch_shapes=[pltpu.VMEM((2 * frames, rows + 4, width, 2 * half), jnp.bfloat16)],
+        out_specs=(*vmem_specs(1), pl.BlockSpec(memory_space=pl.ANY)),
+        scratch_shapes=[
+            pltpu.VMEM((2 * frames, rows + 4, width, 2 * half), jnp.bfloat16),
+            pltpu.VMEM((parties, 2, middle), jnp.float32),
+            pltpu.SemaphoreType.DMA,
+        ],
         compiler_params=params(),
         cost_estimate=cost(4_000_000_000, 1_000_000),
         name="conv_in",

time: 37.1 us -> 36.9 us (level)
  no operation moved by 1% of the time
where the time goes in v10:
time: 36.9 us; the launch traced here: 36.7 us
  starting transfers between devices  20.2 us (55%)
  waiting for transfers between devices  8.77 us (24%)
  Pallas kernels  7.35 us (20%)
    all_to_all x2, starting transfers between devices, to_everyone(): return lax.all_to_all(moments, AXES, 0, 0, tiled=True)  9.01 us
    ppermute x2, starting transfers between devices, shift(): lax.ppermute(value, grid_axes, pairs_for(tms, tiles, tm_step, tile_step))  8.79 us
    all_to_all x2, waiting for transfers between devices, to_everyone(): return lax.all_to_all(moments, AXES, 0, 0, tiled=True)  7.81 us
    pallas_call x1, Pallas kernels, shards(): pl.pallas_call(functools.partial(middle_kernel, tiles, edges), out_shape=...  2.94 us
    ppermute x1, starting transfers between devices, shards(): rims = [lax.ppermute(edge_rows[0], 'tile', [(0, 1), (1, 0)])]  1.83 us
    pallas_call x1, Pallas kernels, shards(): pl.pallas_call(functools.partial(last_kernel, tiles), out_shape=jax.Shape...  1.42 us
    pallas_call x1, Pallas kernels, shards(): pl.pallas_call(functools.partial(own_frames_kernel, tiles), out_shape=(ja...  1.09 us
    ppermute x3, waiting for transfers between devices, swap(): return lax.ppermute(value, 'section', [(0, 1), (1, 0)])  0.95 us
  transfers between devices with their start and end apart: 8, of which 3 were waited for; matrix products, arithmetic and copies ran while one was open for 0% of the time, Pallas kernels for 8%

profile of v10, /device:TPU:0, one launch (start us, length us, event | category | flops | bytes accessed | tf_op | source)
XLA Modules:
  0.0 36.7 jit_solution(16579943968859065491)
XLA Ops:
  0.0 0.0 copy-start.2
  0.0 5.0 %collective-permute-start = (bf16[2,8,64,128]{3,2,1,0:T(8,128)(2,1)}, bf16[2,8,64,128]{3,2,1,0:T(8,128)(2,1)S(1)}, u32[]{:S(2)}, u32[]{:S(2)}) collective-permute-start(bf16[2,8,64,128]{3,2,1,0:T(8,128)(2,1)} %x_ref.7), channel_id=1, source_target_pairs={{0,2},{1,3},{2,4},{3,5},{4,6},{5,7},{6,8},{7,9},{8,10},{9,11},{10,... | collective-permute-start | bytes 786440 | tf_op jit(solution)/shard_map/ppermute | solution.py:392
  5.0 0.0 copy-done.2
  5.0 0.9 %feature_moments.1 = f32[32,2,128]{2,1,0:T(2,128)} custom-call(bf16[2,8,64,128]{3,2,1,0:T(8,128)(2,1)S(1)} %copy-done.2, bf16[128,128]{1,0:T(8,128)(2,1)S(1)} %group_matrix.1.order_ref.matrix_ref), custom_call_target="tpu_custom_call" | custom-call | flops 1000000000 | bytes 1000000 | tf_op jit(solution)/shard_map/feature_moments/pallas_call | solution.py:406
  5.9 0.0 copy-start.4
  5.9 0.0 copy-start.5
  5.9 4.9 %all-to-all-start = ((f32[32,2,128]{2,1,0:T(2,128)}), f32[32,2,128]{2,1,0:T(2,128)S(1)}, u32[]{:S(2)}, u32[]{:S(2)}) async-start(f32[32,2,128]{2,1,0:T(2,128)} %feature_moments.1), calls=%async_computation | async-start | bytes 65536 | tf_op jit(solution)/shard_map/all_to_all | solution.py:366
  10.9 0.0 collective-permute-done.prev_ref
  10.9 1.8 %collective-permute-start.2 = (bf16[4,2,64,128]{3,2,1,0:T(8,128)(2,1)S(1)}, bf16[4,2,64,128]{3,2,1,0:T(8,128)(2,1)S(1)}, u32[]{:S(2)}, u32[]{:S(2)}) collective-permute-start(bf16[4,2,64,128]{3,2,1,0:T(8,128)(2,1)S(1)} %get-tuple-element.18), channel_id=1, source_target_pairs={{0,1},{1,0},{2,3},{3,2},{4,5},{5,4},{6,7},{7,6},{8,9},{9,8},{10,11... | collective-permute-start | bytes 393224 | tf_op jit(solution)/shard_map/ppermute | solution.py:430
  12.8 0.0 collective-permute-start.1
  12.8 0.5 %collective-permute-start.3 = (bf16[2,8,48,128]{3,2,1,0:T(8,128)(2,1)S(1)}, bf16[2,8,48,128]{3,2,1,0:T(8,128)(2,1)S(1)}, u32[]{:S(2)}, u32[]{:S(2)}) collective-permute-start(bf16[2,8,48,128]{3,2,1,0:T(8,128)(2,1)S(1)} %get-tuple-element.20), channel_id=1, source_target_pairs={{0,16},{16,0},{1,17},{17,1},{2,18},{18,2},{3,19},{19,3},{4,20},{20... | collective-permute-start | bytes 589832 | tf_op jit(solution)/shard_map/ppermute | solution.py:395
  13.3 4.8 %all-to-all-done.moments_ref = f32[32,2,128]{2,1,0:T(2,128)S(1)} async-done(((f32[32,2,128]{2,1,0:T(2,128)}), f32[32,2,128]{2,1,0:T(2,128)S(1)}, u32[]{:S(2)}, u32[]{:S(2)}) %all-to-all-start) | async-done | bytes 32800 | tf_op jit(solution)/shard_map/all_to_all | solution.py:366
  18.1 0.0 copy-done.4
  18.1 0.0 copy-done.5
  18.1 0.3 feature_scales.1.norm_ref.refs_4_
  18.4 0.0 copy-start
  18.4 0.0 copy-start.6
  18.4 0.0 collective-permute-done.2.refs_2_
  18.4 0.1 collective-permute-start.4
  18.5 0.0 collective-permute-done.1.other_x_ref
  18.5 0.4 norm_body.1.refs_0_
  18.9 0.0 collective-permute-done.3.refs_1_
  18.9 0.9 %collective-permute-done.4.refs_3_ = bf16[4,2,64,128]{3,2,1,0:T(8,128)(2,1)S(1)} collective-permute-done((bf16[4,2,64,128]{3,2,1,0:T(8,128)(2,1)S(1)}, bf16[4,2,64,128]{3,2,1,0:T(8,128)(2,1)S(1)}, u32[]{:S(2)}, u32[]{:S(2)}) %collective-permute-start.4) | collective-permute-done | bytes 131104 | tf_op jit(solution)/shard_map/ppermute | solution.py:395
  19.8 0.0 copy-done
  19.9 0.0 copy-done.6
  19.9 2.9 %conv_in.1 = (bf16[2,9,48,128]{3,2,1,0:T(8,128)(2,1)S(1)}, f32[32,2,128]{2,1,0:T(2,128)}) custom-call(bf16[4,8,48,256]{3,2,1,0:T(8,128)(2,1)S(1)} %norm_body.1.refs_0_, bf16[2,8,48,128]{3,2,1,0:T(8,128)(2,1)S(1)} %collective-permute-done.3.refs_1_, bf16[4,2,64,128]{3,2,1,0:T(8,128)(2,1)S(1)} %collective-permute-done.2.refs_2_, ...), custom_call_target="tpu_custom_call" | custom-call | flops 4000000000 | bytes 1000000 | tf_op jit(solution)/shard_map/conv_in/pallas_call | solution.py:457
  22.8 4.1 %all-to-all-start.1 = ((f32[32,2,128]{2,1,0:T(2,128)}), f32[32,2,128]{2,1,0:T(2,128)S(1)}, u32[]{:S(2)}, u32[]{:S(2)}) async-start(f32[32,2,128]{2,1,0:T(2,128)} %get-tuple-element.23), calls=%async_computation.1 | async-start | bytes 65536 | tf_op jit(solution)/shard_map/all_to_all | solution.py:366
  26.9 0.0 copy-start.3
  26.9 0.0 copy-start.7
  26.9 0.0 copy-start.8
  26.9 0.0 copy-start.1
  27.0 0.0 copy-start.9
  27.0 0.0 copy-start.10
  27.0 3.8 %collective-permute-start.5 = (bf16[2,10,32,128]{3,2,1,0:T(8,128)(2,1)S(1)}, bf16[2,10,32,128]{3,2,1,0:T(8,128)(2,1)S(1)}, u32[]{:S(2)}, u32[]{:S(2)}) collective-permute-start(bf16[2,10,32,128]{3,2,1,0:T(8,128)(2,1)S(1)} %pack_hidden.1), channel_id=1, source_target_pairs={{0,2},{1,3},{2,4},{3,5},{4,6},{5,7},{6,8},{7,9},{8,10},{9,11},{10,... | collective-permute-start | bytes 491528 | tf_op jit(solution)/shard_map/ppermute | solution.py:392
  30.8 0.0 copy-done.3
  30.9 0.0 copy-done.7
  30.9 0.0 copy-done.8
  30.9 0.2 shortcut.1.shortcut_ref
  31.1 3.0 %all-to-all-done.1.moments_ref = f32[32,2,128]{2,1,0:T(2,128)S(1)} async-done(((f32[32,2,128]{2,1,0:T(2,128)}), f32[32,2,128]{2,1,0:T(2,128)S(1)}, u32[]{:S(2)}, u32[]{:S(2)}) %all-to-all-start.1) | async-done | bytes 32800 | tf_op jit(solution)/shard_map/all_to_all | solution.py:366
  34.1 0.0 copy-done.1
  34.1 0.0 copy-done.9
  34.1 0.0 copy-done.10
  34.1 1.1 %conv_mid_own_frames.1 = (f32[2,8,32,128]{3,2,1,0:T(8,128)S(1)}, f32[3,128]{1,0:T(4,128)S(1)}) custom-call(bf16[2,9,48,128]{3,2,1,0:T(8,128)(2,1)S(1)} %get-tuple-element.22.hidden_ref, f32[32,2,128]{2,1,0:T(2,128)S(1)} %all-to-all-done.1.moments_ref, f32[1,128]{1,0:T(1,128)S(1)} %bitcast.12, f32[1,128]{1,0:T(1,128)S(1)} %bitcast.13, ...), custom_call_target="tpu_custom_call" | custom-call | flops 2000000000 | bytes 1000000 | tf_op jit(solution)/shard_map/conv_mid_own_frames/pallas_call | solution.py:509
  35.2 0.0 collective-permute-done.5.before_ref
  35.2 1.4 %conv_mid_previous_frames.1 = bf16[2,8,32,128]{3,2,1,0:T(8,128)(2,1)} custom-call(bf16[2,9,48,128]{3,2,1,0:T(8,128)(2,1)S(1)} %get-tuple-element.22.hidden_ref, bf16[2,10,32,128]{3,2,1,0:T(8,128)(2,1)S(1)} %collective-permute-done.5.before_ref, f32[3,128]{1,0:T(4,128)S(1)} %get-tuple-element.25.norm_ref, bf16[3,3,3,128,128]{4,3,2,1,0:T(8,128)(2,1)S(1)} %copy-done.1, ...), custom_call_target="tpu_custom_call" | custom-call | flops 2000000000 | bytes 1000000 | tf_op jit(solution)/shard_map/conv_mid_previous_frames/pallas_call | solution.py:529
  (3 shorter events, 0.1 us)
Async XLA Ops:
  0.0 5.0 %copy-start.2 = (bf16[2,8,64,128]{3,2,1,0:T(8,128)(2,1)S(1)}, bf16[2,8,64,128]{3,2,1,0:T(8,128)(2,1)}, u32[]{:S(2)}) copy-start(bf16[2,8,64,128]{3,2,1,0:T(8,128)(2,1)} %x_ref.7) | copy-start | bytes 786436
  0.0 10.9 %collective-permute-start = (bf16[2,8,64,128]{3,2,1,0:T(8,128)(2,1)}, bf16[2,8,64,128]{3,2,1,0:T(8,128)(2,1)S(1)}, u32[]{:S(2)}, u32[]{:S(2)}) collective-permute-start(bf16[2,8,64,128]{3,2,1,0:T(8,128)(2,1)} %x_ref.7), channel_id=1, source_target_pairs={{0,2},{1,3},{2,4},{3,5},{4,6},{5,7},{6,8},{7,9},{8,10},{9,11},{10,... | collective-permute-start | bytes 786440 | tf_op jit(solution)/shard_map/ppermute | solution.py:392
  5.9 12.1 %copy-start.4 = (f32[256]{0:T(256)S(1)}, f32[256]{0:T(256)}, u32[]{:S(2)}) copy-start(f32[256]{0:T(256)} %param.12) | copy-start | bytes 3076
  5.9 12.1 %copy-start.5 = (f32[256]{0:T(256)S(1)}, f32[256]{0:T(256)}, u32[]{:S(2)}) copy-start(f32[256]{0:T(256)} %param.13) | copy-start | bytes 3076
  5.9 12.1 %all-to-all-start = ((f32[32,2,128]{2,1,0:T(2,128)}), f32[32,2,128]{2,1,0:T(2,128)S(1)}, u32[]{:S(2)}, u32[]{:S(2)}) async-start(f32[32,2,128]{2,1,0:T(2,128)} %feature_moments.1), calls=%async_computation | async-start | bytes 65536 | tf_op jit(solution)/shard_map/all_to_all | solution.py:366
  10.9 7.5 %collective-permute-start.2 = (bf16[4,2,64,128]{3,2,1,0:T(8,128)(2,1)S(1)}, bf16[4,2,64,128]{3,2,1,0:T(8,128)(2,1)S(1)}, u32[]{:S(2)}, u32[]{:S(2)}) collective-permute-start(bf16[4,2,64,128]{3,2,1,0:T(8,128)(2,1)S(1)} %get-tuple-element.18), channel_id=1, source_target_pairs={{0,1},{1,0},{2,3},{3,2},{4,5},{5,4},{6,7},{7,6},{8,9},{9,8},{10,11... | collective-permute-start | bytes 393224 | tf_op jit(solution)/shard_map/ppermute | solution.py:430
  12.8 5.7 %collective-permute-start.1 = (bf16[2,8,48,128]{3,2,1,0:T(8,128)(2,1)S(1)}, bf16[2,8,48,128]{3,2,1,0:T(8,128)(2,1)S(1)}, u32[]{:S(2)}, u32[]{:S(2)}) collective-permute-start(bf16[2,8,48,128]{3,2,1,0:T(8,128)(2,1)S(1)} %get-tuple-element.17), channel_id=1, source_target_pairs={{0,16},{16,0},{1,17},{17,1},{2,18},{18,2},{3,19},{19,3},{4,20},{20... | collective-permute-start | bytes 589832 | tf_op jit(solution)/shard_map/ppermute | solution.py:395
  12.8 6.1 %collective-permute-start.3 = (bf16[2,8,48,128]{3,2,1,0:T(8,128)(2,1)S(1)}, bf16[2,8,48,128]{3,2,1,0:T(8,128)(2,1)S(1)}, u32[]{:S(2)}, u32[]{:S(2)}) collective-permute-start(bf16[2,8,48,128]{3,2,1,0:T(8,128)(2,1)S(1)} %get-tuple-element.20), channel_id=1, source_target_pairs={{0,16},{16,0},{1,17},{17,1},{2,18},{18,2},{3,19},{19,3},{4,20},{20... | collective-permute-start | bytes 589832 | tf_op jit(solution)/shard_map/ppermute | solution.py:395
  18.4 1.5 %copy-start = (bf16[3,3,3,256,128]{4,3,2,1,0:T(8,128)(2,1)S(1)}, bf16[3,3,3,256,128]{4,3,2,1,0:T(8,128)(2,1)}, u32[]{:S(2)}) copy-start(bf16[3,3,3,256,128]{4,3,2,1,0:T(8,128)(2,1)} %refs_5_.1) | copy-start | bytes 5308420
  18.4 1.5 %copy-start.6 = (f32[128]{0:T(128)S(1)}, f32[128]{0:T(128)}, u32[]{:S(2)}) copy-start(f32[128]{0:T(128)} %param.15) | copy-start | bytes 1540
  18.4 1.4 %collective-permute-start.4 = (bf16[4,2,64,128]{3,2,1,0:T(8,128)(2,1)S(1)}, bf16[4,2,64,128]{3,2,1,0:T(8,128)(2,1)S(1)}, u32[]{:S(2)}, u32[]{:S(2)}) collective-permute-start(bf16[4,2,64,128]{3,2,1,0:T(8,128)(2,1)S(1)} %collective-permute-done.2.refs_2_), channel_id=1, source_target_pairs={{0,16},{16,0},{1,17},{17,1},{2,18},{18,2},{3,19},{19,3},{4,20},{20... | collective-permute-start | bytes 393224 | tf_op jit(solution)/shard_map/ppermute | solution.py:395
  22.8 11.3 %all-to-all-start.1 = ((f32[32,2,128]{2,1,0:T(2,128)}), f32[32,2,128]{2,1,0:T(2,128)S(1)}, u32[]{:S(2)}, u32[]{:S(2)}) async-start(f32[32,2,128]{2,1,0:T(2,128)} %get-tuple-element.23), calls=%async_computation.1 | async-start | bytes 65536 | tf_op jit(solution)/shard_map/all_to_all | solution.py:366
  26.9 3.9 %copy-start.3 = (bf16[256,128]{1,0:T(8,128)(2,1)S(1)}, bf16[256,128]{1,0:T(8,128)(2,1)}, u32[]{:S(2)}) copy-start(bf16[256,128]{1,0:T(8,128)(2,1)} %skip_ref.1) | copy-start | bytes 196612
  26.9 3.9 %copy-start.7 = (f32[128]{0:T(128)S(1)}, f32[128]{0:T(128)}, u32[]{:S(2)}) copy-start(f32[128]{0:T(128)} %param.21) | copy-start | bytes 1540
  26.9 3.9 %copy-start.8 = (f32[128]{0:T(128)S(1)}, f32[128]{0:T(128)}, u32[]{:S(2)}) copy-start(f32[128]{0:T(128)} %param.19) | copy-start | bytes 1540
  26.9 7.2 %copy-start.1 = (bf16[3,3,3,128,128]{4,3,2,1,0:T(8,128)(2,1)S(1)}, bf16[3,3,3,128,128]{4,3,2,1,0:T(8,128)(2,1)}, u32[]{:S(2)}) copy-start(bf16[3,3,3,128,128]{4,3,2,1,0:T(8,128)(2,1)} %weight_ref.3) | copy-start | bytes 2654212
  27.0 7.2 %copy-start.9 = (f32[128]{0:T(128)S(1)}, f32[128]{0:T(128)}, u32[]{:S(2)}) copy-start(f32[128]{0:T(128)} %param.16) | copy-start | bytes 1540
  27.0 7.2 %copy-start.10 = (f32[128]{0:T(128)S(1)}, f32[128]{0:T(128)}, u32[]{:S(2)}) copy-start(f32[128]{0:T(128)} %param.17) | copy-start | bytes 1540
  27.0 8.2 %collective-permute-start.5 = (bf16[2,10,32,128]{3,2,1,0:T(8,128)(2,1)S(1)}, bf16[2,10,32,128]{3,2,1,0:T(8,128)(2,1)S(1)}, u32[]{:S(2)}, u32[]{:S(2)}) collective-permute-start(bf16[2,10,32,128]{3,2,1,0:T(8,128)(2,1)S(1)} %pack_hidden.1), channel_id=1, source_target_pairs={{0,2},{1,3},{2,4},{3,5},{4,6},{5,7},{6,8},{7,9},{8,10},{9,11},{10,... | collective-permute-start | bytes 491528 | tf_op jit(solution)/shard_map/ppermute | solution.py:392

commit v11 on v8

--- a/solution.py
+++ b/solution.py
@@ -124,12 +124,12 @@
     return middle + before + after
 
 
-def conv_in_rows(act_ref, weight_ref, frames, top, rows, width):
+def conv_in_rows(cells_of, weight_ref, frames, rows, width):
     totals = [None] * frames
-    for a in range(act_ref.shape[0]):
+    for a in range(frames + 2):
         reached = [f for f in range(frames) if 0 <= a - f <= 2]
         for h in range(3):
-            cells = act_ref[a, pl.ds(top + h, rows)]
+            cells = cells_of(a, h)
             cells = cells.reshape(rows * width, cells.shape[-1])
             taps = [column_taps(weight_ref, a - f, h) for f in reached]
             sums = jnp.dot(
@@ -161,7 +161,7 @@
     return 1 - tile if tiles == 2 else 0
 
 
-def body_kernel(x_ref, prev_ref, other_x_ref, norm_ref, body_ref):
+def body_kernel(x_ref, prev_ref, other_x_ref, other_prev_ref, norm_ref, body_ref):
     section = lax.axis_index("section")
     frames, _, columns, half = x_ref.shape
     width = body_ref.shape[2]
@@ -170,35 +170,47 @@
         (section, 0, prev_ref, mine),
         (section, frames, x_ref, mine),
         (1 - section, frames, other_x_ref, slice(None)),
+        (1 - section, 0, other_prev_ref, slice(None)),
     ):
         norm = tuple(norm_ref[which, k : k + 1] for k in range(3))
         lanes = pl.ds(pl.multiple_of(which * half, half), half)
         for f in range(frames):
             body_ref[first + f, :, :, lanes] = apply_norm(ref[f, :, cols, :], norm)
 
+    @pl.when(lax.axis_index("tm") == 0)
+    def _():
+        for f in range(frames):
+            body_ref[f] = body_ref[frames]
+
+
+def inner_kernel(body_ref, weight_ref, bias_ref, inner_ref):
+    frames, rows, width = inner_ref.shape[:3]
+    sums = conv_in_rows(
+        lambda a, h: body_ref[a, h : h + rows], weight_ref, frames, rows, width
+    )
+    for f, hidden in enumerate(sums):
+        inner_ref[f] = (hidden + bias_ref[...]).astype(jnp.bfloat16)
+
 
 def middle_kernel(tiles, sides, *refs):
-    body_ref, other_prev_ref = refs[:2]
+    body_ref, inner_ref = refs[:2]
     rim_refs, other_rim_refs = refs[2 : 2 + sides], refs[2 + sides : 2 + 2 * sides]
     norm_ref, weight_ref, bias_ref, hidden_ref, out_moments_ref, act_ref = refs[2 + 2 * sides :]
     section, tm, tile = (lax.axis_index(axis) for axis in AXES)
     columns, half = rim_refs[0].shape[2:]
     frames, rows, width = body_ref.shape[0] // 2, body_ref.shape[1], body_ref.shape[2]
-    kept = hidden_ref.shape[1]
     own = columns // 2
     first = pl.multiple_of(section * (columns - width), RIM)
     cols = pl.ds(first, width)
-    top = first_row(tiles, tile)
-    rim_rows = (0, rows + 2) if sides == 2 else ((rows + 2) * (1 - tile),)
-    act_ref[:, 2 : 2 + rows] = body_ref[...]
+    act_ref[:, 2:4] = body_ref[:, :2]
+    act_ref[:, 4:6] = body_ref[:, rows - 2 :]
+    rim_rows = (0, 6) if sides == 2 else (6 * (1 - tile),)
     for which, rims in ((section, rim_refs), (1 - section, other_rim_refs)):
         norm = tuple(norm_ref[which, k : k + 1] for k in range(3))
         lanes = pl.ds(pl.multiple_of(which * half, half), half)
         for f in range(2 * frames):
             for row, rim in zip(rim_rows, rims):
                 act_ref[f, pl.ds(row, 2), :, lanes] = apply_norm(rim[f, :, cols, :], norm)
-    for f in range(frames):
-        act_ref[f, 2 : 2 + rows, :, lanes] = apply_norm(other_prev_ref[f], norm)
 
     @pl.when(tile == 0)
     def _():
@@ -208,17 +220,36 @@
     @pl.when(tile == tiles - 1)
     def _():
         for f in range(2 * frames):
-            act_ref[f, rows + 2] = act_ref[f, rows + 1]
+            act_ref[f, 6] = act_ref[f, 5]
 
     @pl.when(tm == 0)
     def _():
         for f in range(frames):
             act_ref[f] = act_ref[frames]
 
-    for f, hidden in enumerate(conv_in_rows(act_ref, weight_ref, frames, top, kept, width)):
-        hidden_ref[f] = (hidden + bias_ref[...]).astype(jnp.bfloat16)
-
-    cells = hidden_ref[:, pl.ds(1 - top, rows), pl.ds(first, own), :]
+    sums = conv_in_rows(
+        lambda a, h: jnp.concatenate(
+            [act_ref[a, h : h + 2], act_ref[a, 4 + h : 6 + h]], axis=0
+        ),
+        weight_ref,
+        frames,
+        4,
+        width,
+    )
+    at = 1 - first_row(tiles, tile)
+    for f, hidden in enumerate(sums):
+        outer = (hidden + bias_ref[...]).astype(jnp.bfloat16)
+        hidden_ref[f, pl.ds(at + 1, rows - 2)] = inner_ref[f]
+        if sides == 2:
+            hidden_ref[f, 0:1] = outer[0:1]
+            hidden_ref[f, rows + 1 : rows + 2] = outer[3:4]
+        else:
+            rim = jnp.where(tile == 0, outer[3:4], outer[0:1])
+            hidden_ref[f, pl.ds(rows * (1 - tile), 1)] = rim
+        hidden_ref[f, pl.ds(at, 1)] = outer[1:2]
+        hidden_ref[f, pl.ds(at + rows - 1, 1)] = outer[2:3]
+
+    cells = hidden_ref[:, pl.ds(at, rows), pl.ds(first, own), :]
     cells = cells.astype(jnp.float32).reshape(-1, cells.shape[-1])
     out_moments_ref[...] = jnp.broadcast_to(moments_of(cells)[None], out_moments_ref.shape)
 
@@ -315,11 +346,13 @@
     first = pl.multiple_of(section * (width - own), RIM)
     beside = pl.multiple_of((1 - section) * own, RIM)
     norm = tuple(norm_ref[k : k + 1] for k in range(3))
-    for f in range(frames):
-        act_ref[f, pl.ds(top, kept), pl.ds(first, own), :] = apply_norm(before_ref[f, :kept], norm)
-        rim = apply_norm(before_ref[f, kept], norm).astype(jnp.float32)[:kept]
-        rim = jnp.broadcast_to(rim[:, None, :], (kept, width - own, outputs))
-        act_ref[f, pl.ds(top, kept), pl.ds(beside, width - own), :] = rim.astype(jnp.bfloat16)
+    @pl.when(tm > 0)
+    def _():
+        for f in range(frames):
+            act_ref[f, pl.ds(top, kept), pl.ds(first, own), :] = apply_norm(before_ref[f, :kept], norm)
+            rim = apply_norm(before_ref[f, kept], norm).astype(jnp.float32)[:kept]
+            rim = jnp.broadcast_to(rim[:, None, :], (kept, width - own, outputs))
+            act_ref[f, pl.ds(top, kept), pl.ds(beside, width - own), :] = rim.astype(jnp.bfloat16)
 
     @pl.when(tm == 0)
     def _():
@@ -425,7 +458,7 @@
         in_specs=vmem_specs(4),
         out_specs=pl.BlockSpec(memory_space=pltpu.VMEM),
         compiler_params=params(),
-        cost_estimate=cost(2_000_000_000, 1_000_000),
+        cost_estimate=cost(3_000_000_000, 1_000_000),
         name="feature_scales",
     )(moments, norm_gain_in.reshape(sections, half), norm_shift_in.reshape(sections, half), matrix)
     norm_in, *rims = lax.optimization_barrier((norm_in, *rims))
@@ -435,12 +468,21 @@
     body = pl.pallas_call(
         body_kernel,
         out_shape=jax.ShapeDtypeStruct((2 * frames, rows, width, 2 * half), jnp.bfloat16),
-        in_specs=vmem_specs(4),
+        in_specs=vmem_specs(5),
         out_specs=pl.BlockSpec(memory_space=pltpu.VMEM),
         compiler_params=params(),
         cost_estimate=cost(1_000_000_000, 1_000_000),
         name="norm_body",
-    )(features, previous, other, norm_in)
+    )(features, previous, other, other_previous, norm_in)
+    inner = pl.pallas_call(
+        inner_kernel,
+        out_shape=jax.ShapeDtypeStruct((frames, rows - 2, width, middle), jnp.bfloat16),
+        in_specs=vmem_specs(3),
+        out_specs=pl.BlockSpec(memory_space=pltpu.VMEM),
+        compiler_params=params(),
+        cost_estimate=cost(1_000_000_000, 1_000_000),
+        name="conv_in_inner",
+    )(body, conv_in_weight, conv_in_bias.reshape(1, middle))
     hidden, moments_mid = pl.pallas_call(
         functools.partial(middle_kernel, tiles, edges),
         out_shape=(
@@ -449,13 +491,13 @@
         ),
         in_specs=vmem_specs(5 + 2 * edges),
         out_specs=tuple(vmem_specs(2)),
-        scratch_shapes=[pltpu.VMEM((2 * frames, rows + 4, width, 2 * half), jnp.bfloat16)],
+        scratch_shapes=[pltpu.VMEM((2 * frames, 8, width, 2 * half), jnp.bfloat16)],
         compiler_params=params(),
         cost_estimate=cost(4_000_000_000, 1_000_000),
         name="conv_in",
     )(
         body,
-        other_previous,
+        inner,
         *rims,
         *other_rims,
         norm_in,

time: 37.1 us -> 36.5 us (0.984)
  waiting for transfers between devices: 8.77 us -> 7.83 us
  local copies, waits for them, and re-layouts: 0.09 us -> 0.9 us
  starting transfers between devices: 20.2 us -> 19.5 us
    pallas_call x0 -> x1, Pallas kernels: none -> 1.34 us  [shards(): pl.pallas_call(inner_kernel, out_shape=jax.ShapeDtypeStruct((frames, rows...]
    pallas_call x1, Pallas kernels: 3.07 us -> 1.9 us  [shards(): pl.pallas_call(functools.partial(middle_kernel, tiles, edges), out_shape=...]
    ppermute x3, waiting for transfers between devices: 0.95 us -> 0.01 us  [swap(): return lax.ppermute(value, 'section', [(0, 1), (1, 0)])]
    unnamed x22, local copies, waits for them, and re-layouts: 0.09 us -> 0.9 us
    all_to_all x2, starting transfers between devices: 8.98 us -> 8.29 us  [to_everyone(): return lax.all_to_all(moments, AXES, 0, 0, tiled=True)]
  transfers between devices with their start and end apart: 8 -> 8, of which waited for: 3 -> 2; matrix products, arithmetic and copies ran while one was open for 0% -> 0% of each run, Pallas kernels for 8% -> 12%
where the time goes in v11:
time: 36.5 us; the launch traced here: 36.2 us
  starting transfers between devices  19.5 us (53%)
  waiting for transfers between devices  7.83 us (21%)
  Pallas kernels  7.77 us (21%)
  local copies, waits for them, and re-layouts  0.9 us (2%)
    ppermute x2, starting transfers between devices, shift(): lax.ppermute(value, grid_axes, pairs_for(tms, tiles, tm_step, tile_step))  8.79 us
    all_to_all x2, starting transfers between devices, to_everyone(): return lax.all_to_all(moments, AXES, 0, 0, tiled=True)  8.29 us
    all_to_all x2, waiting for transfers between devices, to_everyone(): return lax.all_to_all(moments, AXES, 0, 0, tiled=True)  7.82 us
    pallas_call x1, Pallas kernels, shards(): pl.pallas_call(functools.partial(middle_kernel, tiles, edges), out_shape=...  1.9 us
    ppermute x1, starting transfers between devices, shards(): rims = [lax.ppermute(edge_rows[0], 'tile', [(0, 1), (1, 0)])]  1.83 us
    pallas_call x1, Pallas kernels, shards(): pl.pallas_call(functools.partial(last_kernel, tiles), out_shape=jax.Shape...  1.42 us
    pallas_call x1, Pallas kernels, shards(): pl.pallas_call(inner_kernel, out_shape=jax.ShapeDtypeStruct((frames, rows...  1.34 us
    pallas_call x1, Pallas kernels, shards(): pl.pallas_call(functools.partial(own_frames_kernel, tiles), out_shape=(ja...  1.09 us
  transfers between devices with their start and end apart: 8, of which 2 were waited for; matrix products, arithmetic and copies ran while one was open for 0% of the time, Pallas kernels for 12%

profile of v11, /device:TPU:0, one launch (start us, length us, event | category | flops | bytes accessed | tf_op | source)
XLA Modules:
  0.0 36.2 jit_solution(15317380618332822251)
XLA Ops:
  0.0 0.0 copy-start.2
  0.0 5.0 %collective-permute-start = (bf16[2,8,64,128]{3,2,1,0:T(8,128)(2,1)}, bf16[2,8,64,128]{3,2,1,0:T(8,128)(2,1)S(1)}, u32[]{:S(2)}, u32[]{:S(2)}) collective-permute-start(bf16[2,8,64,128]{3,2,1,0:T(8,128)(2,1)} %x_ref.7), channel_id=1, source_target_pairs={{0,2},{1,3},{2,4},{3,5},{4,6},{5,7},{6,8},{7,9},{8,10},{9,11},{10,... | collective-permute-start | bytes 786440 | tf_op jit(solution)/shard_map/ppermute | solution.py:412
  5.0 0.0 copy-done.2
  5.0 0.9 %feature_moments.1 = f32[32,2,128]{2,1,0:T(2,128)} custom-call(bf16[2,8,64,128]{3,2,1,0:T(8,128)(2,1)S(1)} %copy-done.2, bf16[128,128]{1,0:T(8,128)(2,1)S(1)} %group_matrix.1.order_ref.matrix_ref), custom_call_target="tpu_custom_call" | custom-call | flops 1000000000 | bytes 1000000 | tf_op jit(solution)/shard_map/feature_moments/pallas_call | solution.py:426
  5.9 0.0 copy-start.4
  5.9 0.0 copy-start.5
  5.9 4.9 %all-to-all-start = ((f32[32,2,128]{2,1,0:T(2,128)}), f32[32,2,128]{2,1,0:T(2,128)S(1)}, u32[]{:S(2)}, u32[]{:S(2)}) async-start(f32[32,2,128]{2,1,0:T(2,128)} %feature_moments.1), calls=%async_computation | async-start | bytes 65536 | tf_op jit(solution)/shard_map/all_to_all | solution.py:386
  10.9 0.0 collective-permute-done.prev_ref
  10.9 1.8 %collective-permute-start.3 = (bf16[4,2,64,128]{3,2,1,0:T(8,128)(2,1)S(1)}, bf16[4,2,64,128]{3,2,1,0:T(8,128)(2,1)S(1)}, u32[]{:S(2)}, u32[]{:S(2)}) collective-permute-start(bf16[4,2,64,128]{3,2,1,0:T(8,128)(2,1)S(1)} %get-tuple-element.19), channel_id=1, source_target_pairs={{0,1},{1,0},{2,3},{3,2},{4,5},{5,4},{6,7},{7,6},{8,9},{9,8},{10,11... | collective-permute-start | bytes 393224 | tf_op jit(solution)/shard_map/ppermute | solution.py:450
  12.8 0.0 collective-permute-start.1
  12.8 0.5 %collective-permute-start.2 = (bf16[2,8,48,128]{3,2,1,0:T(8,128)(2,1)S(1)}, bf16[2,8,48,128]{3,2,1,0:T(8,128)(2,1)S(1)}, u32[]{:S(2)}, u32[]{:S(2)}) collective-permute-start(bf16[2,8,48,128]{3,2,1,0:T(8,128)(2,1)S(1)} %get-tuple-element.18), channel_id=1, source_target_pairs={{0,16},{16,0},{1,17},{17,1},{2,18},{18,2},{3,19},{19,3},{4,20},{20... | collective-permute-start | bytes 589832 | tf_op jit(solution)/shard_map/ppermute | solution.py:415
  13.3 4.8 %all-to-all-done.moments_ref = f32[32,2,128]{2,1,0:T(2,128)S(1)} async-done(((f32[32,2,128]{2,1,0:T(2,128)}), f32[32,2,128]{2,1,0:T(2,128)S(1)}, u32[]{:S(2)}, u32[]{:S(2)}) %all-to-all-start) | async-done | bytes 32800 | tf_op jit(solution)/shard_map/all_to_all | solution.py:386
  18.1 0.0 copy-done.4
  18.1 0.0 copy-done.5
  18.1 0.3 feature_scales.1.norm_ref.refs_4_
  18.4 0.0 copy-start
  18.4 0.0 copy-start.6
  18.4 0.0 collective-permute-done.3.refs_2_
  18.4 0.1 collective-permute-start.4
  18.5 0.0 collective-permute-done.1.other_x_ref
  18.5 0.0 collective-permute-done.2.other_prev_ref
  18.5 0.5 %norm_body.1.body_ref.refs_0_ = bf16[4,8,48,256]{3,2,1,0:T(8,128)(2,1)S(1)} custom-call(bf16[2,8,64,128]{3,2,1,0:T(8,128)(2,1)S(1)} %copy-done.2, bf16[2,8,64,128]{3,2,1,0:T(8,128)(2,1)S(1)} %collective-permute-done.prev_ref, bf16[2,8,48,128]{3,2,1,0:T(8,128)(2,1)S(1)} %collective-permute-done.1.other_x_ref, ...), custom_call_target="tpu_custom_call" | custom-call | flops 1000000000 | bytes 1000000 | tf_op jit(solution)/shard_map/norm_body/pallas_call | solution.py:468
  19.0 0.8 %copy-done = bf16[3,3,3,256,128]{4,3,2,1,0:T(8,128)(2,1)S(1)} copy-done((bf16[3,3,3,256,128]{4,3,2,1,0:T(8,128)(2,1)S(1)}, bf16[3,3,3,256,128]{4,3,2,1,0:T(8,128)(2,1)}, u32[]{:S(2)}) %copy-start) | copy-done | bytes 1769496
  19.9 0.0 copy-done.6
  19.9 1.3 %conv_in_inner.1.refs_1_ = bf16[2,6,48,128]{3,2,1,0:T(8,128)(2,1)S(1)} custom-call(bf16[4,8,48,256]{3,2,1,0:T(8,128)(2,1)S(1)} %norm_body.1.body_ref.refs_0_, bf16[3,3,3,256,128]{4,3,2,1,0:T(8,128)(2,1)S(1)} %copy-done, f32[1,128]{1,0:T(1,128)S(1)} %bitcast.9), custom_call_target="tpu_custom_call" | custom-call | flops 1000000000 | bytes 1000000 | tf_op jit(solution)/shard_map/conv_in_inner/pallas_call | solution.py:477
  21.2 0.0 collective-permute-done.4.refs_3_
  21.2 1.9 %conv_in.1 = (bf16[2,9,48,128]{3,2,1,0:T(8,128)(2,1)S(1)}, f32[32,2,128]{2,1,0:T(2,128)}) custom-call(bf16[4,8,48,256]{3,2,1,0:T(8,128)(2,1)S(1)} %norm_body.1.body_ref.refs_0_, bf16[2,6,48,128]{3,2,1,0:T(8,128)(2,1)S(1)} %conv_in_inner.1.refs_1_, bf16[4,2,64,128]{3,2,1,0:T(8,128)(2,1)S(1)} %collective-permute-done.3.refs_2_, ...), custom_call_target="tpu_custom_call" | custom-call | flops 4000000000 | bytes 1000000 | tf_op jit(solution)/shard_map/conv_in/pallas_call | solution.py:486
  23.1 3.4 %all-to-all-start.1 = ((f32[32,2,128]{2,1,0:T(2,128)}), f32[32,2,128]{2,1,0:T(2,128)S(1)}, u32[]{:S(2)}, u32[]{:S(2)}) async-start(f32[32,2,128]{2,1,0:T(2,128)} %get-tuple-element.23), calls=%async_computation.1 | async-start | bytes 65536 | tf_op jit(solution)/shard_map/all_to_all | solution.py:386
  26.5 0.0 copy-start.3
  26.5 0.0 copy-start.7
  26.5 0.0 copy-start.8
  26.5 0.0 copy-start.1
  26.5 0.0 copy-start.9
  26.6 0.0 copy-start.10
  26.6 3.8 %collective-permute-start.5 = (bf16[2,10,32,128]{3,2,1,0:T(8,128)(2,1)S(1)}, bf16[2,10,32,128]{3,2,1,0:T(8,128)(2,1)S(1)}, u32[]{:S(2)}, u32[]{:S(2)}) collective-permute-start(bf16[2,10,32,128]{3,2,1,0:T(8,128)(2,1)S(1)} %pack_hidden.1), channel_id=1, source_target_pairs={{0,2},{1,3},{2,4},{3,5},{4,6},{5,7},{6,8},{7,9},{8,10},{9,11},{10,... | collective-permute-start | bytes 491528 | tf_op jit(solution)/shard_map/ppermute | solution.py:412
  30.4 0.0 copy-done.3
  30.4 0.0 copy-done.7
  30.4 0.0 copy-done.8
  30.4 0.2 shortcut.1.shortcut_ref
  30.7 3.0 %all-to-all-done.1.moments_ref = f32[32,2,128]{2,1,0:T(2,128)S(1)} async-done(((f32[32,2,128]{2,1,0:T(2,128)}), f32[32,2,128]{2,1,0:T(2,128)S(1)}, u32[]{:S(2)}, u32[]{:S(2)}) %all-to-all-start.1) | async-done | bytes 32800 | tf_op jit(solution)/shard_map/all_to_all | solution.py:386
  33.7 0.0 copy-done.1
  33.7 0.0 copy-done.9
  33.7 0.0 copy-done.10
  33.7 1.1 %conv_mid_own_frames.1 = (f32[2,8,32,128]{3,2,1,0:T(8,128)S(1)}, f32[3,128]{1,0:T(4,128)S(1)}) custom-call(bf16[2,9,48,128]{3,2,1,0:T(8,128)(2,1)S(1)} %get-tuple-element.22.hidden_ref, f32[32,2,128]{2,1,0:T(2,128)S(1)} %all-to-all-done.1.moments_ref, f32[1,128]{1,0:T(1,128)S(1)} %bitcast.13, f32[1,128]{1,0:T(1,128)S(1)} %bitcast.14, ...), custom_call_target="tpu_custom_call" | custom-call | flops 2000000000 | bytes 1000000 | tf_op jit(solution)/shard_map/conv_mid_own_frames/pallas_call | solution.py:534
  34.8 0.0 collective-permute-done.5.before_ref
  34.8 1.4 %conv_mid_previous_frames.1 = bf16[2,8,32,128]{3,2,1,0:T(8,128)(2,1)} custom-call(bf16[2,9,48,128]{3,2,1,0:T(8,128)(2,1)S(1)} %get-tuple-element.22.hidden_ref, bf16[2,10,32,128]{3,2,1,0:T(8,128)(2,1)S(1)} %collective-permute-done.5.before_ref, f32[3,128]{1,0:T(4,128)S(1)} %get-tuple-element.25.norm_ref, bf16[3,3,3,128,128]{4,3,2,1,0:T(8,128)(2,1)S(1)} %copy-done.1, ...), custom_call_target="tpu_custom_call" | custom-call | flops 2000000000 | bytes 1000000 | tf_op jit(solution)/shard_map/conv_mid_previous_frames/pallas_call | solution.py:554
  (3 shorter events, 0.1 us)
Async XLA Ops:
  0.0 5.0 %copy-start.2 = (bf16[2,8,64,128]{3,2,1,0:T(8,128)(2,1)S(1)}, bf16[2,8,64,128]{3,2,1,0:T(8,128)(2,1)}, u32[]{:S(2)}) copy-start(bf16[2,8,64,128]{3,2,1,0:T(8,128)(2,1)} %x_ref.7) | copy-start | bytes 786436
  0.0 10.9 %collective-permute-start = (bf16[2,8,64,128]{3,2,1,0:T(8,128)(2,1)}, bf16[2,8,64,128]{3,2,1,0:T(8,128)(2,1)S(1)}, u32[]{:S(2)}, u32[]{:S(2)}) collective-permute-start(bf16[2,8,64,128]{3,2,1,0:T(8,128)(2,1)} %x_ref.7), channel_id=1, source_target_pairs={{0,2},{1,3},{2,4},{3,5},{4,6},{5,7},{6,8},{7,9},{8,10},{9,11},{10,... | collective-permute-start | bytes 786440 | tf_op jit(solution)/shard_map/ppermute | solution.py:412
  5.9 12.1 %copy-start.4 = (f32[256]{0:T(256)S(1)}, f32[256]{0:T(256)}, u32[]{:S(2)}) copy-start(f32[256]{0:T(256)} %param.12) | copy-start | bytes 3076
  5.9 12.1 %copy-start.5 = (f32[256]{0:T(256)S(1)}, f32[256]{0:T(256)}, u32[]{:S(2)}) copy-start(f32[256]{0:T(256)} %param.13) | copy-start | bytes 3076
  5.9 12.1 %all-to-all-start = ((f32[32,2,128]{2,1,0:T(2,128)}), f32[32,2,128]{2,1,0:T(2,128)S(1)}, u32[]{:S(2)}, u32[]{:S(2)}) async-start(f32[32,2,128]{2,1,0:T(2,128)} %feature_moments.1), calls=%async_computation | async-start | bytes 65536 | tf_op jit(solution)/shard_map/all_to_all | solution.py:386
  10.9 7.5 %collective-permute-start.3 = (bf16[4,2,64,128]{3,2,1,0:T(8,128)(2,1)S(1)}, bf16[4,2,64,128]{3,2,1,0:T(8,128)(2,1)S(1)}, u32[]{:S(2)}, u32[]{:S(2)}) collective-permute-start(bf16[4,2,64,128]{3,2,1,0:T(8,128)(2,1)S(1)} %get-tuple-element.19), channel_id=1, source_target_pairs={{0,1},{1,0},{2,3},{3,2},{4,5},{5,4},{6,7},{7,6},{8,9},{9,8},{10,11... | collective-permute-start | bytes 393224 | tf_op jit(solution)/shard_map/ppermute | solution.py:450
  12.8 5.7 %collective-permute-start.1 = (bf16[2,8,48,128]{3,2,1,0:T(8,128)(2,1)S(1)}, bf16[2,8,48,128]{3,2,1,0:T(8,128)(2,1)S(1)}, u32[]{:S(2)}, u32[]{:S(2)}) collective-permute-start(bf16[2,8,48,128]{3,2,1,0:T(8,128)(2,1)S(1)} %get-tuple-element.17), channel_id=1, source_target_pairs={{0,16},{16,0},{1,17},{17,1},{2,18},{18,2},{3,19},{19,3},{4,20},{20... | collective-permute-start | bytes 589832 | tf_op jit(solution)/shard_map/ppermute | solution.py:415
  12.8 5.7 %collective-permute-start.2 = (bf16[2,8,48,128]{3,2,1,0:T(8,128)(2,1)S(1)}, bf16[2,8,48,128]{3,2,1,0:T(8,128)(2,1)S(1)}, u32[]{:S(2)}, u32[]{:S(2)}) collective-permute-start(bf16[2,8,48,128]{3,2,1,0:T(8,128)(2,1)S(1)} %get-tuple-element.18), channel_id=1, source_target_pairs={{0,16},{16,0},{1,17},{17,1},{2,18},{18,2},{3,19},{19,3},{4,20},{20... | collective-permute-start | bytes 589832 | tf_op jit(solution)/shard_map/ppermute | solution.py:415
  18.4 1.5 %copy-start = (bf16[3,3,3,256,128]{4,3,2,1,0:T(8,128)(2,1)S(1)}, bf16[3,3,3,256,128]{4,3,2,1,0:T(8,128)(2,1)}, u32[]{:S(2)}) copy-start(bf16[3,3,3,256,128]{4,3,2,1,0:T(8,128)(2,1)} %refs_5_.1) | copy-start | bytes 5308420
  18.4 1.5 %copy-start.6 = (f32[128]{0:T(128)S(1)}, f32[128]{0:T(128)}, u32[]{:S(2)}) copy-start(f32[128]{0:T(128)} %param.15) | copy-start | bytes 1540
  18.4 2.8 %collective-permute-start.4 = (bf16[4,2,64,128]{3,2,1,0:T(8,128)(2,1)S(1)}, bf16[4,2,64,128]{3,2,1,0:T(8,128)(2,1)S(1)}, u32[]{:S(2)}, u32[]{:S(2)}) collective-permute-start(bf16[4,2,64,128]{3,2,1,0:T(8,128)(2,1)S(1)} %collective-permute-done.3.refs_2_), channel_id=1, source_target_pairs={{0,16},{16,0},{1,17},{17,1},{2,18},{18,2},{3,19},{19,3},{4,20},{20... | collective-permute-start | bytes 393224 | tf_op jit(solution)/shard_map/ppermute | solution.py:415
  23.1 10.6 %all-to-all-start.1 = ((f32[32,2,128]{2,1,0:T(2,128)}), f32[32,2,128]{2,1,0:T(2,128)S(1)}, u32[]{:S(2)}, u32[]{:S(2)}) async-start(f32[32,2,128]{2,1,0:T(2,128)} %get-tuple-element.23), calls=%async_computation.1 | async-start | bytes 65536 | tf_op jit(solution)/shard_map/all_to_all | solution.py:386
  26.5 3.9 %copy-start.3 = (bf16[256,128]{1,0:T(8,128)(2,1)S(1)}, bf16[256,128]{1,0:T(8,128)(2,1)}, u32[]{:S(2)}) copy-start(bf16[256,128]{1,0:T(8,128)(2,1)} %skip_ref.1) | copy-start | bytes 196612
  26.5 3.9 %copy-start.7 = (f32[128]{0:T(128)S(1)}, f32[128]{0:T(128)}, u32[]{:S(2)}) copy-start(f32[128]{0:T(128)} %param.21) | copy-start | bytes 1540
  26.5 3.9 %copy-start.8 = (f32[128]{0:T(128)S(1)}, f32[128]{0:T(128)}, u32[]{:S(2)}) copy-start(f32[128]{0:T(128)} %param.19) | copy-start | bytes 1540
  26.5 7.2 %copy-start.1 = (bf16[3,3,3,128,128]{4,3,2,1,0:T(8,128)(2,1)S(1)}, bf16[3,3,3,128,128]{4,3,2,1,0:T(8,128)(2,1)}, u32[]{:S(2)}) copy-start(bf16[3,3,3,128,128]{4,3,2,1,0:T(8,128)(2,1)} %weight_ref.5) | copy-start | bytes 2654212
  26.5 7.2 %copy-start.9 = (f32[128]{0:T(128)S(1)}, f32[128]{0:T(128)}, u32[]{:S(2)}) copy-start(f32[128]{0:T(128)} %param.16) | copy-start | bytes 1540
  26.6 7.2 %copy-start.10 = (f32[128]{0:T(128)S(1)}, f32[128]{0:T(128)}, u32[]{:S(2)}) copy-start(f32[128]{0:T(128)} %param.17) | copy-start | bytes 1540
  26.6 8.2 %collective-permute-start.5 = (bf16[2,10,32,128]{3,2,1,0:T(8,128)(2,1)S(1)}, bf16[2,10,32,128]{3,2,1,0:T(8,128)(2,1)S(1)}, u32[]{:S(2)}, u32[]{:S(2)}) collective-permute-start(bf16[2,10,32,128]{3,2,1,0:T(8,128)(2,1)S(1)} %pack_hidden.1), channel_id=1, source_target_pairs={{0,2},{1,3},{2,4},{3,5},{4,6},{5,7},{6,8},{7,9},{8,10},{9,11},{10,... | collective-permute-start | bytes 491528 | tf_op jit(solution)/shard_map/ppermute | solution.py:412

commit v12 on v11

--- a/solution.py
+++ b/solution.py
@@ -461,8 +461,6 @@
         cost_estimate=cost(3_000_000_000, 1_000_000),
         name="feature_scales",
     )(moments, norm_gain_in.reshape(sections, half), norm_shift_in.reshape(sections, half), matrix)
-    norm_in, *rims = lax.optimization_barrier((norm_in, *rims))
-    other_rims = [swap(rim) for rim in rims]
 
     kept = rows + edges
     body = pl.pallas_call(
@@ -474,6 +472,8 @@
         cost_estimate=cost(1_000_000_000, 1_000_000),
         name="norm_body",
     )(features, previous, other, other_previous, norm_in)
+    body, *rims = lax.optimization_barrier((body, *rims))
+    other_rims = [swap(rim) for rim in rims]
     inner = pl.pallas_call(
         inner_kernel,
         out_shape=jax.ShapeDtypeStruct((frames, rows - 2, width, middle), jnp.bfloat16),

time: 36.5 us -> 36 us (0.986)
  starting transfers between devices: 19.5 us -> 19 us
    all_to_all x2, starting transfers between devices: 8.29 us -> 7.79 us  [to_everyone(): return lax.all_to_all(moments, AXES, 0, 0, tiled=True)]
where the time goes in v12:
time: 36 us; the launch traced here: 35.8 us
  starting transfers between devices  19 us (53%)
  waiting for transfers between devices  7.83 us (22%)
  Pallas kernels  7.78 us (22%)
  local copies, waits for them, and re-layouts  0.9 us (2%)
    ppermute x2, starting transfers between devices, shift(): lax.ppermute(value, grid_axes, pairs_for(tms, tiles, tm_step, tile_step))  8.79 us
    all_to_all x2, waiting for transfers between devices, to_everyone(): return lax.all_to_all(moments, AXES, 0, 0, tiled=True)  7.81 us
    all_to_all x2, starting transfers between devices, to_everyone(): return lax.all_to_all(moments, AXES, 0, 0, tiled=True)  7.79 us
    pallas_call x1, Pallas kernels, shards(): pl.pallas_call(functools.partial(middle_kernel, tiles, edges), out_shape=...  1.9 us
    ppermute x1, starting transfers between devices, shards(): rims = [lax.ppermute(edge_rows[0], 'tile', [(0, 1), (1, 0)])]  1.83 us
    pallas_call x1, Pallas kernels, shards(): pl.pallas_call(functools.partial(last_kernel, tiles), out_shape=jax.Shape...  1.42 us
    pallas_call x1, Pallas kernels, shards(): pl.pallas_call(inner_kernel, out_shape=jax.ShapeDtypeStruct((frames, rows...  1.34 us
    pallas_call x1, Pallas kernels, shards(): pl.pallas_call(functools.partial(own_frames_kernel, tiles), out_shape=(ja...  1.09 us
  transfers between devices with their start and end apart: 8, of which 2 were waited for; matrix products, arithmetic and copies ran while one was open for 0% of the time, Pallas kernels for 12%

profile of v12, /device:TPU:0, one launch (start us, length us, event | category | flops | bytes accessed | tf_op | source)
XLA Modules:
  0.0 35.8 jit_solution(10885025049634090154)
XLA Ops:
  0.0 0.0 copy-start.2
  0.0 5.0 %collective-permute-start = (bf16[2,8,64,128]{3,2,1,0:T(8,128)(2,1)}, bf16[2,8,64,128]{3,2,1,0:T(8,128)(2,1)S(1)}, u32[]{:S(2)}, u32[]{:S(2)}) collective-permute-start(bf16[2,8,64,128]{3,2,1,0:T(8,128)(2,1)} %x_ref.7), channel_id=1, source_target_pairs={{0,2},{1,3},{2,4},{3,5},{4,6},{5,7},{6,8},{7,9},{8,10},{9,11},{10,... | collective-permute-start | bytes 786440 | tf_op jit(solution)/shard_map/ppermute | solution.py:412
  5.0 0.0 copy-done.2
  5.0 0.9 %feature_moments.1 = f32[32,2,128]{2,1,0:T(2,128)} custom-call(bf16[2,8,64,128]{3,2,1,0:T(8,128)(2,1)S(1)} %copy-done.2, bf16[128,128]{1,0:T(8,128)(2,1)S(1)} %group_matrix.1.order_ref.matrix_ref), custom_call_target="tpu_custom_call" | custom-call | flops 1000000000 | bytes 1000000 | tf_op jit(solution)/shard_map/feature_moments/pallas_call | solution.py:426
  5.9 0.0 copy-start.4
  5.9 0.0 copy-start.5
  5.9 4.9 %all-to-all-start = ((f32[32,2,128]{2,1,0:T(2,128)}), f32[32,2,128]{2,1,0:T(2,128)S(1)}, u32[]{:S(2)}, u32[]{:S(2)}) async-start(f32[32,2,128]{2,1,0:T(2,128)} %feature_moments.1), calls=%async_computation | async-start | bytes 65536 | tf_op jit(solution)/shard_map/all_to_all | solution.py:386
  10.9 0.0 collective-permute-done.prev_ref
  10.9 1.8 %collective-permute-start.3 = (bf16[4,2,64,128]{3,2,1,0:T(8,128)(2,1)S(1)}, bf16[4,2,64,128]{3,2,1,0:T(8,128)(2,1)S(1)}, u32[]{:S(2)}, u32[]{:S(2)}) collective-permute-start(bf16[4,2,64,128]{3,2,1,0:T(8,128)(2,1)S(1)} %get-tuple-element.19), channel_id=1, source_target_pairs={{0,1},{1,0},{2,3},{3,2},{4,5},{5,4},{6,7},{7,6},{8,9},{9,8},{10,11... | collective-permute-start | bytes 393224 | tf_op jit(solution)/shard_map/ppermute | solution.py:450
  12.8 0.0 collective-permute-start.1
  12.8 0.5 %collective-permute-start.2 = (bf16[2,8,48,128]{3,2,1,0:T(8,128)(2,1)S(1)}, bf16[2,8,48,128]{3,2,1,0:T(8,128)(2,1)S(1)}, u32[]{:S(2)}, u32[]{:S(2)}) collective-permute-start(bf16[2,8,48,128]{3,2,1,0:T(8,128)(2,1)S(1)} %get-tuple-element.18), channel_id=1, source_target_pairs={{0,16},{16,0},{1,17},{17,1},{2,18},{18,2},{3,19},{19,3},{4,20},{20... | collective-permute-start | bytes 589832 | tf_op jit(solution)/shard_map/ppermute | solution.py:415
  13.3 4.8 %all-to-all-done.moments_ref = f32[32,2,128]{2,1,0:T(2,128)S(1)} async-done(((f32[32,2,128]{2,1,0:T(2,128)}), f32[32,2,128]{2,1,0:T(2,128)S(1)}, u32[]{:S(2)}, u32[]{:S(2)}) %all-to-all-start) | async-done | bytes 32800 | tf_op jit(solution)/shard_map/all_to_all | solution.py:386
  18.1 0.0 copy-done.4
  18.1 0.0 copy-done.5
  18.1 0.3 feature_scales.1.norm_ref.refs_4_
  18.4 0.0 copy-start
  18.4 0.0 copy-start.6
  18.4 0.0 collective-permute-done.1.other_x_ref
  18.4 0.0 collective-permute-done.2.other_prev_ref
  18.4 0.5 %norm_body.1.body_ref.refs_0_ = bf16[4,8,48,256]{3,2,1,0:T(8,128)(2,1)S(1)} custom-call(bf16[2,8,64,128]{3,2,1,0:T(8,128)(2,1)S(1)} %copy-done.2, bf16[2,8,64,128]{3,2,1,0:T(8,128)(2,1)S(1)} %collective-permute-done.prev_ref, bf16[2,8,48,128]{3,2,1,0:T(8,128)(2,1)S(1)} %collective-permute-done.1.other_x_ref, ...), custom_call_target="tpu_custom_call" | custom-call | flops 1000000000 | bytes 1000000 | tf_op jit(solution)/shard_map/norm_body/pallas_call | solution.py:466
  18.9 0.0 collective-permute-done.3.refs_2_
  18.9 0.1 collective-permute-start.4
  19.0 0.8 %copy-done = bf16[3,3,3,256,128]{4,3,2,1,0:T(8,128)(2,1)S(1)} copy-done((bf16[3,3,3,256,128]{4,3,2,1,0:T(8,128)(2,1)S(1)}, bf16[3,3,3,256,128]{4,3,2,1,0:T(8,128)(2,1)}, u32[]{:S(2)}) %copy-start) | copy-done | bytes 1769496
  19.9 0.0 copy-done.6
  19.9 1.3 %conv_in_inner.1.refs_1_ = bf16[2,6,48,128]{3,2,1,0:T(8,128)(2,1)S(1)} custom-call(bf16[4,8,48,256]{3,2,1,0:T(8,128)(2,1)S(1)} %norm_body.1.body_ref.refs_0_, bf16[3,3,3,256,128]{4,3,2,1,0:T(8,128)(2,1)S(1)} %copy-done, f32[1,128]{1,0:T(1,128)S(1)} %bitcast.9), custom_call_target="tpu_custom_call" | custom-call | flops 1000000000 | bytes 1000000 | tf_op jit(solution)/shard_map/conv_in_inner/pallas_call | solution.py:477
  21.2 0.0 collective-permute-done.4.refs_3_
  21.2 1.9 %conv_in.1 = (bf16[2,9,48,128]{3,2,1,0:T(8,128)(2,1)S(1)}, f32[32,2,128]{2,1,0:T(2,128)}) custom-call(bf16[4,8,48,256]{3,2,1,0:T(8,128)(2,1)S(1)} %norm_body.1.body_ref.refs_0_, bf16[2,6,48,128]{3,2,1,0:T(8,128)(2,1)S(1)} %conv_in_inner.1.refs_1_, bf16[4,2,64,128]{3,2,1,0:T(8,128)(2,1)S(1)} %collective-permute-done.3.refs_2_, ...), custom_call_target="tpu_custom_call" | custom-call | flops 4000000000 | bytes 1000000 | tf_op jit(solution)/shard_map/conv_in/pallas_call | solution.py:486
  23.1 2.9 %all-to-all-start.1 = ((f32[32,2,128]{2,1,0:T(2,128)}), f32[32,2,128]{2,1,0:T(2,128)S(1)}, u32[]{:S(2)}, u32[]{:S(2)}) async-start(f32[32,2,128]{2,1,0:T(2,128)} %get-tuple-element.23), calls=%async_computation.1 | async-start | bytes 65536 | tf_op jit(solution)/shard_map/all_to_all | solution.py:386
  26.0 0.0 copy-start.3
  26.0 0.0 copy-start.7
  26.0 0.0 copy-start.8
  26.0 0.0 copy-start.1
  26.0 0.0 copy-start.9
  26.1 0.0 copy-start.10
  26.1 3.8 %collective-permute-start.5 = (bf16[2,10,32,128]{3,2,1,0:T(8,128)(2,1)S(1)}, bf16[2,10,32,128]{3,2,1,0:T(8,128)(2,1)S(1)}, u32[]{:S(2)}, u32[]{:S(2)}) collective-permute-start(bf16[2,10,32,128]{3,2,1,0:T(8,128)(2,1)S(1)} %pack_hidden.1), channel_id=1, source_target_pairs={{0,2},{1,3},{2,4},{3,5},{4,6},{5,7},{6,8},{7,9},{8,10},{9,11},{10,... | collective-permute-start | bytes 491528 | tf_op jit(solution)/shard_map/ppermute | solution.py:412
  29.9 0.0 copy-done.3
  29.9 0.0 copy-done.7
  29.9 0.0 copy-done.8
  30.0 0.2 shortcut.1.shortcut_ref
  30.2 3.0 %all-to-all-done.1.moments_ref = f32[32,2,128]{2,1,0:T(2,128)S(1)} async-done(((f32[32,2,128]{2,1,0:T(2,128)}), f32[32,2,128]{2,1,0:T(2,128)S(1)}, u32[]{:S(2)}, u32[]{:S(2)}) %all-to-all-start.1) | async-done | bytes 32800 | tf_op jit(solution)/shard_map/all_to_all | solution.py:386
  33.2 0.0 copy-done.1
  33.2 0.0 copy-done.9
  33.2 0.0 copy-done.10
  33.2 1.1 %conv_mid_own_frames.1 = (f32[2,8,32,128]{3,2,1,0:T(8,128)S(1)}, f32[3,128]{1,0:T(4,128)S(1)}) custom-call(bf16[2,9,48,128]{3,2,1,0:T(8,128)(2,1)S(1)} %get-tuple-element.22.hidden_ref, f32[32,2,128]{2,1,0:T(2,128)S(1)} %all-to-all-done.1.moments_ref, f32[1,128]{1,0:T(1,128)S(1)} %bitcast.13, f32[1,128]{1,0:T(1,128)S(1)} %bitcast.14, ...), custom_call_target="tpu_custom_call" | custom-call | flops 2000000000 | bytes 1000000 | tf_op jit(solution)/shard_map/conv_mid_own_frames/pallas_call | solution.py:534
  34.3 0.0 collective-permute-done.5.before_ref
  34.3 1.4 %conv_mid_previous_frames.1 = bf16[2,8,32,128]{3,2,1,0:T(8,128)(2,1)} custom-call(bf16[2,9,48,128]{3,2,1,0:T(8,128)(2,1)S(1)} %get-tuple-element.22.hidden_ref, bf16[2,10,32,128]{3,2,1,0:T(8,128)(2,1)S(1)} %collective-permute-done.5.before_ref, f32[3,128]{1,0:T(4,128)S(1)} %get-tuple-element.25.norm_ref, bf16[3,3,3,128,128]{4,3,2,1,0:T(8,128)(2,1)S(1)} %copy-done.1, ...), custom_call_target="tpu_custom_call" | custom-call | flops 2000000000 | bytes 1000000 | tf_op jit(solution)/shard_map/conv_mid_previous_frames/pallas_call | solution.py:554
  (3 shorter events, 0.1 us)
Async XLA Ops:
  0.0 5.0 %copy-start.2 = (bf16[2,8,64,128]{3,2,1,0:T(8,128)(2,1)S(1)}, bf16[2,8,64,128]{3,2,1,0:T(8,128)(2,1)}, u32[]{:S(2)}) copy-start(bf16[2,8,64,128]{3,2,1,0:T(8,128)(2,1)} %x_ref.7) | copy-start | bytes 786436
  0.0 10.9 %collective-permute-start = (bf16[2,8,64,128]{3,2,1,0:T(8,128)(2,1)}, bf16[2,8,64,128]{3,2,1,0:T(8,128)(2,1)S(1)}, u32[]{:S(2)}, u32[]{:S(2)}) collective-permute-start(bf16[2,8,64,128]{3,2,1,0:T(8,128)(2,1)} %x_ref.7), channel_id=1, source_target_pairs={{0,2},{1,3},{2,4},{3,5},{4,6},{5,7},{6,8},{7,9},{8,10},{9,11},{10,... | collective-permute-start | bytes 786440 | tf_op jit(solution)/shard_map/ppermute | solution.py:412
  5.9 12.1 %copy-start.4 = (f32[256]{0:T(256)S(1)}, f32[256]{0:T(256)}, u32[]{:S(2)}) copy-start(f32[256]{0:T(256)} %param.12) | copy-start | bytes 3076
  5.9 12.1 %copy-start.5 = (f32[256]{0:T(256)S(1)}, f32[256]{0:T(256)}, u32[]{:S(2)}) copy-start(f32[256]{0:T(256)} %param.13) | copy-start | bytes 3076
  5.9 12.1 %all-to-all-start = ((f32[32,2,128]{2,1,0:T(2,128)}), f32[32,2,128]{2,1,0:T(2,128)S(1)}, u32[]{:S(2)}, u32[]{:S(2)}) async-start(f32[32,2,128]{2,1,0:T(2,128)} %feature_moments.1), calls=%async_computation | async-start | bytes 65536 | tf_op jit(solution)/shard_map/all_to_all | solution.py:386
  10.9 8.0 %collective-permute-start.3 = (bf16[4,2,64,128]{3,2,1,0:T(8,128)(2,1)S(1)}, bf16[4,2,64,128]{3,2,1,0:T(8,128)(2,1)S(1)}, u32[]{:S(2)}, u32[]{:S(2)}) collective-permute-start(bf16[4,2,64,128]{3,2,1,0:T(8,128)(2,1)S(1)} %get-tuple-element.19), channel_id=1, source_target_pairs={{0,1},{1,0},{2,3},{3,2},{4,5},{5,4},{6,7},{7,6},{8,9},{9,8},{10,11... | collective-permute-start | bytes 393224 | tf_op jit(solution)/shard_map/ppermute | solution.py:450
  12.8 5.6 %collective-permute-start.1 = (bf16[2,8,48,128]{3,2,1,0:T(8,128)(2,1)S(1)}, bf16[2,8,48,128]{3,2,1,0:T(8,128)(2,1)S(1)}, u32[]{:S(2)}, u32[]{:S(2)}) collective-permute-start(bf16[2,8,48,128]{3,2,1,0:T(8,128)(2,1)S(1)} %get-tuple-element.17), channel_id=1, source_target_pairs={{0,16},{16,0},{1,17},{17,1},{2,18},{18,2},{3,19},{19,3},{4,20},{20... | collective-permute-start | bytes 589832 | tf_op jit(solution)/shard_map/ppermute | solution.py:415
  12.8 5.7 %collective-permute-start.2 = (bf16[2,8,48,128]{3,2,1,0:T(8,128)(2,1)S(1)}, bf16[2,8,48,128]{3,2,1,0:T(8,128)(2,1)S(1)}, u32[]{:S(2)}, u32[]{:S(2)}) collective-permute-start(bf16[2,8,48,128]{3,2,1,0:T(8,128)(2,1)S(1)} %get-tuple-element.18), channel_id=1, source_target_pairs={{0,16},{16,0},{1,17},{17,1},{2,18},{18,2},{3,19},{19,3},{4,20},{20... | collective-permute-start | bytes 589832 | tf_op jit(solution)/shard_map/ppermute | solution.py:415
  18.4 1.5 %copy-start = (bf16[3,3,3,256,128]{4,3,2,1,0:T(8,128)(2,1)S(1)}, bf16[3,3,3,256,128]{4,3,2,1,0:T(8,128)(2,1)}, u32[]{:S(2)}) copy-start(bf16[3,3,3,256,128]{4,3,2,1,0:T(8,128)(2,1)} %refs_5_.1) | copy-start | bytes 5308420
  18.4 1.5 %copy-start.6 = (f32[128]{0:T(128)S(1)}, f32[128]{0:T(128)}, u32[]{:S(2)}) copy-start(f32[128]{0:T(128)} %param.15) | copy-start | bytes 1540
  18.9 2.3 %collective-permute-start.4 = (bf16[4,2,64,128]{3,2,1,0:T(8,128)(2,1)S(1)}, bf16[4,2,64,128]{3,2,1,0:T(8,128)(2,1)S(1)}, u32[]{:S(2)}, u32[]{:S(2)}) collective-permute-start(bf16[4,2,64,128]{3,2,1,0:T(8,128)(2,1)S(1)} %collective-permute-done.3.refs_2_), channel_id=1, source_target_pairs={{0,16},{16,0},{1,17},{17,1},{2,18},{18,2},{3,19},{19,3},{4,20},{20... | collective-permute-start | bytes 393224 | tf_op jit(solution)/shard_map/ppermute | solution.py:415
  23.1 10.1 %all-to-all-start.1 = ((f32[32,2,128]{2,1,0:T(2,128)}), f32[32,2,128]{2,1,0:T(2,128)S(1)}, u32[]{:S(2)}, u32[]{:S(2)}) async-start(f32[32,2,128]{2,1,0:T(2,128)} %get-tuple-element.23), calls=%async_computation.1 | async-start | bytes 65536 | tf_op jit(solution)/shard_map/all_to_all | solution.py:386
  26.0 3.9 %copy-start.3 = (bf16[256,128]{1,0:T(8,128)(2,1)S(1)}, bf16[256,128]{1,0:T(8,128)(2,1)}, u32[]{:S(2)}) copy-start(bf16[256,128]{1,0:T(8,128)(2,1)} %skip_ref.1) | copy-start | bytes 196612
  26.0 3.9 %copy-start.7 = (f32[128]{0:T(128)S(1)}, f32[128]{0:T(128)}, u32[]{:S(2)}) copy-start(f32[128]{0:T(128)} %param.21) | copy-start | bytes 1540
  26.0 3.9 %copy-start.8 = (f32[128]{0:T(128)S(1)}, f32[128]{0:T(128)}, u32[]{:S(2)}) copy-start(f32[128]{0:T(128)} %param.19) | copy-start | bytes 1540
  26.0 7.2 %copy-start.1 = (bf16[3,3,3,128,128]{4,3,2,1,0:T(8,128)(2,1)S(1)}, bf16[3,3,3,128,128]{4,3,2,1,0:T(8,128)(2,1)}, u32[]{:S(2)}) copy-start(bf16[3,3,3,128,128]{4,3,2,1,0:T(8,128)(2,1)} %weight_ref.5) | copy-start | bytes 2654212
  26.0 7.2 %copy-start.9 = (f32[128]{0:T(128)S(1)}, f32[128]{0:T(128)}, u32[]{:S(2)}) copy-start(f32[128]{0:T(128)} %param.16) | copy-start | bytes 1540
  26.1 7.2 %copy-start.10 = (f32[128]{0:T(128)S(1)}, f32[128]{0:T(128)}, u32[]{:S(2)}) copy-start(f32[128]{0:T(128)} %param.17) | copy-start | bytes 1540
  26.1 8.2 %collective-permute-start.5 = (bf16[2,10,32,128]{3,2,1,0:T(8,128)(2,1)S(1)}, bf16[2,10,32,128]{3,2,1,0:T(8,128)(2,1)S(1)}, u32[]{:S(2)}, u32[]{:S(2)}) collective-permute-start(bf16[2,10,32,128]{3,2,1,0:T(8,128)(2,1)S(1)} %pack_hidden.1), channel_id=1, source_target_pairs={{0,2},{1,3},{2,4},{3,5},{4,6},{5,7},{6,8},{7,9},{8,10},{9,11},{10,... | collective-permute-start | bytes 491528 | tf_op jit(solution)/shard_map/ppermute | solution.py:412

commit v13 on v12

--- a/solution.py
+++ b/solution.py
@@ -70,8 +70,9 @@
     return silu((values.astype(jnp.float32) - mean) * scale + shift).astype(jnp.bfloat16)
 
 
-def matrix_kernel(width, matrix_ref):
-    matrix_ref[...] = group_matrix(matrix_ref.shape[0], width)
+def matrix_kernel(widths, *matrix_refs):
+    for width, matrix_ref in zip(widths, matrix_refs):
+        matrix_ref[...] = group_matrix(matrix_ref.shape[0], width)
 
 
 def first_kernel(x_ref, order_ref, moments_ref):
@@ -311,6 +312,7 @@
     shift_ref,
     weight_ref,
     shortcut_ref,
+    matrix_ref,
     part_ref,
     norm_ref,
     act_ref,
@@ -324,7 +326,7 @@
         outputs // GROUPS,
         gain_ref[...],
         shift_ref[...],
-        group_matrix(outputs, outputs // GROUPS),
+        matrix_ref[...],
     )
     norm_ref[...] = jnp.concatenate(norm, axis=0)
     for f in range(frames):
@@ -415,10 +417,13 @@
         return lax.ppermute(value, "section", [(0, 1), (1, 0)])
 
     previous = shift(features, 1, 0)
-    matrix = pl.pallas_call(
-        functools.partial(matrix_kernel, half * sections // GROUPS),
-        out_shape=jax.ShapeDtypeStruct((half, half), jnp.bfloat16),
-        out_specs=pl.BlockSpec(memory_space=pltpu.VMEM),
+    matrix, matrix_mid = pl.pallas_call(
+        functools.partial(matrix_kernel, (half * sections // GROUPS, middle // GROUPS)),
+        out_shape=(
+            jax.ShapeDtypeStruct((half, half), jnp.bfloat16),
+            jax.ShapeDtypeStruct((middle, middle), jnp.bfloat16),
+        ),
+        out_specs=tuple(vmem_specs(2)),
         compiler_params=params(),
         cost_estimate=cost(1_000_000_000, 1_000_000),
         name="group_matrix",
@@ -537,7 +542,7 @@
             jax.ShapeDtypeStruct((frames, rows, own, outputs), jnp.float32),
             jax.ShapeDtypeStruct((3, middle), jnp.float32),
         ),
-        in_specs=vmem_specs(6),
+        in_specs=vmem_specs(7),
         out_specs=tuple(vmem_specs(2)),
         scratch_shapes=[pltpu.VMEM((frames, rows + 2, width, middle), jnp.bfloat16)],
         compiler_params=params(),
@@ -550,6 +555,7 @@
         norm_shift_mid.reshape(1, middle),
         conv_mid_weight,
         shortcut,
+        matrix_mid,
     )
     return pl.pallas_call(
         functools.partial(last_kernel, tiles),

time: 36 us -> 36 us (level)
  transfers between devices with their start and end apart: 8 -> 8, of which waited for: 2 -> 2; matrix products, arithmetic and copies ran while one was open for 0% -> 0% of each run, Pallas kernels for 12% -> 13%
where the time goes in v13:
time: 36 us; the launch traced here: 35.7 us
  starting transfers between devices  19 us (53%)
  waiting for transfers between devices  7.83 us (22%)
  Pallas kernels  7.78 us (22%)
  local copies, waits for them, and re-layouts  0.9 us (2%)
    ppermute x2, starting transfers between devices, shift(): lax.ppermute(value, grid_axes, pairs_for(tms, tiles, tm_step, tile_step))  8.79 us
    all_to_all x2, waiting for transfers between devices, to_everyone(): return lax.all_to_all(moments, AXES, 0, 0, tiled=True)  7.81 us
    all_to_all x2, starting transfers between devices, to_everyone(): return lax.all_to_all(moments, AXES, 0, 0, tiled=True)  7.78 us
    pallas_call x1, Pallas kernels, shards(): pl.pallas_call(functools.partial(middle_kernel, tiles, edges), out_shape=...  1.9 us
    ppermute x1, starting transfers between devices, shards(): rims = [lax.ppermute(edge_rows[0], 'tile', [(0, 1), (1, 0)])]  1.83 us
    pallas_call x1, Pallas kernels, shards(): pl.pallas_call(functools.partial(last_kernel, tiles), out_shape=jax.Shape...  1.42 us
    pallas_call x1, Pallas kernels, shards(): pl.pallas_call(inner_kernel, out_shape=jax.ShapeDtypeStruct((frames, rows...  1.34 us
    pallas_call x1, Pallas kernels, shards(): pl.pallas_call(functools.partial(own_frames_kernel, tiles), out_shape=(ja...  1.09 us
  transfers between devices with their start and end apart: 8, of which 2 were waited for; matrix products, arithmetic and copies ran while one was open for 0% of the time, Pallas kernels for 13%

profile of v13, /device:TPU:0, one launch (start us, length us, event | category | flops | bytes accessed | tf_op | source)
XLA Modules:
  0.0 35.7 jit_solution(15594089388435833250)
XLA Ops:
  0.0 0.0 copy-start.2
  0.0 5.0 %collective-permute-start = (bf16[2,8,64,128]{3,2,1,0:T(8,128)(2,1)}, bf16[2,8,64,128]{3,2,1,0:T(8,128)(2,1)S(1)}, u32[]{:S(2)}, u32[]{:S(2)}) collective-permute-start(bf16[2,8,64,128]{3,2,1,0:T(8,128)(2,1)} %x_ref.7), channel_id=1, source_target_pairs={{0,2},{1,3},{2,4},{3,5},{4,6},{5,7},{6,8},{7,9},{8,10},{9,11},{10,... | collective-permute-start | bytes 786440 | tf_op jit(solution)/shard_map/ppermute | solution.py:414
  5.0 0.0 copy-done.2
  5.0 0.9 %feature_moments.1 = f32[32,2,128]{2,1,0:T(2,128)} custom-call(bf16[2,8,64,128]{3,2,1,0:T(8,128)(2,1)S(1)} %copy-done.2, bf16[128,128]{1,0:T(8,128)(2,1)S(1)} %get-tuple-element.18.order_ref.matrix_ref), custom_call_target="tpu_custom_call" | custom-call | flops 1000000000 | bytes 1000000 | tf_op jit(solution)/shard_map/feature_moments/pallas_call | solution.py:431
  5.9 0.0 copy-start.4
  5.9 0.0 copy-start.5
  5.9 4.9 %all-to-all-start = ((f32[32,2,128]{2,1,0:T(2,128)}), f32[32,2,128]{2,1,0:T(2,128)S(1)}, u32[]{:S(2)}, u32[]{:S(2)}) async-start(f32[32,2,128]{2,1,0:T(2,128)} %feature_moments.1), calls=%async_computation | async-start | bytes 65536 | tf_op jit(solution)/shard_map/all_to_all | solution.py:388
  10.9 0.0 collective-permute-done.prev_ref
  10.9 1.8 %collective-permute-start.3 = (bf16[4,2,64,128]{3,2,1,0:T(8,128)(2,1)S(1)}, bf16[4,2,64,128]{3,2,1,0:T(8,128)(2,1)S(1)}, u32[]{:S(2)}, u32[]{:S(2)}) collective-permute-start(bf16[4,2,64,128]{3,2,1,0:T(8,128)(2,1)S(1)} %get-tuple-element.22), channel_id=1, source_target_pairs={{0,1},{1,0},{2,3},{3,2},{4,5},{5,4},{6,7},{7,6},{8,9},{9,8},{10,11... | collective-permute-start | bytes 393224 | tf_op jit(solution)/shard_map/ppermute | solution.py:455
  12.8 0.0 collective-permute-start.1
  12.8 0.5 %collective-permute-start.2 = (bf16[2,8,48,128]{3,2,1,0:T(8,128)(2,1)S(1)}, bf16[2,8,48,128]{3,2,1,0:T(8,128)(2,1)S(1)}, u32[]{:S(2)}, u32[]{:S(2)}) collective-permute-start(bf16[2,8,48,128]{3,2,1,0:T(8,128)(2,1)S(1)} %get-tuple-element.21), channel_id=1, source_target_pairs={{0,16},{16,0},{1,17},{17,1},{2,18},{18,2},{3,19},{19,3},{4,20},{20... | collective-permute-start | bytes 589832 | tf_op jit(solution)/shard_map/ppermute | solution.py:417
  13.3 4.8 %all-to-all-done.moments_ref = f32[32,2,128]{2,1,0:T(2,128)S(1)} async-done(((f32[32,2,128]{2,1,0:T(2,128)}), f32[32,2,128]{2,1,0:T(2,128)S(1)}, u32[]{:S(2)}, u32[]{:S(2)}) %all-to-all-start) | async-done | bytes 32800 | tf_op jit(solution)/shard_map/all_to_all | solution.py:388
  18.1 0.0 copy-done.4
  18.1 0.0 copy-done.5
  18.1 0.3 feature_scales.1.norm_ref.refs_4_
  18.4 0.0 copy-start
  18.4 0.0 copy-start.6
  18.4 0.0 collective-permute-done.1.other_x_ref
  18.4 0.0 collective-permute-done.2.other_prev_ref
  18.4 0.5 %norm_body.1.body_ref.refs_0_ = bf16[4,8,48,256]{3,2,1,0:T(8,128)(2,1)S(1)} custom-call(bf16[2,8,64,128]{3,2,1,0:T(8,128)(2,1)S(1)} %copy-done.2, bf16[2,8,64,128]{3,2,1,0:T(8,128)(2,1)S(1)} %collective-permute-done.prev_ref, bf16[2,8,48,128]{3,2,1,0:T(8,128)(2,1)S(1)} %collective-permute-done.1.other_x_ref, ...), custom_call_target="tpu_custom_call" | custom-call | flops 1000000000 | bytes 1000000 | tf_op jit(solution)/shard_map/norm_body/pallas_call | solution.py:471
  18.9 0.0 collective-permute-done.3.refs_2_
  18.9 0.1 collective-permute-start.4
  19.0 0.8 %copy-done = bf16[3,3,3,256,128]{4,3,2,1,0:T(8,128)(2,1)S(1)} copy-done((bf16[3,3,3,256,128]{4,3,2,1,0:T(8,128)(2,1)S(1)}, bf16[3,3,3,256,128]{4,3,2,1,0:T(8,128)(2,1)}, u32[]{:S(2)}) %copy-start) | copy-done | bytes 1769496
  19.9 0.0 copy-done.6
  19.9 1.3 %conv_in_inner.1.refs_1_ = bf16[2,6,48,128]{3,2,1,0:T(8,128)(2,1)S(1)} custom-call(bf16[4,8,48,256]{3,2,1,0:T(8,128)(2,1)S(1)} %norm_body.1.body_ref.refs_0_, bf16[3,3,3,256,128]{4,3,2,1,0:T(8,128)(2,1)S(1)} %copy-done, f32[1,128]{1,0:T(1,128)S(1)} %bitcast.9), custom_call_target="tpu_custom_call" | custom-call | flops 1000000000 | bytes 1000000 | tf_op jit(solution)/shard_map/conv_in_inner/pallas_call | solution.py:482
  21.2 0.0 collective-permute-done.4.refs_3_
  21.2 1.9 %conv_in.1 = (bf16[2,9,48,128]{3,2,1,0:T(8,128)(2,1)S(1)}, f32[32,2,128]{2,1,0:T(2,128)}) custom-call(bf16[4,8,48,256]{3,2,1,0:T(8,128)(2,1)S(1)} %norm_body.1.body_ref.refs_0_, bf16[2,6,48,128]{3,2,1,0:T(8,128)(2,1)S(1)} %conv_in_inner.1.refs_1_, bf16[4,2,64,128]{3,2,1,0:T(8,128)(2,1)S(1)} %collective-permute-done.3.refs_2_, ...), custom_call_target="tpu_custom_call" | custom-call | flops 4000000000 | bytes 1000000 | tf_op jit(solution)/shard_map/conv_in/pallas_call | solution.py:491
  23.1 2.9 %all-to-all-start.1 = ((f32[32,2,128]{2,1,0:T(2,128)}), f32[32,2,128]{2,1,0:T(2,128)S(1)}, u32[]{:S(2)}, u32[]{:S(2)}) async-start(f32[32,2,128]{2,1,0:T(2,128)} %get-tuple-element.26), calls=%async_computation.1 | async-start | bytes 65536 | tf_op jit(solution)/shard_map/all_to_all | solution.py:388
  26.0 0.0 copy-start.3
  26.0 0.0 copy-start.7
  26.0 0.0 copy-start.8
  26.0 0.0 copy-start.1
  26.0 0.0 copy-start.9
  26.1 0.0 copy-start.10
  26.1 3.8 %collective-permute-start.5 = (bf16[2,10,32,128]{3,2,1,0:T(8,128)(2,1)S(1)}, bf16[2,10,32,128]{3,2,1,0:T(8,128)(2,1)S(1)}, u32[]{:S(2)}, u32[]{:S(2)}) collective-permute-start(bf16[2,10,32,128]{3,2,1,0:T(8,128)(2,1)S(1)} %pack_hidden.1), channel_id=1, source_target_pairs={{0,2},{1,3},{2,4},{3,5},{4,6},{5,7},{6,8},{7,9},{8,10},{9,11},{10,... | collective-permute-start | bytes 491528 | tf_op jit(solution)/shard_map/ppermute | solution.py:414
  29.9 0.0 copy-done.3
  29.9 0.0 copy-done.7
  29.9 0.0 copy-done.8
  30.0 0.2 shortcut.1.shortcut_ref
  30.2 3.0 %all-to-all-done.1.moments_ref = f32[32,2,128]{2,1,0:T(2,128)S(1)} async-done(((f32[32,2,128]{2,1,0:T(2,128)}), f32[32,2,128]{2,1,0:T(2,128)S(1)}, u32[]{:S(2)}, u32[]{:S(2)}) %all-to-all-start.1) | async-done | bytes 32800 | tf_op jit(solution)/shard_map/all_to_all | solution.py:388
  33.2 0.0 copy-done.1
  33.2 0.0 copy-done.9
  33.2 0.0 copy-done.10
  33.2 1.1 %conv_mid_own_frames.1 = (f32[2,8,32,128]{3,2,1,0:T(8,128)S(1)}, f32[3,128]{1,0:T(4,128)S(1)}) custom-call(bf16[2,9,48,128]{3,2,1,0:T(8,128)(2,1)S(1)} %get-tuple-element.25.hidden_ref, f32[32,2,128]{2,1,0:T(2,128)S(1)} %all-to-all-done.1.moments_ref, f32[1,128]{1,0:T(1,128)S(1)} %bitcast.13, f32[1,128]{1,0:T(1,128)S(1)} %bitcast.14, ...), custom_call_target="tpu_custom_call" | custom-call | flops 2000000000 | bytes 1000000 | tf_op jit(solution)/shard_map/conv_mid_own_frames/pallas_call | solution.py:539
  34.3 0.0 collective-permute-done.5.before_ref
  34.3 1.4 %conv_mid_previous_frames.1 = bf16[2,8,32,128]{3,2,1,0:T(8,128)(2,1)} custom-call(bf16[2,9,48,128]{3,2,1,0:T(8,128)(2,1)S(1)} %get-tuple-element.25.hidden_ref, bf16[2,10,32,128]{3,2,1,0:T(8,128)(2,1)S(1)} %collective-permute-done.5.before_ref, f32[3,128]{1,0:T(4,128)S(1)} %get-tuple-element.29.norm_ref, bf16[3,3,3,128,128]{4,3,2,1,0:T(8,128)(2,1)S(1)} %copy-done.1, ...), custom_call_target="tpu_custom_call" | custom-call | flops 2000000000 | bytes 1000000 | tf_op jit(solution)/shard_map/conv_mid_previous_frames/pallas_call | solution.py:560
  (3 shorter events, 0.1 us)
Async XLA Ops:
  0.0 5.0 %copy-start.2 = (bf16[2,8,64,128]{3,2,1,0:T(8,128)(2,1)S(1)}, bf16[2,8,64,128]{3,2,1,0:T(8,128)(2,1)}, u32[]{:S(2)}) copy-start(bf16[2,8,64,128]{3,2,1,0:T(8,128)(2,1)} %x_ref.7) | copy-start | bytes 786436
  0.0 10.9 %collective-permute-start = (bf16[2,8,64,128]{3,2,1,0:T(8,128)(2,1)}, bf16[2,8,64,128]{3,2,1,0:T(8,128)(2,1)S(1)}, u32[]{:S(2)}, u32[]{:S(2)}) collective-permute-start(bf16[2,8,64,128]{3,2,1,0:T(8,128)(2,1)} %x_ref.7), channel_id=1, source_target_pairs={{0,2},{1,3},{2,4},{3,5},{4,6},{5,7},{6,8},{7,9},{8,10},{9,11},{10,... | collective-permute-start | bytes 786440 | tf_op jit(solution)/shard_map/ppermute | solution.py:414
  5.9 12.1 %copy-start.4 = (f32[256]{0:T(256)S(1)}, f32[256]{0:T(256)}, u32[]{:S(2)}) copy-start(f32[256]{0:T(256)} %param.12) | copy-start | bytes 3076
  5.9 12.1 %copy-start.5 = (f32[256]{0:T(256)S(1)}, f32[256]{0:T(256)}, u32[]{:S(2)}) copy-start(f32[256]{0:T(256)} %param.13) | copy-start | bytes 3076
  5.9 12.1 %all-to-all-start = ((f32[32,2,128]{2,1,0:T(2,128)}), f32[32,2,128]{2,1,0:T(2,128)S(1)}, u32[]{:S(2)}, u32[]{:S(2)}) async-start(f32[32,2,128]{2,1,0:T(2,128)} %feature_moments.1), calls=%async_computation | async-start | bytes 65536 | tf_op jit(solution)/shard_map/all_to_all | solution.py:388
  10.9 8.0 %collective-permute-start.3 = (bf16[4,2,64,128]{3,2,1,0:T(8,128)(2,1)S(1)}, bf16[4,2,64,128]{3,2,1,0:T(8,128)(2,1)S(1)}, u32[]{:S(2)}, u32[]{:S(2)}) collective-permute-start(bf16[4,2,64,128]{3,2,1,0:T(8,128)(2,1)S(1)} %get-tuple-element.22), channel_id=1, source_target_pairs={{0,1},{1,0},{2,3},{3,2},{4,5},{5,4},{6,7},{7,6},{8,9},{9,8},{10,11... | collective-permute-start | bytes 393224 | tf_op jit(solution)/shard_map/ppermute | solution.py:455
  12.8 5.6 %collective-permute-start.1 = (bf16[2,8,48,128]{3,2,1,0:T(8,128)(2,1)S(1)}, bf16[2,8,48,128]{3,2,1,0:T(8,128)(2,1)S(1)}, u32[]{:S(2)}, u32[]{:S(2)}) collective-permute-start(bf16[2,8,48,128]{3,2,1,0:T(8,128)(2,1)S(1)} %get-tuple-element.20), channel_id=1, source_target_pairs={{0,16},{16,0},{1,17},{17,1},{2,18},{18,2},{3,19},{19,3},{4,20},{20... | collective-permute-start | bytes 589832 | tf_op jit(solution)/shard_map/ppermute | solution.py:417
  12.8 5.7 %collective-permute-start.2 = (bf16[2,8,48,128]{3,2,1,0:T(8,128)(2,1)S(1)}, bf16[2,8,48,128]{3,2,1,0:T(8,128)(2,1)S(1)}, u32[]{:S(2)}, u32[]{:S(2)}) collective-permute-start(bf16[2,8,48,128]{3,2,1,0:T(8,128)(2,1)S(1)} %get-tuple-element.21), channel_id=1, source_target_pairs={{0,16},{16,0},{1,17},{17,1},{2,18},{18,2},{3,19},{19,3},{4,20},{20... | collective-permute-start | bytes 589832 | tf_op jit(solution)/shard_map/ppermute | solution.py:417
  18.4 1.5 %copy-start = (bf16[3,3,3,256,128]{4,3,2,1,0:T(8,128)(2,1)S(1)}, bf16[3,3,3,256,128]{4,3,2,1,0:T(8,128)(2,1)}, u32[]{:S(2)}) copy-start(bf16[3,3,3,256,128]{4,3,2,1,0:T(8,128)(2,1)} %refs_5_.1) | copy-start | bytes 5308420
  18.4 1.5 %copy-start.6 = (f32[128]{0:T(128)S(1)}, f32[128]{0:T(128)}, u32[]{:S(2)}) copy-start(f32[128]{0:T(128)} %param.15) | copy-start | bytes 1540
  18.9 2.3 %collective-permute-start.4 = (bf16[4,2,64,128]{3,2,1,0:T(8,128)(2,1)S(1)}, bf16[4,2,64,128]{3,2,1,0:T(8,128)(2,1)S(1)}, u32[]{:S(2)}, u32[]{:S(2)}) collective-permute-start(bf16[4,2,64,128]{3,2,1,0:T(8,128)(2,1)S(1)} %collective-permute-done.3.refs_2_), channel_id=1, source_target_pairs={{0,16},{16,0},{1,17},{17,1},{2,18},{18,2},{3,19},{19,3},{4,20},{20... | collective-permute-start | bytes 393224 | tf_op jit(solution)/shard_map/ppermute | solution.py:417
  23.1 10.1 %all-to-all-start.1 = ((f32[32,2,128]{2,1,0:T(2,128)}), f32[32,2,128]{2,1,0:T(2,128)S(1)}, u32[]{:S(2)}, u32[]{:S(2)}) async-start(f32[32,2,128]{2,1,0:T(2,128)} %get-tuple-element.26), calls=%async_computation.1 | async-start | bytes 65536 | tf_op jit(solution)/shard_map/all_to_all | solution.py:388
  26.0 3.9 %copy-start.3 = (bf16[256,128]{1,0:T(8,128)(2,1)S(1)}, bf16[256,128]{1,0:T(8,128)(2,1)}, u32[]{:S(2)}) copy-start(bf16[256,128]{1,0:T(8,128)(2,1)} %skip_ref.1) | copy-start | bytes 196612
  26.0 3.9 %copy-start.7 = (f32[128]{0:T(128)S(1)}, f32[128]{0:T(128)}, u32[]{:S(2)}) copy-start(f32[128]{0:T(128)} %param.21) | copy-start | bytes 1540
  26.0 3.9 %copy-start.8 = (f32[128]{0:T(128)S(1)}, f32[128]{0:T(128)}, u32[]{:S(2)}) copy-start(f32[128]{0:T(128)} %param.19) | copy-start | bytes 1540
  26.0 7.2 %copy-start.1 = (bf16[3,3,3,128,128]{4,3,2,1,0:T(8,128)(2,1)S(1)}, bf16[3,3,3,128,128]{4,3,2,1,0:T(8,128)(2,1)}, u32[]{:S(2)}) copy-start(bf16[3,3,3,128,128]{4,3,2,1,0:T(8,128)(2,1)} %weight_ref.5) | copy-start | bytes 2654212
  26.0 7.2 %copy-start.9 = (f32[128]{0:T(128)S(1)}, f32[128]{0:T(128)}, u32[]{:S(2)}) copy-start(f32[128]{0:T(128)} %param.16) | copy-start | bytes 1540
  26.1 7.2 %copy-start.10 = (f32[128]{0:T(128)S(1)}, f32[128]{0:T(128)}, u32[]{:S(2)}) copy-start(f32[128]{0:T(128)} %param.17) | copy-start | bytes 1540
  26.1 8.2 %collective-permute-start.5 = (bf16[2,10,32,128]{3,2,1,0:T(8,128)(2,1)S(1)}, bf16[2,10,32,128]{3,2,1,0:T(8,128)(2,1)S(1)}, u32[]{:S(2)}, u32[]{:S(2)}) collective-permute-start(bf16[2,10,32,128]{3,2,1,0:T(8,128)(2,1)S(1)} %pack_hidden.1), channel_id=1, source_target_pairs={{0,2},{1,3},{2,4},{3,5},{4,6},{5,7},{6,8},{7,9},{8,10},{9,11},{10,... | collective-permute-start | bytes 491528 | tf_op jit(solution)/shard_map/ppermute | solution.py:414
